TPU v7x, 32 devices: a whole 2x2x4 slice. The times are simulated.
32 devices in a mesh: attn: 2 (over y), exp: 4 (over z), seq: 4 (over x, core).
Axes of the slice: x: 2, y: 2, z: 4, core: 2. Of those that a mesh axis runs over, the one named last changes fastest.
Arguments:
- tokens: bfloat16 [16, 6144], P(('attn', 'exp'), 'seq'), may hold values from -6 to 6
- modality: int32 [16], P(('attn', 'exp')), may hold values from 0 to 1, as said below
- cotangent: bfloat16 [16, 6144], P(('attn', 'exp'), 'seq'), may hold values from -6 to 6
- gate_speech: bfloat16 [6144, 24576], P('seq', ('attn', 'exp')), may hold values from -0.078125 to 0.078125
- up_speech: bfloat16 [6144, 24576], P('seq', ('attn', 'exp')), may hold values from -0.078125 to 0.078125
- down_speech: bfloat16 [24576, 6144], P(('attn', 'exp'), 'seq'), may hold values from -0.078125 to 0.078125
- gate_text: bfloat16 [6144, 16384], P('seq', ('attn', 'exp')), may hold values from -0.078125 to 0.078125
- up_text: bfloat16 [6144, 16384], P('seq', ('attn', 'exp')), may hold values from -0.078125 to 0.078125
- down_text: bfloat16 [16384, 6144], P(('attn', 'exp'), 'seq'), may hold values from -0.09375 to 0.09375
Outputs:
- mixed: bfloat16 [16, 6144], P(('attn', 'exp'), 'seq')
- token_grad: bfloat16 [16, 6144], P(('attn', 'exp'), 'seq')
- down_speech_grad: bfloat16 [24576, 6144], P(('attn', 'exp'), 'seq')
- down_text_grad: bfloat16 [16384, 6144], P(('attn', 'exp'), 'seq')
Inputs may be any that keep to these rules, and one draw needn't show every extreme that they name: Exactly 10 tokens of the window have modality 0 and the other 6 have modality 1, at places drawn from the seed.
All inputs are finite; a program needn't handle non-finite values.
Results may differ from a plain program's by a relative error of at most 0.005.
Values may be sent and summed in bfloat16 or wider, within the bound.
No kernel may reach another device: no remote copies, remote signals or barrier semaphores. Data moves between devices by JAX's collectives and lax.ppermute only.
A program may use at most 256 MiB of HBM per device.

v0:
```python
import jax
import jax.numpy as jnp
from jax import lax
from jax.sharding import PartitionSpec as P


def contract_first(left, right):
    return lax.dot_general(
        left, right, (((0,), (0,)), ((), ())), preferred_element_type=jnp.float32
    )


def contract_last(left, right):
    return lax.dot_general(
        left, right, (((1,), (1,)), ((), ())), preferred_element_type=jnp.float32
    )


def shards(
    tokens, modality, cotangent, gate_speech, up_speech, down_speech, gate_text, up_text, down_text
):
    rows, grads, kinds = (
        lax.all_gather(tokens, ("attn", "exp"), axis=0, tiled=True),
        lax.all_gather(cotangent, ("attn", "exp"), axis=0, tiled=True),
        lax.all_gather(modality, ("attn", "exp"), axis=0, tiled=True),
    )
    speech = (kinds == 0)[:, None]
    features = lax.all_gather(rows, "seq", axis=1, tiled=True)
    full_gs, full_us, full_gt, full_ut = (
        lax.all_gather(gate_speech, "seq", axis=0, tiled=True),
        lax.all_gather(up_speech, "seq", axis=0, tiled=True),
        lax.all_gather(gate_text, "seq", axis=0, tiled=True),
        lax.all_gather(up_text, "seq", axis=0, tiled=True),
    )
    zero = jnp.zeros_like(grads)
    speech_grads = jnp.where(speech, grads, zero)
    text_grads = jnp.where(speech, zero, grads)
    terms = (
        jnp.dot(features, full_gs, preferred_element_type=jnp.float32),
        jnp.dot(features, full_us, preferred_element_type=jnp.float32),
        jnp.dot(features, full_gt, preferred_element_type=jnp.float32),
        jnp.dot(features, full_ut, preferred_element_type=jnp.float32),
    )
    gs, us, gt, ut = terms
    hs = (jax.nn.silu(gs) * us).astype(jnp.bfloat16)
    ht = (jax.nn.silu(gt) * ut).astype(jnp.bfloat16)
    speech_out = jnp.dot(hs, down_speech, preferred_element_type=jnp.float32)
    text_out = jnp.dot(ht, down_text, preferred_element_type=jnp.float32)
    partial_out = jnp.where(speech, speech_out, text_out)
    mixed = lax.psum_scatter(partial_out, ("attn", "exp"), scatter_dimension=0, tiled=True).astype(
        jnp.bfloat16
    )
    dhs, dht = lax.psum(
        (contract_last(speech_grads, down_speech), contract_last(text_grads, down_text)), "seq"
    )
    sig_s = jax.nn.sigmoid(gs)
    sig_t = jax.nn.sigmoid(gt)
    dgs = (dhs * us * sig_s * (1.0 + gs * (1.0 - sig_s))).astype(jnp.bfloat16)
    dus = (dhs * jax.nn.silu(gs)).astype(jnp.bfloat16)
    dgt = (dht * ut * sig_t * (1.0 + gt * (1.0 - sig_t))).astype(jnp.bfloat16)
    dut = (dht * jax.nn.silu(gt)).astype(jnp.bfloat16)
    speech_back = contract_last(dgs, gate_speech) + contract_last(dus, up_speech)
    text_back = contract_last(dgt, gate_text) + contract_last(dut, up_text)
    partial_grad = speech_back + text_back
    token_grad = lax.psum_scatter(
        partial_grad, ("attn", "exp"), scatter_dimension=0, tiled=True
    ).astype(jnp.bfloat16)
    down_speech_grad = contract_first(hs, speech_grads).astype(jnp.bfloat16)
    down_text_grad = contract_first(ht, text_grads).astype(jnp.bfloat16)
    return (mixed, token_grad, down_speech_grad, down_text_grad)


def solution(mesh):
    return jax.shard_map(
        shards,
        mesh=mesh,
        in_specs=(
            P(("attn", "exp"), "seq"),
            P(("attn", "exp")),
            P(("attn", "exp"), "seq"),
            P("seq", ("attn", "exp")),
            P("seq", ("attn", "exp")),
            P(("attn", "exp"), "seq"),
            P("seq", ("attn", "exp")),
            P("seq", ("attn", "exp")),
            P(("attn", "exp"), "seq"),
        ),
        out_specs=(
            P(("attn", "exp"), "seq"),
            P(("attn", "exp"), "seq"),
            P(("attn", "exp"), "seq"),
            P(("attn", "exp"), "seq"),
        ),
        check_vma=False,
    )
```

profile of v0, /device:TPU:0, one launch (start us, length us, event | category | flops | bytes accessed | tf_op | source)
XLA Modules:
  0.0 901.6 jit_solution(7202291387515595924)
XLA Ops:
  10.2 13.0 %all-reduce = s32[16]{0:T(128)S(1)} all-reduce(s32[16]{0:T(128)S(1)} %dynamic-update-slice), channel_id=1, replica_groups=mesh['attn'=2,'exp'=4,'seq'=4] {'attn','exp'}, use_global_device_ids=true, to_apply=%add | all-reduce | flops 16 | bytes 128
  23.2 30.7 %all-gather.1 = bf16[8,2,1536]{2,1,0:T(2,128)(2,1)S(1)} all-gather(bf16[1,2,1536]{2,1,0:T(2,128)(2,1)S(1)} %bitcast.30), channel_id=1, replica_groups=mesh['attn'=2,'exp'=4,'seq'=4] {'attn','exp'}, dimensions={0}, use_global_device_ids=true | all-gather | bytes 55296 | tf_op jit(solution)/shard_map/all_gather | solution.py:24
  54.0 5.2 fusion.10
  59.2 6.9 fusion.9
  67.3 30.7 %all-gather = bf16[8,2,1536]{2,1,0:T(2,128)(2,1)S(1)} all-gather(bf16[1,2,1536]{2,1,0:T(2,128)(2,1)S(1)} %bitcast.31), channel_id=1, replica_groups=mesh['attn'=2,'exp'=4,'seq'=4] {'attn','exp'}, dimensions={0}, use_global_device_ids=true | all-gather | bytes 55296 | tf_op jit(solution)/shard_map/all_gather | solution.py:23
  98.7 7.1 all_gather.26
  105.8 62.4 %all-gather.11.cloned.1.call-done = bf16[6144,2048]{1,0:T(8,128)(2,1)} async-done(((bf16[1536,2048]{1,0:T(8,128)(2,1)}), bf16[6144,2048]{1,0:T(8,128)(2,1)}) %all-gather.11.cloned.1.call-update) | async-done | bytes 25165840 | tf_op jit(solution)/shard_map/all_gather | solution.py:32
  168.2 10.4 %fusion.22 = f32[16,2048]{1,0:T(8,128)S(1)} fusion(bf16[16,6144]{1,0:T(8,128)(2,1)S(1)} %all_gather.26, bf16[6144,2048]{1,0:T(8,128)(2,1)} %all-gather.11.cloned.1.call-done), kind=kOutput, calls=%fused_computation.38 | convolution fusion | flops 402653184 | bytes 25493504 | tf_op jit(solution)/shard_map/dot_general | solution.py:41
  178.6 146.0 %all-gather.13.cloned.1.call-done = bf16[6144,2048]{1,0:T(8,128)(2,1)} async-done(((bf16[1536,2048]{1,0:T(8,128)(2,1)}), bf16[6144,2048]{1,0:T(8,128)(2,1)}) %all-gather.13.cloned.1.call-update) | async-done | bytes 25165840 | tf_op jit(solution)/shard_map/all_gather | solution.py:33
  324.6 9.9 %multiply_convert_fusion.5 = (bf16[16,2048]{1,0:T(8,128)(2,1)S(1)}, f32[16,2048]{1,0:T(8,128)S(1)}) fusion(f32[16,2048]{1,0:T(8,128)S(1)} %fusion.22, bf16[16,6144]{1,0:T(8,128)(2,1)S(1)} %all_gather.26, bf16[6144,2048]{1,0:T(8,128)(2,1)} %all-gather.13.cloned.1.call-done), kind=kOutput, calls=%fused_computation.13 | convolution fusion | flops 402849792 | bytes 25690112 | tf_op jit(solution)/shard_map/dot_general | solution.py:42
  334.5 4.6 convolution_convert_fusion.1
  339.1 21.0 %all-reduce.8.cloned.1.call-done = (f32[16,3072]{1,0:T(8,128)}, f32[16,2048]{1,0:T(8,128)}) async-done(((f32[16,3072]{1,0:T(8,128)}, f32[16,2048]{1,0:T(8,128)}), (f32[16,3072]{1,0:T(8,128)}, f32[16,2048]{1,0:T(8,128)})) %all-reduce.8.cloned.1.call-update) | async-done | bytes 327696 | tf_op jit(solution)/shard_map/psum | solution.py:53
  360.1 4.6 fusion.5
  364.7 224.1 %all-gather.7.cloned.1.call-done = bf16[6144,3072]{1,0:T(8,128)(2,1)} async-done(((bf16[1536,3072]{1,0:T(8,128)(2,1)}), bf16[6144,3072]{1,0:T(8,128)(2,1)}) %all-gather.7.cloned.1.call-update) | async-done | bytes 37748752 | tf_op jit(solution)/shard_map/all_gather | solution.py:30
  588.8 18.6 %fusion.20 = f32[16,3072]{1,0:T(8,128)S(1)} fusion(bf16[16,6144]{1,0:T(8,128)(2,1)S(1)} %all_gather.26, bf16[6144,3072]{1,0:T(8,128)(2,1)} %all-gather.7.cloned.1.call-done), kind=kOutput, calls=%fused_computation.36 | convolution fusion | flops 603979776 | bytes 38141952 | tf_op jit(solution)/shard_map/dot_general | solution.py:39
  607.4 210.1 %all-gather.9.cloned.1.call-done = bf16[6144,3072]{1,0:T(8,128)(2,1)} async-done(((bf16[1536,3072]{1,0:T(8,128)(2,1)}), bf16[6144,3072]{1,0:T(8,128)(2,1)}) %all-gather.9.cloned.1.call-update) | async-done | bytes 37748752 | tf_op jit(solution)/shard_map/all_gather | solution.py:31
  817.5 14.4 %multiply_convert_fusion.2 = (bf16[16,3072]{1,0:T(8,128)(2,1)S(1)}, f32[16,3072]{1,0:T(8,128)S(1)}) fusion(f32[16,3072]{1,0:T(8,128)S(1)} %fusion.20, bf16[16,6144]{1,0:T(8,128)(2,1)S(1)} %all_gather.26, bf16[6144,3072]{1,0:T(8,128)(2,1)} %all-gather.9.cloned.1.call-done), kind=kOutput, calls=%fused_computation.8 | convolution fusion | flops 604274688 | bytes 38436864 | tf_op jit(solution)/shard_map/dot_general | solution.py:40
  831.9 5.1 fusion.21
  837.1 6.0 convolution_convert_fusion
  843.1 3.8 convolution_select_fusion
  846.9 2.5 fusion.3
  849.5 2.5 convolution_add_fusion.1
  852.1 1.7 fusion
  853.8 40.6 %all-reduce.9 = (bf16[16,1536]{1,0:T(8,128)(2,1)S(1)}, bf16[16,1536]{1,0:T(8,128)(2,1)S(1)}) all-reduce(f32[16,1536]{1,0:T(8,128)S(1)} %convolution_select_fusion, f32[16,1536]{1,0:T(8,128)S(1)} %fusion), channel_id=2, replica_groups=mesh['attn'=2,'exp'=4,'seq'=4] {'attn','exp'}, use_global_device_ids=true, to_apply=%region_0.1.clone | all-reduce | flops 49152 | bytes 294912
  (48 shorter events, 4.2 us)
Async XLA Ops:
  7.2 1.6 copy-start.4
  7.2 2.8 copy-start.5
  7.2 16.1 %copy-start.2 = (bf16[2,1536]{1,0:T(2,128)(2,1)S(1)}, bf16[2,1536]{1,0:T(2,128)(2,1)}, u32[]{:S(2)}) copy-start(bf16[2,1536]{1,0:T(2,128)(2,1)} %param.11) | copy-start | bytes 18436
  7.2 161.0 %all-gather.11.cloned.1.call-start = ((), (), s32[]{:S(2)}) async-start(), calls=%async_computation.2 | async-start | bytes 31457280 | tf_op jit(solution)/shard_map/all_gather | solution.py:32
  7.9 316.7 %all-gather.13.cloned.1.call-start = ((), (), s32[]{:S(2)}) async-start(), calls=%async_computation.3 | async-start | bytes 31457280 | tf_op jit(solution)/shard_map/all_gather | solution.py:33
  8.7 351.4 %all-reduce.8.cloned.1.call-start = ((), (), s32[]{:S(2)}) async-start(), calls=%async_computation.4 | async-start | bytes 655360 | tf_op jit(solution)/shard_map/psum | solution.py:53
  66.1 1.2 copy-start.3
  66.1 522.7 %all-gather.7.cloned.1.call-start = ((), (), s32[]{:S(2)}) async-start(), calls=%async_computation | async-start | bytes 47185920 | tf_op jit(solution)/shard_map/all_gather | solution.py:30
  66.7 750.8 %all-gather.9.cloned.1.call-start = ((), (), s32[]{:S(2)}) async-start(), calls=%async_computation.1 | async-start | bytes 47185920 | tf_op jit(solution)/shard_map/all_gather | solution.py:31
  831.9 15.0 %slice-start = ((s8[9437184]{0:T(1024)(128)(4,1)}), s8[4194304]{0:T(1024)(128)(4,1)S(1)}, s32[]{:S(2)}) async-start(s8[9437184]{0:T(1024)(128)(4,1)} %bitcast.24), calls=%async_computation.5 | async-start | bytes 8388608
  831.9 15.0 %slice-start.1 = ((s8[9437184]{0:T(1024)(128)(4,1)}), s8[4194304]{0:T(1024)(128)(4,1)S(1)}, s32[]{:S(2)}) async-start(s8[9437184]{0:T(1024)(128)(4,1)} %bitcast.24), calls=%async_computation.6 | async-start | bytes 8388608
  837.0 9.8 %slice-start.2 = ((s8[9437184]{0:T(1024)(128)(4,1)}), s8[1048576]{0:T(1024)(128)(4,1)S(1)}, s32[]{:S(2)}) async-start(s8[9437184]{0:T(1024)(128)(4,1)} %bitcast.24), calls=%async_computation.7 | async-start | bytes 2097152
  837.1 9.9 %copy-start = (f32[16,3072]{1,0:T(8,128)S(1)}, f32[16,3072]{1,0:T(8,128)}, u32[]{:S(2)}) copy-start(f32[16,3072]{1,0:T(8,128)} %get-tuple-element.6) | copy-start | bytes 589828
  837.1 12.4 %slice-start.3 = ((s8[9437184]{0:T(1024)(128)(4,1)}), s8[4194304]{0:T(1024)(128)(4,1)S(1)}, s32[]{:S(2)}) async-start(s8[9437184]{0:T(1024)(128)(4,1)} %bitcast.26), calls=%async_computation.8 | async-start | bytes 8388608
  837.1 12.4 %slice-start.4 = ((s8[9437184]{0:T(1024)(128)(4,1)}), s8[4194304]{0:T(1024)(128)(4,1)S(1)}, s32[]{:S(2)}) async-start(s8[9437184]{0:T(1024)(128)(4,1)} %bitcast.26), calls=%async_computation.9 | async-start | bytes 8388608
  843.1 6.4 slice-start.5
  846.9 5.2 slice-start.6
  846.9 5.1 slice-start.7
  846.9 5.1 copy-start.1
Sparse Core Ops, SparseCore 0:
  9.6 158.5 all-gather.10
  169.8 154.7 all-gather.12
  327.7 32.3 all-reduce.7
  361.5 227.2 all-gather.6
  590.2 227.2 all-gather.8
where the time goes:
time: 902 us
  waiting for transfers between devices  666 us (74%)
  blocking collectives  122 us (14%)
  matrix products  96.3 us (11%)
  between operations  15.3 us (2%)
    all_gather x1, waiting for transfers between devices, shards(): lax.all_gather(gate_speech, 'seq', axis=0, tiled=True)  224 us
    all_gather x1, waiting for transfers between devices, shards(): lax.all_gather(up_speech, 'seq', axis=0, tiled=True)  210 us
    all_gather x1, waiting for transfers between devices, shards(): lax.all_gather(up_text, 'seq', axis=0, tiled=True)  146 us
    all_gather x1, waiting for transfers between devices, shards(): lax.all_gather(gate_text, 'seq', axis=0, tiled=True)  62.4 us
    unnamed x2, blocking collectives  53.6 us
    all_gather x1, blocking collectives, shards(): lax.all_gather(tokens, ('attn', 'exp'), axis=0, tiled=True)  30.7 us
    all_gather x1, blocking collectives, shards(): lax.all_gather(cotangent, ('attn', 'exp'), axis=0, tiled=True)  30.7 us
    dot_general x6, matrix products, contract_last(): lax.dot_general(left, right, (((1,), (1,)), ((), ())), preferred_element_...  23.5 us
  transfers between devices with their start and end apart: 5, of which 5 were waited for; matrix products, arithmetic and copies ran while one was open for 7% of the time, Pallas kernels for 0%

commit v1 on v0

v1 whole, which is shorter than its diff:
```python
import jax
import jax.numpy as jnp
from jax import lax
from jax.sharding import PartitionSpec as P

TOK = ("attn", "exp")
F32 = jnp.float32
BF16 = jnp.bfloat16


def contract_first(left, right):
    return lax.dot_general(left, right, (((0,), (0,)), ((), ())), preferred_element_type=F32)


def contract_last(left, right):
    return lax.dot_general(left, right, (((1,), (1,)), ((), ())), preferred_element_type=F32)


def flip(value, bit, n):
    return lax.ppermute(value, "seq", [(i, i ^ bit) for i in range(n)])


def sum_and_share(parts, apply, n):
    width = parts[0].shape[1]
    half = width // 2
    odd = lax.axis_index("seq") % 2
    packed = jnp.stack(parts).astype(BF16)
    first, second = packed[:, :, :half], packed[:, :, half:]
    theirs = jnp.where(odd == 1, first, second)
    mine = jnp.where(odd == 1, second, first)
    got = flip(theirs, 1, n)
    mine = mine.astype(F32) + got.astype(F32)
    got = flip(mine.astype(BF16), 2, n)
    mine = mine + got.astype(F32)
    done = jnp.stack(apply(*mine)).astype(BF16)
    other = flip(done, 1, n)
    low = jnp.where(odd == 1, other, done)
    high = jnp.where(odd == 1, done, other)
    return jnp.concatenate([low, high], axis=2)


def middle(g, u, dh):
    sig = jax.nn.sigmoid(g)
    silu = g * sig
    h = silu * u
    dg = dh * u * sig * (1.0 + g * (1.0 - sig))
    du = dh * silu
    return h, dg, du


def shards(sizes, tokens, modality, cotangent, gate_s, up_s, down_s, gate_t, up_t, down_t):
    n_seq, n_tok = sizes
    width = tokens.shape[1]
    fs, ft = gate_s.shape[1], gate_t.shape[1]
    kind = jnp.broadcast_to(modality.astype(BF16)[:, None], (modality.shape[0], 128))
    packed = jnp.concatenate([tokens, cotangent, kind], axis=1)
    packed = lax.all_gather(packed, TOK, axis=0, tiled=True)
    rows, grads = packed[:, :width], packed[:, width : 2 * width]
    speech = packed[:, 2 * width : 2 * width + 1] == 0

    def pick(s, t):
        return jnp.concatenate([jnp.where(speech, s[:, :ft], t), s[:, ft:]], axis=1)

    g = pick(jnp.dot(rows, gate_s, preferred_element_type=F32), jnp.dot(rows, gate_t, preferred_element_type=F32))
    u = pick(jnp.dot(rows, up_s, preferred_element_type=F32), jnp.dot(rows, up_t, preferred_element_type=F32))
    dh = pick(contract_last(grads, down_s), contract_last(grads, down_t))
    h, dg, du = sum_and_share((g, u, dh), middle, n_seq)
    zero = jnp.zeros((), BF16)

    def halves(v):
        return jnp.where(speech, v, zero), jnp.where(speech, zero, v[:, :ft])

    hs, ht = halves(h)
    dgs, dgt = halves(dg)
    dus, dut = halves(du)
    mixed = jnp.dot(hs, down_s, preferred_element_type=F32) + jnp.dot(ht, down_t, preferred_element_type=F32)
    back = (
        contract_last(dgs, gate_s)
        + contract_last(dus, up_s)
        + contract_last(dgt, gate_t)
        + contract_last(dut, up_t)
    )
    out = jnp.concatenate([mixed, back], axis=1).astype(BF16)
    out = out.reshape(n_tok, out.shape[0] // n_tok, out.shape[1])
    out = lax.all_to_all(out, TOK, split_axis=0, concat_axis=0, tiled=True)
    out = jnp.sum(out.astype(F32), axis=0).astype(BF16)
    down_s_grad = contract_first(hs, grads).astype(BF16)
    down_t_grad = contract_first(ht, grads).astype(BF16)
    return out[:, :width], out[:, width:], down_s_grad, down_t_grad


def solution(mesh):
    sizes = (mesh.shape["seq"], mesh.shape["attn"] * mesh.shape["exp"])

    def run(*args):
        return shards(sizes, *args)

    return jax.shard_map(
        run,
        mesh=mesh,
        in_specs=(
            P(TOK, "seq"),
            P(TOK),
            P(TOK, "seq"),
            P("seq", TOK),
            P("seq", TOK),
            P(TOK, "seq"),
            P("seq", TOK),
            P("seq", TOK),
            P(TOK, "seq"),
        ),
        out_specs=(P(TOK, "seq"),) * 4,
        check_vma=False,
    )
```

time: 902 us -> 95.3 us (0.11)
  waiting for transfers between devices: 666 us -> 9.77 us
  blocking collectives: 122 us -> 32.3 us
  matrix products: 96.3 us -> 39.4 us
  between operations: 15.3 us -> 0.9 us
    all_gather x4 -> x0, waiting for transfers between devices: 643 us -> none  [the longest x1 224 us: shards(): lax.all_gather(gate_speech, 'seq', axis=0, tiled=True)]
    unnamed x2 -> x0, blocking collectives: 53.6 us -> none
    dot_general x6, matrix products: 62.2 us -> 13.5 us  [the longest x1 5.16 us: shards(): jnp.dot(rows, up_s, preferred_element_type=F32)]
    all_gather x3 -> x1, blocking collectives: 68.5 us -> 32.3 us  [shards(): packed = lax.all_gather(packed, TOK, axis=0, tiled=True)]
    psum x1 -> x0, waiting for transfers between devices: 21 us -> none  [shards(): lax.psum((contract_last(speech_grads, down_speech), contract_last(text_gr...]
  transfers between devices with their start and end apart: 5 -> 4, of which waited for: 5 -> 4; matrix products, arithmetic and copies ran while one was open for 7% -> 5% of each run, Pallas kernels for 0% -> 0%
where the time goes in v1:
time: 95.3 us; the launch traced here: 94.9 us
  matrix products  39.4 us (41%)
  blocking collectives  32.3 us (34%)
  waiting for transfers between devices  9.77 us (10%)
  starting transfers between devices  7.36 us (8%)
  other arithmetic  2.56 us (3%)
  local copies, waits for them, and re-layouts  2.56 us (3%)
    all_gather x1, blocking collectives, shards(): packed = lax.all_gather(packed, TOK, axis=0, tiled=True)  32.3 us
    dot_general x6, matrix products, contract_last(): lax.dot_general(left, right, (((1,), (1,)), ((), ())), preferred_element_...  15.7 us
    dot_general x2, matrix products, contract_first(): lax.dot_general(left, right, (((0,), (0,)), ((), ())), preferred_element_...  10.2 us
    ppermute x3, waiting for transfers between devices, flip(): return lax.ppermute(value, 'seq', [(i, i ^ bit) for i in range(n)])  7.12 us
    all_to_all x1, starting transfers between devices, shards(): out = lax.all_to_all(out, TOK, split_axis=0, concat_axis=0, tiled=True)  5.66 us
    dot_general x1, matrix products, shards(): jnp.dot(rows, up_s, preferred_element_type=F32)  5.16 us
    dot_general x1, matrix products, shards(): jnp.dot(ht, down_t, preferred_element_type=F32)  3.75 us
    all_to_all x1, waiting for transfers between devices, shards(): out = lax.all_to_all(out, TOK, split_axis=0, concat_axis=0, tiled=True)  2.65 us
  transfers between devices with their start and end apart: 4, of which 4 were waited for; matrix products, arithmetic and copies ran while one was open for 5% of the time, Pallas kernels for 0%

profile of v1, /device:TPU:0, one launch (start us, length us, event | category | flops | bytes accessed | tf_op | source)
XLA Modules:
  0.0 94.9 jit_solution(17397036281969900924)
XLA Ops:
  1.4 0.7 maximum_bitcast_fusion.3
  2.1 32.3 %all-gather = bf16[8,2,3200]{2,1,0:T(2,128)(2,1)S(1)} all-gather(bf16[1,2,3200]{2,1,0:T(2,128)(2,1)S(1)} %maximum_bitcast_fusion.3), channel_id=1, replica_groups=mesh['attn'=2,'exp'=4,'seq'=4] {'attn','exp'}, dimensions={0}, use_global_device_ids=true | all-gather | bytes 115200 | tf_op jit(solution)/shard_map/all_gather | solution.py:57
  34.6 5.2 %fusion.30 = bf16[16,3072]{1,0:T(8,128)(2,1)S(1)} fusion(bf16[1536,3072]{1,0:T(8,128)(2,1)} %param.13, bf16[16,3200]{1,0:T(8,128)(2,1)S(1)} %reshape.15), kind=kOutput, calls=%fused_computation.67 | convolution fusion | flops 150994944 | bytes 9584640 | tf_op jit(solution)/shard_map/dot_general | solution.py:65
  39.8 1.3 %copy-done = bf16[3072,1536]{1,0:T(8,128)(2,1)S(1)} copy-done((bf16[3072,1536]{1,0:T(8,128)(2,1)S(1)}, bf16[3072,1536]{1,0:T(8,128)(2,1)}, u32[]{:S(2)}) %copy-start) | copy-done | bytes 9437208
  41.1 2.5 %fusion.27 = bf16[16,3072]{1,0:T(8,128)(2,1)S(1)} fusion(bf16[3072,1536]{1,0:T(8,128)(2,1)S(1)} %copy-done, bf16[16,3200]{1,0:T(8,128)(2,1)S(1)} %reshape.15), kind=kOutput, calls=%fused_computation.64 | convolution fusion | flops 150994944 | bytes 9584640 | tf_op jit(solution)/shard_map/dot_general | solution.py:16
  43.7 0.9 fusion.1
  44.6 4.7 %fusion.2 = bf16[16,2048]{1,0:T(8,128)(2,1)S(1)} fusion(bf16[2048,1536]{1,0:T(8,128)(2,1)} %param.17, bf16[16,3072]{1,0:T(8,128)(2,1)S(1)} %fusion.27, pred[16]{0:T(512)(128)(4,1)S(1)} %bitcast.38, bf16[16,3200]{1,0:T(8,128)(2,1)S(1)} %reshape.15), kind=kOutput, calls=%fused_computation.11 | convolution fusion | flops 100696064 | bytes 6472192 | tf_op jit(solution)/shard_map/dot_general | solution.py:16
  49.3 1.3 %fusion.33 = bf16[16,3072]{1,0:T(8,128)(2,1)S(1)} fusion(bf16[1536,3072]{1,0:T(8,128)(2,1)S(1)} %bitcast.28, bf16[16,3200]{1,0:T(8,128)(2,1)S(1)} %reshape.15), kind=kOutput, calls=%fused_computation.70 | convolution fusion | flops 150994944 | bytes 9584640 | tf_op jit(solution)/shard_map/dot_general | solution.py:64
  50.9 0.9 fusion
  52.0 1.4 %collective-permute-done = bf16[3,16,1536]{2,1,0:T(8,128)(2,1)S(1)} collective-permute-done((bf16[3,16,1536]{2,1,0:T(8,128)(2,1)S(1)}, bf16[3,16,1536]{2,1,0:T(8,128)(2,1)S(1)}, u32[]{:S(2)}, u32[]{:S(2)}) %collective-permute-start) | collective-permute-done | bytes 147488 | tf_op jit(solution)/shard_map/ppermute | solution.py:20
  53.5 1.6 %collective-permute-start.1 = (bf16[3,16,1536]{2,1,0:T(8,128)(2,1)S(1)}, bf16[3,16,1536]{2,1,0:T(8,128)(2,1)S(1)}, u32[]{:S(2)}, u32[]{:S(2)}) collective-permute-start(bf16[3,16,1536]{2,1,0:T(8,128)(2,1)S(1)} %fusion.5), channel_id=1, source_target_pairs={{0,2},{1,3},{2,0},{3,1},{4,6},{5,7},{6,4},{7,5},{8,10},{9,11},{10,... | collective-permute-start | bytes 442376 | tf_op jit(solution)/shard_map/ppermute | solution.py:20
  55.0 4.4 %collective-permute-done.1 = bf16[3,16,1536]{2,1,0:T(8,128)(2,1)S(1)} collective-permute-done((bf16[3,16,1536]{2,1,0:T(8,128)(2,1)S(1)}, bf16[3,16,1536]{2,1,0:T(8,128)(2,1)S(1)}, u32[]{:S(2)}, u32[]{:S(2)}) %collective-permute-start.1) | collective-permute-done | bytes 147488 | tf_op jit(solution)/shard_map/ppermute | solution.py:20
  59.7 1.4 %collective-permute-done.2 = bf16[3,16,1536]{2,1,0:T(8,128)(2,1)S(1)} collective-permute-done((bf16[3,16,1536]{2,1,0:T(8,128)(2,1)S(1)}, bf16[3,16,1536]{2,1,0:T(8,128)(2,1)S(1)}, u32[]{:S(2)}, u32[]{:S(2)}) %collective-permute-start.2) | collective-permute-done | bytes 147488 | tf_op jit(solution)/shard_map/ppermute | solution.py:20
  61.1 1.4 %fusion.21 = f32[16,1536]{1,0:T(8,128)S(1)} fusion(bf16[3072,1536]{1,0:T(8,128)(2,1)S(1)} %copy-done, bf16[16,3072]{1,0:T(8,128)(2,1)S(1)} %get-tuple-element.4, pred[16]{0:T(512)(128)(4,1)S(1)} %bitcast.40), kind=kOutput, calls=%fused_computation.58 | convolution fusion | flops 151044096 | bytes 9633808 | tf_op jit(solution)/shard_map/dot_general | solution.py:76
  62.5 5.6 %convolution_convert_fusion = bf16[3072,1536]{1,0:T(8,128)(2,1)} fusion(bf16[16,3072]{1,0:T(8,128)(2,1)S(1)} %get-tuple-element.4, pred[16]{0:T(512)(128)(4,1)S(1)} %bitcast.41, bf16[16,3200]{1,0:T(8,128)(2,1)S(1)} %reshape.15), kind=kOutput, calls=%fused_computation | convolution fusion | flops 155762688 | bytes 9585152 | tf_op jit(solution)/shard_map/dot_general | solution.py:12
  68.1 2.5 %fusion.12 = f32[16,1536]{1,0:T(8,128)S(1)} fusion(bf16[1536,3072]{1,0:T(8,128)(2,1)S(1)} %bitcast.28, bf16[16,3072]{1,0:T(8,128)(2,1)S(1)} %get-tuple-element.6, pred[16]{0:T(512)(128)(4,1)S(1)} %bitcast.42), kind=kOutput, calls=%fused_computation.38 | convolution fusion | flops 151044096 | bytes 9633808 | tf_op jit(solution)/shard_map/dot_general | solution.py:16
  70.7 2.5 %convolution_add_fusion.2 = f32[16,1536]{1,0:T(8,128)S(1)} fusion(f32[16,1536]{1,0:T(8,128)S(1)} %fusion.12, bf16[1536,3072]{1,0:T(8,128)(2,1)S(1)} %bitcast.30, bf16[16,3072]{1,0:T(8,128)(2,1)S(1)} %get-tuple-element.5, pred[16]{0:T(512)(128)(4,1)S(1)} %bitcast.43), kind=kOutput, calls=%fused_computation.4 | convolution fusion | flops 151068672 | bytes 9732112 | tf_op jit(solution)/shard_map/dot_general | solution.py:16
  73.2 1.7 %convolution_add_fusion.1 = f32[16,1536]{1,0:T(8,128)S(1)} fusion(f32[16,1536]{1,0:T(8,128)S(1)} %convolution_add_fusion.2, bf16[1536,2048]{1,0:T(8,128)(2,1)S(1)} %bitcast.32, bf16[16,3072]{1,0:T(8,128)(2,1)S(1)} %get-tuple-element.6, pred[16]{0:T(512)(128)(4,1)S(1)} %bitcast.44), kind=kOutput, calls=%fused_computation.3 | convolution fusion | flops 100720640 | bytes 6554112 | tf_op jit(solution)/shard_map/dot_general | solution.py:16
  75.0 1.7 %fusion.4 = bf16[16,1536]{1,0:T(8,128)(2,1)S(1)} fusion(f32[16,1536]{1,0:T(8,128)S(1)} %convolution_add_fusion.1, bf16[1536,2048]{1,0:T(8,128)(2,1)S(1)} %bitcast.36, bf16[16,3072]{1,0:T(8,128)(2,1)S(1)} %get-tuple-element.5, pred[16]{0:T(512)(128)(4,1)S(1)} %bitcast.45), kind=kOutput, calls=%fused_computation.13 | convolution fusion | flops 100745216 | bytes 6504960 | tf_op jit(solution)/shard_map/dot_general | solution.py:16
  76.8 3.8 %fusion.3 = bf16[16,1536]{1,0:T(8,128)(2,1)S(1)} fusion(f32[16,1536]{1,0:T(8,128)S(1)} %fusion.21, bf16[2048,1536]{1,0:T(8,128)(2,1)} %param.17, bf16[16,3072]{1,0:T(8,128)(2,1)S(1)} %get-tuple-element.4, pred[16]{0:T(512)(128)(4,1)S(1)} %bitcast.46), kind=kOutput, calls=%fused_computation.12 | convolution fusion | flops 100745216 | bytes 6504960 | tf_op jit(solution)/shard_map/dot_general | solution.py:76
  80.6 0.7 pad_maximum_fusion.3
  81.3 5.7 %all-to-all-start = ((bf16[8,2,3072]{2,1,0:T(2,128)(2,1)}), bf16[8,2,3072]{2,1,0:T(2,128)(2,1)S(1)}, u32[]{:S(2)}, u32[]{:S(2)}) async-start(bf16[8,2,3072]{2,1,0:T(2,128)(2,1)} %pad_maximum_fusion.3), calls=%async_computation | async-start | bytes 196608 | tf_op jit(solution)/shard_map/all_to_all | solution.py:85
  86.9 4.6 %convolution_convert_fusion.1 = bf16[2048,1536]{1,0:T(8,128)(2,1)} fusion(bf16[16,3200]{1,0:T(8,128)(2,1)S(1)} %reshape.15, bf16[16,3072]{1,0:T(8,128)(2,1)S(1)} %get-tuple-element.4, pred[16]{0:T(512)(128)(4,1)S(1)} %bitcast.47), kind=kOutput, calls=%fused_computation.1 | convolution fusion | flops 103841792 | bytes 6406656 | tf_op jit(solution)/shard_map/dot_general | solution.py:12
  91.6 2.6 %all-to-all-done = bf16[8,2,3072]{2,1,0:T(2,128)(2,1)S(1)} async-done(((bf16[8,2,3072]{2,1,0:T(2,128)(2,1)}), bf16[8,2,3072]{2,1,0:T(2,128)(2,1)S(1)}, u32[]{:S(2)}, u32[]{:S(2)}) %all-to-all-start) | async-done | bytes 98336 | tf_op jit(solution)/shard_map/all_to_all | solution.py:85
  (54 shorter events, 2.5 us)
Async XLA Ops:
  34.5 9.2 %slice-start.8 = ((s8[6291456]{0:T(1024)(128)(4,1)}), s8[2097152]{0:T(1024)(128)(4,1)S(1)}, s32[]{:S(2)}) async-start(s8[6291456]{0:T(1024)(128)(4,1)} %bitcast.33), calls=%async_computation.9 | async-start | bytes 4194304
  34.6 6.5 %copy-start = (bf16[3072,1536]{1,0:T(8,128)(2,1)S(1)}, bf16[3072,1536]{1,0:T(8,128)(2,1)}, u32[]{:S(2)}) copy-start(bf16[3072,1536]{1,0:T(8,128)(2,1)} %param.14) | copy-start | bytes 28311556
  34.6 9.1 %slice-start.9 = ((s8[6291456]{0:T(1024)(128)(4,1)}), s8[4194304]{0:T(1024)(128)(4,1)S(1)}, s32[]{:S(2)}) async-start(s8[6291456]{0:T(1024)(128)(4,1)} %bitcast.33), calls=%async_computation.10 | async-start | bytes 8388608
  41.1 8.2 %slice-start = ((s8[9437184]{0:T(1024)(128)(4,1)}), s8[4194304]{0:T(1024)(128)(4,1)S(1)}, s32[]{:S(2)}) async-start(s8[9437184]{0:T(1024)(128)(4,1)} %bitcast.27), calls=%async_computation.1 | async-start | bytes 8388608
  41.1 8.2 %slice-start.1 = ((s8[9437184]{0:T(1024)(128)(4,1)}), s8[4194304]{0:T(1024)(128)(4,1)S(1)}, s32[]{:S(2)}) async-start(s8[9437184]{0:T(1024)(128)(4,1)} %bitcast.27), calls=%async_computation.2 | async-start | bytes 8388608
  43.7 5.6 %slice-start.2 = ((s8[9437184]{0:T(1024)(128)(4,1)}), s8[1048576]{0:T(1024)(128)(4,1)S(1)}, s32[]{:S(2)}) async-start(s8[9437184]{0:T(1024)(128)(4,1)} %bitcast.27), calls=%async_computation.3 | async-start | bytes 2097152
  44.6 6.1 %slice-start.6 = ((s8[6291456]{0:T(1024)(128)(4,1)}), s8[4194304]{0:T(1024)(128)(4,1)S(1)}, s32[]{:S(2)}) async-start(s8[6291456]{0:T(1024)(128)(4,1)} %bitcast.31), calls=%async_computation.7 | async-start | bytes 8388608
  49.3 1.6 %slice-start.7 = ((s8[6291456]{0:T(1024)(128)(4,1)}), s8[2097152]{0:T(1024)(128)(4,1)S(1)}, s32[]{:S(2)}) async-start(s8[6291456]{0:T(1024)(128)(4,1)} %bitcast.31), calls=%async_computation.8 | async-start | bytes 4194304
  52.0 1.4 %collective-permute-start = (bf16[3,16,1536]{2,1,0:T(8,128)(2,1)S(1)}, bf16[3,16,1536]{2,1,0:T(8,128)(2,1)S(1)}, u32[]{:S(2)}, u32[]{:S(2)}) collective-permute-start(bf16[3,16,1536]{2,1,0:T(8,128)(2,1)S(1)} %broadcast_select_fusion.2), channel_id=1, source_target_pairs={{0,1},{1,0},{2,3},{3,2},{4,5},{5,4},{6,7},{7,6},{8,9},{9,8},{10,11... | collective-permute-start | bytes 442376 | tf_op jit(solution)/shard_map/ppermute | solution.py:20
  53.5 6.0 %collective-permute-start.1 = (bf16[3,16,1536]{2,1,0:T(8,128)(2,1)S(1)}, bf16[3,16,1536]{2,1,0:T(8,128)(2,1)S(1)}, u32[]{:S(2)}, u32[]{:S(2)}) collective-permute-start(bf16[3,16,1536]{2,1,0:T(8,128)(2,1)S(1)} %fusion.5), channel_id=1, source_target_pairs={{0,2},{1,3},{2,0},{3,1},{4,6},{5,7},{6,4},{7,5},{8,10},{9,11},{10,... | collective-permute-start | bytes 442376 | tf_op jit(solution)/shard_map/ppermute | solution.py:20
  59.6 1.4 %collective-permute-start.2 = (bf16[3,16,1536]{2,1,0:T(8,128)(2,1)S(1)}, bf16[3,16,1536]{2,1,0:T(8,128)(2,1)S(1)}, u32[]{:S(2)}, u32[]{:S(2)}) collective-permute-start(bf16[3,16,1536]{2,1,0:T(8,128)(2,1)S(1)} %pad_maximum_fusion.1), channel_id=1, source_target_pairs={{0,1},{1,0},{2,3},{3,2},{4,5},{5,4},{6,7},{7,6},{8,9},{9,8},{10,11... | collective-permute-start | bytes 442376 | tf_op jit(solution)/shard_map/ppermute | solution.py:20
  62.5 8.2 %slice-start.3 = ((s8[9437184]{0:T(1024)(128)(4,1)}), s8[4194304]{0:T(1024)(128)(4,1)S(1)}, s32[]{:S(2)}) async-start(s8[9437184]{0:T(1024)(128)(4,1)} %bitcast.29), calls=%async_computation.4 | async-start | bytes 8388608
  62.5 8.2 %slice-start.4 = ((s8[9437184]{0:T(1024)(128)(4,1)}), s8[4194304]{0:T(1024)(128)(4,1)S(1)}, s32[]{:S(2)}) async-start(s8[9437184]{0:T(1024)(128)(4,1)} %bitcast.29), calls=%async_computation.5 | async-start | bytes 8388608
  68.1 2.6 %slice-start.5 = ((s8[9437184]{0:T(1024)(128)(4,1)}), s8[1048576]{0:T(1024)(128)(4,1)S(1)}, s32[]{:S(2)}) async-start(s8[9437184]{0:T(1024)(128)(4,1)} %bitcast.29), calls=%async_computation.6 | async-start | bytes 2097152
  70.6 4.3 %slice-start.10 = ((s8[6291456]{0:T(1024)(128)(4,1)}), s8[4194304]{0:T(1024)(128)(4,1)S(1)}, s32[]{:S(2)}) async-start(s8[6291456]{0:T(1024)(128)(4,1)} %bitcast.35), calls=%async_computation.11 | async-start | bytes 8388608
  70.7 4.3 %slice-start.11 = ((s8[6291456]{0:T(1024)(128)(4,1)}), s8[2097152]{0:T(1024)(128)(4,1)S(1)}, s32[]{:S(2)}) async-start(s8[6291456]{0:T(1024)(128)(4,1)} %bitcast.35), calls=%async_computation.12 | async-start | bytes 4194304
  81.3 12.9 %all-to-all-start = ((bf16[8,2,3072]{2,1,0:T(2,128)(2,1)}), bf16[8,2,3072]{2,1,0:T(2,128)(2,1)S(1)}, u32[]{:S(2)}, u32[]{:S(2)}) async-start(bf16[8,2,3072]{2,1,0:T(2,128)(2,1)} %pad_maximum_fusion.3), calls=%async_computation | async-start | bytes 196608 | tf_op jit(solution)/shard_map/all_to_all | solution.py:85

commit v2 on v1

v2 whole, which is shorter than its diff:
```python
import functools

import jax
import jax.numpy as jnp
from jax import lax
from jax.experimental import pallas as pl
from jax.experimental.pallas import tpu as pltpu
from jax.sharding import PartitionSpec as P

TOK = ("attn", "exp")
F32 = jnp.float32
BF16 = jnp.bfloat16
MIB = 1 << 20
CUTS = 4
BLOCK = 512
HBM = pl.BlockSpec(memory_space=pl.ANY)
VMEM = pl.BlockSpec(memory_space=pltpu.VMEM)


def contract_first(left, right):
    return lax.dot_general(left, right, (((0,), (0,)), ((), ())), preferred_element_type=F32)


def contract_last(left, right):
    return lax.dot_general(left, right, (((1,), (1,)), ((), ())), preferred_element_type=F32)


def times(left, right):
    return jnp.dot(left, right, preferred_element_type=F32)


def copies_of(src, dst, sems):
    rows = src.shape[0] // CUTS
    cuts = [pl.ds(j * rows, rows) for j in range(CUTS)]
    return [pltpu.make_async_copy(src.at[c], dst.at[c], sems.at[j]) for j, c in enumerate(cuts)]


def blocks(count):
    return pl.loop(0, count)


def at(step, size):
    return pl.ds(pl.multiple_of(step * size, size), size)


def is_speech(arr_ref):
    return arr_ref[:, arr_ref.shape[1] - 1 :] == 0


def hbm(x):
    return pltpu.with_memory_space_constraint(x, pltpu.HBM)


def vmem(x):
    return pltpu.with_memory_space_constraint(x, pltpu.VMEM)


def size_of(*arrays):
    return sum(a.size * a.dtype.itemsize for a in arrays)


def call(body, name, outs, ins, in_vmem, scratch, flops, traffic, limit=8):
    return pl.pallas_call(
        body,
        out_shape=outs,
        in_specs=[VMEM if v else HBM for v in in_vmem],
        out_specs=[VMEM] * len(outs),
        scratch_shapes=scratch,
        compiler_params=pltpu.CompilerParams(vmem_limit_bytes=limit * MIB),
        cost_estimate=pl.CostEstimate(flops=flops, bytes_accessed=traffic, transcendentals=0),
        name=name,
    )(*[(vmem(x) if v else hbm(x)) if v is not None else x for x, v in zip(ins, in_vmem)])


def load_body(after_ref, gate_ref, up_ref, gate_out, up_out, sems):
    copies = copies_of(gate_ref, gate_out, sems.at[0]) + copies_of(up_ref, up_out, sems.at[1])
    for copy in copies:
        copy.start()
    for copy in copies:
        copy.wait()


def load(after, gate, up):
    outs = [pltpu.VMEM(w.shape, w.dtype) for w in (gate, up)]
    return call(
        load_body,
        "load_speech",
        outs,
        (after, gate, up),
        (True, False, False),
        [pltpu.SemaphoreType.DMA((2, CUTS))],
        0,
        size_of(gate, up),
    )


def forward_body(
    arr_ref, gs_ref, us_ref, gt_hbm, ut_hbm, dt_hbm, g_ref, u_ref, gt_ref, ut_ref, dt_ref, sems
):
    copies = [
        copies_of(src, dst, sems.at[i])
        for i, (src, dst) in enumerate(((gt_hbm, gt_ref), (ut_hbm, ut_ref), (dt_hbm, dt_ref)))
    ]
    for group in copies:
        for copy in group:
            copy.start()
    width = gs_ref.shape[0]
    x = arr_ref[:, :width]
    speech = is_speech(arr_ref)

    @blocks(gs_ref.shape[1] // BLOCK)
    def _(j):
        cut = at(j, BLOCK)
        g_ref[:, cut] = times(x, gs_ref[:, cut])
        u_ref[:, cut] = times(x, us_ref[:, cut])

    for group, src, out in ((copies[0], gt_ref, g_ref), (copies[1], ut_ref, u_ref)):
        for copy in group:
            copy.wait()

        @blocks(src.shape[1] // BLOCK)
        def _(j):
            cut = at(j, BLOCK)
            out[:, cut] = jnp.where(speech, out[:, cut], times(x, src[:, cut]))

    for copy in copies[2]:
        copy.wait()


def forward(arr, gate_s, up_s, gate_t, up_t, down_t):
    rows, fs = arr.shape[0], gate_s.shape[1]
    outs = [pltpu.VMEM((rows, fs), F32)] * 2 + [pltpu.VMEM(w.shape, w.dtype) for w in (gate_t, up_t, down_t)]
    return call(
        forward_body,
        "hidden_partials",
        outs,
        (arr, gate_s, up_s, gate_t, up_t, down_t),
        (True, True, True, False, False, False),
        [pltpu.SemaphoreType.DMA((3, CUTS))],
        2 * rows * (gate_s.size + gate_t.size) * 2,
        size_of(gate_t, up_t, down_t),
    )


def hidden_grad_body(arr_ref, dt_ref, ds_hbm, dh_ref, ds_ref, sems):
    copies = copies_of(ds_hbm, ds_ref, sems.at[0])
    for copy in copies:
        copy.start()
    width = dt_ref.shape[1]
    c = arr_ref[:, width : 2 * width]
    speech = is_speech(arr_ref)
    ft = dt_ref.shape[0]

    @blocks(ft // BLOCK)
    def _(j):
        cut = at(j, BLOCK)
        dh_ref[:, cut] = contract_last(c, dt_ref[cut, :])

    per = ds_ref.shape[0] // CUTS
    size = min(per, BLOCK // 2)
    for i in range(CUTS):
        copies[i].wait()

        @blocks(per // size)
        def _(j):
            cut = at(i * (per // size) + j, size)
            value = contract_last(c, ds_ref[cut, :])
            if i * per < ft:
                value = jnp.where(speech, value, dh_ref[:, cut])
            dh_ref[:, cut] = value


def hidden_grad(arr, down_t, down_s):
    rows, fs = arr.shape[0], down_s.shape[0]
    return call(
        hidden_grad_body,
        "hidden_grad_partials",
        [pltpu.VMEM((rows, fs), F32), pltpu.VMEM(down_s.shape, down_s.dtype)],
        (arr, down_t, down_s),
        (True, True, False),
        [pltpu.SemaphoreType.DMA((1, CUTS))],
        2 * rows * (down_s.size + down_t.size),
        size_of(down_s),
    )


def split(value, speech):
    zero = jnp.zeros_like(value)
    return jnp.where(speech, value, zero), jnp.where(speech, zero, value)


def mixed_body(arr_ref, h_ref, ds_ref, dt_ref, out_ref):
    speech = is_speech(arr_ref)
    out_ref[...] = jnp.zeros_like(out_ref)

    @blocks(dt_ref.shape[0] // BLOCK)
    def _(j):
        cut = at(j, BLOCK)
        hs, ht = split(h_ref[:, cut], speech)
        out_ref[...] += times(hs, ds_ref[cut, :]) + times(ht, dt_ref[cut, :])

    @pl.loop(dt_ref.shape[0] // BLOCK, ds_ref.shape[0] // BLOCK)
    def _(j):
        cut = at(j, BLOCK)
        hs, _ = split(h_ref[:, cut], speech)
        out_ref[...] += times(hs, ds_ref[cut, :])


def mixed_part(arr, h, down_s, down_t):
    return call(
        mixed_body,
        "mixed_partial",
        [pltpu.VMEM((h.shape[0], down_s.shape[1]), F32)],
        (arr, h, down_s, down_t),
        (True,) * 4,
        [],
        2 * h.shape[0] * (down_s.size + down_t.size),
        0,
    )[0]


def token_grad_body(arr_ref, dg_ref, du_ref, gs_ref, us_ref, gt_ref, ut_ref, out_ref, dgs, dus, dgt, dut):
    speech = is_speech(arr_ref)
    ft = gt_ref.shape[1]
    for src, s, t in ((dg_ref, dgs, dgt), (du_ref, dus, dut)):
        value = src[...]
        zero = jnp.zeros_like(value)
        s[...] = jnp.where(speech, value, zero)
        t[...] = jnp.where(speech, zero[:, :ft], value[:, :ft])

    size = BLOCK // 2

    @blocks(out_ref.shape[1] // size)
    def _(j):
        cut = at(j, size)
        out_ref[:, cut] = (
            contract_last(dgs[...], gs_ref[cut, :])
            + contract_last(dus[...], us_ref[cut, :])
            + contract_last(dgt[...], gt_ref[cut, :])
            + contract_last(dut[...], ut_ref[cut, :])
        )


def token_grad_part(arr, dg, du, gate_s, up_s, gate_t, up_t):
    rows, fs = dg.shape
    ft = gate_t.shape[1]
    return call(
        token_grad_body,
        "token_grad_partial",
        [pltpu.VMEM((rows, gate_s.shape[0]), F32)],
        (arr, dg, du, gate_s, up_s, gate_t, up_t),
        (True,) * 7,
        [pltpu.VMEM((rows, n), BF16) for n in (fs, fs, ft, ft)],
        2 * rows * (gate_s.size + gate_t.size) * 2,
        0,
    )[0]


def outer_body(keep, arr_ref, h_ref, out_ref):
    speech = is_speech(arr_ref)
    width = out_ref.shape[1]
    h = h_ref[...]
    zero = jnp.zeros_like(h)
    h = jnp.where(speech, h, zero) if keep else jnp.where(speech, zero, h)
    out_ref[...] = contract_first(h, arr_ref[:, width : 2 * width]).astype(BF16)


def outer(arr, h, count, width, keep, name):
    rows = arr.shape[0]
    size = 256
    return pl.pallas_call(
        functools.partial(outer_body, keep),
        grid=(count // size,),
        out_shape=jax.ShapeDtypeStruct((count, width), BF16),
        in_specs=[pl.BlockSpec(arr.shape, lambda i: (0, 0)), pl.BlockSpec((rows, size), lambda i: (0, i))],
        out_specs=pl.BlockSpec((size, width), lambda i: (i, 0)),
        compiler_params=pltpu.CompilerParams(vmem_limit_bytes=8 * MIB),
        cost_estimate=pl.CostEstimate(flops=2 * rows * count * width, bytes_accessed=2 * count * width, transcendentals=0),
        name=name,
    )(arr, h)


def flip(value, axes, bit, n):
    return lax.ppermute(value, axes, [(i, i ^ bit) for i in range(n)])


def sum_over_seq(parts, n):
    half = parts[0].shape[1] // 2
    odd = lax.axis_index("seq") % 2
    packed = jnp.stack(parts)
    first, second = packed[:, :, :half], packed[:, :, half:]
    theirs = jnp.where(odd == 1, first, second)
    mine = jnp.where(odd == 1, second, first)
    mine = mine + flip(theirs, "seq", 1, n)
    return mine + flip(mine.astype(BF16), "seq", 2, n).astype(F32)


def share(done, n):
    odd = lax.axis_index("seq") % 2
    done = jnp.stack(done).astype(BF16)
    other = flip(done, "seq", 1, n)
    low = jnp.where(odd == 1, other, done)
    high = jnp.where(odd == 1, done, other)
    return jnp.concatenate([low, high], axis=2)


def hidden(g, u):
    return g * jax.nn.sigmoid(g) * u


def hidden_back(g, u, dh):
    sig = jax.nn.sigmoid(g)
    return dh * u * sig * (1.0 + g * (1.0 - sig)), dh * (g * sig)


def by_kernels(n_seq, n_tok, tokens, modality, cotangent, gate_s, up_s, down_s, gate_t, up_t, down_t):
    width = tokens.shape[1]
    kind = jnp.broadcast_to(modality.astype(BF16)[:, None], (modality.shape[0], 128))
    packed = jnp.concatenate([tokens, cotangent, kind], axis=1)
    arrived = [packed] + [flip(packed, TOK, k, n_tok) for k in range(1, n_tok)]
    gate_s, up_s = load(packed, gate_s, up_s)
    arr = jnp.concatenate(arrived, axis=0)
    g, u, gate_t, up_t, down_t = forward(arr, gate_s, up_s, gate_t, up_t, down_t)
    dh, down_s = hidden_grad(arr, down_t, down_s)
    g, u = sum_over_seq((g, u), n_seq)
    (h,) = share((hidden(g, u),), n_seq)
    (dh,) = sum_over_seq((dh,), n_seq)
    mixed = mixed_part(arr, h, down_s, down_t)
    dg, du = share(hidden_back(g, u, dh), n_seq)
    back = token_grad_part(arr, dg, du, gate_s, up_s, gate_t, up_t)
    out = jnp.concatenate([mixed, back], axis=1).astype(BF16)
    own = out.shape[0] // n_tok
    total = out[:own].astype(F32)
    for k in range(1, n_tok):
        total = total + flip(out[k * own : (k + 1) * own], TOK, k, n_tok).astype(F32)
    total = total.astype(BF16)
    down_s_grad = outer(arr, h, down_s.shape[0], width, True, "down_speech_grad")
    down_t_grad = outer(arr, h, down_t.shape[0], width, False, "down_text_grad")
    return total[:, :width], total[:, width:], down_s_grad, down_t_grad


def by_arrays(n_seq, n_tok, tokens, modality, cotangent, gate_s, up_s, down_s, gate_t, up_t, down_t):
    width = tokens.shape[1]
    ft = gate_t.shape[1]
    kind = jnp.broadcast_to(modality.astype(BF16)[:, None], (modality.shape[0], 128))
    packed = jnp.concatenate([tokens, cotangent, kind], axis=1)
    arrived = lax.all_gather(packed, TOK, axis=0, tiled=True)
    rows, grads = arrived[:, :width], arrived[:, width : 2 * width]
    speech = arrived[:, 2 * width : 2 * width + 1] == 0

    def pick(s, t):
        return jnp.concatenate([jnp.where(speech, s[:, :ft], t), s[:, ft:]], axis=1)

    g = pick(times(rows, gate_s), times(rows, gate_t))
    u = pick(times(rows, up_s), times(rows, up_t))
    dh = pick(contract_last(grads, down_s), contract_last(grads, down_t))
    g, u, dh = sum_over_seq((g, u, dh), n_seq)
    h, dg, du = share((hidden(g, u), *hidden_back(g, u, dh)), n_seq)
    zero = jnp.zeros((), BF16)

    def halves(v):
        return jnp.where(speech, v, zero), jnp.where(speech, zero, v[:, :ft])

    (hs, ht), (dgs, dgt), (dus, dut) = halves(h), halves(dg), halves(du)
    mixed = times(hs, down_s) + times(ht, down_t)
    back = contract_last(dgs, gate_s) + contract_last(dus, up_s)
    back = back + contract_last(dgt, gate_t) + contract_last(dut, up_t)
    out = jnp.concatenate([mixed, back], axis=1).astype(BF16)
    out = out.reshape(n_tok, out.shape[0] // n_tok, out.shape[1])
    out = lax.all_to_all(out, TOK, split_axis=0, concat_axis=0, tiled=True)
    total = jnp.sum(out.astype(F32), axis=0).astype(BF16)
    down_s_grad = contract_first(hs, grads).astype(BF16)
    down_t_grad = contract_first(ht, grads).astype(BF16)
    return total[:, :width], total[:, width:], down_s_grad, down_t_grad


def solution(mesh):
    n_seq, n_tok = mesh.shape["seq"], mesh.shape["attn"] * mesh.shape["exp"]

    def run(*args):
        fits = n_tok == 8 and all(w.shape[0] % 512 == 0 and w.shape[1] % 512 == 0 for w in args[3:])
        return (by_kernels if fits else by_arrays)(n_seq, n_tok, *args)

    return jax.shard_map(
        run,
        mesh=mesh,
        in_specs=(
            P(TOK, "seq"),
            P(TOK),
            P(TOK, "seq"),
            P("seq", TOK),
            P("seq", TOK),
            P(TOK, "seq"),
            P("seq", TOK),
            P("seq", TOK),
            P(TOK, "seq"),
        ),
        out_specs=(P(TOK, "seq"),) * 4,
        check_vma=False,
    )
```

time: 95.3 us -> 102 us (1.070)
  Pallas kernels: 0 us -> 46.8 us
  matrix products: 39.4 us -> 0 us
  blocking collectives: 32.3 us -> 0 us
  starting transfers between devices: 7.36 us -> 27.4 us
  local copies, waits for them, and re-layouts: 2.56 us -> 21.1 us
  waiting for transfers between devices: 9.77 us -> 4.09 us
    pallas_call x0 -> x7, Pallas kernels: none -> 46.8 us  [the longest x5 32.4 us: call(): pl.pallas_call(body, out_shape=outs, in_specs=[VMEM if v else HBM for v i...]
    dot_general x14 -> x0, matrix products: 39.4 us -> none  [the longest x6 15.7 us: contract_last(): lax.dot_general(left, right, (((1,), (1,)), ((), ())), preferred_element_...]
    all_gather x1 -> x0, blocking collectives: 32.3 us -> none  [shards(): packed = lax.all_gather(packed, TOK, axis=0, tiled=True)]
    ppermute x3 -> x20, starting transfers between devices: 1.7 us -> 27.4 us  [flip(): return lax.ppermute(value, axes, [(i, i ^ bit) for i in range(n)])]
    unnamed x28 -> x30, local copies, waits for them, and re-layouts: 1.79 us -> 20.3 us
    all_to_all x1 -> x0, starting transfers between devices: 5.66 us -> none  [shards(): out = lax.all_to_all(out, TOK, split_axis=0, concat_axis=0, tiled=True)]
    ppermute x3 -> x20, waiting for transfers between devices: 7.12 us -> 4.09 us  [flip(): return lax.ppermute(value, axes, [(i, i ^ bit) for i in range(n)])]
    all_to_all x1 -> x0, waiting for transfers between devices: 2.65 us -> none  [shards(): out = lax.all_to_all(out, TOK, split_axis=0, concat_axis=0, tiled=True)]
  transfers between devices with their start and end apart: 4 -> 20, of which waited for: 4 -> 3; matrix products, arithmetic and copies ran while one was open for 5% -> 0% of each run, Pallas kernels for 0% -> 31%
where the time goes in v2:
time: 102 us
  Pallas kernels  46.8 us (46%)
  starting transfers between devices  27.4 us (27%)
  local copies, waits for them, and re-layouts  21.1 us (21%)
  waiting for transfers between devices  4.09 us (4%)
  other arithmetic  1.79 us (2%)
    pallas_call x5, Pallas kernels, call(): pl.pallas_call(body, out_shape=outs, in_specs=[VMEM if v else HBM for v i...  32.4 us
    ppermute x20, starting transfers between devices, flip(): return lax.ppermute(value, axes, [(i, i ^ bit) for i in range(n)])  27.4 us
    unnamed x30, local copies, waits for them, and re-layouts  20.3 us
    pallas_call x2, Pallas kernels, outer(): pl.pallas_call(functools.partial(outer_body, keep), grid=(count // size,)...  14.3 us
    ppermute x20, waiting for transfers between devices, flip(): return lax.ppermute(value, axes, [(i, i ^ bit) for i in range(n)])  4.09 us
  transfers between devices with their start and end apart: 20, of which 3 were waited for; matrix products, arithmetic and copies ran while one was open for 0% of the time, Pallas kernels for 31%

profile of v2, /device:TPU:0, one launch (start us, length us, event | category | flops | bytes accessed | tf_op | source)
XLA Modules:
  0.0 102.1 jit_solution(11724246753157843563)
XLA Ops:
  2.1 6.1 %collective-permute-start.6 = (bf16[2,3200]{1,0:T(2,128)(2,1)S(1)}, bf16[2,3200]{1,0:T(2,128)(2,1)S(1)}, u32[]{:S(2)}, u32[]{:S(2)}) collective-permute-start(bf16[2,3200]{1,0:T(2,128)(2,1)S(1)} %pad_maximum_fusion.3.after_ref), channel_id=1, source_target_pairs={{0,28},{4,24},{8,20},{12,16},{16,12},{20,8},{24,4},{28,0},{1,29},{... | collective-permute-start | bytes 38408 | tf_op jit(solution)/shard_map/ppermute | solution.py:284
  8.2 1.7 %collective-permute-start.4 = (bf16[2,3200]{1,0:T(2,128)(2,1)S(1)}, bf16[2,3200]{1,0:T(2,128)(2,1)S(1)}, u32[]{:S(2)}, u32[]{:S(2)}) collective-permute-start(bf16[2,3200]{1,0:T(2,128)(2,1)S(1)} %pad_maximum_fusion.3.after_ref), channel_id=1, source_target_pairs={{0,20},{4,16},{8,28},{12,24},{16,4},{20,0},{24,12},{28,8},{1,21},{... | collective-permute-start | bytes 38408 | tf_op jit(solution)/shard_map/ppermute | solution.py:284
  10.3 3.7 %collective-permute-start.2 = (bf16[2,3200]{1,0:T(2,128)(2,1)S(1)}, bf16[2,3200]{1,0:T(2,128)(2,1)S(1)}, u32[]{:S(2)}, u32[]{:S(2)}) collective-permute-start(bf16[2,3200]{1,0:T(2,128)(2,1)S(1)} %pad_maximum_fusion.3.after_ref), channel_id=1, source_target_pairs={{0,12},{4,8},{8,4},{12,0},{16,28},{20,24},{24,20},{28,16},{1,13},{... | collective-permute-start | bytes 38408 | tf_op jit(solution)/shard_map/ppermute | solution.py:284
  14.7 6.5 %load_speech.1 = (bf16[1536,3072]{1,0:T(8,128)(2,1)S(1)}, bf16[1536,3072]{1,0:T(8,128)(2,1)S(1)}) custom-call(bf16[2,3200]{1,0:T(2,128)(2,1)S(1)} %pad_maximum_fusion.3.after_ref, bf16[1536,3072]{1,0:T(8,128)(2,1)} %gate_ref.1, bf16[1536,3072]{1,0:T(8,128)(2,1)} %up_ref.1), custom_call_target="tpu_custom_call" | custom-call | bytes 18874368 | tf_op jit(solution)/shard_map/load_speech/pallas_call | solution.py:63
  21.2 3.7 %copy-done = bf16[1536,3072]{1,0:T(8,128)(2,1)} copy-done((bf16[1536,3072]{1,0:T(8,128)(2,1)}, bf16[1536,3072]{1,0:T(8,128)(2,1)S(1)}, u32[]{:S(2)}) %copy-start) | copy-done | bytes 9437208
  24.9 3.6 %copy-done.2 = bf16[1536,3072]{1,0:T(8,128)(2,1)} copy-done((bf16[1536,3072]{1,0:T(8,128)(2,1)}, bf16[1536,3072]{1,0:T(8,128)(2,1)S(1)}, u32[]{:S(2)}) %copy-start.2) | copy-done | bytes 9437208
  28.8 3.7 %copy-done.1 = bf16[1536,3072]{1,0:T(8,128)(2,1)S(1)} copy-done((bf16[1536,3072]{1,0:T(8,128)(2,1)S(1)}, bf16[1536,3072]{1,0:T(8,128)(2,1)}, u32[]{:S(2)}) %copy-start.1) | copy-done | bytes 9437208
  32.5 3.7 %copy-done.3 = bf16[1536,3072]{1,0:T(8,128)(2,1)S(1)} copy-done((bf16[1536,3072]{1,0:T(8,128)(2,1)S(1)}, bf16[1536,3072]{1,0:T(8,128)(2,1)}, u32[]{:S(2)}) %copy-start.3) | copy-done | bytes 9437208
  36.2 6.5 %hidden_partials.1 = (f32[16,3072]{1,0:T(8,128)S(1)}, f32[16,3072]{1,0:T(8,128)S(1)}, bf16[1536,2048]{1,0:T(8,128)(2,1)S(1)}, bf16[1536,2048]{1,0:T(8,128)(2,1)S(1)}, bf16[2048,1536]{1,0:T(8,128)(2,1)S(1)}) custom-call(bf16[16,3200]{1,0:T(8,128)(2,1)S(1)} %concatenate.17.arr_ref, bf16[1536,3072]{1,0:T(8,128)(2,1)S(1)} %copy-done.1, ...), custom_call_target="tpu_custom_call" | custom-call | flops 503316480 | bytes 18874368 | tf_op jit(solution)/shard_map/hidden_partials/pallas_call | solution.py:63
  42.7 2.7 %copy-done.4 = bf16[1536,2048]{1,0:T(8,128)(2,1)} copy-done((bf16[1536,2048]{1,0:T(8,128)(2,1)}, bf16[1536,2048]{1,0:T(8,128)(2,1)S(1)}, u32[]{:S(2)}) %copy-start.4) | copy-done | bytes 6291480
  45.5 7.5 %hidden_grad_partials.1 = (f32[16,3072]{1,0:T(8,128)S(1)}, bf16[3072,1536]{1,0:T(8,128)(2,1)S(1)}) custom-call(bf16[16,3200]{1,0:T(8,128)(2,1)S(1)} %concatenate.17.arr_ref, bf16[2048,1536]{1,0:T(8,128)(2,1)S(1)} %get-tuple-element.17.dt_ref, bf16[3072,1536]{1,0:T(8,128)(2,1)} %ds_hbm.1), custom_call_target="tpu_custom_call" | custom-call | flops 251658240 | bytes 9437184 | tf_op jit(solution)/shard_map/hidden_grad_partials/pallas_call | solution.py:63
  53.2 1.6 %collective-permute-start.8 = (bf16[2,16,1536]{2,1,0:T(8,128)(2,1)S(1)}, bf16[2,16,1536]{2,1,0:T(8,128)(2,1)S(1)}, u32[]{:S(2)}, u32[]{:S(2)}) collective-permute-start(bf16[2,16,1536]{2,1,0:T(8,128)(2,1)S(1)} %get-tuple-element.22), channel_id=1, source_target_pairs={{0,2},{1,3},{2,0},{3,1},{4,6},{5,7},{6,4},{7,5},{8,10},{9,11},{10,... | collective-permute-start | bytes 294920 | tf_op jit(solution)/shard_map/ppermute | solution.py:284
  54.9 1.2 %collective-permute-start.11 = (bf16[1,16,1536]{2,1,0:T(8,128)(2,1)S(1)}, bf16[1,16,1536]{2,1,0:T(8,128)(2,1)S(1)}, u32[]{:S(2)}, u32[]{:S(2)}) collective-permute-start(bf16[1,16,1536]{2,1,0:T(8,128)(2,1)S(1)} %get-tuple-element.24), channel_id=1, source_target_pairs={{0,2},{1,3},{2,0},{3,1},{4,6},{5,7},{6,4},{7,5},{8,10},{9,11},{10,... | collective-permute-start | bytes 147464 | tf_op jit(solution)/shard_map/ppermute | solution.py:284
  56.1 2.8 %collective-permute-done.8 = bf16[2,16,1536]{2,1,0:T(8,128)(2,1)S(1)} collective-permute-done((bf16[2,16,1536]{2,1,0:T(8,128)(2,1)S(1)}, bf16[2,16,1536]{2,1,0:T(8,128)(2,1)S(1)}, u32[]{:S(2)}, u32[]{:S(2)}) %collective-permute-start.8) | collective-permute-done | bytes 98336 | tf_op jit(solution)/shard_map/ppermute | solution.py:284
  61.0 3.0 %mixed_partial.1 = f32[16,1536]{1,0:T(8,128)S(1)} custom-call(bf16[16,3200]{1,0:T(8,128)(2,1)S(1)} %concatenate.17.arr_ref, bf16[16,3072]{1,0:T(8,128)(2,1)S(1)} %maximum_bitcast_fusion.h_ref, bf16[3072,1536]{1,0:T(8,128)(2,1)S(1)} %get-tuple-element.18.ds_ref, bf16[2048,1536]{1,0:T(8,128)(2,1)S(1)} %get-tuple-element.17.dt_ref), custom_call_target="tpu_custom_call" | custom-call | flops 251658240 | tf_op jit(solution)/shard_map/mixed_partial/pallas_call | solution.py:63
  64.1 2.8 %copy-done.6 = bf16[1536,2048]{1,0:T(8,128)(2,1)S(1)} copy-done((bf16[1536,2048]{1,0:T(8,128)(2,1)S(1)}, bf16[1536,2048]{1,0:T(8,128)(2,1)}, u32[]{:S(2)}) %copy-start.6) | copy-done | bytes 6291480
  66.9 8.9 %token_grad_partial.1 = f32[16,1536]{1,0:T(8,128)S(1)} custom-call(bf16[16,3200]{1,0:T(8,128)(2,1)S(1)} %concatenate.17.arr_ref, bf16[16,3072]{1,0:T(8,128)(2,1)S(1)} %get-tuple-element.30.dg_ref, bf16[16,3072]{1,0:T(8,128)(2,1)S(1)} %get-tuple-element.29.du_ref, bf16[1536,3072]{1,0:T(8,128)(2,1)S(1)} %bitcast.10, bf16[1536,3072]{1,0:T(8,128)(2,1)S(1)} %bitcast.12, ...), custom_call_target="tpu_custom_call" | custom-call | flops 503316480 | tf_op jit(solution)/shard_map/token_grad_partial/pallas_call | solution.py:63
  75.9 1.5 %collective-permute-start.13 = (bf16[2,3072]{1,0:T(2,128)(2,1)S(1)}, bf16[2,3072]{1,0:T(2,128)(2,1)S(1)}, u32[]{:S(2)}, u32[]{:S(2)}) collective-permute-start(bf16[2,3072]{1,0:T(2,128)(2,1)S(1)} %get-tuple-element.33), channel_id=1, source_target_pairs={{0,4},{4,0},{8,12},{12,8},{16,20},{20,16},{24,28},{28,24},{1,5},{5... | collective-permute-start | bytes 36872 | tf_op jit(solution)/shard_map/ppermute | solution.py:284
  77.4 2.9 %collective-permute-start.14 = (bf16[2,3072]{1,0:T(2,128)(2,1)S(1)}, bf16[2,3072]{1,0:T(2,128)(2,1)S(1)}, u32[]{:S(2)}, u32[]{:S(2)}) collective-permute-start(bf16[2,3072]{1,0:T(2,128)(2,1)S(1)} %get-tuple-element.34), channel_id=1, source_target_pairs={{0,8},{4,12},{8,0},{12,4},{16,24},{20,28},{24,16},{28,20},{1,9},{5... | collective-permute-start | bytes 36872 | tf_op jit(solution)/shard_map/ppermute | solution.py:284
  80.2 5.8 %down_text_grad.1 = bf16[2048,1536]{1,0:T(8,128)(2,1)} custom-call(bf16[16,3200]{1,0:T(8,128)(2,1)S(1)} %concatenate.17.arr_ref, bf16[16,3072]{1,0:T(8,128)(2,1)S(1)} %maximum_bitcast_fusion.h_ref), custom_call_target="tpu_custom_call" | custom-call | flops 100663296 | bytes 6291456 | tf_op jit(solution)/shard_map/down_text_grad/pallas_call | solution.py:271
  86.2 1.6 %collective-permute-start.16 = (bf16[2,3072]{1,0:T(2,128)(2,1)S(1)}, bf16[2,3072]{1,0:T(2,128)(2,1)S(1)}, u32[]{:S(2)}, u32[]{:S(2)}) collective-permute-start(bf16[2,3072]{1,0:T(2,128)(2,1)S(1)} %get-tuple-element.36), channel_id=1, source_target_pairs={{0,16},{4,20},{8,24},{12,28},{16,0},{20,4},{24,8},{28,12},{1,17},{... | collective-permute-start | bytes 36872 | tf_op jit(solution)/shard_map/ppermute | solution.py:284
  88.2 3.3 %collective-permute-start.19 = (bf16[2,3072]{1,0:T(2,128)(2,1)S(1)}, bf16[2,3072]{1,0:T(2,128)(2,1)S(1)}, u32[]{:S(2)}, u32[]{:S(2)}) collective-permute-start(bf16[2,3072]{1,0:T(2,128)(2,1)S(1)} %get-tuple-element.38), channel_id=1, source_target_pairs={{0,28},{4,24},{8,20},{12,16},{16,12},{20,8},{24,4},{28,0},{1,29},{... | collective-permute-start | bytes 36872 | tf_op jit(solution)/shard_map/ppermute | solution.py:284
  91.5 1.5 %collective-permute-start.18 = (bf16[2,3072]{1,0:T(2,128)(2,1)S(1)}, bf16[2,3072]{1,0:T(2,128)(2,1)S(1)}, u32[]{:S(2)}, u32[]{:S(2)}) collective-permute-start(bf16[2,3072]{1,0:T(2,128)(2,1)S(1)} %get-tuple-element.39), channel_id=1, source_target_pairs={{0,24},{4,28},{8,16},{12,20},{16,8},{20,12},{24,0},{28,4},{1,25},{... | collective-permute-start | bytes 36872 | tf_op jit(solution)/shard_map/ppermute | solution.py:284
  92.9 8.5 %down_speech_grad.1 = bf16[3072,1536]{1,0:T(8,128)(2,1)} custom-call(bf16[16,3200]{1,0:T(8,128)(2,1)S(1)} %concatenate.17.arr_ref, bf16[16,3072]{1,0:T(8,128)(2,1)S(1)} %maximum_bitcast_fusion.h_ref), custom_call_target="tpu_custom_call" | custom-call | flops 150994944 | bytes 9437184 | tf_op jit(solution)/shard_map/down_speech_grad/pallas_call | solution.py:271
  (76 shorter events, 6.4 us)
Async XLA Ops:
  2.1 11.9 %collective-permute-start.6 = (bf16[2,3200]{1,0:T(2,128)(2,1)S(1)}, bf16[2,3200]{1,0:T(2,128)(2,1)S(1)}, u32[]{:S(2)}, u32[]{:S(2)}) collective-permute-start(bf16[2,3200]{1,0:T(2,128)(2,1)S(1)} %pad_maximum_fusion.3.after_ref), channel_id=1, source_target_pairs={{0,28},{4,24},{8,20},{12,16},{16,12},{20,8},{24,4},{28,0},{1,29},{... | collective-permute-start | bytes 38408 | tf_op jit(solution)/shard_map/ppermute | solution.py:284
  8.2 5.8 %collective-permute-start.5 = (bf16[2,3200]{1,0:T(2,128)(2,1)S(1)}, bf16[2,3200]{1,0:T(2,128)(2,1)S(1)}, u32[]{:S(2)}, u32[]{:S(2)}) collective-permute-start(bf16[2,3200]{1,0:T(2,128)(2,1)S(1)} %pad_maximum_fusion.3.after_ref), channel_id=1, source_target_pairs={{0,24},{4,28},{8,16},{12,20},{16,8},{20,12},{24,0},{28,4},{1,25},{... | collective-permute-start | bytes 38408 | tf_op jit(solution)/shard_map/ppermute | solution.py:284
  8.2 20.4 %collective-permute-start.4 = (bf16[2,3200]{1,0:T(2,128)(2,1)S(1)}, bf16[2,3200]{1,0:T(2,128)(2,1)S(1)}, u32[]{:S(2)}, u32[]{:S(2)}) collective-permute-start(bf16[2,3200]{1,0:T(2,128)(2,1)S(1)} %pad_maximum_fusion.3.after_ref), channel_id=1, source_target_pairs={{0,20},{4,16},{8,28},{12,24},{16,4},{20,0},{24,12},{28,8},{1,21},{... | collective-permute-start | bytes 38408 | tf_op jit(solution)/shard_map/ppermute | solution.py:284
  9.8 18.7 %collective-permute-start.3 = (bf16[2,3200]{1,0:T(2,128)(2,1)S(1)}, bf16[2,3200]{1,0:T(2,128)(2,1)S(1)}, u32[]{:S(2)}, u32[]{:S(2)}) collective-permute-start(bf16[2,3200]{1,0:T(2,128)(2,1)S(1)} %pad_maximum_fusion.3.after_ref), channel_id=1, source_target_pairs={{0,16},{4,20},{8,24},{12,28},{16,0},{20,4},{24,8},{28,12},{1,17},{... | collective-permute-start | bytes 38408 | tf_op jit(solution)/shard_map/ppermute | solution.py:284
  10.3 18.3 %collective-permute-start.2 = (bf16[2,3200]{1,0:T(2,128)(2,1)S(1)}, bf16[2,3200]{1,0:T(2,128)(2,1)S(1)}, u32[]{:S(2)}, u32[]{:S(2)}) collective-permute-start(bf16[2,3200]{1,0:T(2,128)(2,1)S(1)} %pad_maximum_fusion.3.after_ref), channel_id=1, source_target_pairs={{0,12},{4,8},{8,4},{12,0},{16,28},{20,24},{24,20},{28,16},{1,13},{... | collective-permute-start | bytes 38408 | tf_op jit(solution)/shard_map/ppermute | solution.py:284
  14.0 14.6 %collective-permute-start.1 = (bf16[2,3200]{1,0:T(2,128)(2,1)S(1)}, bf16[2,3200]{1,0:T(2,128)(2,1)S(1)}, u32[]{:S(2)}, u32[]{:S(2)}) collective-permute-start(bf16[2,3200]{1,0:T(2,128)(2,1)S(1)} %pad_maximum_fusion.3.after_ref), channel_id=1, source_target_pairs={{0,8},{4,12},{8,0},{12,4},{16,24},{20,28},{24,16},{28,20},{1,9},{5... | collective-permute-start | bytes 38408 | tf_op jit(solution)/shard_map/ppermute | solution.py:284
  14.0 14.6 %collective-permute-start = (bf16[2,3200]{1,0:T(2,128)(2,1)S(1)}, bf16[2,3200]{1,0:T(2,128)(2,1)S(1)}, u32[]{:S(2)}, u32[]{:S(2)}) collective-permute-start(bf16[2,3200]{1,0:T(2,128)(2,1)S(1)} %pad_maximum_fusion.3.after_ref), channel_id=1, source_target_pairs={{0,4},{4,0},{8,12},{12,8},{16,20},{20,16},{24,28},{28,24},{1,5},{5... | collective-permute-start | bytes 38408 | tf_op jit(solution)/shard_map/ppermute | solution.py:284
  45.4 7.7 %collective-permute-start.7 = (f32[2,16,1536]{2,1,0:T(8,128)S(1)}, f32[2,16,1536]{2,1,0:T(8,128)S(1)}, u32[]{:S(2)}, u32[]{:S(2)}) collective-permute-start(f32[2,16,1536]{2,1,0:T(8,128)S(1)} %broadcast_select_fusion.2), channel_id=1, source_target_pairs={{0,1},{1,0},{2,3},{3,2},{4,5},{5,4},{6,7},{7,6},{8,9},{9,8},{10,11... | collective-permute-start | bytes 589832 | tf_op jit(solution)/shard_map/ppermute | solution.py:284
  45.5 18.5 %slice-start.3 = ((s8[9437184]{0:T(1024)(128)(4,1)}), s8[4194304]{0:T(1024)(128)(4,1)S(1)}, s32[]{:S(2)}) async-start(s8[9437184]{0:T(1024)(128)(4,1)} %bitcast.11), calls=%async_computation.3 | async-start | bytes 8388608
  45.5 18.5 %slice-start.4 = ((s8[9437184]{0:T(1024)(128)(4,1)}), s8[4194304]{0:T(1024)(128)(4,1)S(1)}, s32[]{:S(2)}) async-start(s8[9437184]{0:T(1024)(128)(4,1)} %bitcast.11), calls=%async_computation.4 | async-start | bytes 8388608
  45.5 18.5 %slice-start.6 = ((s8[6291456]{0:T(1024)(128)(4,1)}), s8[2097152]{0:T(1024)(128)(4,1)S(1)}, s32[]{:S(2)}) async-start(s8[6291456]{0:T(1024)(128)(4,1)} %bitcast.13), calls=%async_computation.6 | async-start | bytes 4194304
  53.1 1.8 %collective-permute-start.10 = (f32[1,16,1536]{2,1,0:T(8,128)S(1)}, f32[1,16,1536]{2,1,0:T(8,128)S(1)}, u32[]{:S(2)}, u32[]{:S(2)}) collective-permute-start(f32[1,16,1536]{2,1,0:T(8,128)S(1)} %slice_select_fusion), channel_id=1, source_target_pairs={{0,1},{1,0},{2,3},{3,2},{4,5},{5,4},{6,7},{7,6},{8,9},{9,8},{10,11... | collective-permute-start | bytes 294920 | tf_op jit(solution)/shard_map/ppermute | solution.py:284
  53.2 10.8 %slice-start = ((s8[9437184]{0:T(1024)(128)(4,1)}), s8[4194304]{0:T(1024)(128)(4,1)S(1)}, s32[]{:S(2)}) async-start(s8[9437184]{0:T(1024)(128)(4,1)} %bitcast.9), calls=%async_computation | async-start | bytes 8388608
  53.2 5.7 %collective-permute-start.8 = (bf16[2,16,1536]{2,1,0:T(8,128)(2,1)S(1)}, bf16[2,16,1536]{2,1,0:T(8,128)(2,1)S(1)}, u32[]{:S(2)}, u32[]{:S(2)}) collective-permute-start(bf16[2,16,1536]{2,1,0:T(8,128)(2,1)S(1)} %get-tuple-element.22), channel_id=1, source_target_pairs={{0,2},{1,3},{2,0},{3,1},{4,6},{5,7},{6,4},{7,5},{8,10},{9,11},{10,... | collective-permute-start | bytes 294920 | tf_op jit(solution)/shard_map/ppermute | solution.py:284
  54.9 4.6 %collective-permute-start.11 = (bf16[1,16,1536]{2,1,0:T(8,128)(2,1)S(1)}, bf16[1,16,1536]{2,1,0:T(8,128)(2,1)S(1)}, u32[]{:S(2)}, u32[]{:S(2)}) collective-permute-start(bf16[1,16,1536]{2,1,0:T(8,128)(2,1)S(1)} %get-tuple-element.24), channel_id=1, source_target_pairs={{0,2},{1,3},{2,0},{3,1},{4,6},{5,7},{6,4},{7,5},{8,10},{9,11},{10,... | collective-permute-start | bytes 147464 | tf_op jit(solution)/shard_map/ppermute | solution.py:284
  59.6 1.3 %collective-permute-start.9 = (bf16[1,16,1536]{2,1,0:T(8,128)(2,1)S(1)}, bf16[1,16,1536]{2,1,0:T(8,128)(2,1)S(1)}, u32[]{:S(2)}, u32[]{:S(2)}) collective-permute-start(bf16[1,16,1536]{2,1,0:T(8,128)(2,1)S(1)} %get-tuple-element.28), channel_id=1, source_target_pairs={{0,1},{1,0},{2,3},{3,2},{4,5},{5,4},{6,7},{7,6},{8,9},{9,8},{10,11... | collective-permute-start | bytes 147464 | tf_op jit(solution)/shard_map/ppermute | solution.py:284
  59.7 4.3 %collective-permute-start.12 = (bf16[2,16,1536]{2,1,0:T(8,128)(2,1)S(1)}, bf16[2,16,1536]{2,1,0:T(8,128)(2,1)S(1)}, u32[]{:S(2)}, u32[]{:S(2)}) collective-permute-start(bf16[2,16,1536]{2,1,0:T(8,128)(2,1)S(1)} %pad_maximum_fusion.2), channel_id=1, source_target_pairs={{0,1},{1,0},{2,3},{3,2},{4,5},{5,4},{6,7},{7,6},{8,9},{9,8},{10,11... | collective-permute-start | bytes 294920 | tf_op jit(solution)/shard_map/ppermute | solution.py:284
  75.9 12.3 %collective-permute-start.13 = (bf16[2,3072]{1,0:T(2,128)(2,1)S(1)}, bf16[2,3072]{1,0:T(2,128)(2,1)S(1)}, u32[]{:S(2)}, u32[]{:S(2)}) collective-permute-start(bf16[2,3072]{1,0:T(2,128)(2,1)S(1)} %get-tuple-element.33), channel_id=1, source_target_pairs={{0,4},{4,0},{8,12},{12,8},{16,20},{20,16},{24,28},{28,24},{1,5},{5... | collective-permute-start | bytes 36872 | tf_op jit(solution)/shard_map/ppermute | solution.py:284
  77.4 14.1 %collective-permute-start.14 = (bf16[2,3072]{1,0:T(2,128)(2,1)S(1)}, bf16[2,3072]{1,0:T(2,128)(2,1)S(1)}, u32[]{:S(2)}, u32[]{:S(2)}) collective-permute-start(bf16[2,3072]{1,0:T(2,128)(2,1)S(1)} %get-tuple-element.34), channel_id=1, source_target_pairs={{0,8},{4,12},{8,0},{12,4},{16,24},{20,28},{24,16},{28,20},{1,9},{5... | collective-permute-start | bytes 36872 | tf_op jit(solution)/shard_map/ppermute | solution.py:284
  86.0 15.4 %collective-permute-start.15 = (bf16[2,3072]{1,0:T(2,128)(2,1)S(1)}, bf16[2,3072]{1,0:T(2,128)(2,1)S(1)}, u32[]{:S(2)}, u32[]{:S(2)}) collective-permute-start(bf16[2,3072]{1,0:T(2,128)(2,1)S(1)} %get-tuple-element.35), channel_id=1, source_target_pairs={{0,12},{4,8},{8,4},{12,0},{16,28},{20,24},{24,20},{28,16},{1,13},{... | collective-permute-start | bytes 36872 | tf_op jit(solution)/shard_map/ppermute | solution.py:284
  86.2 15.3 %collective-permute-start.16 = (bf16[2,3072]{1,0:T(2,128)(2,1)S(1)}, bf16[2,3072]{1,0:T(2,128)(2,1)S(1)}, u32[]{:S(2)}, u32[]{:S(2)}) collective-permute-start(bf16[2,3072]{1,0:T(2,128)(2,1)S(1)} %get-tuple-element.36), channel_id=1, source_target_pairs={{0,16},{4,20},{8,24},{12,28},{16,0},{20,4},{24,8},{28,12},{1,17},{... | collective-permute-start | bytes 36872 | tf_op jit(solution)/shard_map/ppermute | solution.py:284
  87.8 13.6 %collective-permute-start.17 = (bf16[2,3072]{1,0:T(2,128)(2,1)S(1)}, bf16[2,3072]{1,0:T(2,128)(2,1)S(1)}, u32[]{:S(2)}, u32[]{:S(2)}) collective-permute-start(bf16[2,3072]{1,0:T(2,128)(2,1)S(1)} %get-tuple-element.37), channel_id=1, source_target_pairs={{0,20},{4,16},{8,28},{12,24},{16,4},{20,0},{24,12},{28,8},{1,21},{... | collective-permute-start | bytes 36872 | tf_op jit(solution)/shard_map/ppermute | solution.py:284
  88.2 13.3 %collective-permute-start.19 = (bf16[2,3072]{1,0:T(2,128)(2,1)S(1)}, bf16[2,3072]{1,0:T(2,128)(2,1)S(1)}, u32[]{:S(2)}, u32[]{:S(2)}) collective-permute-start(bf16[2,3072]{1,0:T(2,128)(2,1)S(1)} %get-tuple-element.38), channel_id=1, source_target_pairs={{0,28},{4,24},{8,20},{12,16},{16,12},{20,8},{24,4},{28,0},{1,29},{... | collective-permute-start | bytes 36872 | tf_op jit(solution)/shard_map/ppermute | solution.py:284
  91.5 10.0 %collective-permute-start.18 = (bf16[2,3072]{1,0:T(2,128)(2,1)S(1)}, bf16[2,3072]{1,0:T(2,128)(2,1)S(1)}, u32[]{:S(2)}, u32[]{:S(2)}) collective-permute-start(bf16[2,3072]{1,0:T(2,128)(2,1)S(1)} %get-tuple-element.39), channel_id=1, source_target_pairs={{0,24},{4,28},{8,16},{12,20},{16,8},{20,12},{24,0},{28,4},{1,25},{... | collective-permute-start | bytes 36872 | tf_op jit(solution)/shard_map/ppermute | solution.py:284
  (11 other events, 42.0 us)

commit v3 on v1

v3 whole, which is shorter than its diff:
```python
import functools

import jax
import jax.numpy as jnp
from jax import lax
from jax.experimental import pallas as pl
from jax.experimental.pallas import tpu as pltpu
from jax.sharding import PartitionSpec as P

TOK = ("attn", "exp")
HOPS = (2, 1, 4)
F32 = jnp.float32
BF16 = jnp.bfloat16
MIB = 1 << 20
BLOCK = 512
WIDE = 1024
ROWS = 256
SLOTS = 4
PLACES = {"h": pl.ANY, "v": pltpu.VMEM, "s": pltpu.SMEM}


def contract_first(left, right):
    return lax.dot_general(left, right, (((0,), (0,)), ((), ())), preferred_element_type=F32)


def contract_last(left, right):
    return lax.dot_general(left, right, (((1,), (1,)), ((), ())), preferred_element_type=F32)


def times(left, right):
    return jnp.dot(left, right, preferred_element_type=F32)


def size_of(*arrays):
    return sum(a.size * jnp.dtype(a.dtype).itemsize for a in arrays)


def constrain(x, place):
    if place == "s":
        return x
    return pltpu.with_memory_space_constraint(x, pltpu.VMEM if place == "v" else pltpu.HBM)


def call(
    body, name, outs, ins, places, scratch=(), flops=0, traffic=0, limit=4, out_places=None, aliases=None, also=()
):
    out_places = out_places or "v" * len(outs)
    shapes = [pltpu.VMEM(*o) if p == "v" else jax.ShapeDtypeStruct(*o) for o, p in zip(outs, out_places)]
    count = len(ins)

    def seen(*refs):
        body(*refs[:count], *refs[count + len(also) :])

    ins, places = (*ins, *also), places + "v" * len(also)
    return pl.pallas_call(
        seen,
        out_shape=shapes,
        in_specs=[pl.BlockSpec(memory_space=PLACES[p]) for p in places],
        out_specs=[pl.BlockSpec(memory_space=PLACES[p]) for p in out_places],
        scratch_shapes=list(scratch),
        input_output_aliases=aliases or {},
        compiler_params=pltpu.CompilerParams(vmem_limit_bytes=limit * MIB),
        cost_estimate=pl.CostEstimate(flops=flops, bytes_accessed=traffic, transcendentals=0),
        name=name,
    )(*[constrain(x, p) for x, p in zip(ins, places)])


def like(x):
    return x.shape, x.dtype


def parity():
    return lax.rem(lax.axis_index("seq"), 2)


def is_speech(arr_ref):
    return arr_ref[:, arr_ref.shape[1] - 1 :] == 0


def pack_body(kind_hbm, tok_hbm, cot_hbm, wide_ref, tall_ref, out_ref, tok_ref, cot_ref, kind_ref, sems):
    copies = [
        pltpu.make_async_copy(kind_hbm, kind_ref, sems.at[2]),
        pltpu.make_async_copy(tok_hbm, tok_ref, sems.at[0]),
        pltpu.make_async_copy(cot_hbm, cot_ref, sems.at[1]),
    ]
    for copy in copies:
        copy.start()
    width = tok_ref.shape[1]
    row = lax.broadcasted_iota(jnp.int32, (tok_ref.shape[0], 128), 0)
    kind = jnp.zeros(row.shape, F32)
    for copy in copies:
        copy.wait()
    for i in range(tok_ref.shape[0]):
        kind = jnp.where(row == i, kind_ref[i].astype(F32), kind)
    out_ref[:, 2 * width :] = kind.astype(BF16)
    out_ref[:, :width] = tok_ref[...]
    out_ref[:, width : 2 * width] = cot_ref[...]


def join_body(a_ref, b_ref, out_ref):
    both = jnp.concatenate([a_ref[...].astype(F32), b_ref[...].astype(F32)], axis=0)
    out_ref[...] = both.astype(BF16)


def join(a, b, name, also):
    return call(join_body, name, [((2 * a.shape[0], a.shape[1]), BF16)], (a, b), "vv", also=also)[0]


def column_blocks(src, wide, first):
    return [(src.at[:, pl.ds(i * WIDE, WIDE)], wide.at[first + i]) for i in range(src.shape[1] // WIDE)]


def row_blocks(src, tall, first):
    return [
        (src.at[pl.ds(i, BLOCK)], tall.at[pl.ds(first + i, BLOCK)]) for i in range(0, src.shape[0], BLOCK)
    ]


def started(pairs, sems, first):
    copies = [pltpu.make_async_copy(s, d, sems.at[first + i]) for i, (s, d) in enumerate(pairs)]
    for copy in copies:
        copy.start()
    return copies


def load_body(first, after_ref, src_hbm, old_ref, wide_ref, sems):
    for copy in started(column_blocks(src_hbm, wide_ref, first), sems, 0):
        copy.wait()


def load(after, src, wide, tall, first, name):
    return call(
        functools.partial(load_body, first),
        name,
        [like(wide)],
        (after, src, wide),
        "vhv",
        [pltpu.SemaphoreType.DMA((src.shape[1] // WIDE,))],
        traffic=size_of(src),
        aliases={2: 0},
        also=(tall,),
    )[0]


def partials_body(
    arr_ref, gs_hbm, us_hbm, dt_hbm, ds_hbm, old_wide, old_tall,
    mine_ref, theirs_ref, wide_ref, tall_ref, part, sems,
):
    fs, ft, width = ds_hbm.shape[0], dt_hbm.shape[0], dt_hbm.shape[1]
    ns, nt = fs // WIDE, ft // WIDE
    text_copies = started(column_blocks(gs_hbm, wide_ref, 2 * nt), sems, 0)
    text_copies = [text_copies, started(column_blocks(us_hbm, wide_ref, 2 * nt + ns), sems, ns)]
    dt_copies = started(row_blocks(dt_hbm, tall_ref, fs), sems, 2 * ns)
    ds_copies = started(row_blocks(ds_hbm, tall_ref, 0), sems, 2 * ns + ft // BLOCK)
    x = arr_ref[:, :width]
    c = arr_ref[:, width : 2 * width]
    speech = is_speech(arr_ref)

    for k in range(2):
        for i in range(nt):
            part[k, :, i * WIDE : (i + 1) * WIDE] = times(x, wide_ref[k * nt + i])
    for k in range(2):
        for i in range(ns):
            text_copies[k][i].wait()
            value = times(x, wide_ref[2 * nt + k * ns + i])
            cut = slice(i * WIDE, (i + 1) * WIDE)
            if i < nt:
                value = jnp.where(speech, value, part[k, :, cut])
            part[k, :, cut] = value
    for i, copy in enumerate(dt_copies):
        copy.wait()
        cut = slice(i * BLOCK, (i + 1) * BLOCK)
        part[2, :, cut] = contract_last(c, tall_ref[fs + i * BLOCK : fs + (i + 1) * BLOCK, :])
    for i, copy in enumerate(ds_copies):
        copy.wait()
        cut = slice(i * BLOCK, (i + 1) * BLOCK)
        value = contract_last(c, tall_ref[cut, :])
        if i * BLOCK < ft:
            value = jnp.where(speech, value, part[2, :, cut])
        part[2, :, cut] = value
    half = fs // 2
    odd = parity()
    for k in range(3):
        mine_ref[k] = part[k, :, pl.ds(pl.multiple_of(odd * half, half), half)]
        theirs_ref[k] = part[k, :, pl.ds(pl.multiple_of((1 - odd) * half, half), half)]


def partials(arr, gate_s, up_s, down_s, down_t, wide, tall):
    rows, fs = arr.shape[0], gate_s.shape[1]
    half = ((3, rows, fs // 2), F32)
    n_sems = 2 * fs // WIDE + tall.shape[0] // BLOCK
    return call(
        partials_body,
        "hidden_partials",
        [half, half, like(wide), like(tall)],
        (arr, gate_s, up_s, down_t, down_s, wide, tall),
        "vhhhhvv",
        [pltpu.VMEM((3, rows, fs), F32), pltpu.SemaphoreType.DMA((n_sems,))],
        2 * rows * (wide.size + tall.size),
        size_of(gate_s, up_s, down_s, down_t),
        aliases={5: 2, 6: 3},
    )


def core_sum_body(mine_ref, got_ref, sum_ref, send_ref):
    total = mine_ref[...] + got_ref[...]
    sum_ref[...] = total
    send_ref[...] = total.astype(BF16)


def hidden_body(sum_ref, got_ref, out_ref):
    total = [sum_ref[k] + got_ref[k].astype(F32) for k in range(3)]
    g, u, dh = total
    sig = jax.nn.sigmoid(g)
    silu = g * sig
    out_ref[0] = (silu * u).astype(BF16)
    out_ref[1] = (dh * u * sig * (1.0 + g * (1.0 - sig))).astype(BF16)
    out_ref[2] = (dh * silu).astype(BF16)


def back_body(
    arr_ref, done_ref, other_ref, wide_ref, tall_ref,
    keep_ref, send_ref, hs_ref, ht_ref, dgs, dgt, dus, dut, out,
):
    speech = is_speech(arr_ref)
    fs, ft = hs_ref.shape[1], ht_ref.shape[1]
    ns, nt = fs // WIDE, ft // WIDE
    odd = parity() == 1
    for k, (s, t) in enumerate(((hs_ref, ht_ref), (dgs, dgt), (dus, dut))):
        done, other = done_ref[k], other_ref[k]
        value = jnp.concatenate([jnp.where(odd, other, done), jnp.where(odd, done, other)], axis=1)
        zero = jnp.zeros_like(value)
        s[...] = jnp.where(speech, value, zero)
        t[...] = jnp.where(speech, zero, value)[:, :ft]
    width = tall_ref.shape[1]
    for i in range(0, width, BLOCK):
        cut = slice(i, i + BLOCK)
        out[:, cut] = times(hs_ref[...], tall_ref[:fs, cut]) + times(ht_ref[...], tall_ref[fs:, cut])
    blocks = [(dgt, nt), (dut, nt), (dgs, ns), (dus, ns)]
    blocks = [(ref, i) for ref, n in blocks for i in range(n)]
    size = BLOCK // 2
    for i in range(0, width, size):
        total = jnp.zeros((out.shape[0], size), F32)
        for b, (ref, j) in enumerate(blocks):
            total += contract_last(ref[:, j * WIDE : (j + 1) * WIDE], wide_ref[b, i : i + size, :])
        out[:, width + i : width + i + size] = total
    half = keep_ref.shape[0]
    keep_ref[...] = out[:half]
    send_ref[...] = out[half:].astype(BF16)


def back(arr, done, other, wide, tall, fs, ft):
    rows, width = arr.shape[0], tall.shape[1]
    hidden = [((rows, fs), BF16), ((rows, ft), BF16)]
    return call(
        back_body,
        "token_partials",
        [((rows // 2, 2 * width), F32), ((rows // 2, 2 * width), BF16)] + hidden,
        (arr, done, other, wide, tall),
        "vvvvv",
        [pltpu.VMEM(*s) for s in hidden + hidden] + [pltpu.VMEM((rows, 2 * width), F32)],
        2 * rows * (wide.size + tall.size),
    )


def token_sum_body(keep_ref, got_ref, after_ref, next_ref, send_ref):
    total = keep_ref[...] + got_ref[...].astype(F32)
    half = next_ref.shape[0]
    next_ref[...] = total[:half]
    send_ref[...] = total[half:].astype(send_ref.dtype)


def token_sum(keep, got, after, dtype, name):
    rows, width = keep.shape
    outs = [((rows // 2, width), F32), ((rows // 2, width), dtype)]
    return call(token_sum_body, name, outs, (keep, got, after), "vvh")


def last_sum_body(keep_ref, got_ref, mixed_hbm, grad_hbm, mixed_ref, grad_ref, sems):
    total = (keep_ref[...] + got_ref[...].astype(F32)).astype(BF16)
    width = mixed_ref.shape[1]
    mixed_ref[...] = total[:, :width]
    grad_ref[...] = total[:, width:]
    copies = [
        pltpu.make_async_copy(mixed_ref, mixed_hbm, sems.at[0]),
        pltpu.make_async_copy(grad_ref, grad_hbm, sems.at[1]),
    ]
    for copy in copies:
        copy.start()
    for copy in copies:
        copy.wait()


def outer_body(after_ref, arr_ref, h_ref, out_ref, slots, sems):
    width = out_ref.shape[1]
    steps = out_ref.shape[0] // ROWS
    c = arr_ref[:, width : 2 * width]

    def copy(step, slot):
        start = pl.multiple_of(step * ROWS, ROWS)
        return pltpu.make_async_copy(slots.at[slot], out_ref.at[pl.ds(start, ROWS)], sems.at[slot])

    @pl.loop(0, steps // 2)
    def _(pair):
        for side in range(2):
            step = 2 * pair + side
            slot = 2 * lax.rem(pair, 2) + side

            @pl.when(pair >= 2)
            def _():
                copy(step - 4, slot).wait()

        for side in range(2):
            step = 2 * pair + side
            slot = 2 * lax.rem(pair, 2) + side
            h = h_ref[:, pl.ds(pl.multiple_of(step * ROWS, ROWS), ROWS)]
            slots[slot] = contract_first(h, c).astype(BF16)
        for side in range(2):
            copy(2 * pair + side, 2 * lax.rem(pair, 2) + side).start()

    for step in range(steps - 4, steps):
        copy(step, step % 4).wait()


def outer(after, arr, h, width, name):
    rows, count = h.shape
    return call(
        outer_body,
        name,
        [((count, width), BF16)],
        (after, arr, h),
        "vvv",
        [pltpu.VMEM((SLOTS, ROWS, width), BF16), pltpu.SemaphoreType.DMA((SLOTS,))],
        2 * rows * count * width,
        2 * count * width,
        limit=8,
        out_places="h",
    )[0]


def flip(value, axes, bit, n):
    return lax.ppermute(value, axes, [(i, i ^ bit) for i in range(n)])


def by_kernels(n_seq, n_tok, tokens, modality, cotangent, gate_s, up_s, down_s, gate_t, up_t, down_t):
    rows, width = tokens.shape
    fs, ft = gate_s.shape[1], gate_t.shape[1]
    wide = ((2 * (fs + ft) // WIDE, width, WIDE), BF16)
    tall = ((fs + ft, width), BF16)
    pair = [pltpu.VMEM((rows, width), BF16)] * 2

    packed = ((rows, 2 * width + 128), BF16)
    scratch = pair + [pltpu.SMEM((rows,), jnp.int32), pltpu.SemaphoreType.DMA((3,))]
    wide, tall, arr = call(pack_body, "pack", [wide, tall, packed], (modality, tokens, cotangent), "hhh", scratch)
    got = flip(arr, TOK, HOPS[0], n_tok)
    wide = load(arr, gate_t, wide, tall, 0, "load_gate_text")
    arr = join(arr, got, "join_4", (wide, tall))
    got = flip(arr, TOK, HOPS[1], n_tok)
    wide = load(arr, up_t, wide, tall, ft // WIDE, "load_up_text")
    arr = join(arr, got, "join_8", (wide, tall))
    arr = join(arr, flip(arr, TOK, HOPS[2], n_tok), "join_16", (wide, tall))

    mine, theirs, wide, tall = partials(arr, gate_s, up_s, down_s, down_t, wide, tall)
    got = flip(theirs, "seq", 1, n_seq)
    total, send = call(core_sum_body, "core_sum", [like(mine), (mine.shape, BF16)], (mine, got), "vv", also=(wide, tall))
    got = flip(send, "seq", 2, n_seq)
    done = call(hidden_body, "hidden", [(mine.shape, BF16)], (total, got), "vv", also=(wide, tall))[0]
    other = flip(done, "seq", 1, n_seq)

    keep, send, hs, ht = back(arr, done, other, wide, tall, fs, ft)
    got = flip(send, TOK, HOPS[2], n_tok)
    down_t_grad = outer(keep, arr, ht, width, "down_text_grad")
    keep, send = token_sum(keep, got, down_t_grad, BF16, "token_sum_4")
    got = flip(send, TOK, HOPS[1], n_tok)
    down_s_grad = outer(keep, arr, hs, width, "down_speech_grad")
    keep, send = token_sum(keep, got, down_s_grad, F32, "token_sum_2")
    got = flip(send, TOK, HOPS[0], n_tok)
    outs = [((rows, width), BF16)] * 2
    mixed, token_grad = call(last_sum_body, "token_sum_1", outs, (keep, got), "vv", pair + [pltpu.SemaphoreType.DMA((2,))], out_places="hh")
    return mixed, token_grad, down_s_grad, down_t_grad


def by_arrays(n_seq, n_tok, tokens, modality, cotangent, gate_s, up_s, down_s, gate_t, up_t, down_t):
    width = tokens.shape[1]
    ft = gate_t.shape[1]
    kind = jnp.broadcast_to(modality.astype(BF16)[:, None], (modality.shape[0], 128))
    packed = jnp.concatenate([tokens, cotangent, kind], axis=1)
    arrived = lax.all_gather(packed, TOK, axis=0, tiled=True)
    rows, grads = arrived[:, :width], arrived[:, width : 2 * width]
    speech = arrived[:, 2 * width : 2 * width + 1] == 0

    def pick(s, t):
        return jnp.concatenate([jnp.where(speech, s[:, :ft], t), s[:, ft:]], axis=1)

    def halves(v):
        zero = jnp.zeros((), v.dtype)
        return jnp.where(speech, v, zero), jnp.where(speech, zero, v[:, :ft])

    g = pick(times(rows, gate_s), times(rows, gate_t))
    u = pick(times(rows, up_s), times(rows, up_t))
    dh = pick(contract_last(grads, down_s), contract_last(grads, down_t))
    sums = jnp.stack([g, u, dh])
    sums = sums + flip(sums, "seq", 1, n_seq)
    g, u, dh = sums + flip(sums.astype(BF16), "seq", 2, n_seq).astype(F32)
    sig = jax.nn.sigmoid(g)
    h = (g * sig * u).astype(BF16)
    dg = (dh * u * sig * (1.0 + g * (1.0 - sig))).astype(BF16)
    du = (dh * (g * sig)).astype(BF16)
    (hs, ht), (dgs, dgt), (dus, dut) = halves(h), halves(dg), halves(du)
    mixed = times(hs, down_s) + times(ht, down_t)
    grad = contract_last(dgs, gate_s) + contract_last(dus, up_s)
    grad = grad + contract_last(dgt, gate_t) + contract_last(dut, up_t)
    out = jnp.concatenate([mixed, grad], axis=1).astype(BF16)
    out = out.reshape(n_tok, out.shape[0] // n_tok, out.shape[1])
    out = lax.all_to_all(out, TOK, split_axis=0, concat_axis=0, tiled=True)
    total = jnp.sum(out.astype(F32), axis=0).astype(BF16)
    down_s_grad = contract_first(hs, grads).astype(BF16)
    down_t_grad = contract_first(ht, grads).astype(BF16)
    return total[:, :width], total[:, width:], down_s_grad, down_t_grad


def solution(mesh):
    n_seq, n_tok = mesh.shape["seq"], mesh.shape["attn"] * mesh.shape["exp"]

    def run(*args):
        hidden = args[3].shape[1], args[6].shape[1]
        fits = n_tok == 8 and hidden[0] % WIDE == 0 and hidden[1] % WIDE == 0
        fits = fits and hidden[0] >= hidden[1] and args[0].shape == (2, 3 * BLOCK)
        return (by_kernels if fits else by_arrays)(n_seq, n_tok, *args)

    return jax.shard_map(
        run,
        mesh=mesh,
        in_specs=(
            P(TOK, "seq"),
            P(TOK),
            P(TOK, "seq"),
            P("seq", TOK),
            P("seq", TOK),
            P(TOK, "seq"),
            P("seq", TOK),
            P("seq", TOK),
            P(TOK, "seq"),
        ),
        out_specs=(P(TOK, "seq"),) * 4,
        check_vma=False,
    )
```

time: 95.3 us -> 67.1 us (0.70)
  Pallas kernels: 0 us -> 39.9 us
  matrix products: 39.4 us -> 0 us
  blocking collectives: 32.3 us -> 0 us
  starting transfers between devices: 7.36 us -> 13.4 us
  waiting for transfers between devices: 9.77 us -> 12.9 us
  other arithmetic: 2.56 us -> 0 us
  local copies, waits for them, and re-layouts: 2.56 us -> 0 us
    pallas_call x0 -> x15, Pallas kernels: none -> 39.9 us  [call(): pl.pallas_call(seen, out_shape=shapes, in_specs=[pl.BlockSpec(memory_spac...]
    dot_general x14 -> x0, matrix products: 39.4 us -> none  [the longest x6 15.7 us: contract_last(): lax.dot_general(left, right, (((1,), (1,)), ((), ())), preferred_element_...]
    all_gather x1 -> x0, blocking collectives: 32.3 us -> none  [shards(): packed = lax.all_gather(packed, TOK, axis=0, tiled=True)]
    ppermute x3 -> x9, starting transfers between devices: 1.7 us -> 13.4 us  [flip(): return lax.ppermute(value, axes, [(i, i ^ bit) for i in range(n)])]
    ppermute x3 -> x9, waiting for transfers between devices: 7.12 us -> 12.9 us  [flip(): return lax.ppermute(value, axes, [(i, i ^ bit) for i in range(n)])]
    all_to_all x1 -> x0, starting transfers between devices: 5.66 us -> none  [shards(): out = lax.all_to_all(out, TOK, split_axis=0, concat_axis=0, tiled=True)]
    all_to_all x1 -> x0, waiting for transfers between devices: 2.65 us -> none  [shards(): out = lax.all_to_all(out, TOK, split_axis=0, concat_axis=0, tiled=True)]
    unnamed x28 -> x0, local copies, waits for them, and re-layouts: 1.79 us -> none
  transfers between devices with their start and end apart: 4 -> 9, of which waited for: 4 -> 5; matrix products, arithmetic and copies ran while one was open for 5% -> 0% of each run, Pallas kernels for 0% -> 23%
where the time goes in v3:
time: 67.1 us; the launch traced here: 66.9 us
  Pallas kernels  39.9 us (59%)
  starting transfers between devices  13.4 us (20%)
  waiting for transfers between devices  12.9 us (19%)
  between operations  0.77 us (1%)
    pallas_call x15, Pallas kernels, call(): pl.pallas_call(seen, out_shape=shapes, in_specs=[pl.BlockSpec(memory_spac...  39.9 us
    ppermute x9, starting transfers between devices, flip(): return lax.ppermute(value, axes, [(i, i ^ bit) for i in range(n)])  13.4 us
    ppermute x9, waiting for transfers between devices, flip(): return lax.ppermute(value, axes, [(i, i ^ bit) for i in range(n)])  12.9 us
  transfers between devices with their start and end apart: 9, of which 5 were waited for; matrix products, arithmetic and copies ran while one was open for 0% of the time, Pallas kernels for 23%

profile of v3, /device:TPU:0, one launch (start us, length us, event | category | flops | bytes accessed | tf_op | source)
XLA Modules:
  0.0 66.9 jit_solution(15928535981963871748)
XLA Ops:
  0.6 0.7 %pack.1 = (bf16[10,1536,1024]{2,1,0:T(8,128)(2,1)S(1)}, bf16[5120,1536]{1,0:T(8,128)(2,1)S(1)}, bf16[2,3200]{1,0:T(2,128)(2,1)S(1)}) custom-call(s32[2]{0:T(128)} %refs_0_.1, bf16[2,1536]{1,0:T(2,128)(2,1)} %refs_1_.4, bf16[2,1536]{1,0:T(2,128)(2,1)} %refs_2_.2), custom_call_target="tpu_custom_call" | custom-call | tf_op jit(solution)/shard_map/pack/pallas_call | solution.py:55
  1.4 4.1 %collective-permute-start = (bf16[2,3200]{1,0:T(2,128)(2,1)S(1)}, bf16[2,3200]{1,0:T(2,128)(2,1)S(1)}, u32[]{:S(2)}, u32[]{:S(2)}) collective-permute-start(bf16[2,3200]{1,0:T(2,128)(2,1)S(1)} %get-tuple-element.23.refs_0_), channel_id=1, source_target_pairs={{0,8},{4,12},{8,0},{12,4},{16,24},{20,28},{24,16},{28,20},{1,9},{5... | collective-permute-start | bytes 38408 | tf_op jit(solution)/shard_map/ppermute | solution.py:342
  5.5 2.9 %load_gate_text.1.refs_2_ = bf16[10,1536,1024]{2,1,0:T(8,128)(2,1)S(1)} custom-call(bf16[2,3200]{1,0:T(2,128)(2,1)S(1)} %get-tuple-element.23.refs_0_, bf16[1536,2048]{1,0:T(8,128)(2,1)} %refs_1_.5, bf16[10,1536,1024]{2,1,0:T(8,128)(2,1)S(1)} %get-tuple-element.24.refs_2_, ...), custom_call_target="tpu_custom_call", output_to_operand_aliasing={{}: (2, {})} | custom-call | bytes 6291456 | tf_op jit(solution)/shard_map/load_gate_text/pallas_call | solution.py:55
  8.4 1.6 %collective-permute-start.1 = (bf16[4,3200]{1,0:T(4,128)(2,1)S(1)}, bf16[4,3200]{1,0:T(4,128)(2,1)S(1)}, u32[]{:S(2)}, u32[]{:S(2)}) collective-permute-start(bf16[4,3200]{1,0:T(4,128)(2,1)S(1)} %join_4.1.refs_0_), channel_id=1, source_target_pairs={{0,4},{4,0},{8,12},{12,8},{16,20},{20,16},{24,28},{28,24},{1,5},{5... | collective-permute-start | bytes 76808 | tf_op jit(solution)/shard_map/ppermute | solution.py:342
  10.0 2.9 %load_up_text.1.refs_2_.refs_5_ = bf16[10,1536,1024]{2,1,0:T(8,128)(2,1)S(1)} custom-call(bf16[4,3200]{1,0:T(4,128)(2,1)S(1)} %join_4.1.refs_0_, bf16[1536,2048]{1,0:T(8,128)(2,1)} %refs_1_.6, bf16[10,1536,1024]{2,1,0:T(8,128)(2,1)S(1)} %load_gate_text.1.refs_2_, bf16[5120,1536]{1,0:T(8,128)(2,1)S(1)} %get-tuple-element.25.refs_3_.refs_6_), custom_call_target="tpu_custom_call", output_to_operand_aliasing={{}: (2, {})} | custom-call | bytes 6291456 | tf_op jit(solution)/shard_map/load_up_text/pallas_call | solution.py:55
  12.9 0.0 collective-permute-done.1.refs_1_
  12.9 1.6 %collective-permute-start.2 = (bf16[8,3200]{1,0:T(8,128)(2,1)S(1)}, bf16[8,3200]{1,0:T(8,128)(2,1)S(1)}, u32[]{:S(2)}, u32[]{:S(2)}) collective-permute-start(bf16[8,3200]{1,0:T(8,128)(2,1)S(1)} %join_8.1.refs_0_), channel_id=1, source_target_pairs={{0,16},{4,20},{8,24},{12,28},{16,0},{20,4},{24,8},{28,12},{1,17},{... | collective-permute-start | bytes 153608 | tf_op jit(solution)/shard_map/ppermute | solution.py:342
  14.5 2.6 %collective-permute-done.2.refs_1_ = bf16[8,3200]{1,0:T(8,128)(2,1)S(1)} collective-permute-done((bf16[8,3200]{1,0:T(8,128)(2,1)S(1)}, bf16[8,3200]{1,0:T(8,128)(2,1)S(1)}, u32[]{:S(2)}, u32[]{:S(2)}) %collective-permute-start.2) | collective-permute-done | bytes 51232 | tf_op jit(solution)/shard_map/ppermute | solution.py:342
  17.1 12.4 %hidden_partials.1 = (f32[3,16,1536]{2,1,0:T(8,128)S(1)}, f32[3,16,1536]{2,1,0:T(8,128)S(1)}, bf16[10,1536,1024]{2,1,0:T(8,128)(2,1)S(1)}, bf16[5120,1536]{1,0:T(8,128)(2,1)S(1)}) custom-call(bf16[16,3200]{1,0:T(8,128)(2,1)S(1)} %join_16.1.refs_0_.refs_1_, bf16[1536,3072]{1,0:T(8,128)(2,1)} %refs_1_.7, ...), custom_call_target="tpu_custom_call", output_to_operand_aliasing={{2}: (5, {}), {3}: (6, {})} | custom-call | flops 754974720 | bytes 34603008 | tf_op jit(solution)/shard_map/hidden_partials/pallas_call | solution.py:55
  29.5 0.1 collective-permute-start.3
  29.6 1.6 %collective-permute-done.3.refs_1_ = f32[3,16,1536]{2,1,0:T(8,128)S(1)} collective-permute-done((f32[3,16,1536]{2,1,0:T(8,128)S(1)}, f32[3,16,1536]{2,1,0:T(8,128)S(1)}, u32[]{:S(2)}, u32[]{:S(2)}) %collective-permute-start.3) | collective-permute-done | bytes 294944 | tf_op jit(solution)/shard_map/ppermute | solution.py:342
  31.2 1.6 %collective-permute-start.4 = (bf16[3,16,1536]{2,1,0:T(8,128)(2,1)S(1)}, bf16[3,16,1536]{2,1,0:T(8,128)(2,1)S(1)}, u32[]{:S(2)}, u32[]{:S(2)}) collective-permute-start(bf16[3,16,1536]{2,1,0:T(8,128)(2,1)S(1)} %get-tuple-element.31), channel_id=1, source_target_pairs={{0,2},{1,3},{2,0},{3,1},{4,6},{5,7},{6,4},{7,5},{8,10},{9,11},{10,... | collective-permute-start | bytes 442376 | tf_op jit(solution)/shard_map/ppermute | solution.py:342
  32.8 4.4 %collective-permute-done.4.refs_1_ = bf16[3,16,1536]{2,1,0:T(8,128)(2,1)S(1)} collective-permute-done((bf16[3,16,1536]{2,1,0:T(8,128)(2,1)S(1)}, bf16[3,16,1536]{2,1,0:T(8,128)(2,1)S(1)}, u32[]{:S(2)}, u32[]{:S(2)}) %collective-permute-start.4) | collective-permute-done | bytes 147488 | tf_op jit(solution)/shard_map/ppermute | solution.py:342
  37.2 0.1 hidden.1.refs_1_
  37.3 0.1 collective-permute-start.5
  37.3 1.4 %collective-permute-done.5.refs_2_ = bf16[3,16,1536]{2,1,0:T(8,128)(2,1)S(1)} collective-permute-done((bf16[3,16,1536]{2,1,0:T(8,128)(2,1)S(1)}, bf16[3,16,1536]{2,1,0:T(8,128)(2,1)S(1)}, u32[]{:S(2)}, u32[]{:S(2)}) %collective-permute-start.5) | collective-permute-done | bytes 147488 | tf_op jit(solution)/shard_map/ppermute | solution.py:342
  38.7 10.3 %token_partials.1 = (f32[8,3072]{1,0:T(8,128)S(1)}, bf16[8,3072]{1,0:T(8,128)(2,1)S(1)}, bf16[16,3072]{1,0:T(8,128)(2,1)S(1)}, bf16[16,2048]{1,0:T(8,128)(2,1)S(1)}) custom-call(bf16[16,3200]{1,0:T(8,128)(2,1)S(1)} %join_16.1.refs_0_.refs_1_, bf16[3,16,1536]{2,1,0:T(8,128)(2,1)S(1)} %hidden.1.refs_1_, ...), custom_call_target="tpu_custom_call" | custom-call | flops 754974720 | tf_op jit(solution)/shard_map/token_partials/pallas_call | solution.py:55
  49.0 1.5 %collective-permute-start.6 = (bf16[8,3072]{1,0:T(8,128)(2,1)S(1)}, bf16[8,3072]{1,0:T(8,128)(2,1)S(1)}, u32[]{:S(2)}, u32[]{:S(2)}) collective-permute-start(bf16[8,3072]{1,0:T(8,128)(2,1)S(1)} %get-tuple-element.33), channel_id=1, source_target_pairs={{0,16},{4,20},{8,24},{12,28},{16,0},{20,4},{24,8},{28,12},{1,17},{... | collective-permute-start | bytes 147464 | tf_op jit(solution)/shard_map/ppermute | solution.py:342
  50.5 4.1 %down_text_grad.1.refs_2_ = bf16[2048,1536]{1,0:T(8,128)(2,1)} custom-call(f32[8,3072]{1,0:T(8,128)S(1)} %get-tuple-element.32.refs_0_, bf16[16,3200]{1,0:T(8,128)(2,1)S(1)} %join_16.1.refs_0_.refs_1_, bf16[16,2048]{1,0:T(8,128)(2,1)S(1)} %get-tuple-element.34.refs_2_), custom_call_target="tpu_custom_call" | custom-call | flops 100663296 | bytes 6291456 | tf_op jit(solution)/shard_map/down_text_grad/pallas_call | solution.py:55
  54.6 1.0 %collective-permute-start.7 = (bf16[4,3072]{1,0:T(4,128)(2,1)S(1)}, bf16[4,3072]{1,0:T(4,128)(2,1)S(1)}, u32[]{:S(2)}, u32[]{:S(2)}) collective-permute-start(bf16[4,3072]{1,0:T(4,128)(2,1)S(1)} %get-tuple-element.36), channel_id=1, source_target_pairs={{0,4},{4,0},{8,12},{12,8},{16,20},{20,16},{24,28},{28,24},{1,5},{5... | collective-permute-start | bytes 73736 | tf_op jit(solution)/shard_map/ppermute | solution.py:342
  55.6 5.8 %down_speech_grad.1.refs_2_ = bf16[3072,1536]{1,0:T(8,128)(2,1)} custom-call(f32[4,3072]{1,0:T(4,128)S(1)} %get-tuple-element.35.refs_0_, bf16[16,3200]{1,0:T(8,128)(2,1)S(1)} %join_16.1.refs_0_.refs_1_, bf16[16,3072]{1,0:T(8,128)(2,1)S(1)} %get-tuple-element.37.refs_2_), custom_call_target="tpu_custom_call" | custom-call | flops 150994944 | bytes 9437184 | tf_op jit(solution)/shard_map/down_speech_grad/pallas_call | solution.py:55
  61.5 1.8 %collective-permute-start.8 = (f32[2,3072]{1,0:T(2,128)S(1)}, f32[2,3072]{1,0:T(2,128)S(1)}, u32[]{:S(2)}, u32[]{:S(2)}) collective-permute-start(f32[2,3072]{1,0:T(2,128)S(1)} %get-tuple-element.39), channel_id=1, source_target_pairs={{0,8},{4,12},{8,0},{12,4},{16,24},{20,28},{24,16},{28,20},{1,9},{5... | collective-permute-start | bytes 73736 | tf_op jit(solution)/shard_map/ppermute | solution.py:342
  63.3 3.0 %collective-permute-done.8.refs_1_ = f32[2,3072]{1,0:T(2,128)S(1)} collective-permute-done((f32[2,3072]{1,0:T(2,128)S(1)}, f32[2,3072]{1,0:T(2,128)S(1)}, u32[]{:S(2)}, u32[]{:S(2)}) %collective-permute-start.8) | collective-permute-done | bytes 24608 | tf_op jit(solution)/shard_map/ppermute | solution.py:342
  66.3 0.6 token_sum_1.1
  (9 shorter events, 0.1 us)
Async XLA Ops:
  1.4 7.0 %collective-permute-start = (bf16[2,3200]{1,0:T(2,128)(2,1)S(1)}, bf16[2,3200]{1,0:T(2,128)(2,1)S(1)}, u32[]{:S(2)}, u32[]{:S(2)}) collective-permute-start(bf16[2,3200]{1,0:T(2,128)(2,1)S(1)} %get-tuple-element.23.refs_0_), channel_id=1, source_target_pairs={{0,8},{4,12},{8,0},{12,4},{16,24},{20,28},{24,16},{28,20},{1,9},{5... | collective-permute-start | bytes 38408 | tf_op jit(solution)/shard_map/ppermute | solution.py:342
  8.4 4.5 %collective-permute-start.1 = (bf16[4,3200]{1,0:T(4,128)(2,1)S(1)}, bf16[4,3200]{1,0:T(4,128)(2,1)S(1)}, u32[]{:S(2)}, u32[]{:S(2)}) collective-permute-start(bf16[4,3200]{1,0:T(4,128)(2,1)S(1)} %join_4.1.refs_0_), channel_id=1, source_target_pairs={{0,4},{4,0},{8,12},{12,8},{16,20},{20,16},{24,28},{28,24},{1,5},{5... | collective-permute-start | bytes 76808 | tf_op jit(solution)/shard_map/ppermute | solution.py:342
  12.9 4.2 %collective-permute-start.2 = (bf16[8,3200]{1,0:T(8,128)(2,1)S(1)}, bf16[8,3200]{1,0:T(8,128)(2,1)S(1)}, u32[]{:S(2)}, u32[]{:S(2)}) collective-permute-start(bf16[8,3200]{1,0:T(8,128)(2,1)S(1)} %join_8.1.refs_0_), channel_id=1, source_target_pairs={{0,16},{4,20},{8,24},{12,28},{16,0},{20,4},{24,8},{28,12},{1,17},{... | collective-permute-start | bytes 153608 | tf_op jit(solution)/shard_map/ppermute | solution.py:342
  29.5 1.6 %collective-permute-start.3 = (f32[3,16,1536]{2,1,0:T(8,128)S(1)}, f32[3,16,1536]{2,1,0:T(8,128)S(1)}, u32[]{:S(2)}, u32[]{:S(2)}) collective-permute-start(f32[3,16,1536]{2,1,0:T(8,128)S(1)} %get-tuple-element.27), channel_id=1, source_target_pairs={{0,1},{1,0},{2,3},{3,2},{4,5},{5,4},{6,7},{7,6},{8,9},{9,8},{10,11... | collective-permute-start | bytes 884744 | tf_op jit(solution)/shard_map/ppermute | solution.py:342
  31.2 6.0 %collective-permute-start.4 = (bf16[3,16,1536]{2,1,0:T(8,128)(2,1)S(1)}, bf16[3,16,1536]{2,1,0:T(8,128)(2,1)S(1)}, u32[]{:S(2)}, u32[]{:S(2)}) collective-permute-start(bf16[3,16,1536]{2,1,0:T(8,128)(2,1)S(1)} %get-tuple-element.31), channel_id=1, source_target_pairs={{0,2},{1,3},{2,0},{3,1},{4,6},{5,7},{6,4},{7,5},{8,10},{9,11},{10,... | collective-permute-start | bytes 442376 | tf_op jit(solution)/shard_map/ppermute | solution.py:342
  37.3 1.4 %collective-permute-start.5 = (bf16[3,16,1536]{2,1,0:T(8,128)(2,1)S(1)}, bf16[3,16,1536]{2,1,0:T(8,128)(2,1)S(1)}, u32[]{:S(2)}, u32[]{:S(2)}) collective-permute-start(bf16[3,16,1536]{2,1,0:T(8,128)(2,1)S(1)} %hidden.1.refs_1_), channel_id=1, source_target_pairs={{0,1},{1,0},{2,3},{3,2},{4,5},{5,4},{6,7},{7,6},{8,9},{9,8},{10,11... | collective-permute-start | bytes 442376 | tf_op jit(solution)/shard_map/ppermute | solution.py:342
  49.0 5.6 %collective-permute-start.6 = (bf16[8,3072]{1,0:T(8,128)(2,1)S(1)}, bf16[8,3072]{1,0:T(8,128)(2,1)S(1)}, u32[]{:S(2)}, u32[]{:S(2)}) collective-permute-start(bf16[8,3072]{1,0:T(8,128)(2,1)S(1)} %get-tuple-element.33), channel_id=1, source_target_pairs={{0,16},{4,20},{8,24},{12,28},{16,0},{20,4},{24,8},{28,12},{1,17},{... | collective-permute-start | bytes 147464 | tf_op jit(solution)/shard_map/ppermute | solution.py:342
  54.6 6.9 %collective-permute-start.7 = (bf16[4,3072]{1,0:T(4,128)(2,1)S(1)}, bf16[4,3072]{1,0:T(4,128)(2,1)S(1)}, u32[]{:S(2)}, u32[]{:S(2)}) collective-permute-start(bf16[4,3072]{1,0:T(4,128)(2,1)S(1)} %get-tuple-element.36), channel_id=1, source_target_pairs={{0,4},{4,0},{8,12},{12,8},{16,20},{20,16},{24,28},{28,24},{1,5},{5... | collective-permute-start | bytes 73736 | tf_op jit(solution)/shard_map/ppermute | solution.py:342
  61.5 4.8 %collective-permute-start.8 = (f32[2,3072]{1,0:T(2,128)S(1)}, f32[2,3072]{1,0:T(2,128)S(1)}, u32[]{:S(2)}, u32[]{:S(2)}) collective-permute-start(f32[2,3072]{1,0:T(2,128)S(1)} %get-tuple-element.39), channel_id=1, source_target_pairs={{0,8},{4,12},{8,0},{12,4},{16,24},{20,28},{24,16},{28,20},{1,9},{5... | collective-permute-start | bytes 73736 | tf_op jit(solution)/shard_map/ppermute | solution.py:342

commit v4 on v3

--- a/solution.py
+++ b/solution.py
@@ -15,7 +15,9 @@
 BLOCK = 512
 WIDE = 1024
 ROWS = 256
-SLOTS = 4
+OWN_STEPS = 3
+FIRST_STEPS = 8
+TEXT_STEPS = 1
 PLACES = {"h": pl.ANY, "v": pltpu.VMEM, "s": pltpu.SMEM}
 
 
@@ -106,52 +108,68 @@
     return call(join_body, name, [((2 * a.shape[0], a.shape[1]), BF16)], (a, b), "vv", also=also)[0]
 
 
-def column_blocks(src, wide, first):
-    return [(src.at[:, pl.ds(i * WIDE, WIDE)], wide.at[first + i]) for i in range(src.shape[1] // WIDE)]
+def column_blocks(src, wide, first, cuts):
+    rows = src.shape[0] // cuts
+    parts = [pl.ds(j * rows, rows) for j in range(cuts)]
+    return [
+        [(src.at[part, pl.ds(i * WIDE, WIDE)], wide.at[first + i, part]) for part in parts]
+        for i in range(src.shape[1] // WIDE)
+    ]
 
 
 def row_blocks(src, tall, first):
     return [
-        (src.at[pl.ds(i, BLOCK)], tall.at[pl.ds(first + i, BLOCK)]) for i in range(0, src.shape[0], BLOCK)
+        [(src.at[pl.ds(i, BLOCK)], tall.at[pl.ds(first + i, BLOCK)])] for i in range(0, src.shape[0], BLOCK)
     ]
 
 
-def started(pairs, sems, first):
-    copies = [pltpu.make_async_copy(s, d, sems.at[first + i]) for i, (s, d) in enumerate(pairs)]
-    for copy in copies:
-        copy.start()
+def started(groups, sems):
+    copies, count = [], 0
+    for group in groups:
+        copies.append([pltpu.make_async_copy(s, d, sems.at[count + i]) for i, (s, d) in enumerate(group)])
+        count += len(group)
+    for group in copies:
+        for copy in group:
+            copy.start()
     return copies
 
 
-def load_body(first, after_ref, src_hbm, old_ref, wide_ref, sems):
-    for copy in started(column_blocks(src_hbm, wide_ref, first), sems, 0):
+def wait(group):
+    for copy in group:
         copy.wait()
 
 
-def load(after, src, wide, tall, first, name):
+def load_body(first, after_ref, src_hbm, old_ref, place_ref, sems):
+    if place_ref.ndim == 3:
+        groups = column_blocks(src_hbm, place_ref, first, 4)
+    else:
+        groups = row_blocks(src_hbm, place_ref, first)
+    for group in started(groups, sems):
+        wait(group)
+
+
+def load(after, src, place, also, first, name):
     return call(
         functools.partial(load_body, first),
         name,
-        [like(wide)],
-        (after, src, wide),
+        [like(place)],
+        (after, src, place),
         "vhv",
-        [pltpu.SemaphoreType.DMA((src.shape[1] // WIDE,))],
+        [pltpu.SemaphoreType.DMA((8,))],
         traffic=size_of(src),
         aliases={2: 0},
-        also=(tall,),
+        also=also,
     )[0]
 
 
 def partials_body(
-    arr_ref, gs_hbm, us_hbm, dt_hbm, ds_hbm, old_wide, old_tall,
-    mine_ref, theirs_ref, wide_ref, tall_ref, part, sems,
+    arr_ref, gs_hbm, us_hbm, ds_hbm, old_wide, old_tall, mine_ref, theirs_ref, wide_ref, tall_ref, part, sems
 ):
-    fs, ft, width = ds_hbm.shape[0], dt_hbm.shape[0], dt_hbm.shape[1]
+    fs, width = ds_hbm.shape
+    ft = tall_ref.shape[0] - fs
     ns, nt = fs // WIDE, ft // WIDE
-    text_copies = started(column_blocks(gs_hbm, wide_ref, 2 * nt), sems, 0)
-    text_copies = [text_copies, started(column_blocks(us_hbm, wide_ref, 2 * nt + ns), sems, ns)]
-    dt_copies = started(row_blocks(dt_hbm, tall_ref, fs), sems, 2 * ns)
-    ds_copies = started(row_blocks(ds_hbm, tall_ref, 0), sems, 2 * ns + ft // BLOCK)
+    groups = column_blocks(gs_hbm, wide_ref, 2 * nt, 2) + column_blocks(us_hbm, wide_ref, 2 * nt + ns, 2)
+    copies = started(groups + row_blocks(ds_hbm, tall_ref, 0), sems)
     x = arr_ref[:, :width]
     c = arr_ref[:, width : 2 * width]
     speech = is_speech(arr_ref)
@@ -159,20 +177,18 @@
     for k in range(2):
         for i in range(nt):
             part[k, :, i * WIDE : (i + 1) * WIDE] = times(x, wide_ref[k * nt + i])
+    for i in range(0, ft, BLOCK):
+        part[2, :, i : i + BLOCK] = contract_last(c, tall_ref[fs + i : fs + i + BLOCK, :])
     for k in range(2):
         for i in range(ns):
-            text_copies[k][i].wait()
+            wait(copies[k * ns + i])
             value = times(x, wide_ref[2 * nt + k * ns + i])
             cut = slice(i * WIDE, (i + 1) * WIDE)
             if i < nt:
                 value = jnp.where(speech, value, part[k, :, cut])
             part[k, :, cut] = value
-    for i, copy in enumerate(dt_copies):
-        copy.wait()
-        cut = slice(i * BLOCK, (i + 1) * BLOCK)
-        part[2, :, cut] = contract_last(c, tall_ref[fs + i * BLOCK : fs + (i + 1) * BLOCK, :])
-    for i, copy in enumerate(ds_copies):
-        copy.wait()
+    for i in range(fs // BLOCK):
+        wait(copies[2 * ns + i])
         cut = slice(i * BLOCK, (i + 1) * BLOCK)
         value = contract_last(c, tall_ref[cut, :])
         if i * BLOCK < ft:
@@ -185,20 +201,20 @@
         theirs_ref[k] = part[k, :, pl.ds(pl.multiple_of((1 - odd) * half, half), half)]
 
 
-def partials(arr, gate_s, up_s, down_s, down_t, wide, tall):
+def partials(arr, gate_s, up_s, down_s, wide, tall):
     rows, fs = arr.shape[0], gate_s.shape[1]
     half = ((3, rows, fs // 2), F32)
-    n_sems = 2 * fs // WIDE + tall.shape[0] // BLOCK
+    n_sems = 4 * fs // WIDE + fs // BLOCK
     return call(
         partials_body,
         "hidden_partials",
         [half, half, like(wide), like(tall)],
-        (arr, gate_s, up_s, down_t, down_s, wide, tall),
-        "vhhhhvv",
+        (arr, gate_s, up_s, down_s, wide, tall),
+        "vhhhvv",
         [pltpu.VMEM((3, rows, fs), F32), pltpu.SemaphoreType.DMA((n_sems,))],
         2 * rows * (wide.size + tall.size),
-        size_of(gate_s, up_s, down_s, down_t),
-        aliases={5: 2, 6: 3},
+        size_of(gate_s, up_s, down_s),
+        aliases={4: 2, 5: 3},
     )
 
 
@@ -219,7 +235,7 @@
 
 
 def back_body(
-    arr_ref, done_ref, other_ref, wide_ref, tall_ref,
+    arr_ref, done_ref, other_ref, wide_ref, tall_ref, after_ref,
     keep_ref, send_ref, hs_ref, ht_ref, dgs, dgt, dus, dut, out,
 ):
     speech = is_speech(arr_ref)
@@ -249,15 +265,15 @@
     send_ref[...] = out[half:].astype(BF16)
 
 
-def back(arr, done, other, wide, tall, fs, ft):
+def back(arr, done, other, wide, tall, after, fs, ft):
     rows, width = arr.shape[0], tall.shape[1]
     hidden = [((rows, fs), BF16), ((rows, ft), BF16)]
     return call(
         back_body,
         "token_partials",
         [((rows // 2, 2 * width), F32), ((rows // 2, 2 * width), BF16)] + hidden,
-        (arr, done, other, wide, tall),
-        "vvvvv",
+        (arr, done, other, wide, tall, after),
+        "vvvvvh",
         [pltpu.VMEM(*s) for s in hidden + hidden] + [pltpu.VMEM((rows, 2 * width), F32)],
         2 * rows * (wide.size + tall.size),
     )
@@ -291,51 +307,47 @@
         copy.wait()
 
 
-def outer_body(after_ref, arr_ref, h_ref, out_ref, slots, sems):
-    width = out_ref.shape[1]
-    steps = out_ref.shape[0] // ROWS
+def outer_steps(c, steps, slots, sems):
+    copies = []
+    for i, (h, place) in enumerate(steps):
+        slots[i] = contract_first(h, c).astype(BF16)
+        copies.append(pltpu.make_async_copy(slots.at[i], place, sems.at[i]))
+        copies[-1].start()
+    for copy in copies:
+        copy.wait()
+
+
+def rows_at(ref, start):
+    return ref.at[pl.ds(pl.multiple_of(start, ROWS), ROWS)]
+
+
+def outer_own_body(count, arr_ref, done_ref, out_ref, slots, sems):
+    half, width = done_ref.shape[2], out_ref.shape[1]
     c = arr_ref[:, width : 2 * width]
-
-    def copy(step, slot):
-        start = pl.multiple_of(step * ROWS, ROWS)
-        return pltpu.make_async_copy(slots.at[slot], out_ref.at[pl.ds(start, ROWS)], sems.at[slot])
-
-    @pl.loop(0, steps // 2)
-    def _(pair):
-        for side in range(2):
-            step = 2 * pair + side
-            slot = 2 * lax.rem(pair, 2) + side
-
-            @pl.when(pair >= 2)
-            def _():
-                copy(step - 4, slot).wait()
-
-        for side in range(2):
-            step = 2 * pair + side
-            slot = 2 * lax.rem(pair, 2) + side
-            h = h_ref[:, pl.ds(pl.multiple_of(step * ROWS, ROWS), ROWS)]
-            slots[slot] = contract_first(h, c).astype(BF16)
-        for side in range(2):
-            copy(2 * pair + side, 2 * lax.rem(pair, 2) + side).start()
-
-    for step in range(steps - 4, steps):
-        copy(step, step % 4).wait()
-
-
-def outer(after, arr, h, width, name):
-    rows, count = h.shape
-    return call(
-        outer_body,
-        name,
-        [((count, width), BF16)],
-        (after, arr, h),
-        "vvv",
-        [pltpu.VMEM((SLOTS, ROWS, width), BF16), pltpu.SemaphoreType.DMA((SLOTS,))],
-        2 * rows * count * width,
-        2 * count * width,
-        limit=8,
-        out_places="h",
-    )[0]
+    h = done_ref[0]
+    h = jnp.where(is_speech(arr_ref), h, jnp.zeros_like(h))
+    base = parity() * half
+    steps = [(h[:, i * ROWS : (i + 1) * ROWS], rows_at(out_ref, base + i * ROWS)) for i in range(count)]
+    outer_steps(c, steps, slots, sems)
+
+
+def outer_body(speech, text, after_ref, arr_ref, hs_ref, ht_ref, *refs):
+    slots, sems = refs[-2:]
+    outs = list(refs[1:-2])
+    out_s = outs.pop(0) if len(speech) else None
+    out_t = outs.pop(0) if len(text) else None
+    width = (out_s if len(speech) else out_t).shape[1]
+    c = arr_ref[:, width : 2 * width]
+    half = hs_ref.shape[1] // 2
+    odd = parity()
+    steps = []
+    for i in speech:
+        side = odd if i * ROWS < half else 1 - odd
+        start = side * half + i * ROWS % half
+        steps.append((hs_ref[:, pl.ds(pl.multiple_of(start, ROWS), ROWS)], rows_at(out_s, start)))
+    for i in text:
+        steps.append((ht_ref[:, i * ROWS : (i + 1) * ROWS], rows_at(out_t, i * ROWS)))
+    outer_steps(c, steps, slots, sems)
 
 
 def flip(value, axes, bit, n):
@@ -353,28 +365,61 @@
     scratch = pair + [pltpu.SMEM((rows,), jnp.int32), pltpu.SemaphoreType.DMA((3,))]
     wide, tall, arr = call(pack_body, "pack", [wide, tall, packed], (modality, tokens, cotangent), "hhh", scratch)
     got = flip(arr, TOK, HOPS[0], n_tok)
-    wide = load(arr, gate_t, wide, tall, 0, "load_gate_text")
+    wide = load(arr, gate_t, wide, (tall,), 0, "load_gate_text")
     arr = join(arr, got, "join_4", (wide, tall))
     got = flip(arr, TOK, HOPS[1], n_tok)
-    wide = load(arr, up_t, wide, tall, ft // WIDE, "load_up_text")
+    wide = load(arr, up_t, wide, (tall,), ft // WIDE, "load_up_text")
     arr = join(arr, got, "join_8", (wide, tall))
-    arr = join(arr, flip(arr, TOK, HOPS[2], n_tok), "join_16", (wide, tall))
-
-    mine, theirs, wide, tall = partials(arr, gate_s, up_s, down_s, down_t, wide, tall)
+    got = flip(arr, TOK, HOPS[2], n_tok)
+    tall = load(arr, down_t, tall, (wide,), fs, "load_down_text")
+    arr = join(arr, got, "join_16", (wide, tall))
+
+    mine, theirs, wide, tall = partials(arr, gate_s, up_s, down_s, wide, tall)
     got = flip(theirs, "seq", 1, n_seq)
-    total, send = call(core_sum_body, "core_sum", [like(mine), (mine.shape, BF16)], (mine, got), "vv", also=(wide, tall))
+    total, send = call(
+        core_sum_body, "core_sum", [like(mine), (mine.shape, BF16)], (mine, got), "vv", also=(wide, tall)
+    )
     got = flip(send, "seq", 2, n_seq)
     done = call(hidden_body, "hidden", [(mine.shape, BF16)], (total, got), "vv", also=(wide, tall))[0]
     other = flip(done, "seq", 1, n_seq)
 
-    keep, send, hs, ht = back(arr, done, other, wide, tall, fs, ft)
+    def slots(count):
+        return [pltpu.VMEM((count, ROWS, width), BF16), pltpu.SemaphoreType.DMA((count,))]
+
+    def cost(count):
+        return 2 * arr.shape[0] * count * ROWS * width, 2 * count * ROWS * width
+
+    own = OWN_STEPS
+    down_s_grad = call(
+        functools.partial(outer_own_body, own), "down_grad_own", [like(down_s)], (arr, done), "vv", slots(own),
+        *cost(own), out_places="h", also=(wide, tall),
+    )[0]
+    keep, send, hs, ht = back(arr, done, other, wide, tall, down_s_grad, fs, ft)
+
     got = flip(send, TOK, HOPS[2], n_tok)
-    down_t_grad = outer(keep, arr, ht, width, "down_text_grad")
-    keep, send = token_sum(keep, got, down_t_grad, BF16, "token_sum_4")
+    first, second = range(own, FIRST_STEPS), range(FIRST_STEPS, fs // ROWS)
+    down_s_grad = call(
+        functools.partial(outer_body, first, ()), "down_grad_1", [like(down_s)], (keep, arr, hs, ht, down_s_grad),
+        "vvvvh", slots(len(first)), *cost(len(first)), limit=8, out_places="h", aliases={4: 0},
+    )[0]
+    keep, send = token_sum(keep, got, down_s_grad, BF16, "token_sum_4")
+
     got = flip(send, TOK, HOPS[1], n_tok)
-    down_s_grad = outer(keep, arr, hs, width, "down_speech_grad")
-    keep, send = token_sum(keep, got, down_s_grad, F32, "token_sum_2")
+    text = range(0, TEXT_STEPS)
+    count = len(second) + len(text)
+    down_s_grad, down_t_grad = call(
+        functools.partial(outer_body, second, text), "down_grad_2", [like(down_s), like(down_t)],
+        (keep, arr, hs, ht, down_s_grad), "vvvvh", slots(count), *cost(count), limit=8, out_places="hh",
+        aliases={4: 0},
+    )
+    keep, send = token_sum(keep, got, down_t_grad, F32, "token_sum_2")
+
     got = flip(send, TOK, HOPS[0], n_tok)
+    text = range(TEXT_STEPS, ft // ROWS)
+    down_t_grad = call(
+        functools.partial(outer_body, (), text), "down_grad_3", [like(down_t)], (keep, arr, hs, ht, down_t_grad),
+        "vvvvh", slots(len(text)), *cost(len(text)), limit=8, out_places="h", aliases={4: 0},
+    )[0]
     outs = [((rows, width), BF16)] * 2
     mixed, token_grad = call(last_sum_body, "token_sum_1", outs, (keep, got), "vv", pair + [pltpu.SemaphoreType.DMA((2,))], out_places="hh")
     return mixed, token_grad, down_s_grad, down_t_grad

time: 67.1 us -> 61.8 us (0.921)
  waiting for transfers between devices: 12.9 us -> 7.19 us
    ppermute x9, waiting for transfers between devices: 12.9 us -> 7.19 us  [flip(): return lax.ppermute(value, axes, [(i, i ^ bit) for i in range(n)])]
    pallas_call x15 -> x18, Pallas kernels: 39.9 us -> 40.4 us  [call(): pl.pallas_call(seen, out_shape=shapes, in_specs=[pl.BlockSpec(memory_spac...]
  transfers between devices with their start and end apart: 9 -> 9, of which waited for: 5 -> 5; matrix products, arithmetic and copies ran while one was open for 0% -> 0% of each run, Pallas kernels for 23% -> 29%
where the time goes in v4:
time: 61.8 us; the launch traced here: 61.6 us
  Pallas kernels  40.4 us (65%)
  starting transfers between devices  13.1 us (21%)
  waiting for transfers between devices  7.19 us (12%)
  between operations  0.95 us (2%)
    pallas_call x18, Pallas kernels, call(): pl.pallas_call(seen, out_shape=shapes, in_specs=[pl.BlockSpec(memory_spac...  40.4 us
    ppermute x9, starting transfers between devices, flip(): return lax.ppermute(value, axes, [(i, i ^ bit) for i in range(n)])  13.1 us
    ppermute x9, waiting for transfers between devices, flip(): return lax.ppermute(value, axes, [(i, i ^ bit) for i in range(n)])  7.19 us
  transfers between devices with their start and end apart: 9, of which 5 were waited for; matrix products, arithmetic and copies ran while one was open for 0% of the time, Pallas kernels for 29%

profile of v4, /device:TPU:0, one launch (start us, length us, event | category | flops | bytes accessed | tf_op | source)
XLA Modules:
  0.0 61.6 jit_solution(520046936546749814)
XLA Ops:
  0.6 0.7 %pack.1 = (bf16[10,1536,1024]{2,1,0:T(8,128)(2,1)S(1)}, bf16[5120,1536]{1,0:T(8,128)(2,1)S(1)}, bf16[2,3200]{1,0:T(2,128)(2,1)S(1)}) custom-call(s32[2]{0:T(128)} %refs_0_.1, bf16[2,1536]{1,0:T(2,128)(2,1)} %refs_1_.5, bf16[2,1536]{1,0:T(2,128)(2,1)} %refs_2_.2), custom_call_target="tpu_custom_call" | custom-call | tf_op jit(solution)/shard_map/pack/pallas_call | solution.py:57
  1.4 4.1 %collective-permute-start = (bf16[2,3200]{1,0:T(2,128)(2,1)S(1)}, bf16[2,3200]{1,0:T(2,128)(2,1)S(1)}, u32[]{:S(2)}, u32[]{:S(2)}) collective-permute-start(bf16[2,3200]{1,0:T(2,128)(2,1)S(1)} %get-tuple-element.25.refs_0_), channel_id=1, source_target_pairs={{0,8},{4,12},{8,0},{12,4},{16,24},{20,28},{24,16},{28,20},{1,9},{5... | collective-permute-start | bytes 38408 | tf_op jit(solution)/shard_map/ppermute | solution.py:354
  5.5 2.9 %load_gate_text.1.refs_2_ = bf16[10,1536,1024]{2,1,0:T(8,128)(2,1)S(1)} custom-call(bf16[2,3200]{1,0:T(2,128)(2,1)S(1)} %get-tuple-element.25.refs_0_, bf16[1536,2048]{1,0:T(8,128)(2,1)} %refs_1_.6, bf16[10,1536,1024]{2,1,0:T(8,128)(2,1)S(1)} %get-tuple-element.26.refs_2_, ...), custom_call_target="tpu_custom_call", output_to_operand_aliasing={{}: (2, {})} | custom-call | bytes 6291456 | tf_op jit(solution)/shard_map/load_gate_text/pallas_call | solution.py:57
  8.4 1.6 %collective-permute-start.1 = (bf16[4,3200]{1,0:T(4,128)(2,1)S(1)}, bf16[4,3200]{1,0:T(4,128)(2,1)S(1)}, u32[]{:S(2)}, u32[]{:S(2)}) collective-permute-start(bf16[4,3200]{1,0:T(4,128)(2,1)S(1)} %join_4.1.refs_0_), channel_id=1, source_target_pairs={{0,4},{4,0},{8,12},{12,8},{16,20},{20,16},{24,28},{28,24},{1,5},{5... | collective-permute-start | bytes 76808 | tf_op jit(solution)/shard_map/ppermute | solution.py:354
  10.0 2.9 %load_up_text.1.refs_2_.refs_3_.refs_4_ = bf16[10,1536,1024]{2,1,0:T(8,128)(2,1)S(1)} custom-call(bf16[4,3200]{1,0:T(4,128)(2,1)S(1)} %join_4.1.refs_0_, bf16[1536,2048]{1,0:T(8,128)(2,1)} %refs_1_.7, bf16[10,1536,1024]{2,1,0:T(8,128)(2,1)S(1)} %load_gate_text.1.refs_2_, ...), custom_call_target="tpu_custom_call", output_to_operand_aliasing={{}: (2, {})} | custom-call | bytes 6291456 | tf_op jit(solution)/shard_map/load_up_text/pallas_call | solution.py:57
  12.9 1.6 %collective-permute-start.2 = (bf16[8,3200]{1,0:T(8,128)(2,1)S(1)}, bf16[8,3200]{1,0:T(8,128)(2,1)S(1)}, u32[]{:S(2)}, u32[]{:S(2)}) collective-permute-start(bf16[8,3200]{1,0:T(8,128)(2,1)S(1)} %join_8.1.refs_0_), channel_id=1, source_target_pairs={{0,16},{4,20},{8,24},{12,28},{16,0},{20,4},{24,8},{28,12},{1,17},{... | collective-permute-start | bytes 153608 | tf_op jit(solution)/shard_map/ppermute | solution.py:354
  14.5 2.9 %load_down_text.1.refs_3_.refs_5_ = bf16[5120,1536]{1,0:T(8,128)(2,1)S(1)} custom-call(bf16[8,3200]{1,0:T(8,128)(2,1)S(1)} %join_8.1.refs_0_, bf16[2048,1536]{1,0:T(8,128)(2,1)} %refs_1_.8, bf16[5120,1536]{1,0:T(8,128)(2,1)S(1)} %get-tuple-element.27.refs_3_.refs_2_, ...), custom_call_target="tpu_custom_call", output_to_operand_aliasing={{}: (2, {})} | custom-call | bytes 6291456 | tf_op jit(solution)/shard_map/load_down_text/pallas_call | solution.py:57
  17.5 10.3 %hidden_partials.1 = (f32[3,16,1536]{2,1,0:T(8,128)S(1)}, f32[3,16,1536]{2,1,0:T(8,128)S(1)}, bf16[10,1536,1024]{2,1,0:T(8,128)(2,1)S(1)}, bf16[5120,1536]{1,0:T(8,128)(2,1)S(1)}) custom-call(bf16[16,3200]{1,0:T(8,128)(2,1)S(1)} %join_16.1.refs_0_.refs_1_, bf16[1536,3072]{1,0:T(8,128)(2,1)} %refs_1_.9, ...), custom_call_target="tpu_custom_call", output_to_operand_aliasing={{2}: (4, {}), {3}: (5, {})} | custom-call | flops 754974720 | bytes 28311552 | tf_op jit(solution)/shard_map/hidden_partials/pallas_call | solution.py:57
  27.9 1.6 %collective-permute-done.3.refs_1_ = f32[3,16,1536]{2,1,0:T(8,128)S(1)} collective-permute-done((f32[3,16,1536]{2,1,0:T(8,128)S(1)}, f32[3,16,1536]{2,1,0:T(8,128)S(1)}, u32[]{:S(2)}, u32[]{:S(2)}) %collective-permute-start.3) | collective-permute-done | bytes 294944 | tf_op jit(solution)/shard_map/ppermute | solution.py:354
  29.5 1.6 %collective-permute-start.4 = (bf16[3,16,1536]{2,1,0:T(8,128)(2,1)S(1)}, bf16[3,16,1536]{2,1,0:T(8,128)(2,1)S(1)}, u32[]{:S(2)}, u32[]{:S(2)}) collective-permute-start(bf16[3,16,1536]{2,1,0:T(8,128)(2,1)S(1)} %get-tuple-element.33), channel_id=1, source_target_pairs={{0,2},{1,3},{2,0},{3,1},{4,6},{5,7},{6,4},{7,5},{8,10},{9,11},{10,... | collective-permute-start | bytes 442376 | tf_op jit(solution)/shard_map/ppermute | solution.py:354
  31.0 4.4 %collective-permute-done.4.refs_1_ = bf16[3,16,1536]{2,1,0:T(8,128)(2,1)S(1)} collective-permute-done((bf16[3,16,1536]{2,1,0:T(8,128)(2,1)S(1)}, bf16[3,16,1536]{2,1,0:T(8,128)(2,1)S(1)}, u32[]{:S(2)}, u32[]{:S(2)}) %collective-permute-start.4) | collective-permute-done | bytes 147488 | tf_op jit(solution)/shard_map/ppermute | solution.py:354
  35.5 0.1 collective-permute-start.5
  35.6 1.9 %down_grad_own.1.refs_5_.refs_4_ = bf16[3072,1536]{1,0:T(8,128)(2,1)} custom-call(bf16[16,3200]{1,0:T(8,128)(2,1)S(1)} %join_16.1.refs_0_.refs_1_, bf16[3,16,1536]{2,1,0:T(8,128)(2,1)S(1)} %hidden.1.refs_1_, bf16[10,1536,1024]{2,1,0:T(8,128)(2,1)S(1)} %get-tuple-element.30.refs_2_.refs_3_, bf16[5120,1536]{1,0:T(8,128)(2,1)S(1)} %get-tuple-element.31.refs_3_.refs_4_), custom_call_target="tpu_custom_call" | custom-call | flops 37748736 | bytes 2359296 | tf_op jit(solution)/shard_map/down_grad_own/pallas_call | solution.py:57
  37.5 10.4 %token_partials.1 = (f32[8,3072]{1,0:T(8,128)S(1)}, bf16[8,3072]{1,0:T(8,128)(2,1)S(1)}, bf16[16,3072]{1,0:T(8,128)(2,1)S(1)}, bf16[16,2048]{1,0:T(8,128)(2,1)S(1)}) custom-call(bf16[16,3200]{1,0:T(8,128)(2,1)S(1)} %join_16.1.refs_0_.refs_1_, bf16[3,16,1536]{2,1,0:T(8,128)(2,1)S(1)} %hidden.1.refs_1_, ...), custom_call_target="tpu_custom_call" | custom-call | flops 754974720 | tf_op jit(solution)/shard_map/token_partials/pallas_call | solution.py:57
  47.9 1.2 %collective-permute-start.6 = (bf16[8,3072]{1,0:T(8,128)(2,1)S(1)}, bf16[8,3072]{1,0:T(8,128)(2,1)S(1)}, u32[]{:S(2)}, u32[]{:S(2)}) collective-permute-start(bf16[8,3072]{1,0:T(8,128)(2,1)S(1)} %get-tuple-element.35), channel_id=1, source_target_pairs={{0,16},{4,20},{8,24},{12,28},{16,0},{20,4},{24,8},{28,12},{1,17},{... | collective-permute-start | bytes 147464 | tf_op jit(solution)/shard_map/ppermute | solution.py:354
  49.1 2.3 %down_grad_1.1.refs_2_.refs_4_ = bf16[3072,1536]{1,0:T(8,128)(2,1)} custom-call(f32[8,3072]{1,0:T(8,128)S(1)} %get-tuple-element.34.refs_0_, bf16[16,3200]{1,0:T(8,128)(2,1)S(1)} %join_16.1.refs_0_.refs_1_, bf16[16,3072]{1,0:T(8,128)(2,1)S(1)} %get-tuple-element.36.refs_2_, ...), custom_call_target="tpu_custom_call", output_to_operand_aliasing={{}: (4, {})} | custom-call | flops 62914560 | bytes 3932160 | tf_op jit(solution)/shard_map/down_grad_1/pallas_call | solution.py:57
  51.5 0.6 collective-permute-done.6.refs_1_
  52.1 1.0 %collective-permute-start.7 = (bf16[4,3072]{1,0:T(4,128)(2,1)S(1)}, bf16[4,3072]{1,0:T(4,128)(2,1)S(1)}, u32[]{:S(2)}, u32[]{:S(2)}) collective-permute-start(bf16[4,3072]{1,0:T(4,128)(2,1)S(1)} %get-tuple-element.39), channel_id=1, source_target_pairs={{0,4},{4,0},{8,12},{12,8},{16,20},{20,16},{24,28},{28,24},{1,5},{5... | collective-permute-start | bytes 73736 | tf_op jit(solution)/shard_map/ppermute | solution.py:354
  53.1 2.4 %down_grad_2.1 = (bf16[3072,1536]{1,0:T(8,128)(2,1)}, bf16[2048,1536]{1,0:T(8,128)(2,1)}) custom-call(f32[4,3072]{1,0:T(4,128)S(1)} %get-tuple-element.38.refs_0_, bf16[16,3200]{1,0:T(8,128)(2,1)S(1)} %join_16.1.refs_0_.refs_1_, bf16[16,3072]{1,0:T(8,128)(2,1)S(1)} %get-tuple-element.36.refs_2_, ...), custom_call_target="tpu_custom_call", output_to_operand_aliasing={{0}: (4, {})} | custom-call | flops 62914560 | bytes 3932160 | tf_op jit(solution)/shard_map/down_grad_2/pallas_call | solution.py:57
  55.5 0.5 collective-permute-done.7.refs_1_
  56.0 1.8 %collective-permute-start.8 = (f32[2,3072]{1,0:T(2,128)S(1)}, f32[2,3072]{1,0:T(2,128)S(1)}, u32[]{:S(2)}, u32[]{:S(2)}) collective-permute-start(f32[2,3072]{1,0:T(2,128)S(1)} %get-tuple-element.42), channel_id=1, source_target_pairs={{0,8},{4,12},{8,0},{12,4},{16,24},{20,28},{24,16},{28,20},{1,9},{5... | collective-permute-start | bytes 73736 | tf_op jit(solution)/shard_map/ppermute | solution.py:354
  57.8 2.9 %down_grad_3.1 = bf16[2048,1536]{1,0:T(8,128)(2,1)} custom-call(f32[2,3072]{1,0:T(2,128)S(1)} %get-tuple-element.41.refs_0_, bf16[16,3200]{1,0:T(8,128)(2,1)S(1)} %join_16.1.refs_0_.refs_1_, bf16[16,3072]{1,0:T(8,128)(2,1)S(1)} %get-tuple-element.36.refs_2_, bf16[16,2048]{1,0:T(8,128)(2,1)S(1)} %get-tuple-element.37.refs_3_, ...), custom_call_target="tpu_custom_call", output_to_operand_aliasing={{}: (4, {})} | custom-call | flops 88080384 | bytes 5505024 | tf_op jit(solution)/shard_map/down_grad_3/pallas_call | solution.py:57
  60.7 0.1 collective-permute-done.8.refs_1_
  60.8 0.6 %token_sum_1.1 = (bf16[2,1536]{1,0:T(2,128)(2,1)}, bf16[2,1536]{1,0:T(2,128)(2,1)}) custom-call(f32[2,3072]{1,0:T(2,128)S(1)} %get-tuple-element.41.refs_0_, f32[2,3072]{1,0:T(2,128)S(1)} %collective-permute-done.8.refs_1_), custom_call_target="tpu_custom_call" | custom-call | tf_op jit(solution)/shard_map/token_sum_1/pallas_call | solution.py:57
  (12 shorter events, 0.3 us)
Async XLA Ops:
  1.4 7.0 %collective-permute-start = (bf16[2,3200]{1,0:T(2,128)(2,1)S(1)}, bf16[2,3200]{1,0:T(2,128)(2,1)S(1)}, u32[]{:S(2)}, u32[]{:S(2)}) collective-permute-start(bf16[2,3200]{1,0:T(2,128)(2,1)S(1)} %get-tuple-element.25.refs_0_), channel_id=1, source_target_pairs={{0,8},{4,12},{8,0},{12,4},{16,24},{20,28},{24,16},{28,20},{1,9},{5... | collective-permute-start | bytes 38408 | tf_op jit(solution)/shard_map/ppermute | solution.py:354
  8.4 4.5 %collective-permute-start.1 = (bf16[4,3200]{1,0:T(4,128)(2,1)S(1)}, bf16[4,3200]{1,0:T(4,128)(2,1)S(1)}, u32[]{:S(2)}, u32[]{:S(2)}) collective-permute-start(bf16[4,3200]{1,0:T(4,128)(2,1)S(1)} %join_4.1.refs_0_), channel_id=1, source_target_pairs={{0,4},{4,0},{8,12},{12,8},{16,20},{20,16},{24,28},{28,24},{1,5},{5... | collective-permute-start | bytes 76808 | tf_op jit(solution)/shard_map/ppermute | solution.py:354
  12.9 4.5 %collective-permute-start.2 = (bf16[8,3200]{1,0:T(8,128)(2,1)S(1)}, bf16[8,3200]{1,0:T(8,128)(2,1)S(1)}, u32[]{:S(2)}, u32[]{:S(2)}) collective-permute-start(bf16[8,3200]{1,0:T(8,128)(2,1)S(1)} %join_8.1.refs_0_), channel_id=1, source_target_pairs={{0,16},{4,20},{8,24},{12,28},{16,0},{20,4},{24,8},{28,12},{1,17},{... | collective-permute-start | bytes 153608 | tf_op jit(solution)/shard_map/ppermute | solution.py:354
  27.8 1.6 %collective-permute-start.3 = (f32[3,16,1536]{2,1,0:T(8,128)S(1)}, f32[3,16,1536]{2,1,0:T(8,128)S(1)}, u32[]{:S(2)}, u32[]{:S(2)}) collective-permute-start(f32[3,16,1536]{2,1,0:T(8,128)S(1)} %get-tuple-element.29), channel_id=1, source_target_pairs={{0,1},{1,0},{2,3},{3,2},{4,5},{5,4},{6,7},{7,6},{8,9},{9,8},{10,11... | collective-permute-start | bytes 884744 | tf_op jit(solution)/shard_map/ppermute | solution.py:354
  29.5 6.0 %collective-permute-start.4 = (bf16[3,16,1536]{2,1,0:T(8,128)(2,1)S(1)}, bf16[3,16,1536]{2,1,0:T(8,128)(2,1)S(1)}, u32[]{:S(2)}, u32[]{:S(2)}) collective-permute-start(bf16[3,16,1536]{2,1,0:T(8,128)(2,1)S(1)} %get-tuple-element.33), channel_id=1, source_target_pairs={{0,2},{1,3},{2,0},{3,1},{4,6},{5,7},{6,4},{7,5},{8,10},{9,11},{10,... | collective-permute-start | bytes 442376 | tf_op jit(solution)/shard_map/ppermute | solution.py:354
  35.5 2.0 %collective-permute-start.5 = (bf16[3,16,1536]{2,1,0:T(8,128)(2,1)S(1)}, bf16[3,16,1536]{2,1,0:T(8,128)(2,1)S(1)}, u32[]{:S(2)}, u32[]{:S(2)}) collective-permute-start(bf16[3,16,1536]{2,1,0:T(8,128)(2,1)S(1)} %hidden.1.refs_1_), channel_id=1, source_target_pairs={{0,1},{1,0},{2,3},{3,2},{4,5},{5,4},{6,7},{7,6},{8,9},{9,8},{10,11... | collective-permute-start | bytes 442376 | tf_op jit(solution)/shard_map/ppermute | solution.py:354
  47.9 4.2 %collective-permute-start.6 = (bf16[8,3072]{1,0:T(8,128)(2,1)S(1)}, bf16[8,3072]{1,0:T(8,128)(2,1)S(1)}, u32[]{:S(2)}, u32[]{:S(2)}) collective-permute-start(bf16[8,3072]{1,0:T(8,128)(2,1)S(1)} %get-tuple-element.35), channel_id=1, source_target_pairs={{0,16},{4,20},{8,24},{12,28},{16,0},{20,4},{24,8},{28,12},{1,17},{... | collective-permute-start | bytes 147464 | tf_op jit(solution)/shard_map/ppermute | solution.py:354
  52.1 3.9 %collective-permute-start.7 = (bf16[4,3072]{1,0:T(4,128)(2,1)S(1)}, bf16[4,3072]{1,0:T(4,128)(2,1)S(1)}, u32[]{:S(2)}, u32[]{:S(2)}) collective-permute-start(bf16[4,3072]{1,0:T(4,128)(2,1)S(1)} %get-tuple-element.39), channel_id=1, source_target_pairs={{0,4},{4,0},{8,12},{12,8},{16,20},{20,16},{24,28},{28,24},{1,5},{5... | collective-permute-start | bytes 73736 | tf_op jit(solution)/shard_map/ppermute | solution.py:354
  56.0 4.8 %collective-permute-start.8 = (f32[2,3072]{1,0:T(2,128)S(1)}, f32[2,3072]{1,0:T(2,128)S(1)}, u32[]{:S(2)}, u32[]{:S(2)}) collective-permute-start(f32[2,3072]{1,0:T(2,128)S(1)} %get-tuple-element.42), channel_id=1, source_target_pairs={{0,8},{4,12},{8,0},{12,4},{16,24},{20,28},{24,16},{28,20},{1,9},{5... | collective-permute-start | bytes 73736 | tf_op jit(solution)/shard_map/ppermute | solution.py:354

commit v5 on v4

--- a/solution.py
+++ b/solution.py
@@ -13,11 +13,9 @@
 BF16 = jnp.bfloat16
 MIB = 1 << 20
 BLOCK = 512
-WIDE = 1024
 ROWS = 256
-OWN_STEPS = 3
-FIRST_STEPS = 8
-TEXT_STEPS = 1
+TURN_FIRST = 2
+TURN_SECOND = 6
 PLACES = {"h": pl.ANY, "v": pltpu.VMEM, "s": pltpu.SMEM}
 
 
@@ -108,12 +106,14 @@
     return call(join_body, name, [((2 * a.shape[0], a.shape[1]), BF16)], (a, b), "vv", also=also)[0]
 
 
-def column_blocks(src, wide, first, cuts):
-    rows = src.shape[0] // cuts
-    parts = [pl.ds(j * rows, rows) for j in range(cuts)]
+def column_blocks(src, wide, first):
+    rows = src.shape[0] // BLOCK
     return [
-        [(src.at[part, pl.ds(i * WIDE, WIDE)], wide.at[first + i, part]) for part in parts]
-        for i in range(src.shape[1] // WIDE)
+        [
+            (src.at[pl.ds(r * BLOCK, BLOCK), pl.ds(i * BLOCK, BLOCK)], wide.at[first + i, r])
+            for r in range(rows)
+        ]
+        for i in range(src.shape[1] // BLOCK)
     ]
 
 
@@ -140,8 +140,8 @@
 
 
 def load_body(first, after_ref, src_hbm, old_ref, place_ref, sems):
-    if place_ref.ndim == 3:
-        groups = column_blocks(src_hbm, place_ref, first, 4)
+    if place_ref.ndim == 4:
+        groups = column_blocks(src_hbm, place_ref, first)
     else:
         groups = row_blocks(src_hbm, place_ref, first)
     for group in started(groups, sems):
@@ -155,11 +155,20 @@
         [like(place)],
         (after, src, place),
         "vhv",
-        [pltpu.SemaphoreType.DMA((8,))],
+        [pltpu.SemaphoreType.DMA((src.size // BLOCK**2,))],
         traffic=size_of(src),
         aliases={2: 0},
         also=also,
     )[0]
+
+
+def beside(i, fs, ft):
+    side, rest = divmod(i * BLOCK, ft // 2)
+    return side * (fs // 2) + rest
+
+
+def columns(wide_ref, i):
+    return wide_ref[i].reshape(-1, BLOCK)
 
 
 def partials_body(
@@ -167,33 +176,32 @@
 ):
     fs, width = ds_hbm.shape
     ft = tall_ref.shape[0] - fs
-    ns, nt = fs // WIDE, ft // WIDE
-    groups = column_blocks(gs_hbm, wide_ref, 2 * nt, 2) + column_blocks(us_hbm, wide_ref, 2 * nt + ns, 2)
+    ns, nt = fs // BLOCK, ft // BLOCK
+    groups = column_blocks(gs_hbm, wide_ref, 2 * nt) + column_blocks(us_hbm, wide_ref, 2 * nt + ns)
     copies = started(groups + row_blocks(ds_hbm, tall_ref, 0), sems)
     x = arr_ref[:, :width]
     c = arr_ref[:, width : 2 * width]
     speech = is_speech(arr_ref)
 
+    def put(k, start, value, pick):
+        cut = slice(start, start + BLOCK)
+        if pick and start % (fs // 2) < ft // 2:
+            value = jnp.where(speech, value, part[k, :, cut])
+        part[k, :, cut] = value
+
     for k in range(2):
         for i in range(nt):
-            part[k, :, i * WIDE : (i + 1) * WIDE] = times(x, wide_ref[k * nt + i])
-    for i in range(0, ft, BLOCK):
-        part[2, :, i : i + BLOCK] = contract_last(c, tall_ref[fs + i : fs + i + BLOCK, :])
+            put(k, beside(i, fs, ft), times(x, columns(wide_ref, k * nt + i)), False)
+    for i in range(nt):
+        rows = slice(fs + i * BLOCK, fs + (i + 1) * BLOCK)
+        put(2, beside(i, fs, ft), contract_last(c, tall_ref[rows, :]), False)
     for k in range(2):
         for i in range(ns):
             wait(copies[k * ns + i])
-            value = times(x, wide_ref[2 * nt + k * ns + i])
-            cut = slice(i * WIDE, (i + 1) * WIDE)
-            if i < nt:
-                value = jnp.where(speech, value, part[k, :, cut])
-            part[k, :, cut] = value
-    for i in range(fs // BLOCK):
+            put(k, i * BLOCK, times(x, columns(wide_ref, 2 * nt + k * ns + i)), True)
+    for i in range(ns):
         wait(copies[2 * ns + i])
-        cut = slice(i * BLOCK, (i + 1) * BLOCK)
-        value = contract_last(c, tall_ref[cut, :])
-        if i * BLOCK < ft:
-            value = jnp.where(speech, value, part[2, :, cut])
-        part[2, :, cut] = value
+        put(2, i * BLOCK, contract_last(c, tall_ref[i * BLOCK : (i + 1) * BLOCK, :]), True)
     half = fs // 2
     odd = parity()
     for k in range(3):
@@ -204,7 +212,7 @@
 def partials(arr, gate_s, up_s, down_s, wide, tall):
     rows, fs = arr.shape[0], gate_s.shape[1]
     half = ((3, rows, fs // 2), F32)
-    n_sems = 4 * fs // WIDE + fs // BLOCK
+    n_sems = 2 * gate_s.size // BLOCK**2 + fs // BLOCK
     return call(
         partials_body,
         "hidden_partials",
@@ -234,46 +242,94 @@
     out_ref[2] = (dh * silu).astype(BF16)
 
 
+def turn_body(first, count, by_product, old_ref, wide_ref):
+    row, col = (lax.broadcasted_iota(jnp.int32, (ROWS, ROWS), i) for i in range(2))
+    one = (row == col).astype(BF16)
+    for i in range(first, first + count):
+        for r in range(wide_ref.shape[1]):
+            square = wide_ref[i, r]
+            if by_product:
+                parts = [contract_last(one, square[:, j : j + ROWS]) for j in range(0, BLOCK, ROWS)]
+                turned = jnp.concatenate([p.astype(BF16) for p in parts], axis=0)
+            else:
+                turned = square.T
+            wide_ref[i, r] = turned
+
+
+def turn(wide, tall, first, count, by_product, name):
+    return call(
+        functools.partial(turn_body, first, count, by_product),
+        name,
+        [like(wide)],
+        (wide,),
+        "v",
+        traffic=4 * count * wide.shape[1] * BLOCK**2,
+        aliases={0: 0},
+        also=(tall,),
+    )[0]
+
+
+def mixed_half(h, speech, side, tall_ref, fs):
+    half_s, half_t, width = fs // 2, (tall_ref.shape[0] - fs) // 2, tall_ref.shape[1]
+    zero = jnp.zeros_like(h)
+    hs, ht = jnp.where(speech, h, zero), jnp.where(speech, zero, h)[:, :half_t]
+    rows_s = pl.ds(pl.multiple_of(side * half_s, BLOCK), half_s)
+    rows_t = pl.ds(pl.multiple_of(fs + side * half_t, BLOCK), half_t)
+    cuts = [slice(i, i + BLOCK) for i in range(0, width, BLOCK)]
+    return [times(hs, tall_ref[rows_s, cut]) + times(ht, tall_ref[rows_t, cut]) for cut in cuts]
+
+
+def mixed_own_body(arr_ref, done_ref, tall_ref, out_ref):
+    fs = 2 * done_ref.shape[2]
+    parts = mixed_half(done_ref[0], is_speech(arr_ref), parity(), tall_ref, fs)
+    for i, value in enumerate(parts):
+        out_ref[:, i * BLOCK : (i + 1) * BLOCK] = value
+
+
 def back_body(
-    arr_ref, done_ref, other_ref, wide_ref, tall_ref, after_ref,
+    turned, arr_ref, done_ref, other_ref, own_ref, wide_ref, tall_ref,
     keep_ref, send_ref, hs_ref, ht_ref, dgs, dgt, dus, dut, out,
 ):
     speech = is_speech(arr_ref)
     fs, ft = hs_ref.shape[1], ht_ref.shape[1]
-    ns, nt = fs // WIDE, ft // WIDE
+    ns, nt = fs // BLOCK, ft // BLOCK
     odd = parity() == 1
     for k, (s, t) in enumerate(((hs_ref, ht_ref), (dgs, dgt), (dus, dut))):
         done, other = done_ref[k], other_ref[k]
         value = jnp.concatenate([jnp.where(odd, other, done), jnp.where(odd, done, other)], axis=1)
         zero = jnp.zeros_like(value)
         s[...] = jnp.where(speech, value, zero)
-        t[...] = jnp.where(speech, zero, value)[:, :ft]
+        value = jnp.where(speech, zero, value)
+        for i in range(nt):
+            start = beside(i, fs, ft)
+            t[:, i * BLOCK : (i + 1) * BLOCK] = value[:, start : start + BLOCK]
     width = tall_ref.shape[1]
-    for i in range(0, width, BLOCK):
-        cut = slice(i, i + BLOCK)
-        out[:, cut] = times(hs_ref[...], tall_ref[:fs, cut]) + times(ht_ref[...], tall_ref[fs:, cut])
+    for i, value in enumerate(mixed_half(other_ref[0], speech, 1 - parity(), tall_ref, fs)):
+        cut = slice(i * BLOCK, (i + 1) * BLOCK)
+        out[:, cut] = own_ref[:, cut] + value
     blocks = [(dgt, nt), (dut, nt), (dgs, ns), (dus, ns)]
     blocks = [(ref, i) for ref, n in blocks for i in range(n)]
-    size = BLOCK // 2
-    for i in range(0, width, size):
-        total = jnp.zeros((out.shape[0], size), F32)
+    for r in range(width // BLOCK):
+        total = jnp.zeros((out.shape[0], BLOCK), F32)
         for b, (ref, j) in enumerate(blocks):
-            total += contract_last(ref[:, j * WIDE : (j + 1) * WIDE], wide_ref[b, i : i + size, :])
-        out[:, width + i : width + i + size] = total
+            product = times if b in turned else contract_last
+            total += product(ref[:, j * BLOCK : (j + 1) * BLOCK], wide_ref[b, r])
+        start = width + r * BLOCK
+        out[:, start : start + BLOCK] = total
     half = keep_ref.shape[0]
     keep_ref[...] = out[:half]
     send_ref[...] = out[half:].astype(BF16)
 
 
-def back(arr, done, other, wide, tall, after, fs, ft):
+def back(arr, done, other, own, wide, tall, turned, fs, ft):
     rows, width = arr.shape[0], tall.shape[1]
     hidden = [((rows, fs), BF16), ((rows, ft), BF16)]
     return call(
-        back_body,
+        functools.partial(back_body, turned),
         "token_partials",
         [((rows // 2, 2 * width), F32), ((rows // 2, 2 * width), BF16)] + hidden,
-        (arr, done, other, wide, tall, after),
-        "vvvvvh",
+        (arr, done, other, own, wide, tall),
+        "vvvvvv",
         [pltpu.VMEM(*s) for s in hidden + hidden] + [pltpu.VMEM((rows, 2 * width), F32)],
         2 * rows * (wide.size + tall.size),
     )
@@ -317,37 +373,16 @@
         copy.wait()
 
 
-def rows_at(ref, start):
-    return ref.at[pl.ds(pl.multiple_of(start, ROWS), ROWS)]
-
-
-def outer_own_body(count, arr_ref, done_ref, out_ref, slots, sems):
-    half, width = done_ref.shape[2], out_ref.shape[1]
-    c = arr_ref[:, width : 2 * width]
-    h = done_ref[0]
-    h = jnp.where(is_speech(arr_ref), h, jnp.zeros_like(h))
-    base = parity() * half
-    steps = [(h[:, i * ROWS : (i + 1) * ROWS], rows_at(out_ref, base + i * ROWS)) for i in range(count)]
-    outer_steps(c, steps, slots, sems)
-
-
 def outer_body(speech, text, after_ref, arr_ref, hs_ref, ht_ref, *refs):
     slots, sems = refs[-2:]
-    outs = list(refs[1:-2])
-    out_s = outs.pop(0) if len(speech) else None
-    out_t = outs.pop(0) if len(text) else None
-    width = (out_s if len(speech) else out_t).shape[1]
-    c = arr_ref[:, width : 2 * width]
-    half = hs_ref.shape[1] // 2
-    odd = parity()
+    outs = list(refs[-2 - bool(speech) - bool(text) : -2])
+    width = outs[0].shape[1]
     steps = []
-    for i in speech:
-        side = odd if i * ROWS < half else 1 - odd
-        start = side * half + i * ROWS % half
-        steps.append((hs_ref[:, pl.ds(pl.multiple_of(start, ROWS), ROWS)], rows_at(out_s, start)))
-    for i in text:
-        steps.append((ht_ref[:, i * ROWS : (i + 1) * ROWS], rows_at(out_t, i * ROWS)))
-    outer_steps(c, steps, slots, sems)
+    for h_ref, blocks in ((hs_ref, speech), (ht_ref, text)):
+        out = outs.pop(0) if blocks else None
+        cuts = [slice(i * ROWS, (i + 1) * ROWS) for i in blocks]
+        steps += [(h_ref[:, cut], out.at[cut]) for cut in cuts]
+    outer_steps(arr_ref[:, width : 2 * width], steps, slots, sems)
 
 
 def flip(value, axes, bit, n):
@@ -357,7 +392,7 @@
 def by_kernels(n_seq, n_tok, tokens, modality, cotangent, gate_s, up_s, down_s, gate_t, up_t, down_t):
     rows, width = tokens.shape
     fs, ft = gate_s.shape[1], gate_t.shape[1]
-    wide = ((2 * (fs + ft) // WIDE, width, WIDE), BF16)
+    wide = ((2 * (fs + ft) // BLOCK, width // BLOCK, BLOCK, BLOCK), BF16)
     tall = ((fs + ft, width), BF16)
     pair = [pltpu.VMEM((rows, width), BF16)] * 2
 
@@ -368,7 +403,7 @@
     wide = load(arr, gate_t, wide, (tall,), 0, "load_gate_text")
     arr = join(arr, got, "join_4", (wide, tall))
     got = flip(arr, TOK, HOPS[1], n_tok)
-    wide = load(arr, up_t, wide, (tall,), ft // WIDE, "load_up_text")
+    wide = load(arr, up_t, wide, (tall,), ft // BLOCK, "load_up_text")
     arr = join(arr, got, "join_8", (wide, tall))
     got = flip(arr, TOK, HOPS[2], n_tok)
     tall = load(arr, down_t, tall, (wide,), fs, "load_down_text")
@@ -376,50 +411,41 @@
 
     mine, theirs, wide, tall = partials(arr, gate_s, up_s, down_s, wide, tall)
     got = flip(theirs, "seq", 1, n_seq)
+    wide = turn(wide, tall, 0, TURN_FIRST, False, "turn_1")
     total, send = call(
         core_sum_body, "core_sum", [like(mine), (mine.shape, BF16)], (mine, got), "vv", also=(wide, tall)
     )
     got = flip(send, "seq", 2, n_seq)
+    wide = turn(wide, tall, TURN_FIRST, TURN_SECOND, True, "turn_2")
     done = call(hidden_body, "hidden", [(mine.shape, BF16)], (total, got), "vv", also=(wide, tall))[0]
     other = flip(done, "seq", 1, n_seq)
-
-    def slots(count):
-        return [pltpu.VMEM((count, ROWS, width), BF16), pltpu.SemaphoreType.DMA((count,))]
-
-    def cost(count):
-        return 2 * arr.shape[0] * count * ROWS * width, 2 * count * ROWS * width
-
-    own = OWN_STEPS
-    down_s_grad = call(
-        functools.partial(outer_own_body, own), "down_grad_own", [like(down_s)], (arr, done), "vv", slots(own),
-        *cost(own), out_places="h", also=(wide, tall),
+    own = call(
+        mixed_own_body, "mixed_own", [((arr.shape[0], width), F32)], (arr, done, tall), "vvv",
+        flops=arr.shape[0] * tall.size, also=(wide,),
     )[0]
-    keep, send, hs, ht = back(arr, done, other, wide, tall, down_s_grad, fs, ft)
-
+    keep, send, hs, ht = back(arr, done, other, own, wide, tall, range(TURN_FIRST + TURN_SECOND), fs, ft)
+
+    def outer(after, speech, text, old, name):
+        count = len(speech) + len(text)
+        outs = [like(w) for w, blocks in ((down_s, speech), (down_t, text)) if blocks]
+        return call(
+            functools.partial(outer_body, speech, text), name, outs, (after, arr, hs, ht, *old),
+            "vvvv" + "h" * len(old), [pltpu.VMEM((count, ROWS, width), BF16), pltpu.SemaphoreType.DMA((count,))],
+            2 * arr.shape[0] * count * ROWS * width, 2 * count * ROWS * width, limit=8,
+            out_places="h" * len(outs), aliases={4: 0} if old else None,
+        )
+
+    ns, nt = fs // ROWS, ft // ROWS
     got = flip(send, TOK, HOPS[2], n_tok)
-    first, second = range(own, FIRST_STEPS), range(FIRST_STEPS, fs // ROWS)
-    down_s_grad = call(
-        functools.partial(outer_body, first, ()), "down_grad_1", [like(down_s)], (keep, arr, hs, ht, down_s_grad),
-        "vvvvh", slots(len(first)), *cost(len(first)), limit=8, out_places="h", aliases={4: 0},
-    )[0]
+    down_s_grad = outer(keep, range(ns // 2), (), (), "down_grad_1")[0]
     keep, send = token_sum(keep, got, down_s_grad, BF16, "token_sum_4")
 
     got = flip(send, TOK, HOPS[1], n_tok)
-    text = range(0, TEXT_STEPS)
-    count = len(second) + len(text)
-    down_s_grad, down_t_grad = call(
-        functools.partial(outer_body, second, text), "down_grad_2", [like(down_s), like(down_t)],
-        (keep, arr, hs, ht, down_s_grad), "vvvvh", slots(count), *cost(count), limit=8, out_places="hh",
-        aliases={4: 0},
-    )
+    down_s_grad, down_t_grad = outer(keep, range(ns // 2, ns), range(1), (down_s_grad,), "down_grad_2")
     keep, send = token_sum(keep, got, down_t_grad, F32, "token_sum_2")
 
     got = flip(send, TOK, HOPS[0], n_tok)
-    text = range(TEXT_STEPS, ft // ROWS)
-    down_t_grad = call(
-        functools.partial(outer_body, (), text), "down_grad_3", [like(down_t)], (keep, arr, hs, ht, down_t_grad),
-        "vvvvh", slots(len(text)), *cost(len(text)), limit=8, out_places="h", aliases={4: 0},
-    )[0]
+    down_t_grad = outer(keep, (), range(1, nt), (down_t_grad,), "down_grad_3")[0]
     outs = [((rows, width), BF16)] * 2
     mixed, token_grad = call(last_sum_body, "token_sum_1", outs, (keep, got), "vv", pair + [pltpu.SemaphoreType.DMA((2,))], out_places="hh")
     return mixed, token_grad, down_s_grad, down_t_grad
@@ -468,9 +494,9 @@
     n_seq, n_tok = mesh.shape["seq"], mesh.shape["attn"] * mesh.shape["exp"]
 
     def run(*args):
-        hidden = args[3].shape[1], args[6].shape[1]
-        fits = n_tok == 8 and hidden[0] % WIDE == 0 and hidden[1] % WIDE == 0
-        fits = fits and hidden[0] >= hidden[1] and args[0].shape == (2, 3 * BLOCK)
+        fs, ft, width = args[3].shape[1], args[6].shape[1], args[0].shape[1]
+        fits = n_tok == 8 and args[0].shape[0] == 2 and fs >= ft and ft % (4 * BLOCK) == 0
+        fits = fits and fs % (2 * BLOCK) == 0 and width % BLOCK == 0
         return (by_kernels if fits else by_arrays)(n_seq, n_tok, *args)
 
     return jax.shard_map(

time: 61.8 us -> 59.2 us (0.958)
  waiting for transfers between devices: 7.19 us -> 3.16 us
  Pallas kernels: 40.4 us -> 42 us
    ppermute x9, waiting for transfers between devices: 7.19 us -> 3.16 us  [flip(): return lax.ppermute(value, axes, [(i, i ^ bit) for i in range(n)])]
    pallas_call x18 -> x20, Pallas kernels: 40.4 us -> 42 us  [call(): pl.pallas_call(seen, out_shape=shapes, in_specs=[pl.BlockSpec(memory_spac...]
  transfers between devices with their start and end apart: 9 -> 9, of which waited for: 5 -> 5; matrix products, arithmetic and copies ran while one was open for 0% -> 0% of each run, Pallas kernels for 29% -> 37%
where the time goes in v5:
time: 59.2 us; the launch traced here: 59 us
  Pallas kernels  42 us (71%)
  starting transfers between devices  12.9 us (22%)
  waiting for transfers between devices  3.16 us (5%)
  between operations  0.95 us (2%)
    pallas_call x20, Pallas kernels, call(): pl.pallas_call(seen, out_shape=shapes, in_specs=[pl.BlockSpec(memory_spac...  42 us
    ppermute x9, starting transfers between devices, flip(): return lax.ppermute(value, axes, [(i, i ^ bit) for i in range(n)])  12.9 us
    ppermute x9, waiting for transfers between devices, flip(): return lax.ppermute(value, axes, [(i, i ^ bit) for i in range(n)])  3.16 us
  transfers between devices with their start and end apart: 9, of which 5 were waited for; matrix products, arithmetic and copies ran while one was open for 0% of the time, Pallas kernels for 37%

profile of v5, /device:TPU:0, one launch (start us, length us, event | category | flops | bytes accessed | tf_op | source)
XLA Modules:
  0.0 59.0 jit_solution(4377446826494008594)
XLA Ops:
  0.6 0.7 %pack.1 = (bf16[20,3,512,512]{3,2,1,0:T(8,128)(2,1)S(1)}, bf16[5120,1536]{1,0:T(8,128)(2,1)S(1)}, bf16[2,3200]{1,0:T(2,128)(2,1)S(1)}) custom-call(s32[2]{0:T(128)} %refs_0_.1, bf16[2,1536]{1,0:T(2,128)(2,1)} %refs_1_.5, bf16[2,1536]{1,0:T(2,128)(2,1)} %refs_2_.2), custom_call_target="tpu_custom_call" | custom-call | tf_op jit(solution)/shard_map/pack/pallas_call | solution.py:55
  1.4 4.1 %collective-permute-start = (bf16[2,3200]{1,0:T(2,128)(2,1)S(1)}, bf16[2,3200]{1,0:T(2,128)(2,1)S(1)}, u32[]{:S(2)}, u32[]{:S(2)}) collective-permute-start(bf16[2,3200]{1,0:T(2,128)(2,1)S(1)} %get-tuple-element.25.refs_0_), channel_id=1, source_target_pairs={{0,8},{4,12},{8,0},{12,4},{16,24},{20,28},{24,16},{28,20},{1,9},{5... | collective-permute-start | bytes 38408 | tf_op jit(solution)/shard_map/ppermute | solution.py:389
  5.5 2.9 %load_gate_text.1.refs_2_ = bf16[20,3,512,512]{3,2,1,0:T(8,128)(2,1)S(1)} custom-call(bf16[2,3200]{1,0:T(2,128)(2,1)S(1)} %get-tuple-element.25.refs_0_, bf16[1536,2048]{1,0:T(8,128)(2,1)} %refs_1_.6, bf16[20,3,512,512]{3,2,1,0:T(8,128)(2,1)S(1)} %get-tuple-element.26.refs_2_, ...), custom_call_target="tpu_custom_call", output_to_operand_aliasing={{}: (2, {})} | custom-call | bytes 6291456 | tf_op jit(solution)/shard_map/load_gate_text/pallas_call | solution.py:55
  8.5 1.6 %collective-permute-start.1 = (bf16[4,3200]{1,0:T(4,128)(2,1)S(1)}, bf16[4,3200]{1,0:T(4,128)(2,1)S(1)}, u32[]{:S(2)}, u32[]{:S(2)}) collective-permute-start(bf16[4,3200]{1,0:T(4,128)(2,1)S(1)} %join_4.1.refs_0_), channel_id=1, source_target_pairs={{0,4},{4,0},{8,12},{12,8},{16,20},{20,16},{24,28},{28,24},{1,5},{5... | collective-permute-start | bytes 76808 | tf_op jit(solution)/shard_map/ppermute | solution.py:389
  10.1 2.9 %load_up_text.1.refs_2_.refs_3_.refs_4_ = bf16[20,3,512,512]{3,2,1,0:T(8,128)(2,1)S(1)} custom-call(bf16[4,3200]{1,0:T(4,128)(2,1)S(1)} %join_4.1.refs_0_, bf16[1536,2048]{1,0:T(8,128)(2,1)} %refs_1_.7, bf16[20,3,512,512]{3,2,1,0:T(8,128)(2,1)S(1)} %load_gate_text.1.refs_2_, ...), custom_call_target="tpu_custom_call", output_to_operand_aliasing={{}: (2, {})} | custom-call | bytes 6291456 | tf_op jit(solution)/shard_map/load_up_text/pallas_call | solution.py:55
  13.1 1.6 %collective-permute-start.2 = (bf16[8,3200]{1,0:T(8,128)(2,1)S(1)}, bf16[8,3200]{1,0:T(8,128)(2,1)S(1)}, u32[]{:S(2)}, u32[]{:S(2)}) collective-permute-start(bf16[8,3200]{1,0:T(8,128)(2,1)S(1)} %join_8.1.refs_0_), channel_id=1, source_target_pairs={{0,16},{4,20},{8,24},{12,28},{16,0},{20,4},{24,8},{28,12},{1,17},{... | collective-permute-start | bytes 153608 | tf_op jit(solution)/shard_map/ppermute | solution.py:389
  14.6 2.9 %load_down_text.1.refs_3_.refs_5_ = bf16[5120,1536]{1,0:T(8,128)(2,1)S(1)} custom-call(bf16[8,3200]{1,0:T(8,128)(2,1)S(1)} %join_8.1.refs_0_, bf16[2048,1536]{1,0:T(8,128)(2,1)} %refs_1_.8, bf16[5120,1536]{1,0:T(8,128)(2,1)S(1)} %get-tuple-element.27.refs_3_.refs_2_, ...), custom_call_target="tpu_custom_call", output_to_operand_aliasing={{}: (2, {})} | custom-call | bytes 6291456 | tf_op jit(solution)/shard_map/load_down_text/pallas_call | solution.py:55
  17.6 10.8 %hidden_partials.1 = (f32[3,16,1536]{2,1,0:T(8,128)S(1)}, f32[3,16,1536]{2,1,0:T(8,128)S(1)}, bf16[20,3,512,512]{3,2,1,0:T(8,128)(2,1)S(1)}, bf16[5120,1536]{1,0:T(8,128)(2,1)S(1)}) custom-call(bf16[16,3200]{1,0:T(8,128)(2,1)S(1)} %join_16.1.refs_0_.refs_1_, bf16[1536,3072]{1,0:T(8,128)(2,1)} %refs_1_.9, ...), custom_call_target="tpu_custom_call", output_to_operand_aliasing={{2}: (4, {}), {3}: (5, {})} | custom-call | flops 754974720 | bytes 28311552 | tf_op jit(solution)/shard_map/hidden_partials/pallas_call | solution.py:55
  28.5 0.9 %turn_1.1.refs_2_.refs_0_ = bf16[20,3,512,512]{3,2,1,0:T(8,128)(2,1)S(1)} custom-call(bf16[20,3,512,512]{3,2,1,0:T(8,128)(2,1)S(1)} %get-tuple-element.30.refs_0_, bf16[5120,1536]{1,0:T(8,128)(2,1)S(1)} %get-tuple-element.31.refs_1_.refs_3_.refs_2_.refs_5_), custom_call_target="tpu_custom_call", output_to_operand_aliasing={{}: (0, {})} | custom-call | bytes 6291456 | tf_op jit(solution)/shard_map/turn_1/pallas_call | solution.py:55
  29.4 0.7 %collective-permute-done.3.refs_1_ = f32[3,16,1536]{2,1,0:T(8,128)S(1)} collective-permute-done((f32[3,16,1536]{2,1,0:T(8,128)S(1)}, f32[3,16,1536]{2,1,0:T(8,128)S(1)}, u32[]{:S(2)}, u32[]{:S(2)}) %collective-permute-start.3) | collective-permute-done | bytes 294944 | tf_op jit(solution)/shard_map/ppermute | solution.py:389
  30.1 1.6 %collective-permute-start.4 = (bf16[3,16,1536]{2,1,0:T(8,128)(2,1)S(1)}, bf16[3,16,1536]{2,1,0:T(8,128)(2,1)S(1)}, u32[]{:S(2)}, u32[]{:S(2)}) collective-permute-start(bf16[3,16,1536]{2,1,0:T(8,128)(2,1)S(1)} %get-tuple-element.33), channel_id=1, source_target_pairs={{0,2},{1,3},{2,0},{3,1},{4,6},{5,7},{6,4},{7,5},{8,10},{9,11},{10,... | collective-permute-start | bytes 442376 | tf_op jit(solution)/shard_map/ppermute | solution.py:389
  31.7 2.7 %turn_2.1.refs_2_.refs_3_.refs_4_ = bf16[20,3,512,512]{3,2,1,0:T(8,128)(2,1)S(1)} custom-call(bf16[20,3,512,512]{3,2,1,0:T(8,128)(2,1)S(1)} %turn_1.1.refs_2_.refs_0_, bf16[5120,1536]{1,0:T(8,128)(2,1)S(1)} %get-tuple-element.31.refs_1_.refs_3_.refs_2_.refs_5_), custom_call_target="tpu_custom_call", output_to_operand_aliasing={{}: (0, {})} | custom-call | bytes 18874368 | tf_op jit(solution)/shard_map/turn_2/pallas_call | solution.py:55
  34.3 1.7 %collective-permute-done.4.refs_1_ = bf16[3,16,1536]{2,1,0:T(8,128)(2,1)S(1)} collective-permute-done((bf16[3,16,1536]{2,1,0:T(8,128)(2,1)S(1)}, bf16[3,16,1536]{2,1,0:T(8,128)(2,1)S(1)}, u32[]{:S(2)}, u32[]{:S(2)}) %collective-permute-start.4) | collective-permute-done | bytes 147488 | tf_op jit(solution)/shard_map/ppermute | solution.py:389
  36.2 1.2 %mixed_own.1.refs_3_ = f32[16,1536]{1,0:T(8,128)S(1)} custom-call(bf16[16,3200]{1,0:T(8,128)(2,1)S(1)} %join_16.1.refs_0_.refs_1_, bf16[3,16,1536]{2,1,0:T(8,128)(2,1)S(1)} %hidden.1.refs_1_, bf16[5120,1536]{1,0:T(8,128)(2,1)S(1)} %get-tuple-element.31.refs_1_.refs_3_.refs_2_.refs_5_, bf16[20,3,512,512]{3,2,1,0:T(8,128)(2,1)S(1)} %turn_2.1.refs_2_.refs_3_.refs_4_), custom_call_target="tpu_custom_call" | custom-call | flops 125829120 | tf_op jit(solution)/shard_map/mixed_own/pallas_call | solution.py:55
  37.4 0.2 collective-permute-done.5.refs_2_
  37.6 7.8 %token_partials.1 = (f32[8,3072]{1,0:T(8,128)S(1)}, bf16[8,3072]{1,0:T(8,128)(2,1)S(1)}, bf16[16,3072]{1,0:T(8,128)(2,1)S(1)}, bf16[16,2048]{1,0:T(8,128)(2,1)S(1)}) custom-call(bf16[16,3200]{1,0:T(8,128)(2,1)S(1)} %join_16.1.refs_0_.refs_1_, bf16[3,16,1536]{2,1,0:T(8,128)(2,1)S(1)} %hidden.1.refs_1_, ...), custom_call_target="tpu_custom_call" | custom-call | flops 754974720 | tf_op jit(solution)/shard_map/token_partials/pallas_call | solution.py:55
  45.4 1.2 %collective-permute-start.6 = (bf16[8,3072]{1,0:T(8,128)(2,1)S(1)}, bf16[8,3072]{1,0:T(8,128)(2,1)S(1)}, u32[]{:S(2)}, u32[]{:S(2)}) collective-permute-start(bf16[8,3072]{1,0:T(8,128)(2,1)S(1)} %get-tuple-element.35), channel_id=1, source_target_pairs={{0,16},{4,20},{8,24},{12,28},{16,0},{20,4},{24,8},{28,12},{1,17},{... | collective-permute-start | bytes 147464 | tf_op jit(solution)/shard_map/ppermute | solution.py:389
  46.6 2.6 %down_grad_1.1.refs_2_.refs_4_ = bf16[3072,1536]{1,0:T(8,128)(2,1)} custom-call(f32[8,3072]{1,0:T(8,128)S(1)} %get-tuple-element.34.refs_0_, bf16[16,3200]{1,0:T(8,128)(2,1)S(1)} %join_16.1.refs_0_.refs_1_, bf16[16,3072]{1,0:T(8,128)(2,1)S(1)} %get-tuple-element.36.refs_2_, bf16[16,2048]{1,0:T(8,128)(2,1)S(1)} %get-tuple-element.37.refs_3_), custom_call_target="tpu_custom_call" | custom-call | flops 75497472 | bytes 4718592 | tf_op jit(solution)/shard_map/down_grad_1/pallas_call | solution.py:55
  49.2 0.3 collective-permute-done.6.refs_1_
  49.5 1.0 %collective-permute-start.7 = (bf16[4,3072]{1,0:T(4,128)(2,1)S(1)}, bf16[4,3072]{1,0:T(4,128)(2,1)S(1)}, u32[]{:S(2)}, u32[]{:S(2)}) collective-permute-start(bf16[4,3072]{1,0:T(4,128)(2,1)S(1)} %get-tuple-element.39), channel_id=1, source_target_pairs={{0,4},{4,0},{8,12},{12,8},{16,20},{20,16},{24,28},{28,24},{1,5},{5... | collective-permute-start | bytes 73736 | tf_op jit(solution)/shard_map/ppermute | solution.py:389
  50.5 2.9 %down_grad_2.1 = (bf16[3072,1536]{1,0:T(8,128)(2,1)}, bf16[2048,1536]{1,0:T(8,128)(2,1)}) custom-call(f32[4,3072]{1,0:T(4,128)S(1)} %get-tuple-element.38.refs_0_, bf16[16,3200]{1,0:T(8,128)(2,1)S(1)} %join_16.1.refs_0_.refs_1_, bf16[16,3072]{1,0:T(8,128)(2,1)S(1)} %get-tuple-element.36.refs_2_, ...), custom_call_target="tpu_custom_call", output_to_operand_aliasing={{0}: (4, {})} | custom-call | flops 88080384 | bytes 5505024 | tf_op jit(solution)/shard_map/down_grad_2/pallas_call | solution.py:55
  53.4 1.7 %collective-permute-start.8 = (f32[2,3072]{1,0:T(2,128)S(1)}, f32[2,3072]{1,0:T(2,128)S(1)}, u32[]{:S(2)}, u32[]{:S(2)}) collective-permute-start(f32[2,3072]{1,0:T(2,128)S(1)} %get-tuple-element.42), channel_id=1, source_target_pairs={{0,8},{4,12},{8,0},{12,4},{16,24},{20,28},{24,16},{28,20},{1,9},{5... | collective-permute-start | bytes 73736 | tf_op jit(solution)/shard_map/ppermute | solution.py:389
  55.2 2.9 %down_grad_3.1 = bf16[2048,1536]{1,0:T(8,128)(2,1)} custom-call(f32[2,3072]{1,0:T(2,128)S(1)} %get-tuple-element.41.refs_0_, bf16[16,3200]{1,0:T(8,128)(2,1)S(1)} %join_16.1.refs_0_.refs_1_, bf16[16,3072]{1,0:T(8,128)(2,1)S(1)} %get-tuple-element.36.refs_2_, bf16[16,2048]{1,0:T(8,128)(2,1)S(1)} %get-tuple-element.37.refs_3_, ...), custom_call_target="tpu_custom_call", output_to_operand_aliasing={{}: (4, {})} | custom-call | flops 88080384 | bytes 5505024 | tf_op jit(solution)/shard_map/down_grad_3/pallas_call | solution.py:55
  58.2 0.6 %token_sum_1.1 = (bf16[2,1536]{1,0:T(2,128)(2,1)}, bf16[2,1536]{1,0:T(2,128)(2,1)}) custom-call(f32[2,3072]{1,0:T(2,128)S(1)} %get-tuple-element.41.refs_0_, f32[2,3072]{1,0:T(2,128)S(1)} %collective-permute-done.8.refs_1_), custom_call_target="tpu_custom_call" | custom-call | tf_op jit(solution)/shard_map/token_sum_1/pallas_call | solution.py:55
  (14 shorter events, 0.6 us)
Async XLA Ops:
  1.4 7.0 %collective-permute-start = (bf16[2,3200]{1,0:T(2,128)(2,1)S(1)}, bf16[2,3200]{1,0:T(2,128)(2,1)S(1)}, u32[]{:S(2)}, u32[]{:S(2)}) collective-permute-start(bf16[2,3200]{1,0:T(2,128)(2,1)S(1)} %get-tuple-element.25.refs_0_), channel_id=1, source_target_pairs={{0,8},{4,12},{8,0},{12,4},{16,24},{20,28},{24,16},{28,20},{1,9},{5... | collective-permute-start | bytes 38408 | tf_op jit(solution)/shard_map/ppermute | solution.py:389
  8.5 4.6 %collective-permute-start.1 = (bf16[4,3200]{1,0:T(4,128)(2,1)S(1)}, bf16[4,3200]{1,0:T(4,128)(2,1)S(1)}, u32[]{:S(2)}, u32[]{:S(2)}) collective-permute-start(bf16[4,3200]{1,0:T(4,128)(2,1)S(1)} %join_4.1.refs_0_), channel_id=1, source_target_pairs={{0,4},{4,0},{8,12},{12,8},{16,20},{20,16},{24,28},{28,24},{1,5},{5... | collective-permute-start | bytes 76808 | tf_op jit(solution)/shard_map/ppermute | solution.py:389
  13.1 4.5 %collective-permute-start.2 = (bf16[8,3200]{1,0:T(8,128)(2,1)S(1)}, bf16[8,3200]{1,0:T(8,128)(2,1)S(1)}, u32[]{:S(2)}, u32[]{:S(2)}) collective-permute-start(bf16[8,3200]{1,0:T(8,128)(2,1)S(1)} %join_8.1.refs_0_), channel_id=1, source_target_pairs={{0,16},{4,20},{8,24},{12,28},{16,0},{20,4},{24,8},{28,12},{1,17},{... | collective-permute-start | bytes 153608 | tf_op jit(solution)/shard_map/ppermute | solution.py:389
  28.4 1.6 %collective-permute-start.3 = (f32[3,16,1536]{2,1,0:T(8,128)S(1)}, f32[3,16,1536]{2,1,0:T(8,128)S(1)}, u32[]{:S(2)}, u32[]{:S(2)}) collective-permute-start(f32[3,16,1536]{2,1,0:T(8,128)S(1)} %get-tuple-element.29), channel_id=1, source_target_pairs={{0,1},{1,0},{2,3},{3,2},{4,5},{5,4},{6,7},{7,6},{8,9},{9,8},{10,11... | collective-permute-start | bytes 884744 | tf_op jit(solution)/shard_map/ppermute | solution.py:389
  30.1 6.0 %collective-permute-start.4 = (bf16[3,16,1536]{2,1,0:T(8,128)(2,1)S(1)}, bf16[3,16,1536]{2,1,0:T(8,128)(2,1)S(1)}, u32[]{:S(2)}, u32[]{:S(2)}) collective-permute-start(bf16[3,16,1536]{2,1,0:T(8,128)(2,1)S(1)} %get-tuple-element.33), channel_id=1, source_target_pairs={{0,2},{1,3},{2,0},{3,1},{4,6},{5,7},{6,4},{7,5},{8,10},{9,11},{10,... | collective-permute-start | bytes 442376 | tf_op jit(solution)/shard_map/ppermute | solution.py:389
  36.2 1.4 %collective-permute-start.5 = (bf16[3,16,1536]{2,1,0:T(8,128)(2,1)S(1)}, bf16[3,16,1536]{2,1,0:T(8,128)(2,1)S(1)}, u32[]{:S(2)}, u32[]{:S(2)}) collective-permute-start(bf16[3,16,1536]{2,1,0:T(8,128)(2,1)S(1)} %hidden.1.refs_1_), channel_id=1, source_target_pairs={{0,1},{1,0},{2,3},{3,2},{4,5},{5,4},{6,7},{7,6},{8,9},{9,8},{10,11... | collective-permute-start | bytes 442376 | tf_op jit(solution)/shard_map/ppermute | solution.py:389
  45.4 4.1 %collective-permute-start.6 = (bf16[8,3072]{1,0:T(8,128)(2,1)S(1)}, bf16[8,3072]{1,0:T(8,128)(2,1)S(1)}, u32[]{:S(2)}, u32[]{:S(2)}) collective-permute-start(bf16[8,3072]{1,0:T(8,128)(2,1)S(1)} %get-tuple-element.35), channel_id=1, source_target_pairs={{0,16},{4,20},{8,24},{12,28},{16,0},{20,4},{24,8},{28,12},{1,17},{... | collective-permute-start | bytes 147464 | tf_op jit(solution)/shard_map/ppermute | solution.py:389
  49.5 3.9 %collective-permute-start.7 = (bf16[4,3072]{1,0:T(4,128)(2,1)S(1)}, bf16[4,3072]{1,0:T(4,128)(2,1)S(1)}, u32[]{:S(2)}, u32[]{:S(2)}) collective-permute-start(bf16[4,3072]{1,0:T(4,128)(2,1)S(1)} %get-tuple-element.39), channel_id=1, source_target_pairs={{0,4},{4,0},{8,12},{12,8},{16,20},{20,16},{24,28},{28,24},{1,5},{5... | collective-permute-start | bytes 73736 | tf_op jit(solution)/shard_map/ppermute | solution.py:389
  53.4 4.8 %collective-permute-start.8 = (f32[2,3072]{1,0:T(2,128)S(1)}, f32[2,3072]{1,0:T(2,128)S(1)}, u32[]{:S(2)}, u32[]{:S(2)}) collective-permute-start(f32[2,3072]{1,0:T(2,128)S(1)} %get-tuple-element.42), channel_id=1, source_target_pairs={{0,8},{4,12},{8,0},{12,4},{16,24},{20,28},{24,16},{28,20},{1,9},{5... | collective-permute-start | bytes 73736 | tf_op jit(solution)/shard_map/ppermute | solution.py:389

commit v6 on v5

--- a/solution.py
+++ b/solution.py
@@ -14,8 +14,8 @@
 MIB = 1 << 20
 BLOCK = 512
 ROWS = 256
-TURN_FIRST = 2
-TURN_SECOND = 6
+TURN_FIRST = 4
+TURN_SECOND = 13
 PLACES = {"h": pl.ANY, "v": pltpu.VMEM, "s": pltpu.SMEM}
 
 
@@ -117,10 +117,8 @@
     ]
 
 
-def row_blocks(src, tall, first):
-    return [
-        [(src.at[pl.ds(i, BLOCK)], tall.at[pl.ds(first + i, BLOCK)])] for i in range(0, src.shape[0], BLOCK)
-    ]
+def row_blocks(src, tall, first, rows):
+    return [[(src.at[pl.ds(i, BLOCK)], tall.at[pl.ds(first + i, BLOCK)])] for i in range(*rows, BLOCK)]
 
 
 def started(groups, sems):
@@ -139,18 +137,18 @@
         copy.wait()
 
 
-def load_body(first, after_ref, src_hbm, old_ref, place_ref, sems):
+def load_body(first, rows, after_ref, src_hbm, old_ref, place_ref, sems):
     if place_ref.ndim == 4:
         groups = column_blocks(src_hbm, place_ref, first)
     else:
-        groups = row_blocks(src_hbm, place_ref, first)
+        groups = row_blocks(src_hbm, place_ref, first, (0, rows))
     for group in started(groups, sems):
         wait(group)
 
 
-def load(after, src, place, also, first, name):
+def load(after, src, place, also, first, name, rows=None):
     return call(
-        functools.partial(load_body, first),
+        functools.partial(load_body, first, rows or src.shape[0]),
         name,
         [like(place)],
         (after, src, place),
@@ -172,13 +170,13 @@
 
 
 def partials_body(
-    arr_ref, gs_hbm, us_hbm, ds_hbm, old_wide, old_tall, mine_ref, theirs_ref, wide_ref, tall_ref, part, sems
+    early, arr_ref, ut_ref, gs_hbm, us_hbm, ds_hbm, old_wide, old_tall, mine_ref, theirs_ref, wide_ref, tall_ref, part, sems
 ):
     fs, width = ds_hbm.shape
     ft = tall_ref.shape[0] - fs
     ns, nt = fs // BLOCK, ft // BLOCK
     groups = column_blocks(gs_hbm, wide_ref, 2 * nt) + column_blocks(us_hbm, wide_ref, 2 * nt + ns)
-    copies = started(groups + row_blocks(ds_hbm, tall_ref, 0), sems)
+    copies = started(groups + row_blocks(ds_hbm, tall_ref, 0, (early, fs)) + column_blocks(ut_ref, wide_ref, nt), sems)
     x = arr_ref[:, :width]
     c = arr_ref[:, width : 2 * width]
     speech = is_speech(arr_ref)
@@ -191,7 +189,8 @@
 
     for k in range(2):
         for i in range(nt):
-            put(k, beside(i, fs, ft), times(x, columns(wide_ref, k * nt + i)), False)
+            block = columns(wide_ref, i) if k == 0 else ut_ref[:, i * BLOCK : (i + 1) * BLOCK]
+            put(k, beside(i, fs, ft), times(x, block), False)
     for i in range(nt):
         rows = slice(fs + i * BLOCK, fs + (i + 1) * BLOCK)
         put(2, beside(i, fs, ft), contract_last(c, tall_ref[rows, :]), False)
@@ -200,8 +199,11 @@
             wait(copies[k * ns + i])
             put(k, i * BLOCK, times(x, columns(wide_ref, 2 * nt + k * ns + i)), True)
     for i in range(ns):
-        wait(copies[2 * ns + i])
+        if i * BLOCK >= early:
+            wait(copies[2 * ns + i - early // BLOCK])
         put(2, i * BLOCK, contract_last(c, tall_ref[i * BLOCK : (i + 1) * BLOCK, :]), True)
+    for group in copies[3 * ns - early // BLOCK :]:
+        wait(group)
     half = fs // 2
     odd = parity()
     for k in range(3):
@@ -209,20 +211,20 @@
         theirs_ref[k] = part[k, :, pl.ds(pl.multiple_of((1 - odd) * half, half), half)]
 
 
-def partials(arr, gate_s, up_s, down_s, wide, tall):
+def partials(early, arr, up_t, gate_s, up_s, down_s, wide, tall):
     rows, fs = arr.shape[0], gate_s.shape[1]
     half = ((3, rows, fs // 2), F32)
-    n_sems = 2 * gate_s.size // BLOCK**2 + fs // BLOCK
+    n_sems = (2 * gate_s.size + up_t.size) // BLOCK**2 + fs // BLOCK
     return call(
-        partials_body,
+        functools.partial(partials_body, early),
         "hidden_partials",
         [half, half, like(wide), like(tall)],
-        (arr, gate_s, up_s, down_s, wide, tall),
-        "vhhhvv",
+        (arr, up_t, gate_s, up_s, down_s, wide, tall),
+        "vvhhhvv",
         [pltpu.VMEM((3, rows, fs), F32), pltpu.SemaphoreType.DMA((n_sems,))],
         2 * rows * (wide.size + tall.size),
         size_of(gate_s, up_s, down_s),
-        aliases={4: 2, 5: 3},
+        aliases={5: 2, 6: 3},
     )
 
 
@@ -242,23 +244,24 @@
     out_ref[2] = (dh * silu).astype(BF16)
 
 
-def turn_body(first, count, by_product, old_ref, wide_ref):
+def turn_body(first, count, old_ref, wide_ref):
     row, col = (lax.broadcasted_iota(jnp.int32, (ROWS, ROWS), i) for i in range(2))
     one = (row == col).astype(BF16)
-    for i in range(first, first + count):
-        for r in range(wide_ref.shape[1]):
-            square = wide_ref[i, r]
-            if by_product:
-                parts = [contract_last(one, square[:, j : j + ROWS]) for j in range(0, BLOCK, ROWS)]
-                turned = jnp.concatenate([p.astype(BF16) for p in parts], axis=0)
-            else:
-                turned = square.T
-            wide_ref[i, r] = turned
-
-
-def turn(wide, tall, first, count, by_product, name):
+    squares = wide_ref.shape[1]
+    for n in range(count * squares):
+        i, r = first + n // squares, n % squares
+        square = wide_ref[i, r]
+        if n % 2:
+            turned = square.T
+        else:
+            parts = [contract_last(one, square[:, j : j + ROWS]) for j in range(0, BLOCK, ROWS)]
+            turned = jnp.concatenate([p.astype(BF16) for p in parts], axis=0)
+        wide_ref[i, r] = turned
+
+
+def turn(wide, tall, first, count, name):
     return call(
-        functools.partial(turn_body, first, count, by_product),
+        functools.partial(turn_body, first, count),
         name,
         [like(wide)],
         (wide,),
@@ -399,24 +402,26 @@
     packed = ((rows, 2 * width + 128), BF16)
     scratch = pair + [pltpu.SMEM((rows,), jnp.int32), pltpu.SemaphoreType.DMA((3,))]
     wide, tall, arr = call(pack_body, "pack", [wide, tall, packed], (modality, tokens, cotangent), "hhh", scratch)
+    up_t, arr = lax.optimization_barrier((up_t, arr))
+    up_t = flip(up_t, "seq", 0, n_seq)
     got = flip(arr, TOK, HOPS[0], n_tok)
     wide = load(arr, gate_t, wide, (tall,), 0, "load_gate_text")
     arr = join(arr, got, "join_4", (wide, tall))
     got = flip(arr, TOK, HOPS[1], n_tok)
-    wide = load(arr, up_t, wide, (tall,), ft // BLOCK, "load_up_text")
+    tall = load(arr, down_s, tall, (wide,), 0, "load_down_speech", ft)
     arr = join(arr, got, "join_8", (wide, tall))
     got = flip(arr, TOK, HOPS[2], n_tok)
     tall = load(arr, down_t, tall, (wide,), fs, "load_down_text")
     arr = join(arr, got, "join_16", (wide, tall))
 
-    mine, theirs, wide, tall = partials(arr, gate_s, up_s, down_s, wide, tall)
+    mine, theirs, wide, tall = partials(ft, arr, up_t, gate_s, up_s, down_s, wide, tall)
     got = flip(theirs, "seq", 1, n_seq)
-    wide = turn(wide, tall, 0, TURN_FIRST, False, "turn_1")
+    wide = turn(wide, tall, 0, TURN_FIRST, "turn_1")
     total, send = call(
         core_sum_body, "core_sum", [like(mine), (mine.shape, BF16)], (mine, got), "vv", also=(wide, tall)
     )
     got = flip(send, "seq", 2, n_seq)
-    wide = turn(wide, tall, TURN_FIRST, TURN_SECOND, True, "turn_2")
+    wide = turn(wide, tall, TURN_FIRST, TURN_SECOND, "turn_2")
     done = call(hidden_body, "hidden", [(mine.shape, BF16)], (total, got), "vv", also=(wide, tall))[0]
     other = flip(done, "seq", 1, n_seq)
     own = call(

time: 59.2 us -> 60.8 us (1.027)
  starting transfers between devices: 12.9 us -> 15.6 us
  Pallas kernels: 42 us -> 41.2 us
    ppermute x9 -> x10, starting transfers between devices: 12.9 us -> 15.6 us  [flip(): return lax.ppermute(value, axes, [(i, i ^ bit) for i in range(n)])]
    pallas_call x20, Pallas kernels: 42 us -> 41.2 us  [call(): pl.pallas_call(seen, out_shape=shapes, in_specs=[pl.BlockSpec(memory_spac...]
    ppermute x9 -> x10, waiting for transfers between devices: 3.16 us -> 2.81 us  [flip(): return lax.ppermute(value, axes, [(i, i ^ bit) for i in range(n)])]
  transfers between devices with their start and end apart: 9 -> 10, of which waited for: 5 -> 6; matrix products, arithmetic and copies ran while one was open for 0% -> 0% of each run, Pallas kernels for 37% -> 37%
where the time goes in v6:
time: 60.8 us; the launch traced here: 60.6 us
  Pallas kernels  41.2 us (68%)
  starting transfers between devices  15.6 us (26%)
  waiting for transfers between devices  2.81 us (5%)
  between operations  0.96 us (2%)
    pallas_call x20, Pallas kernels, call(): pl.pallas_call(seen, out_shape=shapes, in_specs=[pl.BlockSpec(memory_spac...  41.2 us
    ppermute x10, starting transfers between devices, flip(): return lax.ppermute(value, axes, [(i, i ^ bit) for i in range(n)])  15.6 us
    ppermute x10, waiting for transfers between devices, flip(): return lax.ppermute(value, axes, [(i, i ^ bit) for i in range(n)])  2.81 us
  transfers between devices with their start and end apart: 10, of which 6 were waited for; matrix products, arithmetic and copies ran while one was open for 0% of the time, Pallas kernels for 37%

profile of v6, /device:TPU:0, one launch (start us, length us, event | category | flops | bytes accessed | tf_op | source)
XLA Modules:
  0.0 60.6 jit_solution(16867174702473157384)
XLA Ops:
  0.6 0.7 %pack.1 = (bf16[20,3,512,512]{3,2,1,0:T(8,128)(2,1)S(1)}, bf16[5120,1536]{1,0:T(8,128)(2,1)S(1)}, bf16[2,3200]{1,0:T(2,128)(2,1)S(1)}) custom-call(s32[2]{0:T(128)} %refs_0_.1, bf16[2,1536]{1,0:T(2,128)(2,1)} %refs_1_.4, bf16[2,1536]{1,0:T(2,128)(2,1)} %refs_2_.2), custom_call_target="tpu_custom_call" | custom-call | tf_op jit(solution)/shard_map/pack/pallas_call | solution.py:55
  1.4 2.8 %collective-permute-start.3 = (bf16[1536,2048]{1,0:T(8,128)(2,1)}, bf16[1536,2048]{1,0:T(8,128)(2,1)S(1)}, u32[]{:S(2)}, u32[]{:S(2)}) collective-permute-start(bf16[1536,2048]{1,0:T(8,128)(2,1)} %param.16), channel_id=1, source_target_pairs={{0,0},{1,1},{2,2},{3,3},{4,4},{5,5},{6,6},{7,7},{8,8},{9,9},{10,10... | collective-permute-start | bytes 18874376 | tf_op jit(solution)/shard_map/ppermute | solution.py:392
  4.2 4.0 %collective-permute-start = (bf16[2,3200]{1,0:T(2,128)(2,1)S(1)}, bf16[2,3200]{1,0:T(2,128)(2,1)S(1)}, u32[]{:S(2)}, u32[]{:S(2)}) collective-permute-start(bf16[2,3200]{1,0:T(2,128)(2,1)S(1)} %get-tuple-element.28.refs_0_), channel_id=1, source_target_pairs={{0,8},{4,12},{8,0},{12,4},{16,24},{20,28},{24,16},{28,20},{1,9},{5... | collective-permute-start | bytes 38408 | tf_op jit(solution)/shard_map/ppermute | solution.py:392
  8.2 2.9 %load_gate_text.1.refs_2_.refs_3_.refs_5_ = bf16[20,3,512,512]{3,2,1,0:T(8,128)(2,1)S(1)} custom-call(bf16[2,3200]{1,0:T(2,128)(2,1)S(1)} %get-tuple-element.28.refs_0_, bf16[1536,2048]{1,0:T(8,128)(2,1)} %refs_1_.5, bf16[20,3,512,512]{3,2,1,0:T(8,128)(2,1)S(1)} %get-tuple-element.29.refs_2_, ...), custom_call_target="tpu_custom_call", output_to_operand_aliasing={{}: (2, {})} | custom-call | bytes 6291456 | tf_op jit(solution)/shard_map/load_gate_text/pallas_call | solution.py:55
  11.2 1.6 %collective-permute-start.1 = (bf16[4,3200]{1,0:T(4,128)(2,1)S(1)}, bf16[4,3200]{1,0:T(4,128)(2,1)S(1)}, u32[]{:S(2)}, u32[]{:S(2)}) collective-permute-start(bf16[4,3200]{1,0:T(4,128)(2,1)S(1)} %join_4.1.refs_0_), channel_id=1, source_target_pairs={{0,4},{4,0},{8,12},{12,8},{16,20},{20,16},{24,28},{28,24},{1,5},{5... | collective-permute-start | bytes 76808 | tf_op jit(solution)/shard_map/ppermute | solution.py:392
  12.8 3.0 %load_down_speech.1.refs_3_.refs_2_ = bf16[5120,1536]{1,0:T(8,128)(2,1)S(1)} custom-call(bf16[4,3200]{1,0:T(4,128)(2,1)S(1)} %join_4.1.refs_0_, bf16[3072,1536]{1,0:T(8,128)(2,1)} %refs_4_.1, bf16[5120,1536]{1,0:T(8,128)(2,1)S(1)} %get-tuple-element.30.refs_3_.refs_2_, ...), custom_call_target="tpu_custom_call", output_to_operand_aliasing={{}: (2, {})} | custom-call | bytes 9437184 | tf_op jit(solution)/shard_map/load_down_speech/pallas_call | solution.py:55
  15.9 1.6 %collective-permute-start.2 = (bf16[8,3200]{1,0:T(8,128)(2,1)S(1)}, bf16[8,3200]{1,0:T(8,128)(2,1)S(1)}, u32[]{:S(2)}, u32[]{:S(2)}) collective-permute-start(bf16[8,3200]{1,0:T(8,128)(2,1)S(1)} %join_8.1.refs_0_), channel_id=1, source_target_pairs={{0,16},{4,20},{8,24},{12,28},{16,0},{20,4},{24,8},{28,12},{1,17},{... | collective-permute-start | bytes 153608 | tf_op jit(solution)/shard_map/ppermute | solution.py:392
  17.4 2.9 %load_down_text.1.refs_3_.refs_6_ = bf16[5120,1536]{1,0:T(8,128)(2,1)S(1)} custom-call(bf16[8,3200]{1,0:T(8,128)(2,1)S(1)} %join_8.1.refs_0_, bf16[2048,1536]{1,0:T(8,128)(2,1)} %refs_1_.7, bf16[5120,1536]{1,0:T(8,128)(2,1)S(1)} %load_down_speech.1.refs_3_.refs_2_, ...), custom_call_target="tpu_custom_call", output_to_operand_aliasing={{}: (2, {})} | custom-call | bytes 6291456 | tf_op jit(solution)/shard_map/load_down_text/pallas_call | solution.py:55
  20.4 11.4 %hidden_partials.1 = (f32[3,16,1536]{2,1,0:T(8,128)S(1)}, f32[3,16,1536]{2,1,0:T(8,128)S(1)}, bf16[20,3,512,512]{3,2,1,0:T(8,128)(2,1)S(1)}, bf16[5120,1536]{1,0:T(8,128)(2,1)S(1)}) custom-call(bf16[16,3200]{1,0:T(8,128)(2,1)S(1)} %join_16.1.refs_0_.refs_1_, ...), custom_call_target="tpu_custom_call", output_to_operand_aliasing={{2}: (5, {}), {3}: (6, {})} | custom-call | flops 754974720 | bytes 28311552 | tf_op jit(solution)/shard_map/hidden_partials/pallas_call | solution.py:55
  31.9 1.0 %turn_1.1.refs_2_.refs_0_ = bf16[20,3,512,512]{3,2,1,0:T(8,128)(2,1)S(1)} custom-call(bf16[20,3,512,512]{3,2,1,0:T(8,128)(2,1)S(1)} %get-tuple-element.34.refs_0_, bf16[5120,1536]{1,0:T(8,128)(2,1)S(1)} %get-tuple-element.35.refs_1_.refs_3_.refs_2_.refs_5_), custom_call_target="tpu_custom_call", output_to_operand_aliasing={{}: (0, {})} | custom-call | bytes 12582912 | tf_op jit(solution)/shard_map/turn_1/pallas_call | solution.py:55
  32.9 0.5 collective-permute-done.4.refs_1_
  33.5 1.6 %collective-permute-start.5 = (bf16[3,16,1536]{2,1,0:T(8,128)(2,1)S(1)}, bf16[3,16,1536]{2,1,0:T(8,128)(2,1)S(1)}, u32[]{:S(2)}, u32[]{:S(2)}) collective-permute-start(bf16[3,16,1536]{2,1,0:T(8,128)(2,1)S(1)} %get-tuple-element.37), channel_id=1, source_target_pairs={{0,2},{1,3},{2,0},{3,1},{4,6},{5,7},{6,4},{7,5},{8,10},{9,11},{10,... | collective-permute-start | bytes 442376 | tf_op jit(solution)/shard_map/ppermute | solution.py:392
  35.0 2.9 %turn_2.1.refs_2_.refs_3_.refs_4_ = bf16[20,3,512,512]{3,2,1,0:T(8,128)(2,1)S(1)} custom-call(bf16[20,3,512,512]{3,2,1,0:T(8,128)(2,1)S(1)} %turn_1.1.refs_2_.refs_0_, bf16[5120,1536]{1,0:T(8,128)(2,1)S(1)} %get-tuple-element.35.refs_1_.refs_3_.refs_2_.refs_5_), custom_call_target="tpu_custom_call", output_to_operand_aliasing={{}: (0, {})} | custom-call | bytes 40894464 | tf_op jit(solution)/shard_map/turn_2/pallas_call | solution.py:55
  38.0 1.5 %collective-permute-done.5.refs_1_ = bf16[3,16,1536]{2,1,0:T(8,128)(2,1)S(1)} collective-permute-done((bf16[3,16,1536]{2,1,0:T(8,128)(2,1)S(1)}, bf16[3,16,1536]{2,1,0:T(8,128)(2,1)S(1)}, u32[]{:S(2)}, u32[]{:S(2)}) %collective-permute-start.5) | collective-permute-done | bytes 147488 | tf_op jit(solution)/shard_map/ppermute | solution.py:392
  39.6 1.2 %mixed_own.1.refs_3_ = f32[16,1536]{1,0:T(8,128)S(1)} custom-call(bf16[16,3200]{1,0:T(8,128)(2,1)S(1)} %join_16.1.refs_0_.refs_1_, bf16[3,16,1536]{2,1,0:T(8,128)(2,1)S(1)} %hidden.1.refs_1_, bf16[5120,1536]{1,0:T(8,128)(2,1)S(1)} %get-tuple-element.35.refs_1_.refs_3_.refs_2_.refs_5_, bf16[20,3,512,512]{3,2,1,0:T(8,128)(2,1)S(1)} %turn_2.1.refs_2_.refs_3_.refs_4_), custom_call_target="tpu_custom_call" | custom-call | flops 125829120 | tf_op jit(solution)/shard_map/mixed_own/pallas_call | solution.py:55
  40.9 6.0 %token_partials.1 = (f32[8,3072]{1,0:T(8,128)S(1)}, bf16[8,3072]{1,0:T(8,128)(2,1)S(1)}, bf16[16,3072]{1,0:T(8,128)(2,1)S(1)}, bf16[16,2048]{1,0:T(8,128)(2,1)S(1)}) custom-call(bf16[16,3200]{1,0:T(8,128)(2,1)S(1)} %join_16.1.refs_0_.refs_1_, bf16[3,16,1536]{2,1,0:T(8,128)(2,1)S(1)} %hidden.1.refs_1_, ...), custom_call_target="tpu_custom_call" | custom-call | flops 754974720 | tf_op jit(solution)/shard_map/token_partials/pallas_call | solution.py:55
  46.9 1.2 %collective-permute-start.7 = (bf16[8,3072]{1,0:T(8,128)(2,1)S(1)}, bf16[8,3072]{1,0:T(8,128)(2,1)S(1)}, u32[]{:S(2)}, u32[]{:S(2)}) collective-permute-start(bf16[8,3072]{1,0:T(8,128)(2,1)S(1)} %get-tuple-element.39), channel_id=1, source_target_pairs={{0,16},{4,20},{8,24},{12,28},{16,0},{20,4},{24,8},{28,12},{1,17},{... | collective-permute-start | bytes 147464 | tf_op jit(solution)/shard_map/ppermute | solution.py:392
  48.1 2.6 %down_grad_1.1.refs_2_.refs_4_ = bf16[3072,1536]{1,0:T(8,128)(2,1)} custom-call(f32[8,3072]{1,0:T(8,128)S(1)} %get-tuple-element.38.refs_0_, bf16[16,3200]{1,0:T(8,128)(2,1)S(1)} %join_16.1.refs_0_.refs_1_, bf16[16,3072]{1,0:T(8,128)(2,1)S(1)} %get-tuple-element.40.refs_2_, bf16[16,2048]{1,0:T(8,128)(2,1)S(1)} %get-tuple-element.41.refs_3_), custom_call_target="tpu_custom_call" | custom-call | flops 75497472 | bytes 4718592 | tf_op jit(solution)/shard_map/down_grad_1/pallas_call | solution.py:55
  50.7 0.3 collective-permute-done.7.refs_1_
  51.1 0.9 %collective-permute-start.8 = (bf16[4,3072]{1,0:T(4,128)(2,1)S(1)}, bf16[4,3072]{1,0:T(4,128)(2,1)S(1)}, u32[]{:S(2)}, u32[]{:S(2)}) collective-permute-start(bf16[4,3072]{1,0:T(4,128)(2,1)S(1)} %get-tuple-element.43), channel_id=1, source_target_pairs={{0,4},{4,0},{8,12},{12,8},{16,20},{20,16},{24,28},{28,24},{1,5},{5... | collective-permute-start | bytes 73736 | tf_op jit(solution)/shard_map/ppermute | solution.py:392
  52.0 2.9 %down_grad_2.1 = (bf16[3072,1536]{1,0:T(8,128)(2,1)}, bf16[2048,1536]{1,0:T(8,128)(2,1)}) custom-call(f32[4,3072]{1,0:T(4,128)S(1)} %get-tuple-element.42.refs_0_, bf16[16,3200]{1,0:T(8,128)(2,1)S(1)} %join_16.1.refs_0_.refs_1_, bf16[16,3072]{1,0:T(8,128)(2,1)S(1)} %get-tuple-element.40.refs_2_, ...), custom_call_target="tpu_custom_call", output_to_operand_aliasing={{0}: (4, {})} | custom-call | flops 88080384 | bytes 5505024 | tf_op jit(solution)/shard_map/down_grad_2/pallas_call | solution.py:55
  55.0 1.7 %collective-permute-start.9 = (f32[2,3072]{1,0:T(2,128)S(1)}, f32[2,3072]{1,0:T(2,128)S(1)}, u32[]{:S(2)}, u32[]{:S(2)}) collective-permute-start(f32[2,3072]{1,0:T(2,128)S(1)} %get-tuple-element.46), channel_id=1, source_target_pairs={{0,8},{4,12},{8,0},{12,4},{16,24},{20,28},{24,16},{28,20},{1,9},{5... | collective-permute-start | bytes 73736 | tf_op jit(solution)/shard_map/ppermute | solution.py:392
  56.7 2.9 %down_grad_3.1 = bf16[2048,1536]{1,0:T(8,128)(2,1)} custom-call(f32[2,3072]{1,0:T(2,128)S(1)} %get-tuple-element.45.refs_0_, bf16[16,3200]{1,0:T(8,128)(2,1)S(1)} %join_16.1.refs_0_.refs_1_, bf16[16,3072]{1,0:T(8,128)(2,1)S(1)} %get-tuple-element.40.refs_2_, bf16[16,2048]{1,0:T(8,128)(2,1)S(1)} %get-tuple-element.41.refs_3_, ...), custom_call_target="tpu_custom_call", output_to_operand_aliasing={{}: (4, {})} | custom-call | flops 88080384 | bytes 5505024 | tf_op jit(solution)/shard_map/down_grad_3/pallas_call | solution.py:55
  59.8 0.6 %token_sum_1.1 = (bf16[2,1536]{1,0:T(2,128)(2,1)}, bf16[2,1536]{1,0:T(2,128)(2,1)}) custom-call(f32[2,3072]{1,0:T(2,128)S(1)} %get-tuple-element.45.refs_0_, f32[2,3072]{1,0:T(2,128)S(1)} %collective-permute-done.9.refs_1_), custom_call_target="tpu_custom_call" | custom-call | tf_op jit(solution)/shard_map/token_sum_1/pallas_call | solution.py:55
  (16 shorter events, 0.8 us)
Async XLA Ops:
  1.4 19.0 %collective-permute-start.3 = (bf16[1536,2048]{1,0:T(8,128)(2,1)}, bf16[1536,2048]{1,0:T(8,128)(2,1)S(1)}, u32[]{:S(2)}, u32[]{:S(2)}) collective-permute-start(bf16[1536,2048]{1,0:T(8,128)(2,1)} %param.16), channel_id=1, source_target_pairs={{0,0},{1,1},{2,2},{3,3},{4,4},{5,5},{6,6},{7,7},{8,8},{9,9},{10,10... | collective-permute-start | bytes 18874376 | tf_op jit(solution)/shard_map/ppermute | solution.py:392
  4.2 7.0 %collective-permute-start = (bf16[2,3200]{1,0:T(2,128)(2,1)S(1)}, bf16[2,3200]{1,0:T(2,128)(2,1)S(1)}, u32[]{:S(2)}, u32[]{:S(2)}) collective-permute-start(bf16[2,3200]{1,0:T(2,128)(2,1)S(1)} %get-tuple-element.28.refs_0_), channel_id=1, source_target_pairs={{0,8},{4,12},{8,0},{12,4},{16,24},{20,28},{24,16},{28,20},{1,9},{5... | collective-permute-start | bytes 38408 | tf_op jit(solution)/shard_map/ppermute | solution.py:392
  11.2 4.6 %collective-permute-start.1 = (bf16[4,3200]{1,0:T(4,128)(2,1)S(1)}, bf16[4,3200]{1,0:T(4,128)(2,1)S(1)}, u32[]{:S(2)}, u32[]{:S(2)}) collective-permute-start(bf16[4,3200]{1,0:T(4,128)(2,1)S(1)} %join_4.1.refs_0_), channel_id=1, source_target_pairs={{0,4},{4,0},{8,12},{12,8},{16,20},{20,16},{24,28},{28,24},{1,5},{5... | collective-permute-start | bytes 76808 | tf_op jit(solution)/shard_map/ppermute | solution.py:392
  15.9 4.5 %collective-permute-start.2 = (bf16[8,3200]{1,0:T(8,128)(2,1)S(1)}, bf16[8,3200]{1,0:T(8,128)(2,1)S(1)}, u32[]{:S(2)}, u32[]{:S(2)}) collective-permute-start(bf16[8,3200]{1,0:T(8,128)(2,1)S(1)} %join_8.1.refs_0_), channel_id=1, source_target_pairs={{0,16},{4,20},{8,24},{12,28},{16,0},{20,4},{24,8},{28,12},{1,17},{... | collective-permute-start | bytes 153608 | tf_op jit(solution)/shard_map/ppermute | solution.py:392
  31.8 1.6 %collective-permute-start.4 = (f32[3,16,1536]{2,1,0:T(8,128)S(1)}, f32[3,16,1536]{2,1,0:T(8,128)S(1)}, u32[]{:S(2)}, u32[]{:S(2)}) collective-permute-start(f32[3,16,1536]{2,1,0:T(8,128)S(1)} %get-tuple-element.33), channel_id=1, source_target_pairs={{0,1},{1,0},{2,3},{3,2},{4,5},{5,4},{6,7},{7,6},{8,9},{9,8},{10,11... | collective-permute-start | bytes 884744 | tf_op jit(solution)/shard_map/ppermute | solution.py:392
  33.5 6.0 %collective-permute-start.5 = (bf16[3,16,1536]{2,1,0:T(8,128)(2,1)S(1)}, bf16[3,16,1536]{2,1,0:T(8,128)(2,1)S(1)}, u32[]{:S(2)}, u32[]{:S(2)}) collective-permute-start(bf16[3,16,1536]{2,1,0:T(8,128)(2,1)S(1)} %get-tuple-element.37), channel_id=1, source_target_pairs={{0,2},{1,3},{2,0},{3,1},{4,6},{5,7},{6,4},{7,5},{8,10},{9,11},{10,... | collective-permute-start | bytes 442376 | tf_op jit(solution)/shard_map/ppermute | solution.py:392
  39.5 1.4 %collective-permute-start.6 = (bf16[3,16,1536]{2,1,0:T(8,128)(2,1)S(1)}, bf16[3,16,1536]{2,1,0:T(8,128)(2,1)S(1)}, u32[]{:S(2)}, u32[]{:S(2)}) collective-permute-start(bf16[3,16,1536]{2,1,0:T(8,128)(2,1)S(1)} %hidden.1.refs_1_), channel_id=1, source_target_pairs={{0,1},{1,0},{2,3},{3,2},{4,5},{5,4},{6,7},{7,6},{8,9},{9,8},{10,11... | collective-permute-start | bytes 442376 | tf_op jit(solution)/shard_map/ppermute | solution.py:392
  46.9 4.1 %collective-permute-start.7 = (bf16[8,3072]{1,0:T(8,128)(2,1)S(1)}, bf16[8,3072]{1,0:T(8,128)(2,1)S(1)}, u32[]{:S(2)}, u32[]{:S(2)}) collective-permute-start(bf16[8,3072]{1,0:T(8,128)(2,1)S(1)} %get-tuple-element.39), channel_id=1, source_target_pairs={{0,16},{4,20},{8,24},{12,28},{16,0},{20,4},{24,8},{28,12},{1,17},{... | collective-permute-start | bytes 147464 | tf_op jit(solution)/shard_map/ppermute | solution.py:392
  51.1 3.9 %collective-permute-start.8 = (bf16[4,3072]{1,0:T(4,128)(2,1)S(1)}, bf16[4,3072]{1,0:T(4,128)(2,1)S(1)}, u32[]{:S(2)}, u32[]{:S(2)}) collective-permute-start(bf16[4,3072]{1,0:T(4,128)(2,1)S(1)} %get-tuple-element.43), channel_id=1, source_target_pairs={{0,4},{4,0},{8,12},{12,8},{16,20},{20,16},{24,28},{28,24},{1,5},{5... | collective-permute-start | bytes 73736 | tf_op jit(solution)/shard_map/ppermute | solution.py:392
  55.0 4.8 %collective-permute-start.9 = (f32[2,3072]{1,0:T(2,128)S(1)}, f32[2,3072]{1,0:T(2,128)S(1)}, u32[]{:S(2)}, u32[]{:S(2)}) collective-permute-start(f32[2,3072]{1,0:T(2,128)S(1)} %get-tuple-element.46), channel_id=1, source_target_pairs={{0,8},{4,12},{8,0},{12,4},{16,24},{20,28},{24,16},{28,20},{1,9},{5... | collective-permute-start | bytes 73736 | tf_op jit(solution)/shard_map/ppermute | solution.py:392

commit v7 on v5

--- a/solution.py
+++ b/solution.py
@@ -13,9 +13,9 @@
 BF16 = jnp.bfloat16
 MIB = 1 << 20
 BLOCK = 512
+WIDE = 1024
 ROWS = 256
-TURN_FIRST = 2
-TURN_SECOND = 6
+TURN_FIRST = 5
 PLACES = {"h": pl.ANY, "v": pltpu.VMEM, "s": pltpu.SMEM}
 
 
@@ -106,15 +106,18 @@
     return call(join_body, name, [((2 * a.shape[0], a.shape[1]), BF16)], (a, b), "vv", also=also)[0]
 
 
-def column_blocks(src, wide, first):
-    rows = src.shape[0] // BLOCK
+def column_blocks(src, wide, first, cuts):
+    rows = src.shape[0] // cuts
+    parts = [pl.ds(j * rows, rows) for j in range(cuts)]
     return [
-        [
-            (src.at[pl.ds(r * BLOCK, BLOCK), pl.ds(i * BLOCK, BLOCK)], wide.at[first + i, r])
-            for r in range(rows)
-        ]
-        for i in range(src.shape[1] // BLOCK)
+        [(src.at[part, pl.ds(i * WIDE, WIDE)], wide.at[first + i, part]) for part in parts]
+        for i in range(src.shape[1] // WIDE)
     ]
+
+
+def square_at(wide_ref, i, r):
+    per = WIDE // BLOCK
+    return wide_ref.at[i // per, pl.ds(r * BLOCK, BLOCK), pl.ds(i % per * BLOCK, BLOCK)]
 
 
 def row_blocks(src, tall, first):
@@ -140,8 +143,8 @@
 
 
 def load_body(first, after_ref, src_hbm, old_ref, place_ref, sems):
-    if place_ref.ndim == 4:
-        groups = column_blocks(src_hbm, place_ref, first)
+    if place_ref.ndim == 3:
+        groups = column_blocks(src_hbm, place_ref, first, 4)
     else:
         groups = row_blocks(src_hbm, place_ref, first)
     for group in started(groups, sems):
@@ -155,7 +158,7 @@
         [like(place)],
         (after, src, place),
         "vhv",
-        [pltpu.SemaphoreType.DMA((src.size // BLOCK**2,))],
+        [pltpu.SemaphoreType.DMA((8,))],
         traffic=size_of(src),
         aliases={2: 0},
         also=also,
@@ -165,10 +168,6 @@
 def beside(i, fs, ft):
     side, rest = divmod(i * BLOCK, ft // 2)
     return side * (fs // 2) + rest
-
-
-def columns(wide_ref, i):
-    return wide_ref[i].reshape(-1, BLOCK)
 
 
 def partials_body(
@@ -176,8 +175,8 @@
 ):
     fs, width = ds_hbm.shape
     ft = tall_ref.shape[0] - fs
-    ns, nt = fs // BLOCK, ft // BLOCK
-    groups = column_blocks(gs_hbm, wide_ref, 2 * nt) + column_blocks(us_hbm, wide_ref, 2 * nt + ns)
+    ns, nt = fs // WIDE, ft // WIDE
+    groups = column_blocks(gs_hbm, wide_ref, 2 * nt, 2) + column_blocks(us_hbm, wide_ref, 2 * nt + ns, 2)
     copies = started(groups + row_blocks(ds_hbm, tall_ref, 0), sems)
     x = arr_ref[:, :width]
     c = arr_ref[:, width : 2 * width]
@@ -189,17 +188,22 @@
             value = jnp.where(speech, value, part[k, :, cut])
         part[k, :, cut] = value
 
+    def put_wide(k, start, value, pick):
+        for i in range(start, start + WIDE, BLOCK):
+            place = i if pick else beside(i // BLOCK, fs, ft)
+            put(k, place, value[:, i - start : i - start + BLOCK], pick)
+
     for k in range(2):
         for i in range(nt):
-            put(k, beside(i, fs, ft), times(x, columns(wide_ref, k * nt + i)), False)
-    for i in range(nt):
+            put_wide(k, i * WIDE, times(x, wide_ref[k * nt + i]), False)
+    for i in range(ft // BLOCK):
         rows = slice(fs + i * BLOCK, fs + (i + 1) * BLOCK)
         put(2, beside(i, fs, ft), contract_last(c, tall_ref[rows, :]), False)
     for k in range(2):
         for i in range(ns):
             wait(copies[k * ns + i])
-            put(k, i * BLOCK, times(x, columns(wide_ref, 2 * nt + k * ns + i)), True)
-    for i in range(ns):
+            put_wide(k, i * WIDE, times(x, wide_ref[2 * nt + k * ns + i]), True)
+    for i in range(fs // BLOCK):
         wait(copies[2 * ns + i])
         put(2, i * BLOCK, contract_last(c, tall_ref[i * BLOCK : (i + 1) * BLOCK, :]), True)
     half = fs // 2
@@ -212,7 +216,7 @@
 def partials(arr, gate_s, up_s, down_s, wide, tall):
     rows, fs = arr.shape[0], gate_s.shape[1]
     half = ((3, rows, fs // 2), F32)
-    n_sems = 2 * gate_s.size // BLOCK**2 + fs // BLOCK
+    n_sems = 4 * fs // WIDE + fs // BLOCK
     return call(
         partials_body,
         "hidden_partials",
@@ -242,28 +246,30 @@
     out_ref[2] = (dh * silu).astype(BF16)
 
 
-def turn_body(first, count, by_product, old_ref, wide_ref):
+def turn_body(first, count, old_ref, wide_ref):
     row, col = (lax.broadcasted_iota(jnp.int32, (ROWS, ROWS), i) for i in range(2))
     one = (row == col).astype(BF16)
-    for i in range(first, first + count):
-        for r in range(wide_ref.shape[1]):
-            square = wide_ref[i, r]
-            if by_product:
-                parts = [contract_last(one, square[:, j : j + ROWS]) for j in range(0, BLOCK, ROWS)]
-                turned = jnp.concatenate([p.astype(BF16) for p in parts], axis=0)
-            else:
-                turned = square.T
-            wide_ref[i, r] = turned
-
-
-def turn(wide, tall, first, count, by_product, name):
+    squares = wide_ref.shape[1] // BLOCK
+    for n in range(count * squares):
+        i, r = first + n // squares, n % squares
+        place = square_at(wide_ref, i, r)
+        square = place[...]
+        if n % 2:
+            turned = square.T
+        else:
+            parts = [contract_last(one, square[:, j : j + ROWS]) for j in range(0, BLOCK, ROWS)]
+            turned = jnp.concatenate([p.astype(BF16) for p in parts], axis=0)
+        place[...] = turned
+
+
+def turn(wide, tall, first, count, name):
     return call(
-        functools.partial(turn_body, first, count, by_product),
+        functools.partial(turn_body, first, count),
         name,
         [like(wide)],
         (wide,),
         "v",
-        traffic=4 * count * wide.shape[1] * BLOCK**2,
+        traffic=4 * count * wide.shape[1] * BLOCK,
         aliases={0: 0},
         also=(tall,),
     )[0]
@@ -313,7 +319,7 @@
         total = jnp.zeros((out.shape[0], BLOCK), F32)
         for b, (ref, j) in enumerate(blocks):
             product = times if b in turned else contract_last
-            total += product(ref[:, j * BLOCK : (j + 1) * BLOCK], wide_ref[b, r])
+            total += product(ref[:, j * BLOCK : (j + 1) * BLOCK], square_at(wide_ref, b, r)[...])
         start = width + r * BLOCK
         out[:, start : start + BLOCK] = total
     half = keep_ref.shape[0]
@@ -392,7 +398,7 @@
 def by_kernels(n_seq, n_tok, tokens, modality, cotangent, gate_s, up_s, down_s, gate_t, up_t, down_t):
     rows, width = tokens.shape
     fs, ft = gate_s.shape[1], gate_t.shape[1]
-    wide = ((2 * (fs + ft) // BLOCK, width // BLOCK, BLOCK, BLOCK), BF16)
+    wide = ((2 * (fs + ft) // WIDE, width, WIDE), BF16)
     tall = ((fs + ft, width), BF16)
     pair = [pltpu.VMEM((rows, width), BF16)] * 2
 
@@ -403,27 +409,28 @@
     wide = load(arr, gate_t, wide, (tall,), 0, "load_gate_text")
     arr = join(arr, got, "join_4", (wide, tall))
     got = flip(arr, TOK, HOPS[1], n_tok)
-    wide = load(arr, up_t, wide, (tall,), ft // BLOCK, "load_up_text")
+    wide = load(arr, up_t, wide, (tall,), ft // WIDE, "load_up_text")
     arr = join(arr, got, "join_8", (wide, tall))
     got = flip(arr, TOK, HOPS[2], n_tok)
     tall = load(arr, down_t, tall, (wide,), fs, "load_down_text")
     arr = join(arr, got, "join_16", (wide, tall))
 
     mine, theirs, wide, tall = partials(arr, gate_s, up_s, down_s, wide, tall)
+    blocks = 2 * (fs + ft) // BLOCK
     got = flip(theirs, "seq", 1, n_seq)
-    wide = turn(wide, tall, 0, TURN_FIRST, False, "turn_1")
+    wide = turn(wide, tall, 0, TURN_FIRST, "turn_1")
     total, send = call(
         core_sum_body, "core_sum", [like(mine), (mine.shape, BF16)], (mine, got), "vv", also=(wide, tall)
     )
     got = flip(send, "seq", 2, n_seq)
-    wide = turn(wide, tall, TURN_FIRST, TURN_SECOND, True, "turn_2")
+    wide = turn(wide, tall, TURN_FIRST, blocks - TURN_FIRST, "turn_2")
     done = call(hidden_body, "hidden", [(mine.shape, BF16)], (total, got), "vv", also=(wide, tall))[0]
     other = flip(done, "seq", 1, n_seq)
     own = call(
         mixed_own_body, "mixed_own", [((arr.shape[0], width), F32)], (arr, done, tall), "vvv",
         flops=arr.shape[0] * tall.size, also=(wide,),
     )[0]
-    keep, send, hs, ht = back(arr, done, other, own, wide, tall, range(TURN_FIRST + TURN_SECOND), fs, ft)
+    keep, send, hs, ht = back(arr, done, other, own, wide, tall, range(blocks), fs, ft)
 
     def outer(after, speech, text, old, name):
         count = len(speech) + len(text)
@@ -437,15 +444,15 @@
 
     ns, nt = fs // ROWS, ft // ROWS
     got = flip(send, TOK, HOPS[2], n_tok)
-    down_s_grad = outer(keep, range(ns // 2), (), (), "down_grad_1")[0]
+    down_s_grad = outer(keep, range(ns - 5), (), (), "down_grad_1")[0]
     keep, send = token_sum(keep, got, down_s_grad, BF16, "token_sum_4")
 
     got = flip(send, TOK, HOPS[1], n_tok)
-    down_s_grad, down_t_grad = outer(keep, range(ns // 2, ns), range(1), (down_s_grad,), "down_grad_2")
-    keep, send = token_sum(keep, got, down_t_grad, F32, "token_sum_2")
+    down_s_grad, down_t_grad = outer(keep, range(ns - 5, ns), range(2), (down_s_grad,), "down_grad_2")
+    keep, send = token_sum(keep, got, down_t_grad, BF16, "token_sum_2")
 
     got = flip(send, TOK, HOPS[0], n_tok)
-    down_t_grad = outer(keep, (), range(1, nt), (down_t_grad,), "down_grad_3")[0]
+    down_t_grad = outer(keep, (), range(2, nt), (down_t_grad,), "down_grad_3")[0]
     outs = [((rows, width), BF16)] * 2
     mixed, token_grad = call(last_sum_body, "token_sum_1", outs, (keep, got), "vv", pair + [pltpu.SemaphoreType.DMA((2,))], out_places="hh")
     return mixed, token_grad, down_s_grad, down_t_grad
@@ -495,8 +502,8 @@
 
     def run(*args):
         fs, ft, width = args[3].shape[1], args[6].shape[1], args[0].shape[1]
-        fits = n_tok == 8 and args[0].shape[0] == 2 and fs >= ft and ft % (4 * BLOCK) == 0
-        fits = fits and fs % (2 * BLOCK) == 0 and width % BLOCK == 0
+        fits = n_tok == 8 and args[0].shape[0] == 2 and fs >= ft and ft % (2 * WIDE) == 0
+        fits = fits and fs % WIDE == 0 and width % BLOCK == 0
         return (by_kernels if fits else by_arrays)(n_seq, n_tok, *args)
 
     return jax.shard_map(

time: 59.2 us -> 56.3 us (0.951)
  waiting for transfers between devices: 3.16 us -> 1.3 us
  Pallas kernels: 42 us -> 40.8 us
    ppermute x9, waiting for transfers between devices: 3.16 us -> 1.3 us  [flip(): return lax.ppermute(value, axes, [(i, i ^ bit) for i in range(n)])]
    pallas_call x20, Pallas kernels: 42 us -> 40.8 us  [call(): pl.pallas_call(seen, out_shape=shapes, in_specs=[pl.BlockSpec(memory_spac...]
  transfers between devices with their start and end apart: 9 -> 9, of which waited for: 5 -> 4; matrix products, arithmetic and copies ran while one was open for 0% -> 0% of each run, Pallas kernels for 37% -> 42%
where the time goes in v7:
time: 56.3 us; the launch traced here: 56.1 us
  Pallas kernels  40.8 us (72%)
  starting transfers between devices  13.1 us (23%)
  waiting for transfers between devices  1.3 us (2%)
  between operations  0.96 us (2%)
    pallas_call x20, Pallas kernels, call(): pl.pallas_call(seen, out_shape=shapes, in_specs=[pl.BlockSpec(memory_spac...  40.8 us
    ppermute x9, starting transfers between devices, flip(): return lax.ppermute(value, axes, [(i, i ^ bit) for i in range(n)])  13.1 us
    ppermute x9, waiting for transfers between devices, flip(): return lax.ppermute(value, axes, [(i, i ^ bit) for i in range(n)])  1.3 us
  transfers between devices with their start and end apart: 9, of which 4 were waited for; matrix products, arithmetic and copies ran while one was open for 0% of the time, Pallas kernels for 42%

profile of v7, /device:TPU:0, one launch (start us, length us, event | category | flops | bytes accessed | tf_op | source)
XLA Modules:
  0.0 56.1 jit_solution(9267120102770503065)
XLA Ops:
  0.6 0.7 %pack.1 = (bf16[10,1536,1024]{2,1,0:T(8,128)(2,1)S(1)}, bf16[5120,1536]{1,0:T(8,128)(2,1)S(1)}, bf16[2,3200]{1,0:T(2,128)(2,1)S(1)}) custom-call(s32[2]{0:T(128)} %refs_0_.1, bf16[2,1536]{1,0:T(2,128)(2,1)} %refs_1_.5, bf16[2,1536]{1,0:T(2,128)(2,1)} %refs_2_.2), custom_call_target="tpu_custom_call" | custom-call | tf_op jit(solution)/shard_map/pack/pallas_call | solution.py:55
  1.4 4.1 %collective-permute-start = (bf16[2,3200]{1,0:T(2,128)(2,1)S(1)}, bf16[2,3200]{1,0:T(2,128)(2,1)S(1)}, u32[]{:S(2)}, u32[]{:S(2)}) collective-permute-start(bf16[2,3200]{1,0:T(2,128)(2,1)S(1)} %get-tuple-element.25.refs_0_), channel_id=1, source_target_pairs={{0,8},{4,12},{8,0},{12,4},{16,24},{20,28},{24,16},{28,20},{1,9},{5... | collective-permute-start | bytes 38408 | tf_op jit(solution)/shard_map/ppermute | solution.py:395
  5.5 2.9 %load_gate_text.1.refs_2_ = bf16[10,1536,1024]{2,1,0:T(8,128)(2,1)S(1)} custom-call(bf16[2,3200]{1,0:T(2,128)(2,1)S(1)} %get-tuple-element.25.refs_0_, bf16[1536,2048]{1,0:T(8,128)(2,1)} %refs_1_.6, bf16[10,1536,1024]{2,1,0:T(8,128)(2,1)S(1)} %get-tuple-element.26.refs_2_, ...), custom_call_target="tpu_custom_call", output_to_operand_aliasing={{}: (2, {})} | custom-call | bytes 6291456 | tf_op jit(solution)/shard_map/load_gate_text/pallas_call | solution.py:55
  8.4 1.6 %collective-permute-start.1 = (bf16[4,3200]{1,0:T(4,128)(2,1)S(1)}, bf16[4,3200]{1,0:T(4,128)(2,1)S(1)}, u32[]{:S(2)}, u32[]{:S(2)}) collective-permute-start(bf16[4,3200]{1,0:T(4,128)(2,1)S(1)} %join_4.1.refs_0_), channel_id=1, source_target_pairs={{0,4},{4,0},{8,12},{12,8},{16,20},{20,16},{24,28},{28,24},{1,5},{5... | collective-permute-start | bytes 76808 | tf_op jit(solution)/shard_map/ppermute | solution.py:395
  10.0 2.9 %load_up_text.1.refs_2_.refs_3_.refs_4_ = bf16[10,1536,1024]{2,1,0:T(8,128)(2,1)S(1)} custom-call(bf16[4,3200]{1,0:T(4,128)(2,1)S(1)} %join_4.1.refs_0_, bf16[1536,2048]{1,0:T(8,128)(2,1)} %refs_1_.7, bf16[10,1536,1024]{2,1,0:T(8,128)(2,1)S(1)} %load_gate_text.1.refs_2_, ...), custom_call_target="tpu_custom_call", output_to_operand_aliasing={{}: (2, {})} | custom-call | bytes 6291456 | tf_op jit(solution)/shard_map/load_up_text/pallas_call | solution.py:55
  12.9 1.6 %collective-permute-start.2 = (bf16[8,3200]{1,0:T(8,128)(2,1)S(1)}, bf16[8,3200]{1,0:T(8,128)(2,1)S(1)}, u32[]{:S(2)}, u32[]{:S(2)}) collective-permute-start(bf16[8,3200]{1,0:T(8,128)(2,1)S(1)} %join_8.1.refs_0_), channel_id=1, source_target_pairs={{0,16},{4,20},{8,24},{12,28},{16,0},{20,4},{24,8},{28,12},{1,17},{... | collective-permute-start | bytes 153608 | tf_op jit(solution)/shard_map/ppermute | solution.py:395
  14.5 2.9 %load_down_text.1.refs_3_.refs_5_ = bf16[5120,1536]{1,0:T(8,128)(2,1)S(1)} custom-call(bf16[8,3200]{1,0:T(8,128)(2,1)S(1)} %join_8.1.refs_0_, bf16[2048,1536]{1,0:T(8,128)(2,1)} %refs_1_.8, bf16[5120,1536]{1,0:T(8,128)(2,1)S(1)} %get-tuple-element.27.refs_3_.refs_2_, ...), custom_call_target="tpu_custom_call", output_to_operand_aliasing={{}: (2, {})} | custom-call | bytes 6291456 | tf_op jit(solution)/shard_map/load_down_text/pallas_call | solution.py:55
  17.5 10.3 %hidden_partials.1 = (f32[3,16,1536]{2,1,0:T(8,128)S(1)}, f32[3,16,1536]{2,1,0:T(8,128)S(1)}, bf16[10,1536,1024]{2,1,0:T(8,128)(2,1)S(1)}, bf16[5120,1536]{1,0:T(8,128)(2,1)S(1)}) custom-call(bf16[16,3200]{1,0:T(8,128)(2,1)S(1)} %join_16.1.refs_0_.refs_1_, bf16[1536,3072]{1,0:T(8,128)(2,1)} %refs_1_.9, ...), custom_call_target="tpu_custom_call", output_to_operand_aliasing={{2}: (4, {}), {3}: (5, {})} | custom-call | flops 754974720 | bytes 28311552 | tf_op jit(solution)/shard_map/hidden_partials/pallas_call | solution.py:55
  27.9 1.4 %turn_1.1.refs_2_.refs_0_ = bf16[10,1536,1024]{2,1,0:T(8,128)(2,1)S(1)} custom-call(bf16[10,1536,1024]{2,1,0:T(8,128)(2,1)S(1)} %get-tuple-element.30.refs_0_, bf16[5120,1536]{1,0:T(8,128)(2,1)S(1)} %get-tuple-element.31.refs_1_.refs_3_.refs_2_.refs_5_), custom_call_target="tpu_custom_call", output_to_operand_aliasing={{}: (0, {})} | custom-call | bytes 15728640 | tf_op jit(solution)/shard_map/turn_1/pallas_call | solution.py:55
  29.3 0.1 collective-permute-done.3.refs_1_
  29.5 1.6 %collective-permute-start.4 = (bf16[3,16,1536]{2,1,0:T(8,128)(2,1)S(1)}, bf16[3,16,1536]{2,1,0:T(8,128)(2,1)S(1)}, u32[]{:S(2)}, u32[]{:S(2)}) collective-permute-start(bf16[3,16,1536]{2,1,0:T(8,128)(2,1)S(1)} %get-tuple-element.33), channel_id=1, source_target_pairs={{0,2},{1,3},{2,0},{3,1},{4,6},{5,7},{6,4},{7,5},{8,10},{9,11},{10,... | collective-permute-start | bytes 442376 | tf_op jit(solution)/shard_map/ppermute | solution.py:395
  31.0 3.9 %turn_2.1.refs_2_.refs_3_.refs_4_ = bf16[10,1536,1024]{2,1,0:T(8,128)(2,1)S(1)} custom-call(bf16[10,1536,1024]{2,1,0:T(8,128)(2,1)S(1)} %turn_1.1.refs_2_.refs_0_, bf16[5120,1536]{1,0:T(8,128)(2,1)S(1)} %get-tuple-element.31.refs_1_.refs_3_.refs_2_.refs_5_), custom_call_target="tpu_custom_call", output_to_operand_aliasing={{}: (0, {})} | custom-call | bytes 47185920 | tf_op jit(solution)/shard_map/turn_2/pallas_call | solution.py:55
  34.9 0.7 %collective-permute-done.4.refs_1_ = bf16[3,16,1536]{2,1,0:T(8,128)(2,1)S(1)} collective-permute-done((bf16[3,16,1536]{2,1,0:T(8,128)(2,1)S(1)}, bf16[3,16,1536]{2,1,0:T(8,128)(2,1)S(1)}, u32[]{:S(2)}, u32[]{:S(2)}) %collective-permute-start.4) | collective-permute-done | bytes 147488 | tf_op jit(solution)/shard_map/ppermute | solution.py:395
  35.8 1.2 %mixed_own.1.refs_3_ = f32[16,1536]{1,0:T(8,128)S(1)} custom-call(bf16[16,3200]{1,0:T(8,128)(2,1)S(1)} %join_16.1.refs_0_.refs_1_, bf16[3,16,1536]{2,1,0:T(8,128)(2,1)S(1)} %hidden.1.refs_1_, bf16[5120,1536]{1,0:T(8,128)(2,1)S(1)} %get-tuple-element.31.refs_1_.refs_3_.refs_2_.refs_5_, bf16[10,1536,1024]{2,1,0:T(8,128)(2,1)S(1)} %turn_2.1.refs_2_.refs_3_.refs_4_), custom_call_target="tpu_custom_call" | custom-call | flops 125829120 | tf_op jit(solution)/shard_map/mixed_own/pallas_call | solution.py:55
  37.0 0.2 collective-permute-done.5.refs_2_
  37.2 5.4 %token_partials.1 = (f32[8,3072]{1,0:T(8,128)S(1)}, bf16[8,3072]{1,0:T(8,128)(2,1)S(1)}, bf16[16,3072]{1,0:T(8,128)(2,1)S(1)}, bf16[16,2048]{1,0:T(8,128)(2,1)S(1)}) custom-call(bf16[16,3200]{1,0:T(8,128)(2,1)S(1)} %join_16.1.refs_0_.refs_1_, bf16[3,16,1536]{2,1,0:T(8,128)(2,1)S(1)} %hidden.1.refs_1_, ...), custom_call_target="tpu_custom_call" | custom-call | flops 754974720 | tf_op jit(solution)/shard_map/token_partials/pallas_call | solution.py:55
  42.6 1.2 %collective-permute-start.6 = (bf16[8,3072]{1,0:T(8,128)(2,1)S(1)}, bf16[8,3072]{1,0:T(8,128)(2,1)S(1)}, u32[]{:S(2)}, u32[]{:S(2)}) collective-permute-start(bf16[8,3072]{1,0:T(8,128)(2,1)S(1)} %get-tuple-element.35), channel_id=1, source_target_pairs={{0,16},{4,20},{8,24},{12,28},{16,0},{20,4},{24,8},{28,12},{1,17},{... | collective-permute-start | bytes 147464 | tf_op jit(solution)/shard_map/ppermute | solution.py:395
  43.8 2.9 %down_grad_1.1.refs_2_.refs_4_ = bf16[3072,1536]{1,0:T(8,128)(2,1)} custom-call(f32[8,3072]{1,0:T(8,128)S(1)} %get-tuple-element.34.refs_0_, bf16[16,3200]{1,0:T(8,128)(2,1)S(1)} %join_16.1.refs_0_.refs_1_, bf16[16,3072]{1,0:T(8,128)(2,1)S(1)} %get-tuple-element.36.refs_2_, bf16[16,2048]{1,0:T(8,128)(2,1)S(1)} %get-tuple-element.37.refs_3_), custom_call_target="tpu_custom_call" | custom-call | flops 88080384 | bytes 5505024 | tf_op jit(solution)/shard_map/down_grad_1/pallas_call | solution.py:55
  46.7 1.0 %collective-permute-start.7 = (bf16[4,3072]{1,0:T(4,128)(2,1)S(1)}, bf16[4,3072]{1,0:T(4,128)(2,1)S(1)}, u32[]{:S(2)}, u32[]{:S(2)}) collective-permute-start(bf16[4,3072]{1,0:T(4,128)(2,1)S(1)} %get-tuple-element.39), channel_id=1, source_target_pairs={{0,4},{4,0},{8,12},{12,8},{16,20},{20,16},{24,28},{28,24},{1,5},{5... | collective-permute-start | bytes 73736 | tf_op jit(solution)/shard_map/ppermute | solution.py:395
  47.7 2.9 %down_grad_2.1 = (bf16[3072,1536]{1,0:T(8,128)(2,1)}, bf16[2048,1536]{1,0:T(8,128)(2,1)}) custom-call(f32[4,3072]{1,0:T(4,128)S(1)} %get-tuple-element.38.refs_0_, bf16[16,3200]{1,0:T(8,128)(2,1)S(1)} %join_16.1.refs_0_.refs_1_, bf16[16,3072]{1,0:T(8,128)(2,1)S(1)} %get-tuple-element.36.refs_2_, ...), custom_call_target="tpu_custom_call", output_to_operand_aliasing={{0}: (4, {})} | custom-call | flops 88080384 | bytes 5505024 | tf_op jit(solution)/shard_map/down_grad_2/pallas_call | solution.py:55
  50.6 1.8 %collective-permute-start.8 = (bf16[2,3072]{1,0:T(2,128)(2,1)S(1)}, bf16[2,3072]{1,0:T(2,128)(2,1)S(1)}, u32[]{:S(2)}, u32[]{:S(2)}) collective-permute-start(bf16[2,3072]{1,0:T(2,128)(2,1)S(1)} %get-tuple-element.42), channel_id=1, source_target_pairs={{0,8},{4,12},{8,0},{12,4},{16,24},{20,28},{24,16},{28,20},{1,9},{5... | collective-permute-start | bytes 36872 | tf_op jit(solution)/shard_map/ppermute | solution.py:395
  52.5 2.6 %down_grad_3.1 = bf16[2048,1536]{1,0:T(8,128)(2,1)} custom-call(f32[2,3072]{1,0:T(2,128)S(1)} %get-tuple-element.41.refs_0_, bf16[16,3200]{1,0:T(8,128)(2,1)S(1)} %join_16.1.refs_0_.refs_1_, bf16[16,3072]{1,0:T(8,128)(2,1)S(1)} %get-tuple-element.36.refs_2_, bf16[16,2048]{1,0:T(8,128)(2,1)S(1)} %get-tuple-element.37.refs_3_, ...), custom_call_target="tpu_custom_call", output_to_operand_aliasing={{}: (4, {})} | custom-call | flops 75497472 | bytes 4718592 | tf_op jit(solution)/shard_map/down_grad_3/pallas_call | solution.py:55
  55.1 0.2 collective-permute-done.8.refs_1_
  55.3 0.6 %token_sum_1.1 = (bf16[2,1536]{1,0:T(2,128)(2,1)}, bf16[2,1536]{1,0:T(2,128)(2,1)}) custom-call(f32[2,3072]{1,0:T(2,128)S(1)} %get-tuple-element.41.refs_0_, bf16[2,3072]{1,0:T(2,128)(2,1)S(1)} %collective-permute-done.8.refs_1_), custom_call_target="tpu_custom_call" | custom-call | tf_op jit(solution)/shard_map/token_sum_1/pallas_call | solution.py:55
  (14 shorter events, 0.4 us)
Async XLA Ops:
  1.4 7.0 %collective-permute-start = (bf16[2,3200]{1,0:T(2,128)(2,1)S(1)}, bf16[2,3200]{1,0:T(2,128)(2,1)S(1)}, u32[]{:S(2)}, u32[]{:S(2)}) collective-permute-start(bf16[2,3200]{1,0:T(2,128)(2,1)S(1)} %get-tuple-element.25.refs_0_), channel_id=1, source_target_pairs={{0,8},{4,12},{8,0},{12,4},{16,24},{20,28},{24,16},{28,20},{1,9},{5... | collective-permute-start | bytes 38408 | tf_op jit(solution)/shard_map/ppermute | solution.py:395
  8.4 4.5 %collective-permute-start.1 = (bf16[4,3200]{1,0:T(4,128)(2,1)S(1)}, bf16[4,3200]{1,0:T(4,128)(2,1)S(1)}, u32[]{:S(2)}, u32[]{:S(2)}) collective-permute-start(bf16[4,3200]{1,0:T(4,128)(2,1)S(1)} %join_4.1.refs_0_), channel_id=1, source_target_pairs={{0,4},{4,0},{8,12},{12,8},{16,20},{20,16},{24,28},{28,24},{1,5},{5... | collective-permute-start | bytes 76808 | tf_op jit(solution)/shard_map/ppermute | solution.py:395
  12.9 4.5 %collective-permute-start.2 = (bf16[8,3200]{1,0:T(8,128)(2,1)S(1)}, bf16[8,3200]{1,0:T(8,128)(2,1)S(1)}, u32[]{:S(2)}, u32[]{:S(2)}) collective-permute-start(bf16[8,3200]{1,0:T(8,128)(2,1)S(1)} %join_8.1.refs_0_), channel_id=1, source_target_pairs={{0,16},{4,20},{8,24},{12,28},{16,0},{20,4},{24,8},{28,12},{1,17},{... | collective-permute-start | bytes 153608 | tf_op jit(solution)/shard_map/ppermute | solution.py:395
  27.8 1.6 %collective-permute-start.3 = (f32[3,16,1536]{2,1,0:T(8,128)S(1)}, f32[3,16,1536]{2,1,0:T(8,128)S(1)}, u32[]{:S(2)}, u32[]{:S(2)}) collective-permute-start(f32[3,16,1536]{2,1,0:T(8,128)S(1)} %get-tuple-element.29), channel_id=1, source_target_pairs={{0,1},{1,0},{2,3},{3,2},{4,5},{5,4},{6,7},{7,6},{8,9},{9,8},{10,11... | collective-permute-start | bytes 884744 | tf_op jit(solution)/shard_map/ppermute | solution.py:395
  29.5 6.2 %collective-permute-start.4 = (bf16[3,16,1536]{2,1,0:T(8,128)(2,1)S(1)}, bf16[3,16,1536]{2,1,0:T(8,128)(2,1)S(1)}, u32[]{:S(2)}, u32[]{:S(2)}) collective-permute-start(bf16[3,16,1536]{2,1,0:T(8,128)(2,1)S(1)} %get-tuple-element.33), channel_id=1, source_target_pairs={{0,2},{1,3},{2,0},{3,1},{4,6},{5,7},{6,4},{7,5},{8,10},{9,11},{10,... | collective-permute-start | bytes 442376 | tf_op jit(solution)/shard_map/ppermute | solution.py:395
  35.8 1.4 %collective-permute-start.5 = (bf16[3,16,1536]{2,1,0:T(8,128)(2,1)S(1)}, bf16[3,16,1536]{2,1,0:T(8,128)(2,1)S(1)}, u32[]{:S(2)}, u32[]{:S(2)}) collective-permute-start(bf16[3,16,1536]{2,1,0:T(8,128)(2,1)S(1)} %hidden.1.refs_1_), channel_id=1, source_target_pairs={{0,1},{1,0},{2,3},{3,2},{4,5},{5,4},{6,7},{7,6},{8,9},{9,8},{10,11... | collective-permute-start | bytes 442376 | tf_op jit(solution)/shard_map/ppermute | solution.py:395
  42.6 4.1 %collective-permute-start.6 = (bf16[8,3072]{1,0:T(8,128)(2,1)S(1)}, bf16[8,3072]{1,0:T(8,128)(2,1)S(1)}, u32[]{:S(2)}, u32[]{:S(2)}) collective-permute-start(bf16[8,3072]{1,0:T(8,128)(2,1)S(1)} %get-tuple-element.35), channel_id=1, source_target_pairs={{0,16},{4,20},{8,24},{12,28},{16,0},{20,4},{24,8},{28,12},{1,17},{... | collective-permute-start | bytes 147464 | tf_op jit(solution)/shard_map/ppermute | solution.py:395
  46.7 3.9 %collective-permute-start.7 = (bf16[4,3072]{1,0:T(4,128)(2,1)S(1)}, bf16[4,3072]{1,0:T(4,128)(2,1)S(1)}, u32[]{:S(2)}, u32[]{:S(2)}) collective-permute-start(bf16[4,3072]{1,0:T(4,128)(2,1)S(1)} %get-tuple-element.39), channel_id=1, source_target_pairs={{0,4},{4,0},{8,12},{12,8},{16,20},{20,16},{24,28},{28,24},{1,5},{5... | collective-permute-start | bytes 73736 | tf_op jit(solution)/shard_map/ppermute | solution.py:395
  50.6 4.7 %collective-permute-start.8 = (bf16[2,3072]{1,0:T(2,128)(2,1)S(1)}, bf16[2,3072]{1,0:T(2,128)(2,1)S(1)}, u32[]{:S(2)}, u32[]{:S(2)}) collective-permute-start(bf16[2,3072]{1,0:T(2,128)(2,1)S(1)} %get-tuple-element.42), channel_id=1, source_target_pairs={{0,8},{4,12},{8,0},{12,4},{16,24},{20,28},{24,16},{28,20},{1,9},{5... | collective-permute-start | bytes 36872 | tf_op jit(solution)/shard_map/ppermute | solution.py:395

commit v8 on v7

--- a/solution.py
+++ b/solution.py
@@ -77,7 +77,7 @@
     return arr_ref[:, arr_ref.shape[1] - 1 :] == 0
 
 
-def pack_body(kind_hbm, tok_hbm, cot_hbm, wide_ref, tall_ref, out_ref, tok_ref, cot_ref, kind_ref, sems):
+def pack_body(kind_hbm, tok_hbm, cot_hbm, wide_ref, out_ref, tok_ref, cot_ref, kind_ref, sems):
     copies = [
         pltpu.make_async_copy(kind_hbm, kind_ref, sems.at[2]),
         pltpu.make_async_copy(tok_hbm, tok_ref, sems.at[0]),
@@ -120,12 +120,6 @@
     return wide_ref.at[i // per, pl.ds(r * BLOCK, BLOCK), pl.ds(i % per * BLOCK, BLOCK)]
 
 
-def row_blocks(src, tall, first):
-    return [
-        [(src.at[pl.ds(i, BLOCK)], tall.at[pl.ds(first + i, BLOCK)])] for i in range(0, src.shape[0], BLOCK)
-    ]
-
-
 def started(groups, sems):
     copies, count = [], 0
     for group in groups:
@@ -143,11 +137,7 @@
 
 
 def load_body(first, after_ref, src_hbm, old_ref, place_ref, sems):
-    if place_ref.ndim == 3:
-        groups = column_blocks(src_hbm, place_ref, first, 4)
-    else:
-        groups = row_blocks(src_hbm, place_ref, first)
-    for group in started(groups, sems):
+    for group in started(column_blocks(src_hbm, place_ref, first, 4), sems):
         wait(group)
 
 
@@ -171,13 +161,14 @@
 
 
 def partials_body(
-    arr_ref, gs_hbm, us_hbm, ds_hbm, old_wide, old_tall, mine_ref, theirs_ref, wide_ref, tall_ref, part, sems
+    arr_ref, dt_ref, ds_ref, ut_hbm, gs_hbm, us_hbm, old_wide, mine_ref, theirs_ref, wide_ref, part, sems
 ):
-    fs, width = ds_hbm.shape
-    ft = tall_ref.shape[0] - fs
+    fs, width = ds_ref.shape
+    ft = dt_ref.shape[0]
     ns, nt = fs // WIDE, ft // WIDE
-    groups = column_blocks(gs_hbm, wide_ref, 2 * nt, 2) + column_blocks(us_hbm, wide_ref, 2 * nt + ns, 2)
-    copies = started(groups + row_blocks(ds_hbm, tall_ref, 0), sems)
+    groups = column_blocks(ut_hbm, wide_ref, nt, 2) + column_blocks(gs_hbm, wide_ref, 2 * nt, 2)
+    groups += column_blocks(us_hbm, wide_ref, 2 * nt + ns, 2)
+    copies = started(groups, sems)
     x = arr_ref[:, :width]
     c = arr_ref[:, width : 2 * width]
     speech = is_speech(arr_ref)
@@ -193,19 +184,19 @@
             place = i if pick else beside(i // BLOCK, fs, ft)
             put(k, place, value[:, i - start : i - start + BLOCK], pick)
 
+    for k, ref in enumerate((dt_ref, ds_ref)):
+        for i in range(0, ref.shape[0], BLOCK):
+            place = i if k else beside(i // BLOCK, fs, ft)
+            put(2, place, contract_last(c, ref[i : i + BLOCK, :]), k == 1)
     for k in range(2):
         for i in range(nt):
+            if k == 1:
+                wait(copies[i])
             put_wide(k, i * WIDE, times(x, wide_ref[k * nt + i]), False)
-    for i in range(ft // BLOCK):
-        rows = slice(fs + i * BLOCK, fs + (i + 1) * BLOCK)
-        put(2, beside(i, fs, ft), contract_last(c, tall_ref[rows, :]), False)
     for k in range(2):
         for i in range(ns):
-            wait(copies[k * ns + i])
+            wait(copies[nt + k * ns + i])
             put_wide(k, i * WIDE, times(x, wide_ref[2 * nt + k * ns + i]), True)
-    for i in range(fs // BLOCK):
-        wait(copies[2 * ns + i])
-        put(2, i * BLOCK, contract_last(c, tall_ref[i * BLOCK : (i + 1) * BLOCK, :]), True)
     half = fs // 2
     odd = parity()
     for k in range(3):
@@ -213,20 +204,19 @@
         theirs_ref[k] = part[k, :, pl.ds(pl.multiple_of((1 - odd) * half, half), half)]
 
 
-def partials(arr, gate_s, up_s, down_s, wide, tall):
+def partials(arr, up_t, gate_s, up_s, down_t, down_s, wide):
     rows, fs = arr.shape[0], gate_s.shape[1]
     half = ((3, rows, fs // 2), F32)
-    n_sems = 4 * fs // WIDE + fs // BLOCK
     return call(
         partials_body,
         "hidden_partials",
-        [half, half, like(wide), like(tall)],
-        (arr, gate_s, up_s, down_s, wide, tall),
-        "vhhhvv",
-        [pltpu.VMEM((3, rows, fs), F32), pltpu.SemaphoreType.DMA((n_sems,))],
-        2 * rows * (wide.size + tall.size),
-        size_of(gate_s, up_s, down_s),
-        aliases={4: 2, 5: 3},
+        [half, half, like(wide)],
+        (arr, down_t, down_s, up_t, gate_s, up_s, wide),
+        "vvvhhhv",
+        [pltpu.VMEM((3, rows, fs), F32), pltpu.SemaphoreType.DMA(((4 * fs + 2 * up_t.shape[1]) // WIDE,))],
+        2 * rows * (wide.size + down_s.size + down_t.size),
+        size_of(up_t, gate_s, up_s),
+        aliases={6: 2},
     )
 
 
@@ -262,7 +252,7 @@
         place[...] = turned
 
 
-def turn(wide, tall, first, count, name):
+def turn(wide, also, first, count, name):
     return call(
         functools.partial(turn_body, first, count),
         name,
@@ -271,29 +261,28 @@
         "v",
         traffic=4 * count * wide.shape[1] * BLOCK,
         aliases={0: 0},
-        also=(tall,),
+        also=also,
     )[0]
 
 
-def mixed_half(h, speech, side, tall_ref, fs):
-    half_s, half_t, width = fs // 2, (tall_ref.shape[0] - fs) // 2, tall_ref.shape[1]
+def mixed_half(h, speech, side, dt_ref, ds_ref):
+    half_s, half_t, width = ds_ref.shape[0] // 2, dt_ref.shape[0] // 2, ds_ref.shape[1]
     zero = jnp.zeros_like(h)
     hs, ht = jnp.where(speech, h, zero), jnp.where(speech, zero, h)[:, :half_t]
     rows_s = pl.ds(pl.multiple_of(side * half_s, BLOCK), half_s)
-    rows_t = pl.ds(pl.multiple_of(fs + side * half_t, BLOCK), half_t)
+    rows_t = pl.ds(pl.multiple_of(side * half_t, BLOCK), half_t)
     cuts = [slice(i, i + BLOCK) for i in range(0, width, BLOCK)]
-    return [times(hs, tall_ref[rows_s, cut]) + times(ht, tall_ref[rows_t, cut]) for cut in cuts]
-
-
-def mixed_own_body(arr_ref, done_ref, tall_ref, out_ref):
-    fs = 2 * done_ref.shape[2]
-    parts = mixed_half(done_ref[0], is_speech(arr_ref), parity(), tall_ref, fs)
+    return [times(hs, ds_ref[rows_s, cut]) + times(ht, dt_ref[rows_t, cut]) for cut in cuts]
+
+
+def mixed_own_body(arr_ref, done_ref, dt_ref, ds_ref, out_ref):
+    parts = mixed_half(done_ref[0], is_speech(arr_ref), parity(), dt_ref, ds_ref)
     for i, value in enumerate(parts):
         out_ref[:, i * BLOCK : (i + 1) * BLOCK] = value
 
 
 def back_body(
-    turned, arr_ref, done_ref, other_ref, own_ref, wide_ref, tall_ref,
+    turned, arr_ref, done_ref, other_ref, own_ref, wide_ref, dt_ref, ds_ref,
     keep_ref, send_ref, hs_ref, ht_ref, dgs, dgt, dus, dut, out,
 ):
     speech = is_speech(arr_ref)
@@ -309,8 +298,8 @@
         for i in range(nt):
             start = beside(i, fs, ft)
             t[:, i * BLOCK : (i + 1) * BLOCK] = value[:, start : start + BLOCK]
-    width = tall_ref.shape[1]
-    for i, value in enumerate(mixed_half(other_ref[0], speech, 1 - parity(), tall_ref, fs)):
+    width = ds_ref.shape[1]
+    for i, value in enumerate(mixed_half(other_ref[0], speech, 1 - parity(), dt_ref, ds_ref)):
         cut = slice(i * BLOCK, (i + 1) * BLOCK)
         out[:, cut] = own_ref[:, cut] + value
     blocks = [(dgt, nt), (dut, nt), (dgs, ns), (dus, ns)]
@@ -327,17 +316,18 @@
     send_ref[...] = out[half:].astype(BF16)
 
 
-def back(arr, done, other, own, wide, tall, turned, fs, ft):
-    rows, width = arr.shape[0], tall.shape[1]
+def back(arr, done, other, own, wide, down_t, down_s, turned):
+    rows, width = arr.shape[0], down_s.shape[1]
+    fs, ft = down_s.shape[0], down_t.shape[0]
     hidden = [((rows, fs), BF16), ((rows, ft), BF16)]
     return call(
         functools.partial(back_body, turned),
         "token_partials",
         [((rows // 2, 2 * width), F32), ((rows // 2, 2 * width), BF16)] + hidden,
-        (arr, done, other, own, wide, tall),
-        "vvvvvv",
+        (arr, done, other, own, wide, down_t, down_s),
+        "vvvvvvv",
         [pltpu.VMEM(*s) for s in hidden + hidden] + [pltpu.VMEM((rows, 2 * width), F32)],
-        2 * rows * (wide.size + tall.size),
+        2 * rows * (wide.size + down_t.size + down_s.size),
     )
 
 
@@ -399,38 +389,34 @@
     rows, width = tokens.shape
     fs, ft = gate_s.shape[1], gate_t.shape[1]
     wide = ((2 * (fs + ft) // WIDE, width, WIDE), BF16)
-    tall = ((fs + ft, width), BF16)
     pair = [pltpu.VMEM((rows, width), BF16)] * 2
 
     packed = ((rows, 2 * width + 128), BF16)
     scratch = pair + [pltpu.SMEM((rows,), jnp.int32), pltpu.SemaphoreType.DMA((3,))]
-    wide, tall, arr = call(pack_body, "pack", [wide, tall, packed], (modality, tokens, cotangent), "hhh", scratch)
+    wide, arr = call(pack_body, "pack", [wide, packed], (modality, tokens, cotangent), "hhh", scratch)
     got = flip(arr, TOK, HOPS[0], n_tok)
-    wide = load(arr, gate_t, wide, (tall,), 0, "load_gate_text")
-    arr = join(arr, got, "join_4", (wide, tall))
+    wide = load(arr, gate_t, wide, (), 0, "load_gate_text")
+    arr = join(arr, got, "join_4", (wide,))
     got = flip(arr, TOK, HOPS[1], n_tok)
-    wide = load(arr, up_t, wide, (tall,), ft // WIDE, "load_up_text")
-    arr = join(arr, got, "join_8", (wide, tall))
-    got = flip(arr, TOK, HOPS[2], n_tok)
-    tall = load(arr, down_t, tall, (wide,), fs, "load_down_text")
-    arr = join(arr, got, "join_16", (wide, tall))
-
-    mine, theirs, wide, tall = partials(arr, gate_s, up_s, down_s, wide, tall)
+    arr = join(arr, got, "join_8", (wide,))
+    arr = join(arr, flip(arr, TOK, HOPS[2], n_tok), "join_16", (wide, down_t, down_s))
+
+    mine, theirs, wide = partials(arr, up_t, gate_s, up_s, down_t, down_s, wide)
     blocks = 2 * (fs + ft) // BLOCK
     got = flip(theirs, "seq", 1, n_seq)
-    wide = turn(wide, tall, 0, TURN_FIRST, "turn_1")
+    wide = turn(wide, (down_t, down_s), 0, TURN_FIRST, "turn_1")
     total, send = call(
-        core_sum_body, "core_sum", [like(mine), (mine.shape, BF16)], (mine, got), "vv", also=(wide, tall)
+        core_sum_body, "core_sum", [like(mine), (mine.shape, BF16)], (mine, got), "vv", also=(wide, down_t, down_s)
     )
     got = flip(send, "seq", 2, n_seq)
-    wide = turn(wide, tall, TURN_FIRST, blocks - TURN_FIRST, "turn_2")
-    done = call(hidden_body, "hidden", [(mine.shape, BF16)], (total, got), "vv", also=(wide, tall))[0]
+    wide = turn(wide, (down_t, down_s), TURN_FIRST, blocks - TURN_FIRST, "turn_2")
+    done = call(hidden_body, "hidden", [(mine.shape, BF16)], (total, got), "vv", also=(wide, down_t, down_s))[0]
     other = flip(done, "seq", 1, n_seq)
     own = call(
-        mixed_own_body, "mixed_own", [((arr.shape[0], width), F32)], (arr, done, tall), "vvv",
-        flops=arr.shape[0] * tall.size, also=(wide,),
+        mixed_own_body, "mixed_own", [((arr.shape[0], width), F32)], (arr, done, down_t, down_s), "vvvv",
+        flops=arr.shape[0] * (down_s.size + down_t.size), also=(wide,),
     )[0]
-    keep, send, hs, ht = back(arr, done, other, own, wide, tall, range(blocks), fs, ft)
+    keep, send, hs, ht = back(arr, done, other, own, wide, down_t, down_s, range(blocks))
 
     def outer(after, speech, text, old, name):
         count = len(speech) + len(text)

time: 56.3 us -> 55.3 us (0.982)
  Pallas kernels: 40.8 us -> 34 us
  waiting for transfers between devices: 1.3 us -> 5.99 us
  starting transfers between devices: 13.1 us -> 14 us
    pallas_call x20 -> x18, Pallas kernels: 40.8 us -> 34 us  [call(): pl.pallas_call(seen, out_shape=shapes, in_specs=[pl.BlockSpec(memory_spac...]
    ppermute x9, waiting for transfers between devices: 1.3 us -> 5.99 us  [flip(): return lax.ppermute(value, axes, [(i, i ^ bit) for i in range(n)])]
    ppermute x9, starting transfers between devices: 13.1 us -> 14 us  [flip(): return lax.ppermute(value, axes, [(i, i ^ bit) for i in range(n)])]
  transfers between devices with their start and end apart: 9 -> 9, of which waited for: 4 -> 5; matrix products, arithmetic and copies ran while one was open for 0% -> 0% of each run, Pallas kernels for 42% -> 32%
where the time goes in v8:
time: 55.3 us; the launch traced here: 55.1 us
  Pallas kernels  34 us (61%)
  starting transfers between devices  14 us (25%)
  waiting for transfers between devices  5.99 us (11%)
  between operations  1.02 us (2%)
    pallas_call x18, Pallas kernels, call(): pl.pallas_call(seen, out_shape=shapes, in_specs=[pl.BlockSpec(memory_spac...  34 us
    ppermute x9, starting transfers between devices, flip(): return lax.ppermute(value, axes, [(i, i ^ bit) for i in range(n)])  14 us
    ppermute x9, waiting for transfers between devices, flip(): return lax.ppermute(value, axes, [(i, i ^ bit) for i in range(n)])  5.99 us
  transfers between devices with their start and end apart: 9, of which 5 were waited for; matrix products, arithmetic and copies ran while one was open for 0% of the time, Pallas kernels for 32%

profile of v8, /device:TPU:0, one launch (start us, length us, event | category | flops | bytes accessed | tf_op | source)
XLA Modules:
  0.0 55.1 jit_solution(263092981725579937)
XLA Ops:
  0.6 0.7 %pack.1 = (bf16[10,1536,1024]{2,1,0:T(8,128)(2,1)S(1)}, bf16[2,3200]{1,0:T(2,128)(2,1)S(1)}) custom-call(s32[2]{0:T(128)} %refs_0_.1, bf16[2,1536]{1,0:T(2,128)(2,1)} %refs_1_.5, bf16[2,1536]{1,0:T(2,128)(2,1)} %refs_2_.5), custom_call_target="tpu_custom_call" | custom-call | tf_op jit(solution)/shard_map/pack/pallas_call | solution.py:55
  1.4 4.1 %collective-permute-start = (bf16[2,3200]{1,0:T(2,128)(2,1)S(1)}, bf16[2,3200]{1,0:T(2,128)(2,1)S(1)}, u32[]{:S(2)}, u32[]{:S(2)}) collective-permute-start(bf16[2,3200]{1,0:T(2,128)(2,1)S(1)} %get-tuple-element.23.refs_0_), channel_id=1, source_target_pairs={{0,8},{4,12},{8,0},{12,4},{16,24},{20,28},{24,16},{28,20},{1,9},{5... | collective-permute-start | bytes 38408 | tf_op jit(solution)/shard_map/ppermute | solution.py:385
  5.5 2.9 %load_gate_text.1.refs_2_.refs_6_ = bf16[10,1536,1024]{2,1,0:T(8,128)(2,1)S(1)} custom-call(bf16[2,3200]{1,0:T(2,128)(2,1)S(1)} %get-tuple-element.23.refs_0_, bf16[1536,2048]{1,0:T(8,128)(2,1)} %refs_1_.6, bf16[10,1536,1024]{2,1,0:T(8,128)(2,1)S(1)} %get-tuple-element.24.refs_2_), custom_call_target="tpu_custom_call", output_to_operand_aliasing={{}: (2, {})} | custom-call | bytes 6291456 | tf_op jit(solution)/shard_map/load_gate_text/pallas_call | solution.py:55
  8.5 1.6 %collective-permute-start.1 = (bf16[4,3200]{1,0:T(4,128)(2,1)S(1)}, bf16[4,3200]{1,0:T(4,128)(2,1)S(1)}, u32[]{:S(2)}, u32[]{:S(2)}) collective-permute-start(bf16[4,3200]{1,0:T(4,128)(2,1)S(1)} %join_4.1.refs_0_), channel_id=1, source_target_pairs={{0,4},{4,0},{8,12},{12,8},{16,20},{20,16},{24,28},{28,24},{1,5},{5... | collective-permute-start | bytes 76808 | tf_op jit(solution)/shard_map/ppermute | solution.py:385
  10.1 2.3 %collective-permute-done.1.refs_1_ = bf16[4,3200]{1,0:T(4,128)(2,1)S(1)} collective-permute-done((bf16[4,3200]{1,0:T(4,128)(2,1)S(1)}, bf16[4,3200]{1,0:T(4,128)(2,1)S(1)}, u32[]{:S(2)}, u32[]{:S(2)}) %collective-permute-start.1) | collective-permute-done | bytes 25632 | tf_op jit(solution)/shard_map/ppermute | solution.py:385
  12.4 1.6 %collective-permute-start.2 = (bf16[8,3200]{1,0:T(8,128)(2,1)S(1)}, bf16[8,3200]{1,0:T(8,128)(2,1)S(1)}, u32[]{:S(2)}, u32[]{:S(2)}) collective-permute-start(bf16[8,3200]{1,0:T(8,128)(2,1)S(1)} %join_8.1.refs_0_), channel_id=1, source_target_pairs={{0,16},{4,20},{8,24},{12,28},{16,0},{20,4},{24,8},{28,12},{1,17},{... | collective-permute-start | bytes 153608 | tf_op jit(solution)/shard_map/ppermute | solution.py:385
  14.0 2.6 %collective-permute-done.2.refs_1_ = bf16[8,3200]{1,0:T(8,128)(2,1)S(1)} collective-permute-done((bf16[8,3200]{1,0:T(8,128)(2,1)S(1)}, bf16[8,3200]{1,0:T(8,128)(2,1)S(1)}, u32[]{:S(2)}, u32[]{:S(2)}) %collective-permute-start.2) | collective-permute-done | bytes 51232 | tf_op jit(solution)/shard_map/ppermute | solution.py:385
  16.6 9.4 %hidden_partials.1 = (f32[3,16,1536]{2,1,0:T(8,128)S(1)}, f32[3,16,1536]{2,1,0:T(8,128)S(1)}, bf16[10,1536,1024]{2,1,0:T(8,128)(2,1)S(1)}) custom-call(bf16[16,3200]{1,0:T(8,128)(2,1)S(1)} %join_16.1.refs_0_.refs_1_, bf16[2048,1536]{1,0:T(8,128)(2,1)S(1)} %bitcast.3, bf16[3072,1536]{1,0:T(8,128)(2,1)S(1)} %bitcast.1, ...), custom_call_target="tpu_custom_call", output_to_operand_aliasing={{2}: (6, {})} | custom-call | flops 754974720 | bytes 25165824 | tf_op jit(solution)/shard_map/hidden_partials/pallas_call | solution.py:55
  26.0 0.1 collective-permute-start.3
  26.1 1.4 %turn_1.1.refs_2_.refs_0_ = bf16[10,1536,1024]{2,1,0:T(8,128)(2,1)S(1)} custom-call(bf16[10,1536,1024]{2,1,0:T(8,128)(2,1)S(1)} %get-tuple-element.27.refs_0_, bf16[2048,1536]{1,0:T(8,128)(2,1)S(1)} %bitcast.3, bf16[3072,1536]{1,0:T(8,128)(2,1)S(1)} %bitcast.1), custom_call_target="tpu_custom_call", output_to_operand_aliasing={{}: (0, {})} | custom-call | bytes 15728640 | tf_op jit(solution)/shard_map/turn_1/pallas_call | solution.py:55
  27.5 0.1 collective-permute-done.3.refs_1_
  27.7 1.6 %collective-permute-start.4 = (bf16[3,16,1536]{2,1,0:T(8,128)(2,1)S(1)}, bf16[3,16,1536]{2,1,0:T(8,128)(2,1)S(1)}, u32[]{:S(2)}, u32[]{:S(2)}) collective-permute-start(bf16[3,16,1536]{2,1,0:T(8,128)(2,1)S(1)} %get-tuple-element.29), channel_id=1, source_target_pairs={{0,2},{1,3},{2,0},{3,1},{4,6},{5,7},{6,4},{7,5},{8,10},{9,11},{10,... | collective-permute-start | bytes 442376 | tf_op jit(solution)/shard_map/ppermute | solution.py:385
  29.3 3.9 %turn_2.1.refs_2_.refs_4_ = bf16[10,1536,1024]{2,1,0:T(8,128)(2,1)S(1)} custom-call(bf16[10,1536,1024]{2,1,0:T(8,128)(2,1)S(1)} %turn_1.1.refs_2_.refs_0_, bf16[2048,1536]{1,0:T(8,128)(2,1)S(1)} %bitcast.3, bf16[3072,1536]{1,0:T(8,128)(2,1)S(1)} %bitcast.1), custom_call_target="tpu_custom_call", output_to_operand_aliasing={{}: (0, {})} | custom-call | bytes 47185920 | tf_op jit(solution)/shard_map/turn_2/pallas_call | solution.py:55
  33.2 0.7 %collective-permute-done.4.refs_1_ = bf16[3,16,1536]{2,1,0:T(8,128)(2,1)S(1)} collective-permute-done((bf16[3,16,1536]{2,1,0:T(8,128)(2,1)S(1)}, bf16[3,16,1536]{2,1,0:T(8,128)(2,1)S(1)}, u32[]{:S(2)}, u32[]{:S(2)}) %collective-permute-start.4) | collective-permute-done | bytes 147488 | tf_op jit(solution)/shard_map/ppermute | solution.py:385
  34.0 1.3 %mixed_own.1.refs_3_ = f32[16,1536]{1,0:T(8,128)S(1)} custom-call(bf16[16,3200]{1,0:T(8,128)(2,1)S(1)} %join_16.1.refs_0_.refs_1_, bf16[3,16,1536]{2,1,0:T(8,128)(2,1)S(1)} %hidden.1.refs_1_, bf16[2048,1536]{1,0:T(8,128)(2,1)S(1)} %bitcast.3, bf16[3072,1536]{1,0:T(8,128)(2,1)S(1)} %bitcast.1, bf16[10,1536,1024]{2,1,0:T(8,128)(2,1)S(1)} %turn_2.1.refs_2_.refs_4_), custom_call_target="tpu_custom_call" | custom-call | flops 125829120 | tf_op jit(solution)/shard_map/mixed_own/pallas_call | solution.py:55
  35.4 5.2 %token_partials.1 = (f32[8,3072]{1,0:T(8,128)S(1)}, bf16[8,3072]{1,0:T(8,128)(2,1)S(1)}, bf16[16,3072]{1,0:T(8,128)(2,1)S(1)}, bf16[16,2048]{1,0:T(8,128)(2,1)S(1)}) custom-call(bf16[16,3200]{1,0:T(8,128)(2,1)S(1)} %join_16.1.refs_0_.refs_1_, bf16[3,16,1536]{2,1,0:T(8,128)(2,1)S(1)} %hidden.1.refs_1_, ...), custom_call_target="tpu_custom_call" | custom-call | flops 754974720 | tf_op jit(solution)/shard_map/token_partials/pallas_call | solution.py:55
  40.6 1.5 %collective-permute-start.6 = (bf16[8,3072]{1,0:T(8,128)(2,1)S(1)}, bf16[8,3072]{1,0:T(8,128)(2,1)S(1)}, u32[]{:S(2)}, u32[]{:S(2)}) collective-permute-start(bf16[8,3072]{1,0:T(8,128)(2,1)S(1)} %get-tuple-element.31), channel_id=1, source_target_pairs={{0,16},{4,20},{8,24},{12,28},{16,0},{20,4},{24,8},{28,12},{1,17},{... | collective-permute-start | bytes 147464 | tf_op jit(solution)/shard_map/ppermute | solution.py:385
  42.2 2.9 %down_grad_1.1.refs_2_.refs_4_ = bf16[3072,1536]{1,0:T(8,128)(2,1)} custom-call(f32[8,3072]{1,0:T(8,128)S(1)} %get-tuple-element.30.refs_0_, bf16[16,3200]{1,0:T(8,128)(2,1)S(1)} %join_16.1.refs_0_.refs_1_, bf16[16,3072]{1,0:T(8,128)(2,1)S(1)} %get-tuple-element.32.refs_2_, bf16[16,2048]{1,0:T(8,128)(2,1)S(1)} %get-tuple-element.33.refs_3_), custom_call_target="tpu_custom_call" | custom-call | flops 88080384 | bytes 5505024 | tf_op jit(solution)/shard_map/down_grad_1/pallas_call | solution.py:55
  45.1 1.6 %collective-permute-start.7 = (bf16[4,3072]{1,0:T(4,128)(2,1)S(1)}, bf16[4,3072]{1,0:T(4,128)(2,1)S(1)}, u32[]{:S(2)}, u32[]{:S(2)}) collective-permute-start(bf16[4,3072]{1,0:T(4,128)(2,1)S(1)} %get-tuple-element.35), channel_id=1, source_target_pairs={{0,4},{4,0},{8,12},{12,8},{16,20},{20,16},{24,28},{28,24},{1,5},{5... | collective-permute-start | bytes 73736 | tf_op jit(solution)/shard_map/ppermute | solution.py:385
  46.7 2.9 %down_grad_2.1 = (bf16[3072,1536]{1,0:T(8,128)(2,1)}, bf16[2048,1536]{1,0:T(8,128)(2,1)}) custom-call(f32[4,3072]{1,0:T(4,128)S(1)} %get-tuple-element.34.refs_0_, bf16[16,3200]{1,0:T(8,128)(2,1)S(1)} %join_16.1.refs_0_.refs_1_, bf16[16,3072]{1,0:T(8,128)(2,1)S(1)} %get-tuple-element.32.refs_2_, ...), custom_call_target="tpu_custom_call", output_to_operand_aliasing={{0}: (4, {})} | custom-call | flops 88080384 | bytes 5505024 | tf_op jit(solution)/shard_map/down_grad_2/pallas_call | solution.py:55
  49.6 1.8 %collective-permute-start.8 = (bf16[2,3072]{1,0:T(2,128)(2,1)S(1)}, bf16[2,3072]{1,0:T(2,128)(2,1)S(1)}, u32[]{:S(2)}, u32[]{:S(2)}) collective-permute-start(bf16[2,3072]{1,0:T(2,128)(2,1)S(1)} %get-tuple-element.38), channel_id=1, source_target_pairs={{0,8},{4,12},{8,0},{12,4},{16,24},{20,28},{24,16},{28,20},{1,9},{5... | collective-permute-start | bytes 36872 | tf_op jit(solution)/shard_map/ppermute | solution.py:385
  51.4 2.6 %down_grad_3.1 = bf16[2048,1536]{1,0:T(8,128)(2,1)} custom-call(f32[2,3072]{1,0:T(2,128)S(1)} %get-tuple-element.37.refs_0_, bf16[16,3200]{1,0:T(8,128)(2,1)S(1)} %join_16.1.refs_0_.refs_1_, bf16[16,3072]{1,0:T(8,128)(2,1)S(1)} %get-tuple-element.32.refs_2_, bf16[16,2048]{1,0:T(8,128)(2,1)S(1)} %get-tuple-element.33.refs_3_, ...), custom_call_target="tpu_custom_call", output_to_operand_aliasing={{}: (4, {})} | custom-call | flops 75497472 | bytes 4718592 | tf_op jit(solution)/shard_map/down_grad_3/pallas_call | solution.py:55
  54.0 0.3 collective-permute-done.8.refs_1_
  54.3 0.6 %token_sum_1.1 = (bf16[2,1536]{1,0:T(2,128)(2,1)}, bf16[2,1536]{1,0:T(2,128)(2,1)}) custom-call(f32[2,3072]{1,0:T(2,128)S(1)} %get-tuple-element.37.refs_0_, bf16[2,3072]{1,0:T(2,128)(2,1)S(1)} %collective-permute-done.8.refs_1_), custom_call_target="tpu_custom_call" | custom-call | tf_op jit(solution)/shard_map/token_sum_1/pallas_call | solution.py:55
  (24 shorter events, 0.3 us)
Async XLA Ops:
  1.4 7.0 %collective-permute-start = (bf16[2,3200]{1,0:T(2,128)(2,1)S(1)}, bf16[2,3200]{1,0:T(2,128)(2,1)S(1)}, u32[]{:S(2)}, u32[]{:S(2)}) collective-permute-start(bf16[2,3200]{1,0:T(2,128)(2,1)S(1)} %get-tuple-element.23.refs_0_), channel_id=1, source_target_pairs={{0,8},{4,12},{8,0},{12,4},{16,24},{20,28},{24,16},{28,20},{1,9},{5... | collective-permute-start | bytes 38408 | tf_op jit(solution)/shard_map/ppermute | solution.py:385
  8.4 8.2 %slice-start = ((s8[9437184]{0:T(1024)(128)(4,1)}), s8[4194304]{0:T(1024)(128)(4,1)S(1)}, s32[]{:S(2)}) async-start(s8[9437184]{0:T(1024)(128)(4,1)} %bitcast), calls=%async_computation | async-start | bytes 8388608
  8.4 8.2 %slice-start.1 = ((s8[9437184]{0:T(1024)(128)(4,1)}), s8[4194304]{0:T(1024)(128)(4,1)S(1)}, s32[]{:S(2)}) async-start(s8[9437184]{0:T(1024)(128)(4,1)} %bitcast), calls=%async_computation.1 | async-start | bytes 8388608
  8.4 8.2 %slice-start.3 = ((s8[6291456]{0:T(1024)(128)(4,1)}), s8[4194304]{0:T(1024)(128)(4,1)S(1)}, s32[]{:S(2)}) async-start(s8[6291456]{0:T(1024)(128)(4,1)} %bitcast.2), calls=%async_computation.3 | async-start | bytes 8388608
  8.4 8.1 %slice-start.2 = ((s8[9437184]{0:T(1024)(128)(4,1)}), s8[1048576]{0:T(1024)(128)(4,1)S(1)}, s32[]{:S(2)}) async-start(s8[9437184]{0:T(1024)(128)(4,1)} %bitcast), calls=%async_computation.2 | async-start | bytes 2097152
  8.4 8.1 %slice-start.4 = ((s8[6291456]{0:T(1024)(128)(4,1)}), s8[2097152]{0:T(1024)(128)(4,1)S(1)}, s32[]{:S(2)}) async-start(s8[6291456]{0:T(1024)(128)(4,1)} %bitcast.2), calls=%async_computation.4 | async-start | bytes 4194304
  8.5 3.9 %collective-permute-start.1 = (bf16[4,3200]{1,0:T(4,128)(2,1)S(1)}, bf16[4,3200]{1,0:T(4,128)(2,1)S(1)}, u32[]{:S(2)}, u32[]{:S(2)}) collective-permute-start(bf16[4,3200]{1,0:T(4,128)(2,1)S(1)} %join_4.1.refs_0_), channel_id=1, source_target_pairs={{0,4},{4,0},{8,12},{12,8},{16,20},{20,16},{24,28},{28,24},{1,5},{5... | collective-permute-start | bytes 76808 | tf_op jit(solution)/shard_map/ppermute | solution.py:385
  12.4 4.2 %collective-permute-start.2 = (bf16[8,3200]{1,0:T(8,128)(2,1)S(1)}, bf16[8,3200]{1,0:T(8,128)(2,1)S(1)}, u32[]{:S(2)}, u32[]{:S(2)}) collective-permute-start(bf16[8,3200]{1,0:T(8,128)(2,1)S(1)} %join_8.1.refs_0_), channel_id=1, source_target_pairs={{0,16},{4,20},{8,24},{12,28},{16,0},{20,4},{24,8},{28,12},{1,17},{... | collective-permute-start | bytes 153608 | tf_op jit(solution)/shard_map/ppermute | solution.py:385
  26.0 1.6 %collective-permute-start.3 = (f32[3,16,1536]{2,1,0:T(8,128)S(1)}, f32[3,16,1536]{2,1,0:T(8,128)S(1)}, u32[]{:S(2)}, u32[]{:S(2)}) collective-permute-start(f32[3,16,1536]{2,1,0:T(8,128)S(1)} %get-tuple-element.26), channel_id=1, source_target_pairs={{0,1},{1,0},{2,3},{3,2},{4,5},{5,4},{6,7},{7,6},{8,9},{9,8},{10,11... | collective-permute-start | bytes 884744 | tf_op jit(solution)/shard_map/ppermute | solution.py:385
  27.7 6.2 %collective-permute-start.4 = (bf16[3,16,1536]{2,1,0:T(8,128)(2,1)S(1)}, bf16[3,16,1536]{2,1,0:T(8,128)(2,1)S(1)}, u32[]{:S(2)}, u32[]{:S(2)}) collective-permute-start(bf16[3,16,1536]{2,1,0:T(8,128)(2,1)S(1)} %get-tuple-element.29), channel_id=1, source_target_pairs={{0,2},{1,3},{2,0},{3,1},{4,6},{5,7},{6,4},{7,5},{8,10},{9,11},{10,... | collective-permute-start | bytes 442376 | tf_op jit(solution)/shard_map/ppermute | solution.py:385
  34.0 1.4 %collective-permute-start.5 = (bf16[3,16,1536]{2,1,0:T(8,128)(2,1)S(1)}, bf16[3,16,1536]{2,1,0:T(8,128)(2,1)S(1)}, u32[]{:S(2)}, u32[]{:S(2)}) collective-permute-start(bf16[3,16,1536]{2,1,0:T(8,128)(2,1)S(1)} %hidden.1.refs_1_), channel_id=1, source_target_pairs={{0,1},{1,0},{2,3},{3,2},{4,5},{5,4},{6,7},{7,6},{8,9},{9,8},{10,11... | collective-permute-start | bytes 442376 | tf_op jit(solution)/shard_map/ppermute | solution.py:385
  40.6 4.4 %collective-permute-start.6 = (bf16[8,3072]{1,0:T(8,128)(2,1)S(1)}, bf16[8,3072]{1,0:T(8,128)(2,1)S(1)}, u32[]{:S(2)}, u32[]{:S(2)}) collective-permute-start(bf16[8,3072]{1,0:T(8,128)(2,1)S(1)} %get-tuple-element.31), channel_id=1, source_target_pairs={{0,16},{4,20},{8,24},{12,28},{16,0},{20,4},{24,8},{28,12},{1,17},{... | collective-permute-start | bytes 147464 | tf_op jit(solution)/shard_map/ppermute | solution.py:385
  45.1 4.5 %collective-permute-start.7 = (bf16[4,3072]{1,0:T(4,128)(2,1)S(1)}, bf16[4,3072]{1,0:T(4,128)(2,1)S(1)}, u32[]{:S(2)}, u32[]{:S(2)}) collective-permute-start(bf16[4,3072]{1,0:T(4,128)(2,1)S(1)} %get-tuple-element.35), channel_id=1, source_target_pairs={{0,4},{4,0},{8,12},{12,8},{16,20},{20,16},{24,28},{28,24},{1,5},{5... | collective-permute-start | bytes 73736 | tf_op jit(solution)/shard_map/ppermute | solution.py:385
  49.6 4.7 %collective-permute-start.8 = (bf16[2,3072]{1,0:T(2,128)(2,1)S(1)}, bf16[2,3072]{1,0:T(2,128)(2,1)S(1)}, u32[]{:S(2)}, u32[]{:S(2)}) collective-permute-start(bf16[2,3072]{1,0:T(2,128)(2,1)S(1)} %get-tuple-element.38), channel_id=1, source_target_pairs={{0,8},{4,12},{8,0},{12,4},{16,24},{20,28},{24,16},{28,20},{1,9},{5... | collective-permute-start | bytes 36872 | tf_op jit(solution)/shard_map/ppermute | solution.py:385

commit v9 on v8

--- a/solution.py
+++ b/solution.py
@@ -12,10 +12,14 @@
 F32 = jnp.float32
 BF16 = jnp.bfloat16
 MIB = 1 << 20
+LIMIT = 6
 BLOCK = 512
 WIDE = 1024
 ROWS = 256
 TURN_FIRST = 5
+SLOTS = 4
+EARLY_ROWS = 2560
+TEXT_FIRST = 3
 PLACES = {"h": pl.ANY, "v": pltpu.VMEM, "s": pltpu.SMEM}
 
 
@@ -42,7 +46,7 @@
 
 
 def call(
-    body, name, outs, ins, places, scratch=(), flops=0, traffic=0, limit=4, out_places=None, aliases=None, also=()
+    body, name, outs, ins, places, scratch=(), flops=0, traffic=0, limit=LIMIT, out_places=None, aliases=None, also=()
 ):
     out_places = out_places or "v" * len(outs)
     shapes = [pltpu.VMEM(*o) if p == "v" else jax.ShapeDtypeStruct(*o) for o, p in zip(outs, out_places)]
@@ -282,8 +286,8 @@
 
 
 def back_body(
-    turned, arr_ref, done_ref, other_ref, own_ref, wide_ref, dt_ref, ds_ref,
-    keep_ref, send_ref, hs_ref, ht_ref, dgs, dgt, dus, dut, out,
+    turned, grad_rows, arr_ref, done_ref, other_ref, own_ref, wide_ref, dt_ref, ds_ref,
+    keep_ref, send_ref, hs_ref, ht_ref, grad_hbm, dgs, dgt, dus, dut, out, slots, sems,
 ):
     speech = is_speech(arr_ref)
     fs, ft = hs_ref.shape[1], ht_ref.shape[1]
@@ -304,48 +308,68 @@
         out[:, cut] = own_ref[:, cut] + value
     blocks = [(dgt, nt), (dut, nt), (dgs, ns), (dus, ns)]
     blocks = [(ref, i) for ref, n in blocks for i in range(n)]
-    for r in range(width // BLOCK):
-        total = jnp.zeros((out.shape[0], BLOCK), F32)
-        for b, (ref, j) in enumerate(blocks):
-            product = times if b in turned else contract_last
-            total += product(ref[:, j * BLOCK : (j + 1) * BLOCK], square_at(wide_ref, b, r)[...])
-        start = width + r * BLOCK
-        out[:, start : start + BLOCK] = total
+    c = arr_ref[:, width : 2 * width]
+    count, n_slots = grad_rows // ROWS, slots.shape[0]
+    squares = [(r, b) for r in range(width // BLOCK) for b in range(len(blocks))]
+    copies, total = [], None
+    for n, (r, b) in enumerate(squares):
+        ref, j = blocks[b]
+        product = times if b in turned else contract_last
+        value = product(ref[:, j * BLOCK : (j + 1) * BLOCK], square_at(wide_ref, b, r)[...])
+        total = value if b == 0 else total + value
+        if b == len(blocks) - 1:
+            start = width + r * BLOCK
+            out[:, start : start + BLOCK] = total
+        while len(copies) * len(squares) < (n + 1) * count:
+            i = len(copies)
+            if i >= n_slots:
+                copies[i - n_slots].wait()
+            cut = slice(i * ROWS, (i + 1) * ROWS)
+            slots[i % n_slots] = contract_first(hs_ref[:, cut], c).astype(BF16)
+            copies.append(pltpu.make_async_copy(slots.at[i % n_slots], grad_hbm.at[cut], sems.at[i % n_slots]))
+            copies[i].start()
+    for copy in copies[-n_slots:]:
+        copy.wait()
     half = keep_ref.shape[0]
     keep_ref[...] = out[:half]
     send_ref[...] = out[half:].astype(BF16)
 
 
-def back(arr, done, other, own, wide, down_t, down_s, turned):
+def back(arr, done, other, own, wide, down_t, down_s, turned, grad_rows):
     rows, width = arr.shape[0], down_s.shape[1]
     fs, ft = down_s.shape[0], down_t.shape[0]
     hidden = [((rows, fs), BF16), ((rows, ft), BF16)]
+    scratch = [pltpu.VMEM(*s) for s in hidden + hidden] + [pltpu.VMEM((rows, 2 * width), F32)]
+    scratch += [pltpu.VMEM((SLOTS, ROWS, width), BF16), pltpu.SemaphoreType.DMA((SLOTS,))]
     return call(
-        functools.partial(back_body, turned),
+        functools.partial(back_body, turned, grad_rows),
         "token_partials",
-        [((rows // 2, 2 * width), F32), ((rows // 2, 2 * width), BF16)] + hidden,
+        [((rows // 2, 2 * width), F32), ((rows // 2, 2 * width), BF16)] + hidden + [like(down_s)],
         (arr, done, other, own, wide, down_t, down_s),
         "vvvvvvv",
-        [pltpu.VMEM(*s) for s in hidden + hidden] + [pltpu.VMEM((rows, 2 * width), F32)],
+        scratch,
         2 * rows * (wide.size + down_t.size + down_s.size),
+        out_places="vvvvh",
     )
 
 
-def token_sum_body(keep_ref, got_ref, after_ref, next_ref, send_ref):
+def token_sum_body(keep_ref, got_ref, after_ref, next_ref, *send_refs):
     total = keep_ref[...] + got_ref[...].astype(F32)
-    half = next_ref.shape[0]
-    next_ref[...] = total[:half]
-    send_ref[...] = total[half:].astype(send_ref.dtype)
-
-
-def token_sum(keep, got, after, dtype, name):
+    own = next_ref.shape[0]
+    next_ref[...] = total[:own]
+    for i, ref in enumerate(send_refs):
+        ref[...] = total[(i + 1) * own : (i + 2) * own].astype(ref.dtype)
+
+
+def token_sum(keep, got, after, own, name):
     rows, width = keep.shape
-    outs = [((rows // 2, width), F32), ((rows // 2, width), dtype)]
+    outs = [((own, width), F32)] + [((own, width), BF16)] * (rows // own - 1)
     return call(token_sum_body, name, outs, (keep, got, after), "vvh")
 
 
-def last_sum_body(keep_ref, got_ref, mixed_hbm, grad_hbm, mixed_ref, grad_ref, sems):
-    total = (keep_ref[...] + got_ref[...].astype(F32)).astype(BF16)
+def last_sum_body(keep_ref, got_a, got_b, got_c, mixed_hbm, grad_hbm, mixed_ref, grad_ref, sems):
+    total = keep_ref[...] + got_a[...].astype(F32)
+    total = (total + got_b[...].astype(F32) + got_c[...].astype(F32)).astype(BF16)
     width = mixed_ref.shape[1]
     mixed_ref[...] = total[:, :width]
     grad_ref[...] = total[:, width:]
@@ -416,7 +440,8 @@
         mixed_own_body, "mixed_own", [((arr.shape[0], width), F32)], (arr, done, down_t, down_s), "vvvv",
         flops=arr.shape[0] * (down_s.size + down_t.size), also=(wide,),
     )[0]
-    keep, send, hs, ht = back(arr, done, other, own, wide, down_t, down_s, range(blocks))
+    early = EARLY_ROWS
+    keep, send, hs, ht, down_s_grad = back(arr, done, other, own, wide, down_t, down_s, range(blocks), early)
 
     def outer(after, speech, text, old, name):
         count = len(speech) + len(text)
@@ -430,17 +455,16 @@
 
     ns, nt = fs // ROWS, ft // ROWS
     got = flip(send, TOK, HOPS[2], n_tok)
-    down_s_grad = outer(keep, range(ns - 5), (), (), "down_grad_1")[0]
-    keep, send = token_sum(keep, got, down_s_grad, BF16, "token_sum_4")
-
-    got = flip(send, TOK, HOPS[1], n_tok)
-    down_s_grad, down_t_grad = outer(keep, range(ns - 5, ns), range(2), (down_s_grad,), "down_grad_2")
-    keep, send = token_sum(keep, got, down_t_grad, BF16, "token_sum_2")
-
-    got = flip(send, TOK, HOPS[0], n_tok)
-    down_t_grad = outer(keep, (), range(2, nt), (down_t_grad,), "down_grad_3")[0]
+    down_s_grad, down_t_grad = outer(keep, range(early // ROWS, ns), range(TEXT_FIRST), (down_s_grad,), "down_grad_1")
+    keep, *sends = token_sum(keep, got, down_t_grad, rows, "token_sum_4")
+    bits = (HOPS[0], HOPS[1], HOPS[0] ^ HOPS[1])
+    gots = [flip(send, TOK, bit, n_tok) for send, bit in zip(sends, bits)]
+    down_t_grad = outer(keep, (), range(TEXT_FIRST, nt), (down_t_grad,), "down_grad_2")[0]
     outs = [((rows, width), BF16)] * 2
-    mixed, token_grad = call(last_sum_body, "token_sum_1", outs, (keep, got), "vv", pair + [pltpu.SemaphoreType.DMA((2,))], out_places="hh")
+    mixed, token_grad = call(
+        last_sum_body, "token_sum_1", outs, (keep, *gots), "vvvv", pair + [pltpu.SemaphoreType.DMA((2,))],
+        out_places="hh",
+    )
     return mixed, token_grad, down_s_grad, down_t_grad
 
 

time: 55.3 us -> 57.6 us (1.042)
  waiting for transfers between devices: 5.99 us -> 8.02 us
  starting transfers between devices: 14 us -> 15.1 us
  Pallas kernels: 34 us -> 33.2 us
    ppermute x9 -> x10, waiting for transfers between devices: 5.99 us -> 8.02 us  [flip(): return lax.ppermute(value, axes, [(i, i ^ bit) for i in range(n)])]
    ppermute x9 -> x10, starting transfers between devices: 14 us -> 15.1 us  [flip(): return lax.ppermute(value, axes, [(i, i ^ bit) for i in range(n)])]
    pallas_call x18 -> x16, Pallas kernels: 34 us -> 33.2 us  [call(): pl.pallas_call(seen, out_shape=shapes, in_specs=[pl.BlockSpec(memory_spac...]
  transfers between devices with their start and end apart: 9 -> 10, of which waited for: 5 -> 6; matrix products, arithmetic and copies ran while one was open for 0% -> 0% of each run, Pallas kernels for 32% -> 25%
where the time goes in v9:
time: 57.6 us; the launch traced here: 57.4 us
  Pallas kernels  33.2 us (58%)
  starting transfers between devices  15.1 us (26%)
  waiting for transfers between devices  8.02 us (14%)
  between operations  1.01 us (2%)
    pallas_call x16, Pallas kernels, call(): pl.pallas_call(seen, out_shape=shapes, in_specs=[pl.BlockSpec(memory_spac...  33.2 us
    ppermute x10, starting transfers between devices, flip(): return lax.ppermute(value, axes, [(i, i ^ bit) for i in range(n)])  15.1 us
    ppermute x10, waiting for transfers between devices, flip(): return lax.ppermute(value, axes, [(i, i ^ bit) for i in range(n)])  8.02 us
  transfers between devices with their start and end apart: 10, of which 6 were waited for; matrix products, arithmetic and copies ran while one was open for 0% of the time, Pallas kernels for 25%

profile of v9, /device:TPU:0, one launch (start us, length us, event | category | flops | bytes accessed | tf_op | source)
XLA Modules:
  0.0 57.4 jit_solution(7418873115440487378)
XLA Ops:
  0.6 0.7 %pack.1 = (bf16[10,1536,1024]{2,1,0:T(8,128)(2,1)S(1)}, bf16[2,3200]{1,0:T(2,128)(2,1)S(1)}) custom-call(s32[2]{0:T(128)} %refs_0_.1, bf16[2,1536]{1,0:T(2,128)(2,1)} %refs_1_.5, bf16[2,1536]{1,0:T(2,128)(2,1)} %refs_2_.5), custom_call_target="tpu_custom_call" | custom-call | tf_op jit(solution)/shard_map/pack/pallas_call | solution.py:59
  1.4 4.1 %collective-permute-start = (bf16[2,3200]{1,0:T(2,128)(2,1)S(1)}, bf16[2,3200]{1,0:T(2,128)(2,1)S(1)}, u32[]{:S(2)}, u32[]{:S(2)}) collective-permute-start(bf16[2,3200]{1,0:T(2,128)(2,1)S(1)} %get-tuple-element.24.refs_0_), channel_id=1, source_target_pairs={{0,8},{4,12},{8,0},{12,4},{16,24},{20,28},{24,16},{28,20},{1,9},{5... | collective-permute-start | bytes 38408 | tf_op jit(solution)/shard_map/ppermute | solution.py:409
  5.5 2.9 %load_gate_text.1.refs_2_.refs_6_ = bf16[10,1536,1024]{2,1,0:T(8,128)(2,1)S(1)} custom-call(bf16[2,3200]{1,0:T(2,128)(2,1)S(1)} %get-tuple-element.24.refs_0_, bf16[1536,2048]{1,0:T(8,128)(2,1)} %refs_1_.6, bf16[10,1536,1024]{2,1,0:T(8,128)(2,1)S(1)} %get-tuple-element.25.refs_2_), custom_call_target="tpu_custom_call", output_to_operand_aliasing={{}: (2, {})} | custom-call | bytes 6291456 | tf_op jit(solution)/shard_map/load_gate_text/pallas_call | solution.py:59
  8.5 1.6 %collective-permute-start.1 = (bf16[4,3200]{1,0:T(4,128)(2,1)S(1)}, bf16[4,3200]{1,0:T(4,128)(2,1)S(1)}, u32[]{:S(2)}, u32[]{:S(2)}) collective-permute-start(bf16[4,3200]{1,0:T(4,128)(2,1)S(1)} %join_4.1.refs_0_), channel_id=1, source_target_pairs={{0,4},{4,0},{8,12},{12,8},{16,20},{20,16},{24,28},{28,24},{1,5},{5... | collective-permute-start | bytes 76808 | tf_op jit(solution)/shard_map/ppermute | solution.py:409
  10.1 2.3 %collective-permute-done.1.refs_1_ = bf16[4,3200]{1,0:T(4,128)(2,1)S(1)} collective-permute-done((bf16[4,3200]{1,0:T(4,128)(2,1)S(1)}, bf16[4,3200]{1,0:T(4,128)(2,1)S(1)}, u32[]{:S(2)}, u32[]{:S(2)}) %collective-permute-start.1) | collective-permute-done | bytes 25632 | tf_op jit(solution)/shard_map/ppermute | solution.py:409
  12.4 1.6 %collective-permute-start.2 = (bf16[8,3200]{1,0:T(8,128)(2,1)S(1)}, bf16[8,3200]{1,0:T(8,128)(2,1)S(1)}, u32[]{:S(2)}, u32[]{:S(2)}) collective-permute-start(bf16[8,3200]{1,0:T(8,128)(2,1)S(1)} %join_8.1.refs_0_), channel_id=1, source_target_pairs={{0,16},{4,20},{8,24},{12,28},{16,0},{20,4},{24,8},{28,12},{1,17},{... | collective-permute-start | bytes 153608 | tf_op jit(solution)/shard_map/ppermute | solution.py:409
  14.0 2.6 %collective-permute-done.2.refs_1_ = bf16[8,3200]{1,0:T(8,128)(2,1)S(1)} collective-permute-done((bf16[8,3200]{1,0:T(8,128)(2,1)S(1)}, bf16[8,3200]{1,0:T(8,128)(2,1)S(1)}, u32[]{:S(2)}, u32[]{:S(2)}) %collective-permute-start.2) | collective-permute-done | bytes 51232 | tf_op jit(solution)/shard_map/ppermute | solution.py:409
  16.6 9.4 %hidden_partials.1 = (f32[3,16,1536]{2,1,0:T(8,128)S(1)}, f32[3,16,1536]{2,1,0:T(8,128)S(1)}, bf16[10,1536,1024]{2,1,0:T(8,128)(2,1)S(1)}) custom-call(bf16[16,3200]{1,0:T(8,128)(2,1)S(1)} %join_16.1.refs_0_.refs_1_, bf16[2048,1536]{1,0:T(8,128)(2,1)S(1)} %bitcast.3, bf16[3072,1536]{1,0:T(8,128)(2,1)S(1)} %bitcast.1, ...), custom_call_target="tpu_custom_call", output_to_operand_aliasing={{2}: (6, {})} | custom-call | flops 754974720 | bytes 25165824 | tf_op jit(solution)/shard_map/hidden_partials/pallas_call | solution.py:59
  26.1 1.4 %turn_1.1.refs_2_.refs_0_ = bf16[10,1536,1024]{2,1,0:T(8,128)(2,1)S(1)} custom-call(bf16[10,1536,1024]{2,1,0:T(8,128)(2,1)S(1)} %get-tuple-element.28.refs_0_, bf16[2048,1536]{1,0:T(8,128)(2,1)S(1)} %bitcast.3, bf16[3072,1536]{1,0:T(8,128)(2,1)S(1)} %bitcast.1), custom_call_target="tpu_custom_call", output_to_operand_aliasing={{}: (0, {})} | custom-call | bytes 15728640 | tf_op jit(solution)/shard_map/turn_1/pallas_call | solution.py:59
  27.5 0.1 collective-permute-done.3.refs_1_
  27.7 1.6 %collective-permute-start.4 = (bf16[3,16,1536]{2,1,0:T(8,128)(2,1)S(1)}, bf16[3,16,1536]{2,1,0:T(8,128)(2,1)S(1)}, u32[]{:S(2)}, u32[]{:S(2)}) collective-permute-start(bf16[3,16,1536]{2,1,0:T(8,128)(2,1)S(1)} %get-tuple-element.30), channel_id=1, source_target_pairs={{0,2},{1,3},{2,0},{3,1},{4,6},{5,7},{6,4},{7,5},{8,10},{9,11},{10,... | collective-permute-start | bytes 442376 | tf_op jit(solution)/shard_map/ppermute | solution.py:409
  29.3 3.9 %turn_2.1.refs_2_.refs_4_ = bf16[10,1536,1024]{2,1,0:T(8,128)(2,1)S(1)} custom-call(bf16[10,1536,1024]{2,1,0:T(8,128)(2,1)S(1)} %turn_1.1.refs_2_.refs_0_, bf16[2048,1536]{1,0:T(8,128)(2,1)S(1)} %bitcast.3, bf16[3072,1536]{1,0:T(8,128)(2,1)S(1)} %bitcast.1), custom_call_target="tpu_custom_call", output_to_operand_aliasing={{}: (0, {})} | custom-call | bytes 47185920 | tf_op jit(solution)/shard_map/turn_2/pallas_call | solution.py:59
  33.2 0.7 %collective-permute-done.4.refs_1_ = bf16[3,16,1536]{2,1,0:T(8,128)(2,1)S(1)} collective-permute-done((bf16[3,16,1536]{2,1,0:T(8,128)(2,1)S(1)}, bf16[3,16,1536]{2,1,0:T(8,128)(2,1)S(1)}, u32[]{:S(2)}, u32[]{:S(2)}) %collective-permute-start.4) | collective-permute-done | bytes 147488 | tf_op jit(solution)/shard_map/ppermute | solution.py:409
  34.0 1.3 %mixed_own.1.refs_3_ = f32[16,1536]{1,0:T(8,128)S(1)} custom-call(bf16[16,3200]{1,0:T(8,128)(2,1)S(1)} %join_16.1.refs_0_.refs_1_, bf16[3,16,1536]{2,1,0:T(8,128)(2,1)S(1)} %hidden.1.refs_1_, bf16[2048,1536]{1,0:T(8,128)(2,1)S(1)} %bitcast.3, bf16[3072,1536]{1,0:T(8,128)(2,1)S(1)} %bitcast.1, bf16[10,1536,1024]{2,1,0:T(8,128)(2,1)S(1)} %turn_2.1.refs_2_.refs_4_), custom_call_target="tpu_custom_call" | custom-call | flops 125829120 | tf_op jit(solution)/shard_map/mixed_own/pallas_call | solution.py:59
  35.4 8.1 %token_partials.1 = (f32[8,3072]{1,0:T(8,128)S(1)}, bf16[8,3072]{1,0:T(8,128)(2,1)S(1)}, bf16[16,3072]{1,0:T(8,128)(2,1)S(1)}, bf16[16,2048]{1,0:T(8,128)(2,1)S(1)}, bf16[3072,1536]{1,0:T(8,128)(2,1)}) custom-call(bf16[16,3200]{1,0:T(8,128)(2,1)S(1)} %join_16.1.refs_0_.refs_1_, bf16[3,16,1536]{2,1,0:T(8,128)(2,1)S(1)} %hidden.1.refs_1_, ...), custom_call_target="tpu_custom_call" | custom-call | flops 754974720 | tf_op jit(solution)/shard_map/token_partials/pallas_call | solution.py:59
  43.5 1.6 %collective-permute-start.6 = (bf16[8,3072]{1,0:T(8,128)(2,1)S(1)}, bf16[8,3072]{1,0:T(8,128)(2,1)S(1)}, u32[]{:S(2)}, u32[]{:S(2)}) collective-permute-start(bf16[8,3072]{1,0:T(8,128)(2,1)S(1)} %get-tuple-element.32), channel_id=1, source_target_pairs={{0,16},{4,20},{8,24},{12,28},{16,0},{20,4},{24,8},{28,12},{1,17},{... | collective-permute-start | bytes 147464 | tf_op jit(solution)/shard_map/ppermute | solution.py:409
  45.1 2.3 %down_grad_1.1 = (bf16[3072,1536]{1,0:T(8,128)(2,1)}, bf16[2048,1536]{1,0:T(8,128)(2,1)}) custom-call(f32[8,3072]{1,0:T(8,128)S(1)} %get-tuple-element.31.refs_0_, bf16[16,3200]{1,0:T(8,128)(2,1)S(1)} %join_16.1.refs_0_.refs_1_, bf16[16,3072]{1,0:T(8,128)(2,1)S(1)} %get-tuple-element.33.refs_2_, ...), custom_call_target="tpu_custom_call", output_to_operand_aliasing={{0}: (4, {})} | custom-call | flops 62914560 | bytes 3932160 | tf_op jit(solution)/shard_map/down_grad_1/pallas_call | solution.py:59
  47.4 0.3 collective-permute-done.6.refs_1_
  47.7 1.8 %collective-permute-start.7 = (bf16[2,3072]{1,0:T(2,128)(2,1)S(1)}, bf16[2,3072]{1,0:T(2,128)(2,1)S(1)}, u32[]{:S(2)}, u32[]{:S(2)}) collective-permute-start(bf16[2,3072]{1,0:T(2,128)(2,1)S(1)} %get-tuple-element.38), channel_id=1, source_target_pairs={{0,8},{4,12},{8,0},{12,4},{16,24},{20,28},{24,16},{28,20},{1,9},{5... | collective-permute-start | bytes 36872 | tf_op jit(solution)/shard_map/ppermute | solution.py:409
  49.5 1.6 %collective-permute-start.8 = (bf16[2,3072]{1,0:T(2,128)(2,1)S(1)}, bf16[2,3072]{1,0:T(2,128)(2,1)S(1)}, u32[]{:S(2)}, u32[]{:S(2)}) collective-permute-start(bf16[2,3072]{1,0:T(2,128)(2,1)S(1)} %get-tuple-element.39), channel_id=1, source_target_pairs={{0,4},{4,0},{8,12},{12,8},{16,20},{20,16},{24,28},{28,24},{1,5},{5... | collective-permute-start | bytes 36872 | tf_op jit(solution)/shard_map/ppermute | solution.py:409
  51.1 1.1 %collective-permute-start.9 = (bf16[2,3072]{1,0:T(2,128)(2,1)S(1)}, bf16[2,3072]{1,0:T(2,128)(2,1)S(1)}, u32[]{:S(2)}, u32[]{:S(2)}) collective-permute-start(bf16[2,3072]{1,0:T(2,128)(2,1)S(1)} %get-tuple-element.40), channel_id=1, source_target_pairs={{0,12},{4,8},{8,4},{12,0},{16,28},{20,24},{24,20},{28,16},{1,13},{... | collective-permute-start | bytes 36872 | tf_op jit(solution)/shard_map/ppermute | solution.py:409
  52.2 2.3 %down_grad_2.1 = bf16[2048,1536]{1,0:T(8,128)(2,1)} custom-call(f32[2,3072]{1,0:T(2,128)S(1)} %get-tuple-element.37.refs_0_, bf16[16,3200]{1,0:T(8,128)(2,1)S(1)} %join_16.1.refs_0_.refs_1_, bf16[16,3072]{1,0:T(8,128)(2,1)S(1)} %get-tuple-element.33.refs_2_, bf16[16,2048]{1,0:T(8,128)(2,1)S(1)} %get-tuple-element.34.refs_3_, ...), custom_call_target="tpu_custom_call", output_to_operand_aliasing={{}: (4, {})} | custom-call | flops 62914560 | bytes 3932160 | tf_op jit(solution)/shard_map/down_grad_2/pallas_call | solution.py:59
  54.5 2.0 %collective-permute-done.9.refs_3_ = bf16[2,3072]{1,0:T(2,128)(2,1)S(1)} collective-permute-done((bf16[2,3072]{1,0:T(2,128)(2,1)S(1)}, bf16[2,3072]{1,0:T(2,128)(2,1)S(1)}, u32[]{:S(2)}, u32[]{:S(2)}) %collective-permute-start.9) | collective-permute-done | bytes 12320 | tf_op jit(solution)/shard_map/ppermute | solution.py:409
  56.6 0.6 %token_sum_1.1 = (bf16[2,1536]{1,0:T(2,128)(2,1)}, bf16[2,1536]{1,0:T(2,128)(2,1)}) custom-call(f32[2,3072]{1,0:T(2,128)S(1)} %get-tuple-element.37.refs_0_, bf16[2,3072]{1,0:T(2,128)(2,1)S(1)} %collective-permute-done.7.refs_1_, bf16[2,3072]{1,0:T(2,128)(2,1)S(1)} %collective-permute-done.8.refs_2_, bf16[2,3072]{1,0:T(2,128)(2,1)S(1)} %collective-permute-done.9.refs_3_), custom_call_target="tpu_custom_call" | custom-call | tf_op jit(solution)/shard_map/token_sum_1/pallas_call | solution.py:59
  (24 shorter events, 0.4 us)
Async XLA Ops:
  1.4 7.0 %collective-permute-start = (bf16[2,3200]{1,0:T(2,128)(2,1)S(1)}, bf16[2,3200]{1,0:T(2,128)(2,1)S(1)}, u32[]{:S(2)}, u32[]{:S(2)}) collective-permute-start(bf16[2,3200]{1,0:T(2,128)(2,1)S(1)} %get-tuple-element.24.refs_0_), channel_id=1, source_target_pairs={{0,8},{4,12},{8,0},{12,4},{16,24},{20,28},{24,16},{28,20},{1,9},{5... | collective-permute-start | bytes 38408 | tf_op jit(solution)/shard_map/ppermute | solution.py:409
  8.4 8.2 %slice-start = ((s8[9437184]{0:T(1024)(128)(4,1)}), s8[4194304]{0:T(1024)(128)(4,1)S(1)}, s32[]{:S(2)}) async-start(s8[9437184]{0:T(1024)(128)(4,1)} %bitcast), calls=%async_computation | async-start | bytes 8388608
  8.4 8.2 %slice-start.1 = ((s8[9437184]{0:T(1024)(128)(4,1)}), s8[4194304]{0:T(1024)(128)(4,1)S(1)}, s32[]{:S(2)}) async-start(s8[9437184]{0:T(1024)(128)(4,1)} %bitcast), calls=%async_computation.1 | async-start | bytes 8388608
  8.4 8.2 %slice-start.3 = ((s8[6291456]{0:T(1024)(128)(4,1)}), s8[4194304]{0:T(1024)(128)(4,1)S(1)}, s32[]{:S(2)}) async-start(s8[6291456]{0:T(1024)(128)(4,1)} %bitcast.2), calls=%async_computation.3 | async-start | bytes 8388608
  8.4 8.1 %slice-start.2 = ((s8[9437184]{0:T(1024)(128)(4,1)}), s8[1048576]{0:T(1024)(128)(4,1)S(1)}, s32[]{:S(2)}) async-start(s8[9437184]{0:T(1024)(128)(4,1)} %bitcast), calls=%async_computation.2 | async-start | bytes 2097152
  8.4 8.1 %slice-start.4 = ((s8[6291456]{0:T(1024)(128)(4,1)}), s8[2097152]{0:T(1024)(128)(4,1)S(1)}, s32[]{:S(2)}) async-start(s8[6291456]{0:T(1024)(128)(4,1)} %bitcast.2), calls=%async_computation.4 | async-start | bytes 4194304
  8.5 3.9 %collective-permute-start.1 = (bf16[4,3200]{1,0:T(4,128)(2,1)S(1)}, bf16[4,3200]{1,0:T(4,128)(2,1)S(1)}, u32[]{:S(2)}, u32[]{:S(2)}) collective-permute-start(bf16[4,3200]{1,0:T(4,128)(2,1)S(1)} %join_4.1.refs_0_), channel_id=1, source_target_pairs={{0,4},{4,0},{8,12},{12,8},{16,20},{20,16},{24,28},{28,24},{1,5},{5... | collective-permute-start | bytes 76808 | tf_op jit(solution)/shard_map/ppermute | solution.py:409
  12.4 4.2 %collective-permute-start.2 = (bf16[8,3200]{1,0:T(8,128)(2,1)S(1)}, bf16[8,3200]{1,0:T(8,128)(2,1)S(1)}, u32[]{:S(2)}, u32[]{:S(2)}) collective-permute-start(bf16[8,3200]{1,0:T(8,128)(2,1)S(1)} %join_8.1.refs_0_), channel_id=1, source_target_pairs={{0,16},{4,20},{8,24},{12,28},{16,0},{20,4},{24,8},{28,12},{1,17},{... | collective-permute-start | bytes 153608 | tf_op jit(solution)/shard_map/ppermute | solution.py:409
  26.0 1.6 %collective-permute-start.3 = (f32[3,16,1536]{2,1,0:T(8,128)S(1)}, f32[3,16,1536]{2,1,0:T(8,128)S(1)}, u32[]{:S(2)}, u32[]{:S(2)}) collective-permute-start(f32[3,16,1536]{2,1,0:T(8,128)S(1)} %get-tuple-element.27), channel_id=1, source_target_pairs={{0,1},{1,0},{2,3},{3,2},{4,5},{5,4},{6,7},{7,6},{8,9},{9,8},{10,11... | collective-permute-start | bytes 884744 | tf_op jit(solution)/shard_map/ppermute | solution.py:409
  27.7 6.2 %collective-permute-start.4 = (bf16[3,16,1536]{2,1,0:T(8,128)(2,1)S(1)}, bf16[3,16,1536]{2,1,0:T(8,128)(2,1)S(1)}, u32[]{:S(2)}, u32[]{:S(2)}) collective-permute-start(bf16[3,16,1536]{2,1,0:T(8,128)(2,1)S(1)} %get-tuple-element.30), channel_id=1, source_target_pairs={{0,2},{1,3},{2,0},{3,1},{4,6},{5,7},{6,4},{7,5},{8,10},{9,11},{10,... | collective-permute-start | bytes 442376 | tf_op jit(solution)/shard_map/ppermute | solution.py:409
  34.0 1.4 %collective-permute-start.5 = (bf16[3,16,1536]{2,1,0:T(8,128)(2,1)S(1)}, bf16[3,16,1536]{2,1,0:T(8,128)(2,1)S(1)}, u32[]{:S(2)}, u32[]{:S(2)}) collective-permute-start(bf16[3,16,1536]{2,1,0:T(8,128)(2,1)S(1)} %hidden.1.refs_1_), channel_id=1, source_target_pairs={{0,1},{1,0},{2,3},{3,2},{4,5},{5,4},{6,7},{7,6},{8,9},{9,8},{10,11... | collective-permute-start | bytes 442376 | tf_op jit(solution)/shard_map/ppermute | solution.py:409
  43.5 4.2 %collective-permute-start.6 = (bf16[8,3072]{1,0:T(8,128)(2,1)S(1)}, bf16[8,3072]{1,0:T(8,128)(2,1)S(1)}, u32[]{:S(2)}, u32[]{:S(2)}) collective-permute-start(bf16[8,3072]{1,0:T(8,128)(2,1)S(1)} %get-tuple-element.32), channel_id=1, source_target_pairs={{0,16},{4,20},{8,24},{12,28},{16,0},{20,4},{24,8},{28,12},{1,17},{... | collective-permute-start | bytes 147464 | tf_op jit(solution)/shard_map/ppermute | solution.py:409
  47.7 6.8 %collective-permute-start.7 = (bf16[2,3072]{1,0:T(2,128)(2,1)S(1)}, bf16[2,3072]{1,0:T(2,128)(2,1)S(1)}, u32[]{:S(2)}, u32[]{:S(2)}) collective-permute-start(bf16[2,3072]{1,0:T(2,128)(2,1)S(1)} %get-tuple-element.38), channel_id=1, source_target_pairs={{0,8},{4,12},{8,0},{12,4},{16,24},{20,28},{24,16},{28,20},{1,9},{5... | collective-permute-start | bytes 36872 | tf_op jit(solution)/shard_map/ppermute | solution.py:409
  49.5 5.1 %collective-permute-start.8 = (bf16[2,3072]{1,0:T(2,128)(2,1)S(1)}, bf16[2,3072]{1,0:T(2,128)(2,1)S(1)}, u32[]{:S(2)}, u32[]{:S(2)}) collective-permute-start(bf16[2,3072]{1,0:T(2,128)(2,1)S(1)} %get-tuple-element.39), channel_id=1, source_target_pairs={{0,4},{4,0},{8,12},{12,8},{16,20},{20,16},{24,28},{28,24},{1,5},{5... | collective-permute-start | bytes 36872 | tf_op jit(solution)/shard_map/ppermute | solution.py:409
  51.1 5.5 %collective-permute-start.9 = (bf16[2,3072]{1,0:T(2,128)(2,1)S(1)}, bf16[2,3072]{1,0:T(2,128)(2,1)S(1)}, u32[]{:S(2)}, u32[]{:S(2)}) collective-permute-start(bf16[2,3072]{1,0:T(2,128)(2,1)S(1)} %get-tuple-element.40), channel_id=1, source_target_pairs={{0,12},{4,8},{8,4},{12,0},{16,28},{20,24},{24,20},{28,16},{1,13},{... | collective-permute-start | bytes 36872 | tf_op jit(solution)/shard_map/ppermute | solution.py:409

commit v10 on v9

--- a/solution.py
+++ b/solution.py
@@ -16,10 +16,11 @@
 BLOCK = 512
 WIDE = 1024
 ROWS = 256
+TILE = 128
 TURN_FIRST = 5
 SLOTS = 4
-EARLY_ROWS = 2560
-TEXT_FIRST = 3
+EARLY_ROWS = 2048
+TEXT_FIRST = 2
 PLACES = {"h": pl.ANY, "v": pltpu.VMEM, "s": pltpu.SMEM}
 
 
@@ -325,7 +326,7 @@
             if i >= n_slots:
                 copies[i - n_slots].wait()
             cut = slice(i * ROWS, (i + 1) * ROWS)
-            slots[i % n_slots] = contract_first(hs_ref[:, cut], c).astype(BF16)
+            outer_block(hs_ref[:, cut], c, slots.at[i % n_slots])
             copies.append(pltpu.make_async_copy(slots.at[i % n_slots], grad_hbm.at[cut], sems.at[i % n_slots]))
             copies[i].start()
     for copy in copies[-n_slots:]:
@@ -383,10 +384,17 @@
         copy.wait()
 
 
+def outer_block(h, c, place):
+    for i in range(0, h.shape[1], TILE):
+        turned = h[:, i : i + TILE].T
+        for j in range(0, c.shape[1], 2 * TILE):
+            place[i : i + TILE, j : j + 2 * TILE] = times(turned, c[:, j : j + 2 * TILE]).astype(BF16)
+
+
 def outer_steps(c, steps, slots, sems):
     copies = []
     for i, (h, place) in enumerate(steps):
-        slots[i] = contract_first(h, c).astype(BF16)
+        outer_block(h, c, slots.at[i])
         copies.append(pltpu.make_async_copy(slots.at[i], place, sems.at[i]))
         copies[-1].start()
     for copy in copies:
@@ -458,7 +466,7 @@
     down_s_grad, down_t_grad = outer(keep, range(early // ROWS, ns), range(TEXT_FIRST), (down_s_grad,), "down_grad_1")
     keep, *sends = token_sum(keep, got, down_t_grad, rows, "token_sum_4")
     bits = (HOPS[0], HOPS[1], HOPS[0] ^ HOPS[1])
-    gots = [flip(send, TOK, bit, n_tok) for send, bit in zip(sends, bits)]
+    gots = [flip(sends[i], TOK, bits[i], n_tok) for i in (2, 0, 1)]
     down_t_grad = outer(keep, (), range(TEXT_FIRST, nt), (down_t_grad,), "down_grad_2")[0]
     outs = [((rows, width), BF16)] * 2
     mixed, token_grad = call(

time: 57.6 us -> 55.5 us (0.964)
  waiting for transfers between devices: 8.02 us -> 6.03 us
    ppermute x10, waiting for transfers between devices: 8.02 us -> 6.03 us  [flip(): return lax.ppermute(value, axes, [(i, i ^ bit) for i in range(n)])]
  transfers between devices with their start and end apart: 10 -> 10, of which waited for: 6 -> 5; matrix products, arithmetic and copies ran while one was open for 0% -> 0% of each run, Pallas kernels for 25% -> 27%
where the time goes in v10:
time: 55.5 us; the launch traced here: 55.3 us
  Pallas kernels  33.1 us (60%)
  starting transfers between devices  15.1 us (27%)
  waiting for transfers between devices  6.03 us (11%)
  between operations  1.01 us (2%)
    pallas_call x16, Pallas kernels, call(): pl.pallas_call(seen, out_shape=shapes, in_specs=[pl.BlockSpec(memory_spac...  33.1 us
    ppermute x10, starting transfers between devices, flip(): return lax.ppermute(value, axes, [(i, i ^ bit) for i in range(n)])  15.1 us
    ppermute x10, waiting for transfers between devices, flip(): return lax.ppermute(value, axes, [(i, i ^ bit) for i in range(n)])  6.03 us
  transfers between devices with their start and end apart: 10, of which 5 were waited for; matrix products, arithmetic and copies ran while one was open for 0% of the time, Pallas kernels for 27%

profile of v10, /device:TPU:0, one launch (start us, length us, event | category | flops | bytes accessed | tf_op | source)
XLA Modules:
  0.0 55.3 jit_solution(7929677056370467306)
XLA Ops:
  0.6 0.7 %pack.1 = (bf16[10,1536,1024]{2,1,0:T(8,128)(2,1)S(1)}, bf16[2,3200]{1,0:T(2,128)(2,1)S(1)}) custom-call(s32[2]{0:T(128)} %refs_0_.1, bf16[2,1536]{1,0:T(2,128)(2,1)} %refs_1_.5, bf16[2,1536]{1,0:T(2,128)(2,1)} %refs_2_.5), custom_call_target="tpu_custom_call" | custom-call | tf_op jit(solution)/shard_map/pack/pallas_call | solution.py:60
  1.4 4.1 %collective-permute-start = (bf16[2,3200]{1,0:T(2,128)(2,1)S(1)}, bf16[2,3200]{1,0:T(2,128)(2,1)S(1)}, u32[]{:S(2)}, u32[]{:S(2)}) collective-permute-start(bf16[2,3200]{1,0:T(2,128)(2,1)S(1)} %get-tuple-element.24.refs_0_), channel_id=1, source_target_pairs={{0,8},{4,12},{8,0},{12,4},{16,24},{20,28},{24,16},{28,20},{1,9},{5... | collective-permute-start | bytes 38408 | tf_op jit(solution)/shard_map/ppermute | solution.py:417
  5.5 2.9 %load_gate_text.1.refs_2_.refs_6_ = bf16[10,1536,1024]{2,1,0:T(8,128)(2,1)S(1)} custom-call(bf16[2,3200]{1,0:T(2,128)(2,1)S(1)} %get-tuple-element.24.refs_0_, bf16[1536,2048]{1,0:T(8,128)(2,1)} %refs_1_.6, bf16[10,1536,1024]{2,1,0:T(8,128)(2,1)S(1)} %get-tuple-element.25.refs_2_), custom_call_target="tpu_custom_call", output_to_operand_aliasing={{}: (2, {})} | custom-call | bytes 6291456 | tf_op jit(solution)/shard_map/load_gate_text/pallas_call | solution.py:60
  8.5 1.6 %collective-permute-start.1 = (bf16[4,3200]{1,0:T(4,128)(2,1)S(1)}, bf16[4,3200]{1,0:T(4,128)(2,1)S(1)}, u32[]{:S(2)}, u32[]{:S(2)}) collective-permute-start(bf16[4,3200]{1,0:T(4,128)(2,1)S(1)} %join_4.1.refs_0_), channel_id=1, source_target_pairs={{0,4},{4,0},{8,12},{12,8},{16,20},{20,16},{24,28},{28,24},{1,5},{5... | collective-permute-start | bytes 76808 | tf_op jit(solution)/shard_map/ppermute | solution.py:417
  10.1 2.3 %collective-permute-done.1.refs_1_ = bf16[4,3200]{1,0:T(4,128)(2,1)S(1)} collective-permute-done((bf16[4,3200]{1,0:T(4,128)(2,1)S(1)}, bf16[4,3200]{1,0:T(4,128)(2,1)S(1)}, u32[]{:S(2)}, u32[]{:S(2)}) %collective-permute-start.1) | collective-permute-done | bytes 25632 | tf_op jit(solution)/shard_map/ppermute | solution.py:417
  12.4 1.6 %collective-permute-start.2 = (bf16[8,3200]{1,0:T(8,128)(2,1)S(1)}, bf16[8,3200]{1,0:T(8,128)(2,1)S(1)}, u32[]{:S(2)}, u32[]{:S(2)}) collective-permute-start(bf16[8,3200]{1,0:T(8,128)(2,1)S(1)} %join_8.1.refs_0_), channel_id=1, source_target_pairs={{0,16},{4,20},{8,24},{12,28},{16,0},{20,4},{24,8},{28,12},{1,17},{... | collective-permute-start | bytes 153608 | tf_op jit(solution)/shard_map/ppermute | solution.py:417
  14.0 2.6 %collective-permute-done.2.refs_1_ = bf16[8,3200]{1,0:T(8,128)(2,1)S(1)} collective-permute-done((bf16[8,3200]{1,0:T(8,128)(2,1)S(1)}, bf16[8,3200]{1,0:T(8,128)(2,1)S(1)}, u32[]{:S(2)}, u32[]{:S(2)}) %collective-permute-start.2) | collective-permute-done | bytes 51232 | tf_op jit(solution)/shard_map/ppermute | solution.py:417
  16.6 9.4 %hidden_partials.1 = (f32[3,16,1536]{2,1,0:T(8,128)S(1)}, f32[3,16,1536]{2,1,0:T(8,128)S(1)}, bf16[10,1536,1024]{2,1,0:T(8,128)(2,1)S(1)}) custom-call(bf16[16,3200]{1,0:T(8,128)(2,1)S(1)} %join_16.1.refs_0_.refs_1_, bf16[2048,1536]{1,0:T(8,128)(2,1)S(1)} %bitcast.3, bf16[3072,1536]{1,0:T(8,128)(2,1)S(1)} %bitcast.1, ...), custom_call_target="tpu_custom_call", output_to_operand_aliasing={{2}: (6, {})} | custom-call | flops 754974720 | bytes 25165824 | tf_op jit(solution)/shard_map/hidden_partials/pallas_call | solution.py:60
  26.1 1.4 %turn_1.1.refs_2_.refs_0_ = bf16[10,1536,1024]{2,1,0:T(8,128)(2,1)S(1)} custom-call(bf16[10,1536,1024]{2,1,0:T(8,128)(2,1)S(1)} %get-tuple-element.28.refs_0_, bf16[2048,1536]{1,0:T(8,128)(2,1)S(1)} %bitcast.3, bf16[3072,1536]{1,0:T(8,128)(2,1)S(1)} %bitcast.1), custom_call_target="tpu_custom_call", output_to_operand_aliasing={{}: (0, {})} | custom-call | bytes 15728640 | tf_op jit(solution)/shard_map/turn_1/pallas_call | solution.py:60
  27.5 0.1 collective-permute-done.3.refs_1_
  27.7 1.6 %collective-permute-start.4 = (bf16[3,16,1536]{2,1,0:T(8,128)(2,1)S(1)}, bf16[3,16,1536]{2,1,0:T(8,128)(2,1)S(1)}, u32[]{:S(2)}, u32[]{:S(2)}) collective-permute-start(bf16[3,16,1536]{2,1,0:T(8,128)(2,1)S(1)} %get-tuple-element.30), channel_id=1, source_target_pairs={{0,2},{1,3},{2,0},{3,1},{4,6},{5,7},{6,4},{7,5},{8,10},{9,11},{10,... | collective-permute-start | bytes 442376 | tf_op jit(solution)/shard_map/ppermute | solution.py:417
  29.3 3.9 %turn_2.1.refs_2_.refs_4_ = bf16[10,1536,1024]{2,1,0:T(8,128)(2,1)S(1)} custom-call(bf16[10,1536,1024]{2,1,0:T(8,128)(2,1)S(1)} %turn_1.1.refs_2_.refs_0_, bf16[2048,1536]{1,0:T(8,128)(2,1)S(1)} %bitcast.3, bf16[3072,1536]{1,0:T(8,128)(2,1)S(1)} %bitcast.1), custom_call_target="tpu_custom_call", output_to_operand_aliasing={{}: (0, {})} | custom-call | bytes 47185920 | tf_op jit(solution)/shard_map/turn_2/pallas_call | solution.py:60
  33.2 0.7 %collective-permute-done.4.refs_1_ = bf16[3,16,1536]{2,1,0:T(8,128)(2,1)S(1)} collective-permute-done((bf16[3,16,1536]{2,1,0:T(8,128)(2,1)S(1)}, bf16[3,16,1536]{2,1,0:T(8,128)(2,1)S(1)}, u32[]{:S(2)}, u32[]{:S(2)}) %collective-permute-start.4) | collective-permute-done | bytes 147488 | tf_op jit(solution)/shard_map/ppermute | solution.py:417
  34.0 0.1 collective-permute-start.5
  34.0 1.3 %mixed_own.1.refs_3_ = f32[16,1536]{1,0:T(8,128)S(1)} custom-call(bf16[16,3200]{1,0:T(8,128)(2,1)S(1)} %join_16.1.refs_0_.refs_1_, bf16[3,16,1536]{2,1,0:T(8,128)(2,1)S(1)} %hidden.1.refs_1_, bf16[2048,1536]{1,0:T(8,128)(2,1)S(1)} %bitcast.3, bf16[3072,1536]{1,0:T(8,128)(2,1)S(1)} %bitcast.1, bf16[10,1536,1024]{2,1,0:T(8,128)(2,1)S(1)} %turn_2.1.refs_2_.refs_4_), custom_call_target="tpu_custom_call" | custom-call | flops 125829120 | tf_op jit(solution)/shard_map/mixed_own/pallas_call | solution.py:60
  35.4 7.5 %token_partials.1 = (f32[8,3072]{1,0:T(8,128)S(1)}, bf16[8,3072]{1,0:T(8,128)(2,1)S(1)}, bf16[16,3072]{1,0:T(8,128)(2,1)S(1)}, bf16[16,2048]{1,0:T(8,128)(2,1)S(1)}, bf16[3072,1536]{1,0:T(8,128)(2,1)}) custom-call(bf16[16,3200]{1,0:T(8,128)(2,1)S(1)} %join_16.1.refs_0_.refs_1_, bf16[3,16,1536]{2,1,0:T(8,128)(2,1)S(1)} %hidden.1.refs_1_, ...), custom_call_target="tpu_custom_call" | custom-call | flops 754974720 | tf_op jit(solution)/shard_map/token_partials/pallas_call | solution.py:60
  42.9 1.6 %collective-permute-start.6 = (bf16[8,3072]{1,0:T(8,128)(2,1)S(1)}, bf16[8,3072]{1,0:T(8,128)(2,1)S(1)}, u32[]{:S(2)}, u32[]{:S(2)}) collective-permute-start(bf16[8,3072]{1,0:T(8,128)(2,1)S(1)} %get-tuple-element.32), channel_id=1, source_target_pairs={{0,16},{4,20},{8,24},{12,28},{16,0},{20,4},{24,8},{28,12},{1,17},{... | collective-permute-start | bytes 147464 | tf_op jit(solution)/shard_map/ppermute | solution.py:417
  44.5 2.6 %down_grad_1.1 = (bf16[3072,1536]{1,0:T(8,128)(2,1)}, bf16[2048,1536]{1,0:T(8,128)(2,1)}) custom-call(f32[8,3072]{1,0:T(8,128)S(1)} %get-tuple-element.31.refs_0_, bf16[16,3200]{1,0:T(8,128)(2,1)S(1)} %join_16.1.refs_0_.refs_1_, bf16[16,3072]{1,0:T(8,128)(2,1)S(1)} %get-tuple-element.33.refs_2_, ...), custom_call_target="tpu_custom_call", output_to_operand_aliasing={{0}: (4, {})} | custom-call | flops 75497472 | bytes 4718592 | tf_op jit(solution)/shard_map/down_grad_1/pallas_call | solution.py:60
  47.1 2.8 %collective-permute-start.7 = (bf16[2,3072]{1,0:T(2,128)(2,1)S(1)}, bf16[2,3072]{1,0:T(2,128)(2,1)S(1)}, u32[]{:S(2)}, u32[]{:S(2)}) collective-permute-start(bf16[2,3072]{1,0:T(2,128)(2,1)S(1)} %get-tuple-element.38), channel_id=1, source_target_pairs={{0,12},{4,8},{8,4},{12,0},{16,28},{20,24},{24,20},{28,16},{1,13},{... | collective-permute-start | bytes 36872 | tf_op jit(solution)/shard_map/ppermute | solution.py:417
  49.9 0.3 collective-permute-start.8
  50.2 1.3 %collective-permute-start.9 = (bf16[2,3072]{1,0:T(2,128)(2,1)S(1)}, bf16[2,3072]{1,0:T(2,128)(2,1)S(1)}, u32[]{:S(2)}, u32[]{:S(2)}) collective-permute-start(bf16[2,3072]{1,0:T(2,128)(2,1)S(1)} %get-tuple-element.40), channel_id=1, source_target_pairs={{0,4},{4,0},{8,12},{12,8},{16,20},{20,16},{24,28},{28,24},{1,5},{5... | collective-permute-start | bytes 36872 | tf_op jit(solution)/shard_map/ppermute | solution.py:417
  51.6 2.6 %down_grad_2.1 = bf16[2048,1536]{1,0:T(8,128)(2,1)} custom-call(f32[2,3072]{1,0:T(2,128)S(1)} %get-tuple-element.37.refs_0_, bf16[16,3200]{1,0:T(8,128)(2,1)S(1)} %join_16.1.refs_0_.refs_1_, bf16[16,3072]{1,0:T(8,128)(2,1)S(1)} %get-tuple-element.33.refs_2_, bf16[16,2048]{1,0:T(8,128)(2,1)S(1)} %get-tuple-element.34.refs_3_, ...), custom_call_target="tpu_custom_call", output_to_operand_aliasing={{}: (4, {})} | custom-call | flops 75497472 | bytes 4718592 | tf_op jit(solution)/shard_map/down_grad_2/pallas_call | solution.py:60
  54.2 0.3 collective-permute-done.8.refs_2_
  54.5 0.6 %token_sum_1.1 = (bf16[2,1536]{1,0:T(2,128)(2,1)}, bf16[2,1536]{1,0:T(2,128)(2,1)}) custom-call(f32[2,3072]{1,0:T(2,128)S(1)} %get-tuple-element.37.refs_0_, bf16[2,3072]{1,0:T(2,128)(2,1)S(1)} %collective-permute-done.7.refs_1_, bf16[2,3072]{1,0:T(2,128)(2,1)S(1)} %collective-permute-done.8.refs_2_, bf16[2,3072]{1,0:T(2,128)(2,1)S(1)} %collective-permute-done.9.refs_3_), custom_call_target="tpu_custom_call" | custom-call | tf_op jit(solution)/shard_map/token_sum_1/pallas_call | solution.py:60
  (24 shorter events, 0.3 us)
Async XLA Ops:
  1.4 7.0 %collective-permute-start = (bf16[2,3200]{1,0:T(2,128)(2,1)S(1)}, bf16[2,3200]{1,0:T(2,128)(2,1)S(1)}, u32[]{:S(2)}, u32[]{:S(2)}) collective-permute-start(bf16[2,3200]{1,0:T(2,128)(2,1)S(1)} %get-tuple-element.24.refs_0_), channel_id=1, source_target_pairs={{0,8},{4,12},{8,0},{12,4},{16,24},{20,28},{24,16},{28,20},{1,9},{5... | collective-permute-start | bytes 38408 | tf_op jit(solution)/shard_map/ppermute | solution.py:417
  8.4 8.2 %slice-start = ((s8[9437184]{0:T(1024)(128)(4,1)}), s8[4194304]{0:T(1024)(128)(4,1)S(1)}, s32[]{:S(2)}) async-start(s8[9437184]{0:T(1024)(128)(4,1)} %bitcast), calls=%async_computation | async-start | bytes 8388608
  8.4 8.2 %slice-start.1 = ((s8[9437184]{0:T(1024)(128)(4,1)}), s8[4194304]{0:T(1024)(128)(4,1)S(1)}, s32[]{:S(2)}) async-start(s8[9437184]{0:T(1024)(128)(4,1)} %bitcast), calls=%async_computation.1 | async-start | bytes 8388608
  8.4 8.2 %slice-start.3 = ((s8[6291456]{0:T(1024)(128)(4,1)}), s8[4194304]{0:T(1024)(128)(4,1)S(1)}, s32[]{:S(2)}) async-start(s8[6291456]{0:T(1024)(128)(4,1)} %bitcast.2), calls=%async_computation.3 | async-start | bytes 8388608
  8.4 8.1 %slice-start.2 = ((s8[9437184]{0:T(1024)(128)(4,1)}), s8[1048576]{0:T(1024)(128)(4,1)S(1)}, s32[]{:S(2)}) async-start(s8[9437184]{0:T(1024)(128)(4,1)} %bitcast), calls=%async_computation.2 | async-start | bytes 2097152
  8.4 8.1 %slice-start.4 = ((s8[6291456]{0:T(1024)(128)(4,1)}), s8[2097152]{0:T(1024)(128)(4,1)S(1)}, s32[]{:S(2)}) async-start(s8[6291456]{0:T(1024)(128)(4,1)} %bitcast.2), calls=%async_computation.4 | async-start | bytes 4194304
  8.5 3.9 %collective-permute-start.1 = (bf16[4,3200]{1,0:T(4,128)(2,1)S(1)}, bf16[4,3200]{1,0:T(4,128)(2,1)S(1)}, u32[]{:S(2)}, u32[]{:S(2)}) collective-permute-start(bf16[4,3200]{1,0:T(4,128)(2,1)S(1)} %join_4.1.refs_0_), channel_id=1, source_target_pairs={{0,4},{4,0},{8,12},{12,8},{16,20},{20,16},{24,28},{28,24},{1,5},{5... | collective-permute-start | bytes 76808 | tf_op jit(solution)/shard_map/ppermute | solution.py:417
  12.4 4.2 %collective-permute-start.2 = (bf16[8,3200]{1,0:T(8,128)(2,1)S(1)}, bf16[8,3200]{1,0:T(8,128)(2,1)S(1)}, u32[]{:S(2)}, u32[]{:S(2)}) collective-permute-start(bf16[8,3200]{1,0:T(8,128)(2,1)S(1)} %join_8.1.refs_0_), channel_id=1, source_target_pairs={{0,16},{4,20},{8,24},{12,28},{16,0},{20,4},{24,8},{28,12},{1,17},{... | collective-permute-start | bytes 153608 | tf_op jit(solution)/shard_map/ppermute | solution.py:417
  26.0 1.6 %collective-permute-start.3 = (f32[3,16,1536]{2,1,0:T(8,128)S(1)}, f32[3,16,1536]{2,1,0:T(8,128)S(1)}, u32[]{:S(2)}, u32[]{:S(2)}) collective-permute-start(f32[3,16,1536]{2,1,0:T(8,128)S(1)} %get-tuple-element.27), channel_id=1, source_target_pairs={{0,1},{1,0},{2,3},{3,2},{4,5},{5,4},{6,7},{7,6},{8,9},{9,8},{10,11... | collective-permute-start | bytes 884744 | tf_op jit(solution)/shard_map/ppermute | solution.py:417
  27.7 6.2 %collective-permute-start.4 = (bf16[3,16,1536]{2,1,0:T(8,128)(2,1)S(1)}, bf16[3,16,1536]{2,1,0:T(8,128)(2,1)S(1)}, u32[]{:S(2)}, u32[]{:S(2)}) collective-permute-start(bf16[3,16,1536]{2,1,0:T(8,128)(2,1)S(1)} %get-tuple-element.30), channel_id=1, source_target_pairs={{0,2},{1,3},{2,0},{3,1},{4,6},{5,7},{6,4},{7,5},{8,10},{9,11},{10,... | collective-permute-start | bytes 442376 | tf_op jit(solution)/shard_map/ppermute | solution.py:417
  34.0 1.4 %collective-permute-start.5 = (bf16[3,16,1536]{2,1,0:T(8,128)(2,1)S(1)}, bf16[3,16,1536]{2,1,0:T(8,128)(2,1)S(1)}, u32[]{:S(2)}, u32[]{:S(2)}) collective-permute-start(bf16[3,16,1536]{2,1,0:T(8,128)(2,1)S(1)} %hidden.1.refs_1_), channel_id=1, source_target_pairs={{0,1},{1,0},{2,3},{3,2},{4,5},{5,4},{6,7},{7,6},{8,9},{9,8},{10,11... | collective-permute-start | bytes 442376 | tf_op jit(solution)/shard_map/ppermute | solution.py:417
  42.9 4.2 %collective-permute-start.6 = (bf16[8,3072]{1,0:T(8,128)(2,1)S(1)}, bf16[8,3072]{1,0:T(8,128)(2,1)S(1)}, u32[]{:S(2)}, u32[]{:S(2)}) collective-permute-start(bf16[8,3072]{1,0:T(8,128)(2,1)S(1)} %get-tuple-element.32), channel_id=1, source_target_pairs={{0,16},{4,20},{8,24},{12,28},{16,0},{20,4},{24,8},{28,12},{1,17},{... | collective-permute-start | bytes 147464 | tf_op jit(solution)/shard_map/ppermute | solution.py:417
  47.1 7.1 %collective-permute-start.7 = (bf16[2,3072]{1,0:T(2,128)(2,1)S(1)}, bf16[2,3072]{1,0:T(2,128)(2,1)S(1)}, u32[]{:S(2)}, u32[]{:S(2)}) collective-permute-start(bf16[2,3072]{1,0:T(2,128)(2,1)S(1)} %get-tuple-element.38), channel_id=1, source_target_pairs={{0,12},{4,8},{8,4},{12,0},{16,28},{20,24},{24,20},{28,16},{1,13},{... | collective-permute-start | bytes 36872 | tf_op jit(solution)/shard_map/ppermute | solution.py:417
  49.9 4.6 %collective-permute-start.8 = (bf16[2,3072]{1,0:T(2,128)(2,1)S(1)}, bf16[2,3072]{1,0:T(2,128)(2,1)S(1)}, u32[]{:S(2)}, u32[]{:S(2)}) collective-permute-start(bf16[2,3072]{1,0:T(2,128)(2,1)S(1)} %get-tuple-element.39), channel_id=1, source_target_pairs={{0,8},{4,12},{8,0},{12,4},{16,24},{20,28},{24,16},{28,20},{1,9},{5... | collective-permute-start | bytes 36872 | tf_op jit(solution)/shard_map/ppermute | solution.py:417
  50.2 4.3 %collective-permute-start.9 = (bf16[2,3072]{1,0:T(2,128)(2,1)S(1)}, bf16[2,3072]{1,0:T(2,128)(2,1)S(1)}, u32[]{:S(2)}, u32[]{:S(2)}) collective-permute-start(bf16[2,3072]{1,0:T(2,128)(2,1)S(1)} %get-tuple-element.40), channel_id=1, source_target_pairs={{0,4},{4,0},{8,12},{12,8},{16,20},{20,16},{24,28},{28,24},{1,5},{5... | collective-permute-start | bytes 36872 | tf_op jit(solution)/shard_map/ppermute | solution.py:417

commit v11 on v10

--- a/solution.py
+++ b/solution.py
@@ -12,13 +12,12 @@
 F32 = jnp.float32
 BF16 = jnp.bfloat16
 MIB = 1 << 20
-LIMIT = 6
+LIMIT = 8
 BLOCK = 512
 WIDE = 1024
 ROWS = 256
 TILE = 128
 TURN_FIRST = 5
-SLOTS = 4
 EARLY_ROWS = 2048
 TEXT_FIRST = 2
 PLACES = {"h": pl.ANY, "v": pltpu.VMEM, "s": pltpu.SMEM}
@@ -310,26 +309,21 @@
     blocks = [(dgt, nt), (dut, nt), (dgs, ns), (dus, ns)]
     blocks = [(ref, i) for ref, n in blocks for i in range(n)]
     c = arr_ref[:, width : 2 * width]
-    count, n_slots = grad_rows // ROWS, slots.shape[0]
-    squares = [(r, b) for r in range(width // BLOCK) for b in range(len(blocks))]
-    copies, total = [], None
-    for n, (r, b) in enumerate(squares):
-        ref, j = blocks[b]
-        product = times if b in turned else contract_last
-        value = product(ref[:, j * BLOCK : (j + 1) * BLOCK], square_at(wide_ref, b, r)[...])
-        total = value if b == 0 else total + value
-        if b == len(blocks) - 1:
-            start = width + r * BLOCK
-            out[:, start : start + BLOCK] = total
-        while len(copies) * len(squares) < (n + 1) * count:
-            i = len(copies)
-            if i >= n_slots:
-                copies[i - n_slots].wait()
-            cut = slice(i * ROWS, (i + 1) * ROWS)
-            outer_block(hs_ref[:, cut], c, slots.at[i % n_slots])
-            copies.append(pltpu.make_async_copy(slots.at[i % n_slots], grad_hbm.at[cut], sems.at[i % n_slots]))
-            copies[i].start()
-    for copy in copies[-n_slots:]:
+    copies = []
+    for i in range(grad_rows // ROWS):
+        cut = slice(i * ROWS, (i + 1) * ROWS)
+        outer_block(hs_ref[:, cut], c, slots.at[i])
+        copies.append(pltpu.make_async_copy(slots.at[i], grad_hbm.at[cut], sems.at[i]))
+    for copy in copies:
+        copy.start()
+    for r in range(width // BLOCK):
+        total = jnp.zeros((out.shape[0], BLOCK), F32)
+        for b, (ref, j) in enumerate(blocks):
+            product = times if b in turned else contract_last
+            total += product(ref[:, j * BLOCK : (j + 1) * BLOCK], square_at(wide_ref, b, r)[...])
+        start = width + r * BLOCK
+        out[:, start : start + BLOCK] = total
+    for copy in copies:
         copy.wait()
     half = keep_ref.shape[0]
     keep_ref[...] = out[:half]
@@ -339,9 +333,10 @@
 def back(arr, done, other, own, wide, down_t, down_s, turned, grad_rows):
     rows, width = arr.shape[0], down_s.shape[1]
     fs, ft = down_s.shape[0], down_t.shape[0]
+    count = grad_rows // ROWS
     hidden = [((rows, fs), BF16), ((rows, ft), BF16)]
     scratch = [pltpu.VMEM(*s) for s in hidden + hidden] + [pltpu.VMEM((rows, 2 * width), F32)]
-    scratch += [pltpu.VMEM((SLOTS, ROWS, width), BF16), pltpu.SemaphoreType.DMA((SLOTS,))]
+    scratch += [pltpu.VMEM((count, ROWS, width), BF16), pltpu.SemaphoreType.DMA((count,))]
     return call(
         functools.partial(back_body, turned, grad_rows),
         "token_partials",

time: 55.5 us -> 55 us (level)
  no operation moved by 1% of the time
where the time goes in v11:
time: 55 us; the launch traced here: 54.8 us
  Pallas kernels  32.6 us (59%)
  starting transfers between devices  15.1 us (27%)
  waiting for transfers between devices  6.03 us (11%)
  between operations  1.01 us (2%)
    pallas_call x16, Pallas kernels, call(): pl.pallas_call(seen, out_shape=shapes, in_specs=[pl.BlockSpec(memory_spac...  32.6 us
    ppermute x10, starting transfers between devices, flip(): return lax.ppermute(value, axes, [(i, i ^ bit) for i in range(n)])  15.1 us
    ppermute x10, waiting for transfers between devices, flip(): return lax.ppermute(value, axes, [(i, i ^ bit) for i in range(n)])  6.03 us
  transfers between devices with their start and end apart: 10, of which 5 were waited for; matrix products, arithmetic and copies ran while one was open for 0% of the time, Pallas kernels for 27%

profile of v11, /device:TPU:0, one launch (start us, length us, event | category | flops | bytes accessed | tf_op | source)
XLA Modules:
  0.0 54.8 jit_solution(10346853088106357546)
XLA Ops:
  0.6 0.7 %pack.1 = (bf16[10,1536,1024]{2,1,0:T(8,128)(2,1)S(1)}, bf16[2,3200]{1,0:T(2,128)(2,1)S(1)}) custom-call(s32[2]{0:T(128)} %refs_0_.1, bf16[2,1536]{1,0:T(2,128)(2,1)} %refs_1_.5, bf16[2,1536]{1,0:T(2,128)(2,1)} %refs_2_.5), custom_call_target="tpu_custom_call" | custom-call | tf_op jit(solution)/shard_map/pack/pallas_call | solution.py:59
  1.4 4.1 %collective-permute-start = (bf16[2,3200]{1,0:T(2,128)(2,1)S(1)}, bf16[2,3200]{1,0:T(2,128)(2,1)S(1)}, u32[]{:S(2)}, u32[]{:S(2)}) collective-permute-start(bf16[2,3200]{1,0:T(2,128)(2,1)S(1)} %get-tuple-element.24.refs_0_), channel_id=1, source_target_pairs={{0,8},{4,12},{8,0},{12,4},{16,24},{20,28},{24,16},{28,20},{1,9},{5... | collective-permute-start | bytes 38408 | tf_op jit(solution)/shard_map/ppermute | solution.py:412
  5.5 2.9 %load_gate_text.1.refs_2_.refs_6_ = bf16[10,1536,1024]{2,1,0:T(8,128)(2,1)S(1)} custom-call(bf16[2,3200]{1,0:T(2,128)(2,1)S(1)} %get-tuple-element.24.refs_0_, bf16[1536,2048]{1,0:T(8,128)(2,1)} %refs_1_.6, bf16[10,1536,1024]{2,1,0:T(8,128)(2,1)S(1)} %get-tuple-element.25.refs_2_), custom_call_target="tpu_custom_call", output_to_operand_aliasing={{}: (2, {})} | custom-call | bytes 6291456 | tf_op jit(solution)/shard_map/load_gate_text/pallas_call | solution.py:59
  8.5 1.6 %collective-permute-start.1 = (bf16[4,3200]{1,0:T(4,128)(2,1)S(1)}, bf16[4,3200]{1,0:T(4,128)(2,1)S(1)}, u32[]{:S(2)}, u32[]{:S(2)}) collective-permute-start(bf16[4,3200]{1,0:T(4,128)(2,1)S(1)} %join_4.1.refs_0_), channel_id=1, source_target_pairs={{0,4},{4,0},{8,12},{12,8},{16,20},{20,16},{24,28},{28,24},{1,5},{5... | collective-permute-start | bytes 76808 | tf_op jit(solution)/shard_map/ppermute | solution.py:412
  10.1 2.3 %collective-permute-done.1.refs_1_ = bf16[4,3200]{1,0:T(4,128)(2,1)S(1)} collective-permute-done((bf16[4,3200]{1,0:T(4,128)(2,1)S(1)}, bf16[4,3200]{1,0:T(4,128)(2,1)S(1)}, u32[]{:S(2)}, u32[]{:S(2)}) %collective-permute-start.1) | collective-permute-done | bytes 25632 | tf_op jit(solution)/shard_map/ppermute | solution.py:412
  12.4 1.6 %collective-permute-start.2 = (bf16[8,3200]{1,0:T(8,128)(2,1)S(1)}, bf16[8,3200]{1,0:T(8,128)(2,1)S(1)}, u32[]{:S(2)}, u32[]{:S(2)}) collective-permute-start(bf16[8,3200]{1,0:T(8,128)(2,1)S(1)} %join_8.1.refs_0_), channel_id=1, source_target_pairs={{0,16},{4,20},{8,24},{12,28},{16,0},{20,4},{24,8},{28,12},{1,17},{... | collective-permute-start | bytes 153608 | tf_op jit(solution)/shard_map/ppermute | solution.py:412
  14.0 2.6 %collective-permute-done.2.refs_1_ = bf16[8,3200]{1,0:T(8,128)(2,1)S(1)} collective-permute-done((bf16[8,3200]{1,0:T(8,128)(2,1)S(1)}, bf16[8,3200]{1,0:T(8,128)(2,1)S(1)}, u32[]{:S(2)}, u32[]{:S(2)}) %collective-permute-start.2) | collective-permute-done | bytes 51232 | tf_op jit(solution)/shard_map/ppermute | solution.py:412
  16.6 9.4 %hidden_partials.1 = (f32[3,16,1536]{2,1,0:T(8,128)S(1)}, f32[3,16,1536]{2,1,0:T(8,128)S(1)}, bf16[10,1536,1024]{2,1,0:T(8,128)(2,1)S(1)}) custom-call(bf16[16,3200]{1,0:T(8,128)(2,1)S(1)} %join_16.1.refs_0_.refs_1_, bf16[2048,1536]{1,0:T(8,128)(2,1)S(1)} %bitcast.3, bf16[3072,1536]{1,0:T(8,128)(2,1)S(1)} %bitcast.1, ...), custom_call_target="tpu_custom_call", output_to_operand_aliasing={{2}: (6, {})} | custom-call | flops 754974720 | bytes 25165824 | tf_op jit(solution)/shard_map/hidden_partials/pallas_call | solution.py:59
  26.1 1.4 %turn_1.1.refs_2_.refs_0_ = bf16[10,1536,1024]{2,1,0:T(8,128)(2,1)S(1)} custom-call(bf16[10,1536,1024]{2,1,0:T(8,128)(2,1)S(1)} %get-tuple-element.28.refs_0_, bf16[2048,1536]{1,0:T(8,128)(2,1)S(1)} %bitcast.3, bf16[3072,1536]{1,0:T(8,128)(2,1)S(1)} %bitcast.1), custom_call_target="tpu_custom_call", output_to_operand_aliasing={{}: (0, {})} | custom-call | bytes 15728640 | tf_op jit(solution)/shard_map/turn_1/pallas_call | solution.py:59
  27.5 0.1 collective-permute-done.3.refs_1_
  27.7 1.6 %collective-permute-start.4 = (bf16[3,16,1536]{2,1,0:T(8,128)(2,1)S(1)}, bf16[3,16,1536]{2,1,0:T(8,128)(2,1)S(1)}, u32[]{:S(2)}, u32[]{:S(2)}) collective-permute-start(bf16[3,16,1536]{2,1,0:T(8,128)(2,1)S(1)} %get-tuple-element.30), channel_id=1, source_target_pairs={{0,2},{1,3},{2,0},{3,1},{4,6},{5,7},{6,4},{7,5},{8,10},{9,11},{10,... | collective-permute-start | bytes 442376 | tf_op jit(solution)/shard_map/ppermute | solution.py:412
  29.3 3.9 %turn_2.1.refs_2_.refs_4_ = bf16[10,1536,1024]{2,1,0:T(8,128)(2,1)S(1)} custom-call(bf16[10,1536,1024]{2,1,0:T(8,128)(2,1)S(1)} %turn_1.1.refs_2_.refs_0_, bf16[2048,1536]{1,0:T(8,128)(2,1)S(1)} %bitcast.3, bf16[3072,1536]{1,0:T(8,128)(2,1)S(1)} %bitcast.1), custom_call_target="tpu_custom_call", output_to_operand_aliasing={{}: (0, {})} | custom-call | bytes 47185920 | tf_op jit(solution)/shard_map/turn_2/pallas_call | solution.py:59
  33.2 0.7 %collective-permute-done.4.refs_1_ = bf16[3,16,1536]{2,1,0:T(8,128)(2,1)S(1)} collective-permute-done((bf16[3,16,1536]{2,1,0:T(8,128)(2,1)S(1)}, bf16[3,16,1536]{2,1,0:T(8,128)(2,1)S(1)}, u32[]{:S(2)}, u32[]{:S(2)}) %collective-permute-start.4) | collective-permute-done | bytes 147488 | tf_op jit(solution)/shard_map/ppermute | solution.py:412
  34.0 0.1 collective-permute-start.5
  34.0 1.3 %mixed_own.1.refs_3_ = f32[16,1536]{1,0:T(8,128)S(1)} custom-call(bf16[16,3200]{1,0:T(8,128)(2,1)S(1)} %join_16.1.refs_0_.refs_1_, bf16[3,16,1536]{2,1,0:T(8,128)(2,1)S(1)} %hidden.1.refs_1_, bf16[2048,1536]{1,0:T(8,128)(2,1)S(1)} %bitcast.3, bf16[3072,1536]{1,0:T(8,128)(2,1)S(1)} %bitcast.1, bf16[10,1536,1024]{2,1,0:T(8,128)(2,1)S(1)} %turn_2.1.refs_2_.refs_4_), custom_call_target="tpu_custom_call" | custom-call | flops 125829120 | tf_op jit(solution)/shard_map/mixed_own/pallas_call | solution.py:59
  35.4 7.0 %token_partials.1 = (f32[8,3072]{1,0:T(8,128)S(1)}, bf16[8,3072]{1,0:T(8,128)(2,1)S(1)}, bf16[16,3072]{1,0:T(8,128)(2,1)S(1)}, bf16[16,2048]{1,0:T(8,128)(2,1)S(1)}, bf16[3072,1536]{1,0:T(8,128)(2,1)}) custom-call(bf16[16,3200]{1,0:T(8,128)(2,1)S(1)} %join_16.1.refs_0_.refs_1_, bf16[3,16,1536]{2,1,0:T(8,128)(2,1)S(1)} %hidden.1.refs_1_, ...), custom_call_target="tpu_custom_call" | custom-call | flops 754974720 | tf_op jit(solution)/shard_map/token_partials/pallas_call | solution.py:59
  42.4 1.6 %collective-permute-start.6 = (bf16[8,3072]{1,0:T(8,128)(2,1)S(1)}, bf16[8,3072]{1,0:T(8,128)(2,1)S(1)}, u32[]{:S(2)}, u32[]{:S(2)}) collective-permute-start(bf16[8,3072]{1,0:T(8,128)(2,1)S(1)} %get-tuple-element.32), channel_id=1, source_target_pairs={{0,16},{4,20},{8,24},{12,28},{16,0},{20,4},{24,8},{28,12},{1,17},{... | collective-permute-start | bytes 147464 | tf_op jit(solution)/shard_map/ppermute | solution.py:412
  44.0 2.6 %down_grad_1.1 = (bf16[3072,1536]{1,0:T(8,128)(2,1)}, bf16[2048,1536]{1,0:T(8,128)(2,1)}) custom-call(f32[8,3072]{1,0:T(8,128)S(1)} %get-tuple-element.31.refs_0_, bf16[16,3200]{1,0:T(8,128)(2,1)S(1)} %join_16.1.refs_0_.refs_1_, bf16[16,3072]{1,0:T(8,128)(2,1)S(1)} %get-tuple-element.33.refs_2_, ...), custom_call_target="tpu_custom_call", output_to_operand_aliasing={{0}: (4, {})} | custom-call | flops 75497472 | bytes 4718592 | tf_op jit(solution)/shard_map/down_grad_1/pallas_call | solution.py:59
  46.6 2.8 %collective-permute-start.7 = (bf16[2,3072]{1,0:T(2,128)(2,1)S(1)}, bf16[2,3072]{1,0:T(2,128)(2,1)S(1)}, u32[]{:S(2)}, u32[]{:S(2)}) collective-permute-start(bf16[2,3072]{1,0:T(2,128)(2,1)S(1)} %get-tuple-element.38), channel_id=1, source_target_pairs={{0,12},{4,8},{8,4},{12,0},{16,28},{20,24},{24,20},{28,16},{1,13},{... | collective-permute-start | bytes 36872 | tf_op jit(solution)/shard_map/ppermute | solution.py:412
  49.4 0.3 collective-permute-start.8
  49.7 1.4 %collective-permute-start.9 = (bf16[2,3072]{1,0:T(2,128)(2,1)S(1)}, bf16[2,3072]{1,0:T(2,128)(2,1)S(1)}, u32[]{:S(2)}, u32[]{:S(2)}) collective-permute-start(bf16[2,3072]{1,0:T(2,128)(2,1)S(1)} %get-tuple-element.40), channel_id=1, source_target_pairs={{0,4},{4,0},{8,12},{12,8},{16,20},{20,16},{24,28},{28,24},{1,5},{5... | collective-permute-start | bytes 36872 | tf_op jit(solution)/shard_map/ppermute | solution.py:412
  51.1 2.6 %down_grad_2.1 = bf16[2048,1536]{1,0:T(8,128)(2,1)} custom-call(f32[2,3072]{1,0:T(2,128)S(1)} %get-tuple-element.37.refs_0_, bf16[16,3200]{1,0:T(8,128)(2,1)S(1)} %join_16.1.refs_0_.refs_1_, bf16[16,3072]{1,0:T(8,128)(2,1)S(1)} %get-tuple-element.33.refs_2_, bf16[16,2048]{1,0:T(8,128)(2,1)S(1)} %get-tuple-element.34.refs_3_, ...), custom_call_target="tpu_custom_call", output_to_operand_aliasing={{}: (4, {})} | custom-call | flops 75497472 | bytes 4718592 | tf_op jit(solution)/shard_map/down_grad_2/pallas_call | solution.py:59
  53.7 0.3 collective-permute-done.8.refs_2_
  54.0 0.6 %token_sum_1.1 = (bf16[2,1536]{1,0:T(2,128)(2,1)}, bf16[2,1536]{1,0:T(2,128)(2,1)}) custom-call(f32[2,3072]{1,0:T(2,128)S(1)} %get-tuple-element.37.refs_0_, bf16[2,3072]{1,0:T(2,128)(2,1)S(1)} %collective-permute-done.7.refs_1_, bf16[2,3072]{1,0:T(2,128)(2,1)S(1)} %collective-permute-done.8.refs_2_, bf16[2,3072]{1,0:T(2,128)(2,1)S(1)} %collective-permute-done.9.refs_3_), custom_call_target="tpu_custom_call" | custom-call | tf_op jit(solution)/shard_map/token_sum_1/pallas_call | solution.py:59
  (24 shorter events, 0.3 us)
Async XLA Ops:
  1.4 7.0 %collective-permute-start = (bf16[2,3200]{1,0:T(2,128)(2,1)S(1)}, bf16[2,3200]{1,0:T(2,128)(2,1)S(1)}, u32[]{:S(2)}, u32[]{:S(2)}) collective-permute-start(bf16[2,3200]{1,0:T(2,128)(2,1)S(1)} %get-tuple-element.24.refs_0_), channel_id=1, source_target_pairs={{0,8},{4,12},{8,0},{12,4},{16,24},{20,28},{24,16},{28,20},{1,9},{5... | collective-permute-start | bytes 38408 | tf_op jit(solution)/shard_map/ppermute | solution.py:412
  8.4 8.2 %slice-start = ((s8[9437184]{0:T(1024)(128)(4,1)}), s8[4194304]{0:T(1024)(128)(4,1)S(1)}, s32[]{:S(2)}) async-start(s8[9437184]{0:T(1024)(128)(4,1)} %bitcast), calls=%async_computation | async-start | bytes 8388608
  8.4 8.2 %slice-start.1 = ((s8[9437184]{0:T(1024)(128)(4,1)}), s8[4194304]{0:T(1024)(128)(4,1)S(1)}, s32[]{:S(2)}) async-start(s8[9437184]{0:T(1024)(128)(4,1)} %bitcast), calls=%async_computation.1 | async-start | bytes 8388608
  8.4 8.2 %slice-start.3 = ((s8[6291456]{0:T(1024)(128)(4,1)}), s8[4194304]{0:T(1024)(128)(4,1)S(1)}, s32[]{:S(2)}) async-start(s8[6291456]{0:T(1024)(128)(4,1)} %bitcast.2), calls=%async_computation.3 | async-start | bytes 8388608
  8.4 8.1 %slice-start.2 = ((s8[9437184]{0:T(1024)(128)(4,1)}), s8[1048576]{0:T(1024)(128)(4,1)S(1)}, s32[]{:S(2)}) async-start(s8[9437184]{0:T(1024)(128)(4,1)} %bitcast), calls=%async_computation.2 | async-start | bytes 2097152
  8.4 8.1 %slice-start.4 = ((s8[6291456]{0:T(1024)(128)(4,1)}), s8[2097152]{0:T(1024)(128)(4,1)S(1)}, s32[]{:S(2)}) async-start(s8[6291456]{0:T(1024)(128)(4,1)} %bitcast.2), calls=%async_computation.4 | async-start | bytes 4194304
  8.5 3.9 %collective-permute-start.1 = (bf16[4,3200]{1,0:T(4,128)(2,1)S(1)}, bf16[4,3200]{1,0:T(4,128)(2,1)S(1)}, u32[]{:S(2)}, u32[]{:S(2)}) collective-permute-start(bf16[4,3200]{1,0:T(4,128)(2,1)S(1)} %join_4.1.refs_0_), channel_id=1, source_target_pairs={{0,4},{4,0},{8,12},{12,8},{16,20},{20,16},{24,28},{28,24},{1,5},{5... | collective-permute-start | bytes 76808 | tf_op jit(solution)/shard_map/ppermute | solution.py:412
  12.4 4.2 %collective-permute-start.2 = (bf16[8,3200]{1,0:T(8,128)(2,1)S(1)}, bf16[8,3200]{1,0:T(8,128)(2,1)S(1)}, u32[]{:S(2)}, u32[]{:S(2)}) collective-permute-start(bf16[8,3200]{1,0:T(8,128)(2,1)S(1)} %join_8.1.refs_0_), channel_id=1, source_target_pairs={{0,16},{4,20},{8,24},{12,28},{16,0},{20,4},{24,8},{28,12},{1,17},{... | collective-permute-start | bytes 153608 | tf_op jit(solution)/shard_map/ppermute | solution.py:412
  26.0 1.6 %collective-permute-start.3 = (f32[3,16,1536]{2,1,0:T(8,128)S(1)}, f32[3,16,1536]{2,1,0:T(8,128)S(1)}, u32[]{:S(2)}, u32[]{:S(2)}) collective-permute-start(f32[3,16,1536]{2,1,0:T(8,128)S(1)} %get-tuple-element.27), channel_id=1, source_target_pairs={{0,1},{1,0},{2,3},{3,2},{4,5},{5,4},{6,7},{7,6},{8,9},{9,8},{10,11... | collective-permute-start | bytes 884744 | tf_op jit(solution)/shard_map/ppermute | solution.py:412
  27.7 6.2 %collective-permute-start.4 = (bf16[3,16,1536]{2,1,0:T(8,128)(2,1)S(1)}, bf16[3,16,1536]{2,1,0:T(8,128)(2,1)S(1)}, u32[]{:S(2)}, u32[]{:S(2)}) collective-permute-start(bf16[3,16,1536]{2,1,0:T(8,128)(2,1)S(1)} %get-tuple-element.30), channel_id=1, source_target_pairs={{0,2},{1,3},{2,0},{3,1},{4,6},{5,7},{6,4},{7,5},{8,10},{9,11},{10,... | collective-permute-start | bytes 442376 | tf_op jit(solution)/shard_map/ppermute | solution.py:412
  34.0 1.4 %collective-permute-start.5 = (bf16[3,16,1536]{2,1,0:T(8,128)(2,1)S(1)}, bf16[3,16,1536]{2,1,0:T(8,128)(2,1)S(1)}, u32[]{:S(2)}, u32[]{:S(2)}) collective-permute-start(bf16[3,16,1536]{2,1,0:T(8,128)(2,1)S(1)} %hidden.1.refs_1_), channel_id=1, source_target_pairs={{0,1},{1,0},{2,3},{3,2},{4,5},{5,4},{6,7},{7,6},{8,9},{9,8},{10,11... | collective-permute-start | bytes 442376 | tf_op jit(solution)/shard_map/ppermute | solution.py:412
  42.4 4.2 %collective-permute-start.6 = (bf16[8,3072]{1,0:T(8,128)(2,1)S(1)}, bf16[8,3072]{1,0:T(8,128)(2,1)S(1)}, u32[]{:S(2)}, u32[]{:S(2)}) collective-permute-start(bf16[8,3072]{1,0:T(8,128)(2,1)S(1)} %get-tuple-element.32), channel_id=1, source_target_pairs={{0,16},{4,20},{8,24},{12,28},{16,0},{20,4},{24,8},{28,12},{1,17},{... | collective-permute-start | bytes 147464 | tf_op jit(solution)/shard_map/ppermute | solution.py:412
  46.6 7.1 %collective-permute-start.7 = (bf16[2,3072]{1,0:T(2,128)(2,1)S(1)}, bf16[2,3072]{1,0:T(2,128)(2,1)S(1)}, u32[]{:S(2)}, u32[]{:S(2)}) collective-permute-start(bf16[2,3072]{1,0:T(2,128)(2,1)S(1)} %get-tuple-element.38), channel_id=1, source_target_pairs={{0,12},{4,8},{8,4},{12,0},{16,28},{20,24},{24,20},{28,16},{1,13},{... | collective-permute-start | bytes 36872 | tf_op jit(solution)/shard_map/ppermute | solution.py:412
  49.4 4.6 %collective-permute-start.8 = (bf16[2,3072]{1,0:T(2,128)(2,1)S(1)}, bf16[2,3072]{1,0:T(2,128)(2,1)S(1)}, u32[]{:S(2)}, u32[]{:S(2)}) collective-permute-start(bf16[2,3072]{1,0:T(2,128)(2,1)S(1)} %get-tuple-element.39), channel_id=1, source_target_pairs={{0,8},{4,12},{8,0},{12,4},{16,24},{20,28},{24,16},{28,20},{1,9},{5... | collective-permute-start | bytes 36872 | tf_op jit(solution)/shard_map/ppermute | solution.py:412
  49.7 4.3 %collective-permute-start.9 = (bf16[2,3072]{1,0:T(2,128)(2,1)S(1)}, bf16[2,3072]{1,0:T(2,128)(2,1)S(1)}, u32[]{:S(2)}, u32[]{:S(2)}) collective-permute-start(bf16[2,3072]{1,0:T(2,128)(2,1)S(1)} %get-tuple-element.40), channel_id=1, source_target_pairs={{0,4},{4,0},{8,12},{12,8},{16,20},{20,16},{24,28},{28,24},{1,5},{5... | collective-permute-start | bytes 36872 | tf_op jit(solution)/shard_map/ppermute | solution.py:412

commit v12 on v11

--- a/solution.py
+++ b/solution.py
@@ -18,6 +18,7 @@
 ROWS = 256
 TILE = 128
 TURN_FIRST = 5
+EARLY_BLOCKS = 1
 EARLY_ROWS = 2048
 TEXT_FIRST = 2
 PLACES = {"h": pl.ANY, "v": pltpu.VMEM, "s": pltpu.SMEM}
@@ -101,13 +102,15 @@
     out_ref[:, width : 2 * width] = cot_ref[...]
 
 
-def join_body(a_ref, b_ref, out_ref):
-    both = jnp.concatenate([a_ref[...].astype(F32), b_ref[...].astype(F32)], axis=0)
-    out_ref[...] = both.astype(BF16)
-
-
-def join(a, b, name, also):
-    return call(join_body, name, [((2 * a.shape[0], a.shape[1]), BF16)], (a, b), "vv", also=also)[0]
+def join_body(*refs):
+    *parts, out_ref = refs
+    out_ref[...] = jnp.concatenate([part[...].astype(F32) for part in parts], axis=0).astype(BF16)
+
+
+def join(parts, name, also):
+    rows, width = parts[0].shape
+    outs = [((len(parts) * rows, width), BF16)]
+    return call(join_body, name, outs, parts, "v" * len(parts), also=also)[0]
 
 
 def column_blocks(src, wide, first, cuts):
@@ -140,14 +143,14 @@
         copy.wait()
 
 
-def load_body(first, after_ref, src_hbm, old_ref, place_ref, sems):
-    for group in started(column_blocks(src_hbm, place_ref, first, 4), sems):
+def load_body(first, count, after_ref, src_hbm, old_ref, place_ref, sems):
+    for group in started(column_blocks(src_hbm, place_ref, first, 4)[:count], sems):
         wait(group)
 
 
-def load(after, src, place, also, first, name):
+def load(after, src, place, also, first, count, name):
     return call(
-        functools.partial(load_body, first),
+        functools.partial(load_body, first, count),
         name,
         [like(place)],
         (after, src, place),
@@ -165,12 +168,13 @@
 
 
 def partials_body(
-    arr_ref, dt_ref, ds_ref, ut_hbm, gs_hbm, us_hbm, old_wide, mine_ref, theirs_ref, wide_ref, part, sems
+    arr_ref, dt_ref, ds_ref, gt_hbm, ut_hbm, gs_hbm, us_hbm, old_wide, mine_ref, theirs_ref, wide_ref, part, sems
 ):
     fs, width = ds_ref.shape
     ft = dt_ref.shape[0]
     ns, nt = fs // WIDE, ft // WIDE
-    groups = column_blocks(ut_hbm, wide_ref, nt, 2) + column_blocks(gs_hbm, wide_ref, 2 * nt, 2)
+    groups = column_blocks(gt_hbm, wide_ref, 0, 2)[EARLY_BLOCKS:] + column_blocks(ut_hbm, wide_ref, nt, 2)
+    groups += column_blocks(gs_hbm, wide_ref, 2 * nt, 2)
     groups += column_blocks(us_hbm, wide_ref, 2 * nt + ns, 2)
     copies = started(groups, sems)
     x = arr_ref[:, :width]
@@ -194,12 +198,12 @@
             put(2, place, contract_last(c, ref[i : i + BLOCK, :]), k == 1)
     for k in range(2):
         for i in range(nt):
-            if k == 1:
-                wait(copies[i])
+            if k * nt + i >= EARLY_BLOCKS:
+                wait(copies[k * nt + i - EARLY_BLOCKS])
             put_wide(k, i * WIDE, times(x, wide_ref[k * nt + i]), False)
     for k in range(2):
         for i in range(ns):
-            wait(copies[nt + k * ns + i])
+            wait(copies[2 * nt - EARLY_BLOCKS + k * ns + i])
             put_wide(k, i * WIDE, times(x, wide_ref[2 * nt + k * ns + i]), True)
     half = fs // 2
     odd = parity()
@@ -208,19 +212,19 @@
         theirs_ref[k] = part[k, :, pl.ds(pl.multiple_of((1 - odd) * half, half), half)]
 
 
-def partials(arr, up_t, gate_s, up_s, down_t, down_s, wide):
+def partials(arr, gate_t, up_t, gate_s, up_s, down_t, down_s, wide):
     rows, fs = arr.shape[0], gate_s.shape[1]
     half = ((3, rows, fs // 2), F32)
     return call(
         partials_body,
         "hidden_partials",
         [half, half, like(wide)],
-        (arr, down_t, down_s, up_t, gate_s, up_s, wide),
-        "vvvhhhv",
-        [pltpu.VMEM((3, rows, fs), F32), pltpu.SemaphoreType.DMA(((4 * fs + 2 * up_t.shape[1]) // WIDE,))],
+        (arr, down_t, down_s, gate_t, up_t, gate_s, up_s, wide),
+        "vvvhhhhv",
+        [pltpu.VMEM((3, rows, fs), F32), pltpu.SemaphoreType.DMA((4 * (fs + up_t.shape[1]) // WIDE,))],
         2 * rows * (wide.size + down_s.size + down_t.size),
         size_of(up_t, gate_s, up_s),
-        aliases={6: 2},
+        aliases={7: 2},
     )
 
 
@@ -421,14 +425,13 @@
     packed = ((rows, 2 * width + 128), BF16)
     scratch = pair + [pltpu.SMEM((rows,), jnp.int32), pltpu.SemaphoreType.DMA((3,))]
     wide, arr = call(pack_body, "pack", [wide, packed], (modality, tokens, cotangent), "hhh", scratch)
-    got = flip(arr, TOK, HOPS[0], n_tok)
-    wide = load(arr, gate_t, wide, (), 0, "load_gate_text")
-    arr = join(arr, got, "join_4", (wide,))
-    got = flip(arr, TOK, HOPS[1], n_tok)
-    arr = join(arr, got, "join_8", (wide,))
-    arr = join(arr, flip(arr, TOK, HOPS[2], n_tok), "join_16", (wide, down_t, down_s))
-
-    mine, theirs, wide = partials(arr, up_t, gate_s, up_s, down_t, down_s, wide)
+    bits = (HOPS[0], HOPS[1], HOPS[0] ^ HOPS[1])
+    far, *near = [flip(arr, TOK, bits[i], n_tok) for i in (2, 0, 1)]
+    wide = load(arr, gate_t, wide, (), 0, EARLY_BLOCKS, "load_gate_text")
+    arr = join((arr, *near, far), "join_8", (wide,))
+    arr = join((arr, flip(arr, TOK, HOPS[2], n_tok)), "join_16", (wide, down_t, down_s))
+
+    mine, theirs, wide = partials(arr, gate_t, up_t, gate_s, up_s, down_t, down_s, wide)
     blocks = 2 * (fs + ft) // BLOCK
     got = flip(theirs, "seq", 1, n_seq)
     wide = turn(wide, (down_t, down_s), 0, TURN_FIRST, "turn_1")
@@ -460,7 +463,6 @@
     got = flip(send, TOK, HOPS[2], n_tok)
     down_s_grad, down_t_grad = outer(keep, range(early // ROWS, ns), range(TEXT_FIRST), (down_s_grad,), "down_grad_1")
     keep, *sends = token_sum(keep, got, down_t_grad, rows, "token_sum_4")
-    bits = (HOPS[0], HOPS[1], HOPS[0] ^ HOPS[1])
     gots = [flip(sends[i], TOK, bits[i], n_tok) for i in (2, 0, 1)]
     down_t_grad = outer(keep, (), range(TEXT_FIRST, nt), (down_t_grad,), "down_grad_2")[0]
     outs = [((rows, width), BF16)] * 2

time: 55 us -> 55.7 us (1.013)
  Pallas kernels: 32.6 us -> 33.9 us
    pallas_call x16 -> x15, Pallas kernels: 32.6 us -> 33.9 us  [call(): pl.pallas_call(seen, out_shape=shapes, in_specs=[pl.BlockSpec(memory_spac...]
    ppermute x10 -> x11, waiting for transfers between devices: 6.03 us -> 5.48 us  [flip(): return lax.ppermute(value, axes, [(i, i ^ bit) for i in range(n)])]
    ppermute x10 -> x11, starting transfers between devices: 15.1 us -> 15.1 us  [flip(): return lax.ppermute(value, axes, [(i, i ^ bit) for i in range(n)])]
  transfers between devices with their start and end apart: 10 -> 11, of which waited for: 5 -> 6; matrix products, arithmetic and copies ran while one was open for 0% -> 0% of each run, Pallas kernels for 27% -> 25%
where the time goes in v12:
time: 55.7 us; the launch traced here: 55.5 us
  Pallas kernels  33.9 us (61%)
  starting transfers between devices  15.1 us (27%)
  waiting for transfers between devices  5.48 us (10%)
  between operations  0.98 us (2%)
    pallas_call x15, Pallas kernels, call(): pl.pallas_call(seen, out_shape=shapes, in_specs=[pl.BlockSpec(memory_spac...  33.9 us
    ppermute x11, starting transfers between devices, flip(): return lax.ppermute(value, axes, [(i, i ^ bit) for i in range(n)])  15.1 us
    ppermute x11, waiting for transfers between devices, flip(): return lax.ppermute(value, axes, [(i, i ^ bit) for i in range(n)])  5.48 us
  transfers between devices with their start and end apart: 11, of which 6 were waited for; matrix products, arithmetic and copies ran while one was open for 0% of the time, Pallas kernels for 25%

profile of v12, /device:TPU:0, one launch (start us, length us, event | category | flops | bytes accessed | tf_op | source)
XLA Modules:
  0.0 55.5 jit_solution(10975843981189162805)
XLA Ops:
  0.6 0.7 %pack.1 = (bf16[10,1536,1024]{2,1,0:T(8,128)(2,1)S(1)}, bf16[2,3200]{1,0:T(2,128)(2,1)S(1)}) custom-call(s32[2]{0:T(128)} %refs_0_.1, bf16[2,1536]{1,0:T(2,128)(2,1)} %refs_1_.5, bf16[2,1536]{1,0:T(2,128)(2,1)} %refs_2_.5), custom_call_target="tpu_custom_call" | custom-call | tf_op jit(solution)/shard_map/pack/pallas_call | solution.py:60
  1.4 5.1 %collective-permute-start.2 = (bf16[2,3200]{1,0:T(2,128)(2,1)S(1)}, bf16[2,3200]{1,0:T(2,128)(2,1)S(1)}, u32[]{:S(2)}, u32[]{:S(2)}) collective-permute-start(bf16[2,3200]{1,0:T(2,128)(2,1)S(1)} %get-tuple-element.24.refs_0_), channel_id=1, source_target_pairs={{0,12},{4,8},{8,4},{12,0},{16,28},{20,24},{24,20},{28,16},{1,13},{... | collective-permute-start | bytes 38408 | tf_op jit(solution)/shard_map/ppermute | solution.py:416
  6.5 0.6 %collective-permute-start = (bf16[2,3200]{1,0:T(2,128)(2,1)S(1)}, bf16[2,3200]{1,0:T(2,128)(2,1)S(1)}, u32[]{:S(2)}, u32[]{:S(2)}) collective-permute-start(bf16[2,3200]{1,0:T(2,128)(2,1)S(1)} %get-tuple-element.24.refs_0_), channel_id=1, source_target_pairs={{0,8},{4,12},{8,0},{12,4},{16,24},{20,28},{24,16},{28,20},{1,9},{5... | collective-permute-start | bytes 38408 | tf_op jit(solution)/shard_map/ppermute | solution.py:416
  7.2 2.1 %load_gate_text.1.refs_4_.refs_2_.refs_7_ = bf16[10,1536,1024]{2,1,0:T(8,128)(2,1)S(1)} custom-call(bf16[2,3200]{1,0:T(2,128)(2,1)S(1)} %get-tuple-element.24.refs_0_, bf16[1536,2048]{1,0:T(8,128)(2,1)} %refs_3_.6, bf16[10,1536,1024]{2,1,0:T(8,128)(2,1)S(1)} %get-tuple-element.25.refs_2_), custom_call_target="tpu_custom_call", output_to_operand_aliasing={{}: (2, {})} | custom-call | bytes 6291456 | tf_op jit(solution)/shard_map/load_gate_text/pallas_call | solution.py:60
  9.2 1.0 %collective-permute-done.1.refs_2_ = bf16[2,3200]{1,0:T(2,128)(2,1)S(1)} collective-permute-done((bf16[2,3200]{1,0:T(2,128)(2,1)S(1)}, bf16[2,3200]{1,0:T(2,128)(2,1)S(1)}, u32[]{:S(2)}, u32[]{:S(2)}) %collective-permute-start.1) | collective-permute-done | bytes 12832 | tf_op jit(solution)/shard_map/ppermute | solution.py:416
  10.2 0.9 %collective-permute-done.refs_1_ = bf16[2,3200]{1,0:T(2,128)(2,1)S(1)} collective-permute-done((bf16[2,3200]{1,0:T(2,128)(2,1)S(1)}, bf16[2,3200]{1,0:T(2,128)(2,1)S(1)}, u32[]{:S(2)}, u32[]{:S(2)}) %collective-permute-start) | collective-permute-done | bytes 12832 | tf_op jit(solution)/shard_map/ppermute | solution.py:416
  11.1 1.6 %collective-permute-start.3 = (bf16[8,3200]{1,0:T(8,128)(2,1)S(1)}, bf16[8,3200]{1,0:T(8,128)(2,1)S(1)}, u32[]{:S(2)}, u32[]{:S(2)}) collective-permute-start(bf16[8,3200]{1,0:T(8,128)(2,1)S(1)} %join_8.1.refs_0_), channel_id=1, source_target_pairs={{0,16},{4,20},{8,24},{12,28},{16,0},{20,4},{24,8},{28,12},{1,17},{... | collective-permute-start | bytes 153608 | tf_op jit(solution)/shard_map/ppermute | solution.py:416
  12.7 2.6 %collective-permute-done.3.refs_1_ = bf16[8,3200]{1,0:T(8,128)(2,1)S(1)} collective-permute-done((bf16[8,3200]{1,0:T(8,128)(2,1)S(1)}, bf16[8,3200]{1,0:T(8,128)(2,1)S(1)}, u32[]{:S(2)}, u32[]{:S(2)}) %collective-permute-start.3) | collective-permute-done | bytes 51232 | tf_op jit(solution)/shard_map/ppermute | solution.py:416
  15.4 11.4 %hidden_partials.1 = (f32[3,16,1536]{2,1,0:T(8,128)S(1)}, f32[3,16,1536]{2,1,0:T(8,128)S(1)}, bf16[10,1536,1024]{2,1,0:T(8,128)(2,1)S(1)}) custom-call(bf16[16,3200]{1,0:T(8,128)(2,1)S(1)} %join_16.1.refs_0_.refs_1_, bf16[2048,1536]{1,0:T(8,128)(2,1)S(1)} %bitcast.3, bf16[3072,1536]{1,0:T(8,128)(2,1)S(1)} %bitcast.1, ...), custom_call_target="tpu_custom_call", output_to_operand_aliasing={{2}: (7, {})} | custom-call | flops 754974720 | bytes 25165824 | tf_op jit(solution)/shard_map/hidden_partials/pallas_call | solution.py:60
  26.9 1.4 %turn_1.1.refs_2_.refs_0_ = bf16[10,1536,1024]{2,1,0:T(8,128)(2,1)S(1)} custom-call(bf16[10,1536,1024]{2,1,0:T(8,128)(2,1)S(1)} %get-tuple-element.28.refs_0_, bf16[2048,1536]{1,0:T(8,128)(2,1)S(1)} %bitcast.3, bf16[3072,1536]{1,0:T(8,128)(2,1)S(1)} %bitcast.1), custom_call_target="tpu_custom_call", output_to_operand_aliasing={{}: (0, {})} | custom-call | bytes 15728640 | tf_op jit(solution)/shard_map/turn_1/pallas_call | solution.py:60
  28.4 0.1 collective-permute-done.4.refs_1_
  28.5 1.6 %collective-permute-start.5 = (bf16[3,16,1536]{2,1,0:T(8,128)(2,1)S(1)}, bf16[3,16,1536]{2,1,0:T(8,128)(2,1)S(1)}, u32[]{:S(2)}, u32[]{:S(2)}) collective-permute-start(bf16[3,16,1536]{2,1,0:T(8,128)(2,1)S(1)} %get-tuple-element.30), channel_id=1, source_target_pairs={{0,2},{1,3},{2,0},{3,1},{4,6},{5,7},{6,4},{7,5},{8,10},{9,11},{10,... | collective-permute-start | bytes 442376 | tf_op jit(solution)/shard_map/ppermute | solution.py:416
  30.1 3.9 %turn_2.1.refs_2_.refs_4_ = bf16[10,1536,1024]{2,1,0:T(8,128)(2,1)S(1)} custom-call(bf16[10,1536,1024]{2,1,0:T(8,128)(2,1)S(1)} %turn_1.1.refs_2_.refs_0_, bf16[2048,1536]{1,0:T(8,128)(2,1)S(1)} %bitcast.3, bf16[3072,1536]{1,0:T(8,128)(2,1)S(1)} %bitcast.1), custom_call_target="tpu_custom_call", output_to_operand_aliasing={{}: (0, {})} | custom-call | bytes 47185920 | tf_op jit(solution)/shard_map/turn_2/pallas_call | solution.py:60
  34.0 0.7 %collective-permute-done.5.refs_1_ = bf16[3,16,1536]{2,1,0:T(8,128)(2,1)S(1)} collective-permute-done((bf16[3,16,1536]{2,1,0:T(8,128)(2,1)S(1)}, bf16[3,16,1536]{2,1,0:T(8,128)(2,1)S(1)}, u32[]{:S(2)}, u32[]{:S(2)}) %collective-permute-start.5) | collective-permute-done | bytes 147488 | tf_op jit(solution)/shard_map/ppermute | solution.py:416
  34.9 1.3 %mixed_own.1.refs_3_ = f32[16,1536]{1,0:T(8,128)S(1)} custom-call(bf16[16,3200]{1,0:T(8,128)(2,1)S(1)} %join_16.1.refs_0_.refs_1_, bf16[3,16,1536]{2,1,0:T(8,128)(2,1)S(1)} %hidden.1.refs_1_, bf16[2048,1536]{1,0:T(8,128)(2,1)S(1)} %bitcast.3, bf16[3072,1536]{1,0:T(8,128)(2,1)S(1)} %bitcast.1, bf16[10,1536,1024]{2,1,0:T(8,128)(2,1)S(1)} %turn_2.1.refs_2_.refs_4_), custom_call_target="tpu_custom_call" | custom-call | flops 125829120 | tf_op jit(solution)/shard_map/mixed_own/pallas_call | solution.py:60
  36.2 7.0 %token_partials.1 = (f32[8,3072]{1,0:T(8,128)S(1)}, bf16[8,3072]{1,0:T(8,128)(2,1)S(1)}, bf16[16,3072]{1,0:T(8,128)(2,1)S(1)}, bf16[16,2048]{1,0:T(8,128)(2,1)S(1)}, bf16[3072,1536]{1,0:T(8,128)(2,1)}) custom-call(bf16[16,3200]{1,0:T(8,128)(2,1)S(1)} %join_16.1.refs_0_.refs_1_, bf16[3,16,1536]{2,1,0:T(8,128)(2,1)S(1)} %hidden.1.refs_1_, ...), custom_call_target="tpu_custom_call" | custom-call | flops 754974720 | tf_op jit(solution)/shard_map/token_partials/pallas_call | solution.py:60
  43.2 1.6 %collective-permute-start.7 = (bf16[8,3072]{1,0:T(8,128)(2,1)S(1)}, bf16[8,3072]{1,0:T(8,128)(2,1)S(1)}, u32[]{:S(2)}, u32[]{:S(2)}) collective-permute-start(bf16[8,3072]{1,0:T(8,128)(2,1)S(1)} %get-tuple-element.32), channel_id=1, source_target_pairs={{0,16},{4,20},{8,24},{12,28},{16,0},{20,4},{24,8},{28,12},{1,17},{... | collective-permute-start | bytes 147464 | tf_op jit(solution)/shard_map/ppermute | solution.py:416
  44.8 2.6 %down_grad_1.1 = (bf16[3072,1536]{1,0:T(8,128)(2,1)}, bf16[2048,1536]{1,0:T(8,128)(2,1)}) custom-call(f32[8,3072]{1,0:T(8,128)S(1)} %get-tuple-element.31.refs_0_, bf16[16,3200]{1,0:T(8,128)(2,1)S(1)} %join_16.1.refs_0_.refs_1_, bf16[16,3072]{1,0:T(8,128)(2,1)S(1)} %get-tuple-element.33.refs_2_, ...), custom_call_target="tpu_custom_call", output_to_operand_aliasing={{0}: (4, {})} | custom-call | flops 75497472 | bytes 4718592 | tf_op jit(solution)/shard_map/down_grad_1/pallas_call | solution.py:60
  47.4 2.1 %collective-permute-start.8 = (bf16[2,3072]{1,0:T(2,128)(2,1)S(1)}, bf16[2,3072]{1,0:T(2,128)(2,1)S(1)}, u32[]{:S(2)}, u32[]{:S(2)}) collective-permute-start(bf16[2,3072]{1,0:T(2,128)(2,1)S(1)} %get-tuple-element.38), channel_id=1, source_target_pairs={{0,12},{4,8},{8,4},{12,0},{16,28},{20,24},{24,20},{28,16},{1,13},{... | collective-permute-start | bytes 36872 | tf_op jit(solution)/shard_map/ppermute | solution.py:416
  49.5 1.5 %collective-permute-start.9 = (bf16[2,3072]{1,0:T(2,128)(2,1)S(1)}, bf16[2,3072]{1,0:T(2,128)(2,1)S(1)}, u32[]{:S(2)}, u32[]{:S(2)}) collective-permute-start(bf16[2,3072]{1,0:T(2,128)(2,1)S(1)} %get-tuple-element.39), channel_id=1, source_target_pairs={{0,8},{4,12},{8,0},{12,4},{16,24},{20,28},{24,16},{28,20},{1,9},{5... | collective-permute-start | bytes 36872 | tf_op jit(solution)/shard_map/ppermute | solution.py:416
  51.0 0.9 %collective-permute-start.10 = (bf16[2,3072]{1,0:T(2,128)(2,1)S(1)}, bf16[2,3072]{1,0:T(2,128)(2,1)S(1)}, u32[]{:S(2)}, u32[]{:S(2)}) collective-permute-start(bf16[2,3072]{1,0:T(2,128)(2,1)S(1)} %get-tuple-element.40), channel_id=1, source_target_pairs={{0,4},{4,0},{8,12},{12,8},{16,20},{20,16},{24,28},{28,24},{1,5},{5... | collective-permute-start | bytes 36872 | tf_op jit(solution)/shard_map/ppermute | solution.py:416
  51.9 2.6 %down_grad_2.1 = bf16[2048,1536]{1,0:T(8,128)(2,1)} custom-call(f32[2,3072]{1,0:T(2,128)S(1)} %get-tuple-element.37.refs_0_, bf16[16,3200]{1,0:T(8,128)(2,1)S(1)} %join_16.1.refs_0_.refs_1_, bf16[16,3072]{1,0:T(8,128)(2,1)S(1)} %get-tuple-element.33.refs_2_, bf16[16,2048]{1,0:T(8,128)(2,1)S(1)} %get-tuple-element.34.refs_3_, ...), custom_call_target="tpu_custom_call", output_to_operand_aliasing={{}: (4, {})} | custom-call | flops 75497472 | bytes 4718592 | tf_op jit(solution)/shard_map/down_grad_2/pallas_call | solution.py:60
  54.5 0.2 collective-permute-done.10.refs_3_
  54.7 0.6 %token_sum_1.1 = (bf16[2,1536]{1,0:T(2,128)(2,1)}, bf16[2,1536]{1,0:T(2,128)(2,1)}) custom-call(f32[2,3072]{1,0:T(2,128)S(1)} %get-tuple-element.37.refs_0_, bf16[2,3072]{1,0:T(2,128)(2,1)S(1)} %collective-permute-done.8.refs_1_, bf16[2,3072]{1,0:T(2,128)(2,1)S(1)} %collective-permute-done.9.refs_2_, bf16[2,3072]{1,0:T(2,128)(2,1)S(1)} %collective-permute-done.10.refs_3_), custom_call_target="tpu_custom_call" | custom-call | tf_op jit(solution)/shard_map/token_sum_1/pallas_call | solution.py:60
  (25 shorter events, 0.4 us)
Async XLA Ops:
  1.4 7.9 %collective-permute-start.2 = (bf16[2,3200]{1,0:T(2,128)(2,1)S(1)}, bf16[2,3200]{1,0:T(2,128)(2,1)S(1)}, u32[]{:S(2)}, u32[]{:S(2)}) collective-permute-start(bf16[2,3200]{1,0:T(2,128)(2,1)S(1)} %get-tuple-element.24.refs_0_), channel_id=1, source_target_pairs={{0,12},{4,8},{8,4},{12,0},{16,28},{20,24},{24,20},{28,16},{1,13},{... | collective-permute-start | bytes 38408 | tf_op jit(solution)/shard_map/ppermute | solution.py:416
  6.5 3.7 %collective-permute-start.1 = (bf16[2,3200]{1,0:T(2,128)(2,1)S(1)}, bf16[2,3200]{1,0:T(2,128)(2,1)S(1)}, u32[]{:S(2)}, u32[]{:S(2)}) collective-permute-start(bf16[2,3200]{1,0:T(2,128)(2,1)S(1)} %get-tuple-element.24.refs_0_), channel_id=1, source_target_pairs={{0,4},{4,0},{8,12},{12,8},{16,20},{20,16},{24,28},{28,24},{1,5},{5... | collective-permute-start | bytes 38408 | tf_op jit(solution)/shard_map/ppermute | solution.py:416
  6.5 4.6 %collective-permute-start = (bf16[2,3200]{1,0:T(2,128)(2,1)S(1)}, bf16[2,3200]{1,0:T(2,128)(2,1)S(1)}, u32[]{:S(2)}, u32[]{:S(2)}) collective-permute-start(bf16[2,3200]{1,0:T(2,128)(2,1)S(1)} %get-tuple-element.24.refs_0_), channel_id=1, source_target_pairs={{0,8},{4,12},{8,0},{12,4},{16,24},{20,28},{24,16},{28,20},{1,9},{5... | collective-permute-start | bytes 38408 | tf_op jit(solution)/shard_map/ppermute | solution.py:416
  7.1 8.2 %slice-start = ((s8[9437184]{0:T(1024)(128)(4,1)}), s8[4194304]{0:T(1024)(128)(4,1)S(1)}, s32[]{:S(2)}) async-start(s8[9437184]{0:T(1024)(128)(4,1)} %bitcast), calls=%async_computation | async-start | bytes 8388608
  7.1 8.2 %slice-start.3 = ((s8[6291456]{0:T(1024)(128)(4,1)}), s8[4194304]{0:T(1024)(128)(4,1)S(1)}, s32[]{:S(2)}) async-start(s8[6291456]{0:T(1024)(128)(4,1)} %bitcast.2), calls=%async_computation.3 | async-start | bytes 8388608
  7.1 8.2 %slice-start.1 = ((s8[9437184]{0:T(1024)(128)(4,1)}), s8[4194304]{0:T(1024)(128)(4,1)S(1)}, s32[]{:S(2)}) async-start(s8[9437184]{0:T(1024)(128)(4,1)} %bitcast), calls=%async_computation.1 | async-start | bytes 8388608
  7.1 8.2 %slice-start.2 = ((s8[9437184]{0:T(1024)(128)(4,1)}), s8[1048576]{0:T(1024)(128)(4,1)S(1)}, s32[]{:S(2)}) async-start(s8[9437184]{0:T(1024)(128)(4,1)} %bitcast), calls=%async_computation.2 | async-start | bytes 2097152
  7.1 8.2 %slice-start.4 = ((s8[6291456]{0:T(1024)(128)(4,1)}), s8[2097152]{0:T(1024)(128)(4,1)S(1)}, s32[]{:S(2)}) async-start(s8[6291456]{0:T(1024)(128)(4,1)} %bitcast.2), calls=%async_computation.4 | async-start | bytes 4194304
  11.1 4.2 %collective-permute-start.3 = (bf16[8,3200]{1,0:T(8,128)(2,1)S(1)}, bf16[8,3200]{1,0:T(8,128)(2,1)S(1)}, u32[]{:S(2)}, u32[]{:S(2)}) collective-permute-start(bf16[8,3200]{1,0:T(8,128)(2,1)S(1)} %join_8.1.refs_0_), channel_id=1, source_target_pairs={{0,16},{4,20},{8,24},{12,28},{16,0},{20,4},{24,8},{28,12},{1,17},{... | collective-permute-start | bytes 153608 | tf_op jit(solution)/shard_map/ppermute | solution.py:416
  26.8 1.6 %collective-permute-start.4 = (f32[3,16,1536]{2,1,0:T(8,128)S(1)}, f32[3,16,1536]{2,1,0:T(8,128)S(1)}, u32[]{:S(2)}, u32[]{:S(2)}) collective-permute-start(f32[3,16,1536]{2,1,0:T(8,128)S(1)} %get-tuple-element.27), channel_id=1, source_target_pairs={{0,1},{1,0},{2,3},{3,2},{4,5},{5,4},{6,7},{7,6},{8,9},{9,8},{10,11... | collective-permute-start | bytes 884744 | tf_op jit(solution)/shard_map/ppermute | solution.py:416
  28.5 6.2 %collective-permute-start.5 = (bf16[3,16,1536]{2,1,0:T(8,128)(2,1)S(1)}, bf16[3,16,1536]{2,1,0:T(8,128)(2,1)S(1)}, u32[]{:S(2)}, u32[]{:S(2)}) collective-permute-start(bf16[3,16,1536]{2,1,0:T(8,128)(2,1)S(1)} %get-tuple-element.30), channel_id=1, source_target_pairs={{0,2},{1,3},{2,0},{3,1},{4,6},{5,7},{6,4},{7,5},{8,10},{9,11},{10,... | collective-permute-start | bytes 442376 | tf_op jit(solution)/shard_map/ppermute | solution.py:416
  34.8 1.4 %collective-permute-start.6 = (bf16[3,16,1536]{2,1,0:T(8,128)(2,1)S(1)}, bf16[3,16,1536]{2,1,0:T(8,128)(2,1)S(1)}, u32[]{:S(2)}, u32[]{:S(2)}) collective-permute-start(bf16[3,16,1536]{2,1,0:T(8,128)(2,1)S(1)} %hidden.1.refs_1_), channel_id=1, source_target_pairs={{0,1},{1,0},{2,3},{3,2},{4,5},{5,4},{6,7},{7,6},{8,9},{9,8},{10,11... | collective-permute-start | bytes 442376 | tf_op jit(solution)/shard_map/ppermute | solution.py:416
  43.2 4.2 %collective-permute-start.7 = (bf16[8,3072]{1,0:T(8,128)(2,1)S(1)}, bf16[8,3072]{1,0:T(8,128)(2,1)S(1)}, u32[]{:S(2)}, u32[]{:S(2)}) collective-permute-start(bf16[8,3072]{1,0:T(8,128)(2,1)S(1)} %get-tuple-element.32), channel_id=1, source_target_pairs={{0,16},{4,20},{8,24},{12,28},{16,0},{20,4},{24,8},{28,12},{1,17},{... | collective-permute-start | bytes 147464 | tf_op jit(solution)/shard_map/ppermute | solution.py:416
  47.4 7.1 %collective-permute-start.8 = (bf16[2,3072]{1,0:T(2,128)(2,1)S(1)}, bf16[2,3072]{1,0:T(2,128)(2,1)S(1)}, u32[]{:S(2)}, u32[]{:S(2)}) collective-permute-start(bf16[2,3072]{1,0:T(2,128)(2,1)S(1)} %get-tuple-element.38), channel_id=1, source_target_pairs={{0,12},{4,8},{8,4},{12,0},{16,28},{20,24},{24,20},{28,16},{1,13},{... | collective-permute-start | bytes 36872 | tf_op jit(solution)/shard_map/ppermute | solution.py:416
  49.5 5.0 %collective-permute-start.9 = (bf16[2,3072]{1,0:T(2,128)(2,1)S(1)}, bf16[2,3072]{1,0:T(2,128)(2,1)S(1)}, u32[]{:S(2)}, u32[]{:S(2)}) collective-permute-start(bf16[2,3072]{1,0:T(2,128)(2,1)S(1)} %get-tuple-element.39), channel_id=1, source_target_pairs={{0,8},{4,12},{8,0},{12,4},{16,24},{20,28},{24,16},{28,20},{1,9},{5... | collective-permute-start | bytes 36872 | tf_op jit(solution)/shard_map/ppermute | solution.py:416
  51.0 3.7 %collective-permute-start.10 = (bf16[2,3072]{1,0:T(2,128)(2,1)S(1)}, bf16[2,3072]{1,0:T(2,128)(2,1)S(1)}, u32[]{:S(2)}, u32[]{:S(2)}) collective-permute-start(bf16[2,3072]{1,0:T(2,128)(2,1)S(1)} %get-tuple-element.40), channel_id=1, source_target_pairs={{0,4},{4,0},{8,12},{12,8},{16,20},{20,16},{24,28},{28,24},{1,5},{5... | collective-permute-start | bytes 36872 | tf_op jit(solution)/shard_map/ppermute | solution.py:416

commit v13 on v11

--- a/solution.py
+++ b/solution.py
@@ -101,13 +101,15 @@
     out_ref[:, width : 2 * width] = cot_ref[...]
 
 
-def join_body(a_ref, b_ref, out_ref):
-    both = jnp.concatenate([a_ref[...].astype(F32), b_ref[...].astype(F32)], axis=0)
-    out_ref[...] = both.astype(BF16)
-
-
-def join(a, b, name, also):
-    return call(join_body, name, [((2 * a.shape[0], a.shape[1]), BF16)], (a, b), "vv", also=also)[0]
+def join_body(*refs):
+    *parts, out_ref = refs
+    out_ref[...] = jnp.concatenate([part[...].astype(F32) for part in parts], axis=0).astype(BF16)
+
+
+def join(parts, name, also):
+    rows, width = parts[0].shape
+    outs = [((len(parts) * rows, width), BF16)]
+    return call(join_body, name, outs, parts, "v" * len(parts), also=also)[0]
 
 
 def column_blocks(src, wide, first, cuts):
@@ -421,12 +423,11 @@
     packed = ((rows, 2 * width + 128), BF16)
     scratch = pair + [pltpu.SMEM((rows,), jnp.int32), pltpu.SemaphoreType.DMA((3,))]
     wide, arr = call(pack_body, "pack", [wide, packed], (modality, tokens, cotangent), "hhh", scratch)
-    got = flip(arr, TOK, HOPS[0], n_tok)
+    bits = (HOPS[0], HOPS[1], HOPS[0] ^ HOPS[1])
+    far, *near = [flip(arr, TOK, bits[i], n_tok) for i in (2, 0, 1)]
     wide = load(arr, gate_t, wide, (), 0, "load_gate_text")
-    arr = join(arr, got, "join_4", (wide,))
-    got = flip(arr, TOK, HOPS[1], n_tok)
-    arr = join(arr, got, "join_8", (wide,))
-    arr = join(arr, flip(arr, TOK, HOPS[2], n_tok), "join_16", (wide, down_t, down_s))
+    arr = join((arr, *near, far), "join_8", (wide,))
+    arr = join((arr, flip(arr, TOK, HOPS[2], n_tok)), "join_16", (wide, down_t, down_s))
 
     mine, theirs, wide = partials(arr, up_t, gate_s, up_s, down_t, down_s, wide)
     blocks = 2 * (fs + ft) // BLOCK
@@ -460,7 +461,6 @@
     got = flip(send, TOK, HOPS[2], n_tok)
     down_s_grad, down_t_grad = outer(keep, range(early // ROWS, ns), range(TEXT_FIRST), (down_s_grad,), "down_grad_1")
     keep, *sends = token_sum(keep, got, down_t_grad, rows, "token_sum_4")
-    bits = (HOPS[0], HOPS[1], HOPS[0] ^ HOPS[1])
     gots = [flip(sends[i], TOK, bits[i], n_tok) for i in (2, 0, 1)]
     down_t_grad = outer(keep, (), range(TEXT_FIRST, nt), (down_t_grad,), "down_grad_2")[0]
     outs = [((rows, width), BF16)] * 2

time: 55 us -> 54 us (0.982)
  waiting for transfers between devices: 6.03 us -> 4.9 us
    ppermute x10 -> x11, waiting for transfers between devices: 6.03 us -> 4.9 us  [flip(): return lax.ppermute(value, axes, [(i, i ^ bit) for i in range(n)])]
    pallas_call x16 -> x15, Pallas kernels: 32.6 us -> 32.8 us  [call(): pl.pallas_call(seen, out_shape=shapes, in_specs=[pl.BlockSpec(memory_spac...]
    ppermute x10 -> x11, starting transfers between devices: 15.1 us -> 15.1 us  [flip(): return lax.ppermute(value, axes, [(i, i ^ bit) for i in range(n)])]
  transfers between devices with their start and end apart: 10 -> 11, of which waited for: 5 -> 5; matrix products, arithmetic and copies ran while one was open for 0% -> 0% of each run, Pallas kernels for 27% -> 28%
where the time goes in v13:
time: 54 us; the launch traced here: 53.8 us
  Pallas kernels  32.8 us (61%)
  starting transfers between devices  15.1 us (28%)
  waiting for transfers between devices  4.9 us (9%)
  between operations  0.98 us (2%)
    pallas_call x15, Pallas kernels, call(): pl.pallas_call(seen, out_shape=shapes, in_specs=[pl.BlockSpec(memory_spac...  32.8 us
    ppermute x11, starting transfers between devices, flip(): return lax.ppermute(value, axes, [(i, i ^ bit) for i in range(n)])  15.1 us
    ppermute x11, waiting for transfers between devices, flip(): return lax.ppermute(value, axes, [(i, i ^ bit) for i in range(n)])  4.9 us
  transfers between devices with their start and end apart: 11, of which 5 were waited for; matrix products, arithmetic and copies ran while one was open for 0% of the time, Pallas kernels for 28%

profile of v13, /device:TPU:0, one launch (start us, length us, event | category | flops | bytes accessed | tf_op | source)
XLA Modules:
  0.0 53.8 jit_solution(8493926610009161378)
XLA Ops:
  0.6 0.7 %pack.1 = (bf16[10,1536,1024]{2,1,0:T(8,128)(2,1)S(1)}, bf16[2,3200]{1,0:T(2,128)(2,1)S(1)}) custom-call(s32[2]{0:T(128)} %refs_0_.1, bf16[2,1536]{1,0:T(2,128)(2,1)} %refs_1_.5, bf16[2,1536]{1,0:T(2,128)(2,1)} %refs_2_.5), custom_call_target="tpu_custom_call" | custom-call | tf_op jit(solution)/shard_map/pack/pallas_call | solution.py:59
  1.4 5.1 %collective-permute-start.2 = (bf16[2,3200]{1,0:T(2,128)(2,1)S(1)}, bf16[2,3200]{1,0:T(2,128)(2,1)S(1)}, u32[]{:S(2)}, u32[]{:S(2)}) collective-permute-start(bf16[2,3200]{1,0:T(2,128)(2,1)S(1)} %get-tuple-element.24.refs_0_), channel_id=1, source_target_pairs={{0,12},{4,8},{8,4},{12,0},{16,28},{20,24},{24,20},{28,16},{1,13},{... | collective-permute-start | bytes 38408 | tf_op jit(solution)/shard_map/ppermute | solution.py:414
  6.5 0.6 %collective-permute-start = (bf16[2,3200]{1,0:T(2,128)(2,1)S(1)}, bf16[2,3200]{1,0:T(2,128)(2,1)S(1)}, u32[]{:S(2)}, u32[]{:S(2)}) collective-permute-start(bf16[2,3200]{1,0:T(2,128)(2,1)S(1)} %get-tuple-element.24.refs_0_), channel_id=1, source_target_pairs={{0,8},{4,12},{8,0},{12,4},{16,24},{20,28},{24,16},{28,20},{1,9},{5... | collective-permute-start | bytes 38408 | tf_op jit(solution)/shard_map/ppermute | solution.py:414
  7.2 3.0 %load_gate_text.1.refs_4_.refs_2_.refs_6_ = bf16[10,1536,1024]{2,1,0:T(8,128)(2,1)S(1)} custom-call(bf16[2,3200]{1,0:T(2,128)(2,1)S(1)} %get-tuple-element.24.refs_0_, bf16[1536,2048]{1,0:T(8,128)(2,1)} %refs_1_.6, bf16[10,1536,1024]{2,1,0:T(8,128)(2,1)S(1)} %get-tuple-element.25.refs_2_), custom_call_target="tpu_custom_call", output_to_operand_aliasing={{}: (2, {})} | custom-call | bytes 6291456 | tf_op jit(solution)/shard_map/load_gate_text/pallas_call | solution.py:59
  10.2 0.9 %collective-permute-done.refs_1_ = bf16[2,3200]{1,0:T(2,128)(2,1)S(1)} collective-permute-done((bf16[2,3200]{1,0:T(2,128)(2,1)S(1)}, bf16[2,3200]{1,0:T(2,128)(2,1)S(1)}, u32[]{:S(2)}, u32[]{:S(2)}) %collective-permute-start) | collective-permute-done | bytes 12832 | tf_op jit(solution)/shard_map/ppermute | solution.py:414
  11.1 1.6 %collective-permute-start.3 = (bf16[8,3200]{1,0:T(8,128)(2,1)S(1)}, bf16[8,3200]{1,0:T(8,128)(2,1)S(1)}, u32[]{:S(2)}, u32[]{:S(2)}) collective-permute-start(bf16[8,3200]{1,0:T(8,128)(2,1)S(1)} %join_8.1.refs_0_), channel_id=1, source_target_pairs={{0,16},{4,20},{8,24},{12,28},{16,0},{20,4},{24,8},{28,12},{1,17},{... | collective-permute-start | bytes 153608 | tf_op jit(solution)/shard_map/ppermute | solution.py:414
  12.7 2.6 %collective-permute-done.3.refs_1_ = bf16[8,3200]{1,0:T(8,128)(2,1)S(1)} collective-permute-done((bf16[8,3200]{1,0:T(8,128)(2,1)S(1)}, bf16[8,3200]{1,0:T(8,128)(2,1)S(1)}, u32[]{:S(2)}, u32[]{:S(2)}) %collective-permute-start.3) | collective-permute-done | bytes 51232 | tf_op jit(solution)/shard_map/ppermute | solution.py:414
  15.4 9.4 %hidden_partials.1 = (f32[3,16,1536]{2,1,0:T(8,128)S(1)}, f32[3,16,1536]{2,1,0:T(8,128)S(1)}, bf16[10,1536,1024]{2,1,0:T(8,128)(2,1)S(1)}) custom-call(bf16[16,3200]{1,0:T(8,128)(2,1)S(1)} %join_16.1.refs_0_.refs_1_, bf16[2048,1536]{1,0:T(8,128)(2,1)S(1)} %bitcast.3, bf16[3072,1536]{1,0:T(8,128)(2,1)S(1)} %bitcast.1, ...), custom_call_target="tpu_custom_call", output_to_operand_aliasing={{2}: (6, {})} | custom-call | flops 754974720 | bytes 25165824 | tf_op jit(solution)/shard_map/hidden_partials/pallas_call | solution.py:59
  24.8 0.1 collective-permute-start.4
  24.8 1.4 %turn_1.1.refs_2_.refs_0_ = bf16[10,1536,1024]{2,1,0:T(8,128)(2,1)S(1)} custom-call(bf16[10,1536,1024]{2,1,0:T(8,128)(2,1)S(1)} %get-tuple-element.28.refs_0_, bf16[2048,1536]{1,0:T(8,128)(2,1)S(1)} %bitcast.3, bf16[3072,1536]{1,0:T(8,128)(2,1)S(1)} %bitcast.1), custom_call_target="tpu_custom_call", output_to_operand_aliasing={{}: (0, {})} | custom-call | bytes 15728640 | tf_op jit(solution)/shard_map/turn_1/pallas_call | solution.py:59
  26.3 0.1 collective-permute-done.4.refs_1_
  26.4 1.6 %collective-permute-start.5 = (bf16[3,16,1536]{2,1,0:T(8,128)(2,1)S(1)}, bf16[3,16,1536]{2,1,0:T(8,128)(2,1)S(1)}, u32[]{:S(2)}, u32[]{:S(2)}) collective-permute-start(bf16[3,16,1536]{2,1,0:T(8,128)(2,1)S(1)} %get-tuple-element.30), channel_id=1, source_target_pairs={{0,2},{1,3},{2,0},{3,1},{4,6},{5,7},{6,4},{7,5},{8,10},{9,11},{10,... | collective-permute-start | bytes 442376 | tf_op jit(solution)/shard_map/ppermute | solution.py:414
  28.0 3.9 %turn_2.1.refs_2_.refs_4_ = bf16[10,1536,1024]{2,1,0:T(8,128)(2,1)S(1)} custom-call(bf16[10,1536,1024]{2,1,0:T(8,128)(2,1)S(1)} %turn_1.1.refs_2_.refs_0_, bf16[2048,1536]{1,0:T(8,128)(2,1)S(1)} %bitcast.3, bf16[3072,1536]{1,0:T(8,128)(2,1)S(1)} %bitcast.1), custom_call_target="tpu_custom_call", output_to_operand_aliasing={{}: (0, {})} | custom-call | bytes 47185920 | tf_op jit(solution)/shard_map/turn_2/pallas_call | solution.py:59
  31.9 0.7 %collective-permute-done.5.refs_1_ = bf16[3,16,1536]{2,1,0:T(8,128)(2,1)S(1)} collective-permute-done((bf16[3,16,1536]{2,1,0:T(8,128)(2,1)S(1)}, bf16[3,16,1536]{2,1,0:T(8,128)(2,1)S(1)}, u32[]{:S(2)}, u32[]{:S(2)}) %collective-permute-start.5) | collective-permute-done | bytes 147488 | tf_op jit(solution)/shard_map/ppermute | solution.py:414
  32.8 1.3 %mixed_own.1.refs_3_ = f32[16,1536]{1,0:T(8,128)S(1)} custom-call(bf16[16,3200]{1,0:T(8,128)(2,1)S(1)} %join_16.1.refs_0_.refs_1_, bf16[3,16,1536]{2,1,0:T(8,128)(2,1)S(1)} %hidden.1.refs_1_, bf16[2048,1536]{1,0:T(8,128)(2,1)S(1)} %bitcast.3, bf16[3072,1536]{1,0:T(8,128)(2,1)S(1)} %bitcast.1, bf16[10,1536,1024]{2,1,0:T(8,128)(2,1)S(1)} %turn_2.1.refs_2_.refs_4_), custom_call_target="tpu_custom_call" | custom-call | flops 125829120 | tf_op jit(solution)/shard_map/mixed_own/pallas_call | solution.py:59
  34.2 7.0 %token_partials.1 = (f32[8,3072]{1,0:T(8,128)S(1)}, bf16[8,3072]{1,0:T(8,128)(2,1)S(1)}, bf16[16,3072]{1,0:T(8,128)(2,1)S(1)}, bf16[16,2048]{1,0:T(8,128)(2,1)S(1)}, bf16[3072,1536]{1,0:T(8,128)(2,1)}) custom-call(bf16[16,3200]{1,0:T(8,128)(2,1)S(1)} %join_16.1.refs_0_.refs_1_, bf16[3,16,1536]{2,1,0:T(8,128)(2,1)S(1)} %hidden.1.refs_1_, ...), custom_call_target="tpu_custom_call" | custom-call | flops 754974720 | tf_op jit(solution)/shard_map/token_partials/pallas_call | solution.py:59
  41.1 1.6 %collective-permute-start.7 = (bf16[8,3072]{1,0:T(8,128)(2,1)S(1)}, bf16[8,3072]{1,0:T(8,128)(2,1)S(1)}, u32[]{:S(2)}, u32[]{:S(2)}) collective-permute-start(bf16[8,3072]{1,0:T(8,128)(2,1)S(1)} %get-tuple-element.32), channel_id=1, source_target_pairs={{0,16},{4,20},{8,24},{12,28},{16,0},{20,4},{24,8},{28,12},{1,17},{... | collective-permute-start | bytes 147464 | tf_op jit(solution)/shard_map/ppermute | solution.py:414
  42.7 2.6 %down_grad_1.1 = (bf16[3072,1536]{1,0:T(8,128)(2,1)}, bf16[2048,1536]{1,0:T(8,128)(2,1)}) custom-call(f32[8,3072]{1,0:T(8,128)S(1)} %get-tuple-element.31.refs_0_, bf16[16,3200]{1,0:T(8,128)(2,1)S(1)} %join_16.1.refs_0_.refs_1_, bf16[16,3072]{1,0:T(8,128)(2,1)S(1)} %get-tuple-element.33.refs_2_, ...), custom_call_target="tpu_custom_call", output_to_operand_aliasing={{0}: (4, {})} | custom-call | flops 75497472 | bytes 4718592 | tf_op jit(solution)/shard_map/down_grad_1/pallas_call | solution.py:59
  45.4 3.0 %collective-permute-start.8 = (bf16[2,3072]{1,0:T(2,128)(2,1)S(1)}, bf16[2,3072]{1,0:T(2,128)(2,1)S(1)}, u32[]{:S(2)}, u32[]{:S(2)}) collective-permute-start(bf16[2,3072]{1,0:T(2,128)(2,1)S(1)} %get-tuple-element.38), channel_id=1, source_target_pairs={{0,12},{4,8},{8,4},{12,0},{16,28},{20,24},{24,20},{28,16},{1,13},{... | collective-permute-start | bytes 36872 | tf_op jit(solution)/shard_map/ppermute | solution.py:414
  48.4 0.5 %collective-permute-start.9 = (bf16[2,3072]{1,0:T(2,128)(2,1)S(1)}, bf16[2,3072]{1,0:T(2,128)(2,1)S(1)}, u32[]{:S(2)}, u32[]{:S(2)}) collective-permute-start(bf16[2,3072]{1,0:T(2,128)(2,1)S(1)} %get-tuple-element.39), channel_id=1, source_target_pairs={{0,8},{4,12},{8,0},{12,4},{16,24},{20,28},{24,16},{28,20},{1,9},{5... | collective-permute-start | bytes 36872 | tf_op jit(solution)/shard_map/ppermute | solution.py:414
  48.9 0.9 %collective-permute-start.10 = (bf16[2,3072]{1,0:T(2,128)(2,1)S(1)}, bf16[2,3072]{1,0:T(2,128)(2,1)S(1)}, u32[]{:S(2)}, u32[]{:S(2)}) collective-permute-start(bf16[2,3072]{1,0:T(2,128)(2,1)S(1)} %get-tuple-element.40), channel_id=1, source_target_pairs={{0,4},{4,0},{8,12},{12,8},{16,20},{20,16},{24,28},{28,24},{1,5},{5... | collective-permute-start | bytes 36872 | tf_op jit(solution)/shard_map/ppermute | solution.py:414
  49.8 2.6 %down_grad_2.1 = bf16[2048,1536]{1,0:T(8,128)(2,1)} custom-call(f32[2,3072]{1,0:T(2,128)S(1)} %get-tuple-element.37.refs_0_, bf16[16,3200]{1,0:T(8,128)(2,1)S(1)} %join_16.1.refs_0_.refs_1_, bf16[16,3072]{1,0:T(8,128)(2,1)S(1)} %get-tuple-element.33.refs_2_, bf16[16,2048]{1,0:T(8,128)(2,1)S(1)} %get-tuple-element.34.refs_3_, ...), custom_call_target="tpu_custom_call", output_to_operand_aliasing={{}: (4, {})} | custom-call | flops 75497472 | bytes 4718592 | tf_op jit(solution)/shard_map/down_grad_2/pallas_call | solution.py:59
  52.5 0.5 collective-permute-done.9.refs_2_
  53.0 0.6 %token_sum_1.1 = (bf16[2,1536]{1,0:T(2,128)(2,1)}, bf16[2,1536]{1,0:T(2,128)(2,1)}) custom-call(f32[2,3072]{1,0:T(2,128)S(1)} %get-tuple-element.37.refs_0_, bf16[2,3072]{1,0:T(2,128)(2,1)S(1)} %collective-permute-done.8.refs_1_, bf16[2,3072]{1,0:T(2,128)(2,1)S(1)} %collective-permute-done.9.refs_2_, bf16[2,3072]{1,0:T(2,128)(2,1)S(1)} %collective-permute-done.10.refs_3_), custom_call_target="tpu_custom_call" | custom-call | tf_op jit(solution)/shard_map/token_sum_1/pallas_call | solution.py:59
  (25 shorter events, 0.3 us)
Async XLA Ops:
  1.4 8.8 %collective-permute-start.2 = (bf16[2,3200]{1,0:T(2,128)(2,1)S(1)}, bf16[2,3200]{1,0:T(2,128)(2,1)S(1)}, u32[]{:S(2)}, u32[]{:S(2)}) collective-permute-start(bf16[2,3200]{1,0:T(2,128)(2,1)S(1)} %get-tuple-element.24.refs_0_), channel_id=1, source_target_pairs={{0,12},{4,8},{8,4},{12,0},{16,28},{20,24},{24,20},{28,16},{1,13},{... | collective-permute-start | bytes 38408 | tf_op jit(solution)/shard_map/ppermute | solution.py:414
  6.5 3.7 %collective-permute-start.1 = (bf16[2,3200]{1,0:T(2,128)(2,1)S(1)}, bf16[2,3200]{1,0:T(2,128)(2,1)S(1)}, u32[]{:S(2)}, u32[]{:S(2)}) collective-permute-start(bf16[2,3200]{1,0:T(2,128)(2,1)S(1)} %get-tuple-element.24.refs_0_), channel_id=1, source_target_pairs={{0,4},{4,0},{8,12},{12,8},{16,20},{20,16},{24,28},{28,24},{1,5},{5... | collective-permute-start | bytes 38408 | tf_op jit(solution)/shard_map/ppermute | solution.py:414
  6.5 4.6 %collective-permute-start = (bf16[2,3200]{1,0:T(2,128)(2,1)S(1)}, bf16[2,3200]{1,0:T(2,128)(2,1)S(1)}, u32[]{:S(2)}, u32[]{:S(2)}) collective-permute-start(bf16[2,3200]{1,0:T(2,128)(2,1)S(1)} %get-tuple-element.24.refs_0_), channel_id=1, source_target_pairs={{0,8},{4,12},{8,0},{12,4},{16,24},{20,28},{24,16},{28,20},{1,9},{5... | collective-permute-start | bytes 38408 | tf_op jit(solution)/shard_map/ppermute | solution.py:414
  7.1 8.2 %slice-start = ((s8[9437184]{0:T(1024)(128)(4,1)}), s8[4194304]{0:T(1024)(128)(4,1)S(1)}, s32[]{:S(2)}) async-start(s8[9437184]{0:T(1024)(128)(4,1)} %bitcast), calls=%async_computation | async-start | bytes 8388608
  7.1 8.2 %slice-start.3 = ((s8[6291456]{0:T(1024)(128)(4,1)}), s8[4194304]{0:T(1024)(128)(4,1)S(1)}, s32[]{:S(2)}) async-start(s8[6291456]{0:T(1024)(128)(4,1)} %bitcast.2), calls=%async_computation.3 | async-start | bytes 8388608
  7.1 8.2 %slice-start.1 = ((s8[9437184]{0:T(1024)(128)(4,1)}), s8[4194304]{0:T(1024)(128)(4,1)S(1)}, s32[]{:S(2)}) async-start(s8[9437184]{0:T(1024)(128)(4,1)} %bitcast), calls=%async_computation.1 | async-start | bytes 8388608
  7.1 8.2 %slice-start.2 = ((s8[9437184]{0:T(1024)(128)(4,1)}), s8[1048576]{0:T(1024)(128)(4,1)S(1)}, s32[]{:S(2)}) async-start(s8[9437184]{0:T(1024)(128)(4,1)} %bitcast), calls=%async_computation.2 | async-start | bytes 2097152
  7.1 8.2 %slice-start.4 = ((s8[6291456]{0:T(1024)(128)(4,1)}), s8[2097152]{0:T(1024)(128)(4,1)S(1)}, s32[]{:S(2)}) async-start(s8[6291456]{0:T(1024)(128)(4,1)} %bitcast.2), calls=%async_computation.4 | async-start | bytes 4194304
  11.1 4.2 %collective-permute-start.3 = (bf16[8,3200]{1,0:T(8,128)(2,1)S(1)}, bf16[8,3200]{1,0:T(8,128)(2,1)S(1)}, u32[]{:S(2)}, u32[]{:S(2)}) collective-permute-start(bf16[8,3200]{1,0:T(8,128)(2,1)S(1)} %join_8.1.refs_0_), channel_id=1, source_target_pairs={{0,16},{4,20},{8,24},{12,28},{16,0},{20,4},{24,8},{28,12},{1,17},{... | collective-permute-start | bytes 153608 | tf_op jit(solution)/shard_map/ppermute | solution.py:414
  24.8 1.6 %collective-permute-start.4 = (f32[3,16,1536]{2,1,0:T(8,128)S(1)}, f32[3,16,1536]{2,1,0:T(8,128)S(1)}, u32[]{:S(2)}, u32[]{:S(2)}) collective-permute-start(f32[3,16,1536]{2,1,0:T(8,128)S(1)} %get-tuple-element.27), channel_id=1, source_target_pairs={{0,1},{1,0},{2,3},{3,2},{4,5},{5,4},{6,7},{7,6},{8,9},{9,8},{10,11... | collective-permute-start | bytes 884744 | tf_op jit(solution)/shard_map/ppermute | solution.py:414
  26.4 6.2 %collective-permute-start.5 = (bf16[3,16,1536]{2,1,0:T(8,128)(2,1)S(1)}, bf16[3,16,1536]{2,1,0:T(8,128)(2,1)S(1)}, u32[]{:S(2)}, u32[]{:S(2)}) collective-permute-start(bf16[3,16,1536]{2,1,0:T(8,128)(2,1)S(1)} %get-tuple-element.30), channel_id=1, source_target_pairs={{0,2},{1,3},{2,0},{3,1},{4,6},{5,7},{6,4},{7,5},{8,10},{9,11},{10,... | collective-permute-start | bytes 442376 | tf_op jit(solution)/shard_map/ppermute | solution.py:414
  32.7 1.4 %collective-permute-start.6 = (bf16[3,16,1536]{2,1,0:T(8,128)(2,1)S(1)}, bf16[3,16,1536]{2,1,0:T(8,128)(2,1)S(1)}, u32[]{:S(2)}, u32[]{:S(2)}) collective-permute-start(bf16[3,16,1536]{2,1,0:T(8,128)(2,1)S(1)} %hidden.1.refs_1_), channel_id=1, source_target_pairs={{0,1},{1,0},{2,3},{3,2},{4,5},{5,4},{6,7},{7,6},{8,9},{9,8},{10,11... | collective-permute-start | bytes 442376 | tf_op jit(solution)/shard_map/ppermute | solution.py:414
  41.1 4.2 %collective-permute-start.7 = (bf16[8,3072]{1,0:T(8,128)(2,1)S(1)}, bf16[8,3072]{1,0:T(8,128)(2,1)S(1)}, u32[]{:S(2)}, u32[]{:S(2)}) collective-permute-start(bf16[8,3072]{1,0:T(8,128)(2,1)S(1)} %get-tuple-element.32), channel_id=1, source_target_pairs={{0,16},{4,20},{8,24},{12,28},{16,0},{20,4},{24,8},{28,12},{1,17},{... | collective-permute-start | bytes 147464 | tf_op jit(solution)/shard_map/ppermute | solution.py:414
  45.4 7.1 %collective-permute-start.8 = (bf16[2,3072]{1,0:T(2,128)(2,1)S(1)}, bf16[2,3072]{1,0:T(2,128)(2,1)S(1)}, u32[]{:S(2)}, u32[]{:S(2)}) collective-permute-start(bf16[2,3072]{1,0:T(2,128)(2,1)S(1)} %get-tuple-element.38), channel_id=1, source_target_pairs={{0,12},{4,8},{8,4},{12,0},{16,28},{20,24},{24,20},{28,16},{1,13},{... | collective-permute-start | bytes 36872 | tf_op jit(solution)/shard_map/ppermute | solution.py:414
  48.4 4.6 %collective-permute-start.9 = (bf16[2,3072]{1,0:T(2,128)(2,1)S(1)}, bf16[2,3072]{1,0:T(2,128)(2,1)S(1)}, u32[]{:S(2)}, u32[]{:S(2)}) collective-permute-start(bf16[2,3072]{1,0:T(2,128)(2,1)S(1)} %get-tuple-element.39), channel_id=1, source_target_pairs={{0,8},{4,12},{8,0},{12,4},{16,24},{20,28},{24,16},{28,20},{1,9},{5... | collective-permute-start | bytes 36872 | tf_op jit(solution)/shard_map/ppermute | solution.py:414
  48.9 4.1 %collective-permute-start.10 = (bf16[2,3072]{1,0:T(2,128)(2,1)S(1)}, bf16[2,3072]{1,0:T(2,128)(2,1)S(1)}, u32[]{:S(2)}, u32[]{:S(2)}) collective-permute-start(bf16[2,3072]{1,0:T(2,128)(2,1)S(1)} %get-tuple-element.40), channel_id=1, source_target_pairs={{0,4},{4,0},{8,12},{12,8},{16,20},{20,16},{24,28},{28,24},{1,5},{5... | collective-permute-start | bytes 36872 | tf_op jit(solution)/shard_map/ppermute | solution.py:414

commit v14 on v13

--- a/solution.py
+++ b/solution.py
@@ -18,8 +18,8 @@
 ROWS = 256
 TILE = 128
 TURN_FIRST = 5
-EARLY_ROWS = 2048
-TEXT_FIRST = 2
+EARLY_ROWS = 1792
+TEXT_FIRST = 1
 PLACES = {"h": pl.ANY, "v": pltpu.VMEM, "s": pltpu.SMEM}
 
 

time: 54 us -> 53.8 us (level)
  no operation moved by 1% of the time
where the time goes in v14:
time: 53.8 us; the launch traced here: 53.6 us
  Pallas kernels  32.8 us (61%)
  starting transfers between devices  15.1 us (28%)
  waiting for transfers between devices  4.64 us (9%)
  between operations  0.98 us (2%)
    pallas_call x15, Pallas kernels, call(): pl.pallas_call(seen, out_shape=shapes, in_specs=[pl.BlockSpec(memory_spac...  32.8 us
    ppermute x11, starting transfers between devices, flip(): return lax.ppermute(value, axes, [(i, i ^ bit) for i in range(n)])  15.1 us
    ppermute x11, waiting for transfers between devices, flip(): return lax.ppermute(value, axes, [(i, i ^ bit) for i in range(n)])  4.64 us
  transfers between devices with their start and end apart: 11, of which 5 were waited for; matrix products, arithmetic and copies ran while one was open for 0% of the time, Pallas kernels for 28%

profile of v14, /device:TPU:0, one launch (start us, length us, event | category | flops | bytes accessed | tf_op | source)
XLA Modules:
  0.0 53.6 jit_solution(15226605374853201674)
XLA Ops:
  0.6 0.7 %pack.1 = (bf16[10,1536,1024]{2,1,0:T(8,128)(2,1)S(1)}, bf16[2,3200]{1,0:T(2,128)(2,1)S(1)}) custom-call(s32[2]{0:T(128)} %refs_0_.1, bf16[2,1536]{1,0:T(2,128)(2,1)} %refs_1_.5, bf16[2,1536]{1,0:T(2,128)(2,1)} %refs_2_.5), custom_call_target="tpu_custom_call" | custom-call | tf_op jit(solution)/shard_map/pack/pallas_call | solution.py:59
  1.4 5.1 %collective-permute-start.2 = (bf16[2,3200]{1,0:T(2,128)(2,1)S(1)}, bf16[2,3200]{1,0:T(2,128)(2,1)S(1)}, u32[]{:S(2)}, u32[]{:S(2)}) collective-permute-start(bf16[2,3200]{1,0:T(2,128)(2,1)S(1)} %get-tuple-element.24.refs_0_), channel_id=1, source_target_pairs={{0,12},{4,8},{8,4},{12,0},{16,28},{20,24},{24,20},{28,16},{1,13},{... | collective-permute-start | bytes 38408 | tf_op jit(solution)/shard_map/ppermute | solution.py:414
  6.5 0.6 %collective-permute-start = (bf16[2,3200]{1,0:T(2,128)(2,1)S(1)}, bf16[2,3200]{1,0:T(2,128)(2,1)S(1)}, u32[]{:S(2)}, u32[]{:S(2)}) collective-permute-start(bf16[2,3200]{1,0:T(2,128)(2,1)S(1)} %get-tuple-element.24.refs_0_), channel_id=1, source_target_pairs={{0,8},{4,12},{8,0},{12,4},{16,24},{20,28},{24,16},{28,20},{1,9},{5... | collective-permute-start | bytes 38408 | tf_op jit(solution)/shard_map/ppermute | solution.py:414
  7.2 3.0 %load_gate_text.1.refs_4_.refs_2_.refs_6_ = bf16[10,1536,1024]{2,1,0:T(8,128)(2,1)S(1)} custom-call(bf16[2,3200]{1,0:T(2,128)(2,1)S(1)} %get-tuple-element.24.refs_0_, bf16[1536,2048]{1,0:T(8,128)(2,1)} %refs_1_.6, bf16[10,1536,1024]{2,1,0:T(8,128)(2,1)S(1)} %get-tuple-element.25.refs_2_), custom_call_target="tpu_custom_call", output_to_operand_aliasing={{}: (2, {})} | custom-call | bytes 6291456 | tf_op jit(solution)/shard_map/load_gate_text/pallas_call | solution.py:59
  10.2 0.9 %collective-permute-done.refs_1_ = bf16[2,3200]{1,0:T(2,128)(2,1)S(1)} collective-permute-done((bf16[2,3200]{1,0:T(2,128)(2,1)S(1)}, bf16[2,3200]{1,0:T(2,128)(2,1)S(1)}, u32[]{:S(2)}, u32[]{:S(2)}) %collective-permute-start) | collective-permute-done | bytes 12832 | tf_op jit(solution)/shard_map/ppermute | solution.py:414
  11.1 1.6 %collective-permute-start.3 = (bf16[8,3200]{1,0:T(8,128)(2,1)S(1)}, bf16[8,3200]{1,0:T(8,128)(2,1)S(1)}, u32[]{:S(2)}, u32[]{:S(2)}) collective-permute-start(bf16[8,3200]{1,0:T(8,128)(2,1)S(1)} %join_8.1.refs_0_), channel_id=1, source_target_pairs={{0,16},{4,20},{8,24},{12,28},{16,0},{20,4},{24,8},{28,12},{1,17},{... | collective-permute-start | bytes 153608 | tf_op jit(solution)/shard_map/ppermute | solution.py:414
  12.7 2.6 %collective-permute-done.3.refs_1_ = bf16[8,3200]{1,0:T(8,128)(2,1)S(1)} collective-permute-done((bf16[8,3200]{1,0:T(8,128)(2,1)S(1)}, bf16[8,3200]{1,0:T(8,128)(2,1)S(1)}, u32[]{:S(2)}, u32[]{:S(2)}) %collective-permute-start.3) | collective-permute-done | bytes 51232 | tf_op jit(solution)/shard_map/ppermute | solution.py:414
  15.4 9.4 %hidden_partials.1 = (f32[3,16,1536]{2,1,0:T(8,128)S(1)}, f32[3,16,1536]{2,1,0:T(8,128)S(1)}, bf16[10,1536,1024]{2,1,0:T(8,128)(2,1)S(1)}) custom-call(bf16[16,3200]{1,0:T(8,128)(2,1)S(1)} %join_16.1.refs_0_.refs_1_, bf16[2048,1536]{1,0:T(8,128)(2,1)S(1)} %bitcast.3, bf16[3072,1536]{1,0:T(8,128)(2,1)S(1)} %bitcast.1, ...), custom_call_target="tpu_custom_call", output_to_operand_aliasing={{2}: (6, {})} | custom-call | flops 754974720 | bytes 25165824 | tf_op jit(solution)/shard_map/hidden_partials/pallas_call | solution.py:59
  24.8 1.4 %turn_1.1.refs_2_.refs_0_ = bf16[10,1536,1024]{2,1,0:T(8,128)(2,1)S(1)} custom-call(bf16[10,1536,1024]{2,1,0:T(8,128)(2,1)S(1)} %get-tuple-element.28.refs_0_, bf16[2048,1536]{1,0:T(8,128)(2,1)S(1)} %bitcast.3, bf16[3072,1536]{1,0:T(8,128)(2,1)S(1)} %bitcast.1), custom_call_target="tpu_custom_call", output_to_operand_aliasing={{}: (0, {})} | custom-call | bytes 15728640 | tf_op jit(solution)/shard_map/turn_1/pallas_call | solution.py:59
  26.3 0.1 collective-permute-done.4.refs_1_
  26.4 1.6 %collective-permute-start.5 = (bf16[3,16,1536]{2,1,0:T(8,128)(2,1)S(1)}, bf16[3,16,1536]{2,1,0:T(8,128)(2,1)S(1)}, u32[]{:S(2)}, u32[]{:S(2)}) collective-permute-start(bf16[3,16,1536]{2,1,0:T(8,128)(2,1)S(1)} %get-tuple-element.30), channel_id=1, source_target_pairs={{0,2},{1,3},{2,0},{3,1},{4,6},{5,7},{6,4},{7,5},{8,10},{9,11},{10,... | collective-permute-start | bytes 442376 | tf_op jit(solution)/shard_map/ppermute | solution.py:414
  28.0 3.9 %turn_2.1.refs_2_.refs_4_ = bf16[10,1536,1024]{2,1,0:T(8,128)(2,1)S(1)} custom-call(bf16[10,1536,1024]{2,1,0:T(8,128)(2,1)S(1)} %turn_1.1.refs_2_.refs_0_, bf16[2048,1536]{1,0:T(8,128)(2,1)S(1)} %bitcast.3, bf16[3072,1536]{1,0:T(8,128)(2,1)S(1)} %bitcast.1), custom_call_target="tpu_custom_call", output_to_operand_aliasing={{}: (0, {})} | custom-call | bytes 47185920 | tf_op jit(solution)/shard_map/turn_2/pallas_call | solution.py:59
  31.9 0.7 %collective-permute-done.5.refs_1_ = bf16[3,16,1536]{2,1,0:T(8,128)(2,1)S(1)} collective-permute-done((bf16[3,16,1536]{2,1,0:T(8,128)(2,1)S(1)}, bf16[3,16,1536]{2,1,0:T(8,128)(2,1)S(1)}, u32[]{:S(2)}, u32[]{:S(2)}) %collective-permute-start.5) | collective-permute-done | bytes 147488 | tf_op jit(solution)/shard_map/ppermute | solution.py:414
  32.7 0.1 collective-permute-start.6
  32.8 1.3 %mixed_own.1.refs_3_ = f32[16,1536]{1,0:T(8,128)S(1)} custom-call(bf16[16,3200]{1,0:T(8,128)(2,1)S(1)} %join_16.1.refs_0_.refs_1_, bf16[3,16,1536]{2,1,0:T(8,128)(2,1)S(1)} %hidden.1.refs_1_, bf16[2048,1536]{1,0:T(8,128)(2,1)S(1)} %bitcast.3, bf16[3072,1536]{1,0:T(8,128)(2,1)S(1)} %bitcast.1, bf16[10,1536,1024]{2,1,0:T(8,128)(2,1)S(1)} %turn_2.1.refs_2_.refs_4_), custom_call_target="tpu_custom_call" | custom-call | flops 125829120 | tf_op jit(solution)/shard_map/mixed_own/pallas_call | solution.py:59
  34.2 6.7 %token_partials.1 = (f32[8,3072]{1,0:T(8,128)S(1)}, bf16[8,3072]{1,0:T(8,128)(2,1)S(1)}, bf16[16,3072]{1,0:T(8,128)(2,1)S(1)}, bf16[16,2048]{1,0:T(8,128)(2,1)S(1)}, bf16[3072,1536]{1,0:T(8,128)(2,1)}) custom-call(bf16[16,3200]{1,0:T(8,128)(2,1)S(1)} %join_16.1.refs_0_.refs_1_, bf16[3,16,1536]{2,1,0:T(8,128)(2,1)S(1)} %hidden.1.refs_1_, ...), custom_call_target="tpu_custom_call" | custom-call | flops 754974720 | tf_op jit(solution)/shard_map/token_partials/pallas_call | solution.py:59
  40.9 1.6 %collective-permute-start.7 = (bf16[8,3072]{1,0:T(8,128)(2,1)S(1)}, bf16[8,3072]{1,0:T(8,128)(2,1)S(1)}, u32[]{:S(2)}, u32[]{:S(2)}) collective-permute-start(bf16[8,3072]{1,0:T(8,128)(2,1)S(1)} %get-tuple-element.32), channel_id=1, source_target_pairs={{0,16},{4,20},{8,24},{12,28},{16,0},{20,4},{24,8},{28,12},{1,17},{... | collective-permute-start | bytes 147464 | tf_op jit(solution)/shard_map/ppermute | solution.py:414
  42.5 2.6 %down_grad_1.1 = (bf16[3072,1536]{1,0:T(8,128)(2,1)}, bf16[2048,1536]{1,0:T(8,128)(2,1)}) custom-call(f32[8,3072]{1,0:T(8,128)S(1)} %get-tuple-element.31.refs_0_, bf16[16,3200]{1,0:T(8,128)(2,1)S(1)} %join_16.1.refs_0_.refs_1_, bf16[16,3072]{1,0:T(8,128)(2,1)S(1)} %get-tuple-element.33.refs_2_, ...), custom_call_target="tpu_custom_call", output_to_operand_aliasing={{0}: (4, {})} | custom-call | flops 75497472 | bytes 4718592 | tf_op jit(solution)/shard_map/down_grad_1/pallas_call | solution.py:59
  45.2 3.0 %collective-permute-start.8 = (bf16[2,3072]{1,0:T(2,128)(2,1)S(1)}, bf16[2,3072]{1,0:T(2,128)(2,1)S(1)}, u32[]{:S(2)}, u32[]{:S(2)}) collective-permute-start(bf16[2,3072]{1,0:T(2,128)(2,1)S(1)} %get-tuple-element.38), channel_id=1, source_target_pairs={{0,12},{4,8},{8,4},{12,0},{16,28},{20,24},{24,20},{28,16},{1,13},{... | collective-permute-start | bytes 36872 | tf_op jit(solution)/shard_map/ppermute | solution.py:414
  48.2 0.5 %collective-permute-start.9 = (bf16[2,3072]{1,0:T(2,128)(2,1)S(1)}, bf16[2,3072]{1,0:T(2,128)(2,1)S(1)}, u32[]{:S(2)}, u32[]{:S(2)}) collective-permute-start(bf16[2,3072]{1,0:T(2,128)(2,1)S(1)} %get-tuple-element.39), channel_id=1, source_target_pairs={{0,8},{4,12},{8,0},{12,4},{16,24},{20,28},{24,16},{28,20},{1,9},{5... | collective-permute-start | bytes 36872 | tf_op jit(solution)/shard_map/ppermute | solution.py:414
  48.7 0.9 %collective-permute-start.10 = (bf16[2,3072]{1,0:T(2,128)(2,1)S(1)}, bf16[2,3072]{1,0:T(2,128)(2,1)S(1)}, u32[]{:S(2)}, u32[]{:S(2)}) collective-permute-start(bf16[2,3072]{1,0:T(2,128)(2,1)S(1)} %get-tuple-element.40), channel_id=1, source_target_pairs={{0,4},{4,0},{8,12},{12,8},{16,20},{20,16},{24,28},{28,24},{1,5},{5... | collective-permute-start | bytes 36872 | tf_op jit(solution)/shard_map/ppermute | solution.py:414
  49.6 2.9 %down_grad_2.1 = bf16[2048,1536]{1,0:T(8,128)(2,1)} custom-call(f32[2,3072]{1,0:T(2,128)S(1)} %get-tuple-element.37.refs_0_, bf16[16,3200]{1,0:T(8,128)(2,1)S(1)} %join_16.1.refs_0_.refs_1_, bf16[16,3072]{1,0:T(8,128)(2,1)S(1)} %get-tuple-element.33.refs_2_, bf16[16,2048]{1,0:T(8,128)(2,1)S(1)} %get-tuple-element.34.refs_3_, ...), custom_call_target="tpu_custom_call", output_to_operand_aliasing={{}: (4, {})} | custom-call | flops 88080384 | bytes 5505024 | tf_op jit(solution)/shard_map/down_grad_2/pallas_call | solution.py:59
  52.5 0.3 collective-permute-done.9.refs_2_
  52.8 0.6 %token_sum_1.1 = (bf16[2,1536]{1,0:T(2,128)(2,1)}, bf16[2,1536]{1,0:T(2,128)(2,1)}) custom-call(f32[2,3072]{1,0:T(2,128)S(1)} %get-tuple-element.37.refs_0_, bf16[2,3072]{1,0:T(2,128)(2,1)S(1)} %collective-permute-done.8.refs_1_, bf16[2,3072]{1,0:T(2,128)(2,1)S(1)} %collective-permute-done.9.refs_2_, bf16[2,3072]{1,0:T(2,128)(2,1)S(1)} %collective-permute-done.10.refs_3_), custom_call_target="tpu_custom_call" | custom-call | tf_op jit(solution)/shard_map/token_sum_1/pallas_call | solution.py:59
  (25 shorter events, 0.3 us)
Async XLA Ops:
  1.4 8.8 %collective-permute-start.2 = (bf16[2,3200]{1,0:T(2,128)(2,1)S(1)}, bf16[2,3200]{1,0:T(2,128)(2,1)S(1)}, u32[]{:S(2)}, u32[]{:S(2)}) collective-permute-start(bf16[2,3200]{1,0:T(2,128)(2,1)S(1)} %get-tuple-element.24.refs_0_), channel_id=1, source_target_pairs={{0,12},{4,8},{8,4},{12,0},{16,28},{20,24},{24,20},{28,16},{1,13},{... | collective-permute-start | bytes 38408 | tf_op jit(solution)/shard_map/ppermute | solution.py:414
  6.5 3.7 %collective-permute-start.1 = (bf16[2,3200]{1,0:T(2,128)(2,1)S(1)}, bf16[2,3200]{1,0:T(2,128)(2,1)S(1)}, u32[]{:S(2)}, u32[]{:S(2)}) collective-permute-start(bf16[2,3200]{1,0:T(2,128)(2,1)S(1)} %get-tuple-element.24.refs_0_), channel_id=1, source_target_pairs={{0,4},{4,0},{8,12},{12,8},{16,20},{20,16},{24,28},{28,24},{1,5},{5... | collective-permute-start | bytes 38408 | tf_op jit(solution)/shard_map/ppermute | solution.py:414
  6.5 4.6 %collective-permute-start = (bf16[2,3200]{1,0:T(2,128)(2,1)S(1)}, bf16[2,3200]{1,0:T(2,128)(2,1)S(1)}, u32[]{:S(2)}, u32[]{:S(2)}) collective-permute-start(bf16[2,3200]{1,0:T(2,128)(2,1)S(1)} %get-tuple-element.24.refs_0_), channel_id=1, source_target_pairs={{0,8},{4,12},{8,0},{12,4},{16,24},{20,28},{24,16},{28,20},{1,9},{5... | collective-permute-start | bytes 38408 | tf_op jit(solution)/shard_map/ppermute | solution.py:414
  7.1 8.2 %slice-start = ((s8[9437184]{0:T(1024)(128)(4,1)}), s8[4194304]{0:T(1024)(128)(4,1)S(1)}, s32[]{:S(2)}) async-start(s8[9437184]{0:T(1024)(128)(4,1)} %bitcast), calls=%async_computation | async-start | bytes 8388608
  7.1 8.2 %slice-start.3 = ((s8[6291456]{0:T(1024)(128)(4,1)}), s8[4194304]{0:T(1024)(128)(4,1)S(1)}, s32[]{:S(2)}) async-start(s8[6291456]{0:T(1024)(128)(4,1)} %bitcast.2), calls=%async_computation.3 | async-start | bytes 8388608
  7.1 8.2 %slice-start.1 = ((s8[9437184]{0:T(1024)(128)(4,1)}), s8[4194304]{0:T(1024)(128)(4,1)S(1)}, s32[]{:S(2)}) async-start(s8[9437184]{0:T(1024)(128)(4,1)} %bitcast), calls=%async_computation.1 | async-start | bytes 8388608
  7.1 8.2 %slice-start.2 = ((s8[9437184]{0:T(1024)(128)(4,1)}), s8[1048576]{0:T(1024)(128)(4,1)S(1)}, s32[]{:S(2)}) async-start(s8[9437184]{0:T(1024)(128)(4,1)} %bitcast), calls=%async_computation.2 | async-start | bytes 2097152
  7.1 8.2 %slice-start.4 = ((s8[6291456]{0:T(1024)(128)(4,1)}), s8[2097152]{0:T(1024)(128)(4,1)S(1)}, s32[]{:S(2)}) async-start(s8[6291456]{0:T(1024)(128)(4,1)} %bitcast.2), calls=%async_computation.4 | async-start | bytes 4194304
  11.1 4.2 %collective-permute-start.3 = (bf16[8,3200]{1,0:T(8,128)(2,1)S(1)}, bf16[8,3200]{1,0:T(8,128)(2,1)S(1)}, u32[]{:S(2)}, u32[]{:S(2)}) collective-permute-start(bf16[8,3200]{1,0:T(8,128)(2,1)S(1)} %join_8.1.refs_0_), channel_id=1, source_target_pairs={{0,16},{4,20},{8,24},{12,28},{16,0},{20,4},{24,8},{28,12},{1,17},{... | collective-permute-start | bytes 153608 | tf_op jit(solution)/shard_map/ppermute | solution.py:414
  24.8 1.6 %collective-permute-start.4 = (f32[3,16,1536]{2,1,0:T(8,128)S(1)}, f32[3,16,1536]{2,1,0:T(8,128)S(1)}, u32[]{:S(2)}, u32[]{:S(2)}) collective-permute-start(f32[3,16,1536]{2,1,0:T(8,128)S(1)} %get-tuple-element.27), channel_id=1, source_target_pairs={{0,1},{1,0},{2,3},{3,2},{4,5},{5,4},{6,7},{7,6},{8,9},{9,8},{10,11... | collective-permute-start | bytes 884744 | tf_op jit(solution)/shard_map/ppermute | solution.py:414
  26.4 6.2 %collective-permute-start.5 = (bf16[3,16,1536]{2,1,0:T(8,128)(2,1)S(1)}, bf16[3,16,1536]{2,1,0:T(8,128)(2,1)S(1)}, u32[]{:S(2)}, u32[]{:S(2)}) collective-permute-start(bf16[3,16,1536]{2,1,0:T(8,128)(2,1)S(1)} %get-tuple-element.30), channel_id=1, source_target_pairs={{0,2},{1,3},{2,0},{3,1},{4,6},{5,7},{6,4},{7,5},{8,10},{9,11},{10,... | collective-permute-start | bytes 442376 | tf_op jit(solution)/shard_map/ppermute | solution.py:414
  32.7 1.4 %collective-permute-start.6 = (bf16[3,16,1536]{2,1,0:T(8,128)(2,1)S(1)}, bf16[3,16,1536]{2,1,0:T(8,128)(2,1)S(1)}, u32[]{:S(2)}, u32[]{:S(2)}) collective-permute-start(bf16[3,16,1536]{2,1,0:T(8,128)(2,1)S(1)} %hidden.1.refs_1_), channel_id=1, source_target_pairs={{0,1},{1,0},{2,3},{3,2},{4,5},{5,4},{6,7},{7,6},{8,9},{9,8},{10,11... | collective-permute-start | bytes 442376 | tf_op jit(solution)/shard_map/ppermute | solution.py:414
  40.9 4.2 %collective-permute-start.7 = (bf16[8,3072]{1,0:T(8,128)(2,1)S(1)}, bf16[8,3072]{1,0:T(8,128)(2,1)S(1)}, u32[]{:S(2)}, u32[]{:S(2)}) collective-permute-start(bf16[8,3072]{1,0:T(8,128)(2,1)S(1)} %get-tuple-element.32), channel_id=1, source_target_pairs={{0,16},{4,20},{8,24},{12,28},{16,0},{20,4},{24,8},{28,12},{1,17},{... | collective-permute-start | bytes 147464 | tf_op jit(solution)/shard_map/ppermute | solution.py:414
  45.2 7.3 %collective-permute-start.8 = (bf16[2,3072]{1,0:T(2,128)(2,1)S(1)}, bf16[2,3072]{1,0:T(2,128)(2,1)S(1)}, u32[]{:S(2)}, u32[]{:S(2)}) collective-permute-start(bf16[2,3072]{1,0:T(2,128)(2,1)S(1)} %get-tuple-element.38), channel_id=1, source_target_pairs={{0,12},{4,8},{8,4},{12,0},{16,28},{20,24},{24,20},{28,16},{1,13},{... | collective-permute-start | bytes 36872 | tf_op jit(solution)/shard_map/ppermute | solution.py:414
  48.2 4.6 %collective-permute-start.9 = (bf16[2,3072]{1,0:T(2,128)(2,1)S(1)}, bf16[2,3072]{1,0:T(2,128)(2,1)S(1)}, u32[]{:S(2)}, u32[]{:S(2)}) collective-permute-start(bf16[2,3072]{1,0:T(2,128)(2,1)S(1)} %get-tuple-element.39), channel_id=1, source_target_pairs={{0,8},{4,12},{8,0},{12,4},{16,24},{20,28},{24,16},{28,20},{1,9},{5... | collective-permute-start | bytes 36872 | tf_op jit(solution)/shard_map/ppermute | solution.py:414
  48.7 4.1 %collective-permute-start.10 = (bf16[2,3072]{1,0:T(2,128)(2,1)S(1)}, bf16[2,3072]{1,0:T(2,128)(2,1)S(1)}, u32[]{:S(2)}, u32[]{:S(2)}) collective-permute-start(bf16[2,3072]{1,0:T(2,128)(2,1)S(1)} %get-tuple-element.40), channel_id=1, source_target_pairs={{0,4},{4,0},{8,12},{12,8},{16,20},{20,16},{24,28},{28,24},{1,5},{5... | collective-permute-start | bytes 36872 | tf_op jit(solution)/shard_map/ppermute | solution.py:414
